TPU v7x, 32 devices: a whole 2x2x4 slice. The times are simulated.
32 devices in a mesh: seq: 8 (over z, y), ch: 4 (over x, core).
Axes of the slice: x: 2, y: 2, z: 4, core: 2. Of those that a mesh axis runs over, the one named last changes fastest.
Arguments:
- tokens: int32 [4096], P('seq'), may hold values from 0 to 3
- hidden: bfloat16 [4096, 1024], P('seq', 'ch'), may hold values from -6 to 6
- embedding: bfloat16 [4, 1024], P(None, 'ch'), may hold values from -6 to 6
- w_in: bfloat16 [1024, 1024], P(None, 'ch'), may hold values from -0.1875 to 0.1875
- w_gate: bfloat16 [1024, 1024], P(None, 'ch'), may hold values from -0.1875 to 0.1875
- conv_w: float32 [3, 4, 1024], P(None, None, 'ch'), may hold values from -3 to 3
- channel_order: int32 [1024], replicated, may hold values from 0 to 1023, each once
- gain: float32 [1024], replicated, may hold values from 0.5 to 1.5
- w_out: bfloat16 [1024, 1024], P(None, 'ch'), may hold values from -0.1875 to 0.1875
- cotangent: bfloat16 [4096, 1024], P('seq', 'ch'), may hold values from -6 to 6
Outputs:
- output: bfloat16 [4096, 1024], P('seq', 'ch')
- grad_in: bfloat16 [1024, 1024], P(None, 'ch')
- grad_gate: bfloat16 [1024, 1024], P(None, 'ch')
- grad_out: bfloat16 [1024, 1024], P(None, 'ch')
- grad_conv: float32 [3, 4, 1024], P(None, None, 'ch')
Inputs may be any that keep to these rules, and one draw needn't show every extreme that they name: `channel_order`: each channel index once.
All inputs are finite; a program needn't handle non-finite values.
Results may differ from a plain program's by a relative error of at most 0.025.
Values may be sent and summed in bfloat16 or wider, within the bound.
No kernel may reach another device: no remote copies, remote signals or barrier semaphores. Data moves between devices by JAX's collectives and lax.ppermute only.
A program may use at most 64 MiB of HBM per device.

v0:
```python
import jax
import jax.numpy as jnp
from jax import lax
from jax.sharding import PartitionSpec as P

DILATIONS = (1, 8, 64)
EPSILON = 1e-06


def extended(cells, sides, width):
    for axis, dim in sides:
        count = lax.axis_size(axis)
        ends = count - 1
        head = lax.slice_in_dim(cells, 0, width, axis=dim)
        tail = lax.slice_in_dim(cells, cells.shape[dim] - width, cells.shape[dim], axis=dim)
        cells = jnp.concatenate(
            [
                lax.ppermute(tail, axis, [(i, (i + 1) % count) for i in range(ends)]),
                cells,
                lax.ppermute(head, axis, [((i + 1) % count, i) for i in range(ends)]),
            ],
            axis=dim,
        )
    return cells


def partner(block, axis, bit):
    count = lax.axis_size(axis)
    route = []
    for low in range(count):
        high = low | 1 << bit
        if high != low and high < count:
            route += [(low, high), (high, low)]
    return lax.ppermute(block, axis, route)


def conv_apply(padded, weights, dilation, rows):
    total = jnp.zeros((rows, padded.shape[1]), jnp.float32)
    for position in range(4):
        begin = 2 * dilation + (position - 2) * dilation
        total = total + weights[position][None, :] * padded[begin : begin + rows].astype(
            jnp.float32
        )
    return total


def conv_transpose(padded_grad, weights, dilation, rows):
    total = jnp.zeros((rows, padded_grad.shape[1]), jnp.float32)
    for position in range(4):
        begin = 2 * dilation - (position - 2) * dilation
        total = total + weights[position][None, :] * padded_grad[begin : begin + rows].astype(
            jnp.float32
        )
    return total


def conv_weight_grad(upstream, padded_source, dilation, rows):
    upstream_wide = upstream.astype(jnp.float32)
    weight_rows = []
    for position in range(4):
        start = 2 * dilation + (position - 2) * dilation
        weight_rows.append(
            jnp.sum(upstream_wide * padded_source[start : start + rows].astype(jnp.float32), axis=0)
        )
    return jnp.stack(weight_rows)


def local(tokens, hidden, embedding, w_in, w_gate, conv_w, channel_order, gain, w_out, cotangent):
    rows = hidden.shape[0]
    width_local = hidden.shape[1]
    width_full = gain.shape[0]
    start_col = lax.axis_index("ch") * width_local
    seq_bits = lax.axis_size("seq").bit_length() - 1
    one_hot = (tokens[:, None] == jnp.arange(4, dtype=jnp.int32)[None, :]).astype(jnp.bfloat16)
    embed_rows = jnp.dot(one_hot, embedding, preferred_element_type=jnp.float32)
    local_input = (hidden.astype(jnp.float32) + embed_rows).astype(jnp.bfloat16)
    full_input = lax.all_gather(local_input, "ch", axis=1, tiled=True)
    projected = jnp.dot(full_input, w_in, preferred_element_type=jnp.float32).astype(jnp.bfloat16)
    gate_pre = jnp.dot(full_input, w_gate, preferred_element_type=jnp.float32)
    saved = []
    current = projected
    for level in range(3):
        dilation = DILATIONS[level]
        padded = extended(current, (("seq", 0),), 2 * dilation)
        saved.append(padded)
        current = conv_apply(padded, conv_w[level], dilation, rows).astype(jnp.bfloat16)
    gate_act = jax.nn.silu(gate_pre)
    gated = (current.astype(jnp.float32) * gate_act).astype(jnp.bfloat16)
    gated_full = lax.all_gather(gated, "ch", axis=1, tiled=True)
    mirrored = gated_full
    for bit_number in range(seq_bits):
        mirrored = partner(mirrored, "seq", bit_number)
    mirror_full = mirrored[::-1]
    combined = gated_full.astype(jnp.float32) + jnp.take(mirror_full, channel_order, axis=1).astype(
        jnp.float32
    )
    inv_scale = lax.rsqrt(jnp.mean(combined * combined, axis=1, keepdims=True) + EPSILON)
    normalized = (combined * inv_scale * gain[None, :]).astype(jnp.bfloat16)
    output = (
        local_input.astype(jnp.float32)
        + jnp.dot(normalized, w_out, preferred_element_type=jnp.float32)
    ).astype(jnp.bfloat16)
    grad_terms = lax.dot_general(
        cotangent, w_out, (((1,), (1,)), ((), ())), preferred_element_type=jnp.float32
    )
    grad_norm = lax.psum_scatter(
        grad_terms.astype(jnp.bfloat16), "ch", scatter_dimension=1, tiled=True
    ).astype(jnp.float32)
    own_hat = lax.dynamic_slice_in_dim(combined, start_col, width_local, 1) * inv_scale
    own_gain = lax.dynamic_slice_in_dim(gain, start_col, width_local, 0)
    scaled = grad_norm * own_gain[None, :]
    row_total = lax.psum(jnp.sum(scaled * own_hat, axis=1, keepdims=True), "ch")
    grad_comb = (inv_scale * (scaled - own_hat * row_total / width_full)).astype(jnp.bfloat16)
    grad_full = lax.all_gather(grad_comb, "ch", axis=1, tiled=True)
    inverse = (
        jnp.zeros_like(channel_order).at[channel_order].set(jnp.arange(width_full, dtype=jnp.int32))
    )
    own_inverse = lax.dynamic_slice_in_dim(inverse, start_col, width_local, 0)
    grad_mirror = jnp.take(grad_full, own_inverse, axis=1)
    for bit_number in range(seq_bits):
        grad_mirror = partner(grad_mirror, "seq", bit_number)
    grad_gated = grad_comb.astype(jnp.float32) + grad_mirror[::-1].astype(jnp.float32)
    upstream = (grad_gated * gate_act).astype(jnp.bfloat16)
    sigmoid_gate = jax.nn.sigmoid(gate_pre)
    grad_gate_pre = (
        grad_gated
        * current.astype(jnp.float32)
        * sigmoid_gate
        * (1.0 + gate_pre * (1.0 - sigmoid_gate))
    ).astype(jnp.bfloat16)
    tap_grads = [None, None, None]
    for level in (2, 1, 0):
        dilation = DILATIONS[level]
        padded_grad = extended(upstream, (("seq", 0),), 2 * dilation)
        tap_grads[level] = conv_weight_grad(upstream, saved[level], dilation, rows)
        upstream = conv_transpose(padded_grad, conv_w[level], dilation, rows).astype(jnp.bfloat16)
    contract_rows = (((0,), (0,)), ((), ()))
    local_in = lax.dot_general(
        full_input, upstream, contract_rows, preferred_element_type=jnp.float32
    )
    local_gate = lax.dot_general(
        full_input, grad_gate_pre, contract_rows, preferred_element_type=jnp.float32
    )
    local_out = lax.dot_general(
        normalized, cotangent, contract_rows, preferred_element_type=jnp.float32
    )
    summed = lax.psum((local_in, local_gate, local_out, jnp.stack(tap_grads)), "seq")
    return (
        output,
        summed[0].astype(jnp.bfloat16),
        summed[1].astype(jnp.bfloat16),
        summed[2].astype(jnp.bfloat16),
        summed[3],
    )


def solution(mesh):
    placed = (
        P("seq"),
        P("seq", "ch"),
        P(None, "ch"),
        P(None, "ch"),
        P(None, "ch"),
        P(None, None, "ch"),
        P(),
        P(),
        P(None, "ch"),
        P("seq", "ch"),
    )
    return jax.shard_map(
        local,
        mesh=mesh,
        in_specs=placed,
        out_specs=(
            P("seq", "ch"),
            P(None, "ch"),
            P(None, "ch"),
            P(None, "ch"),
            P(None, None, "ch"),
        ),
        check_vma=False,
    )
```

profile of v0, /device:TPU:0, one launch (start us, length us, event | category | flops | bytes accessed | tf_op | source)
XLA Modules:
  0.0 417.8 jit_solution(251647166987030858)
XLA Ops:
  9.4 20.4 %all-gather.4.cloned.1.call-done = bf16[512,1024]{1,0:T(8,128)(2,1)} async-done(((bf16[512,256]{1,0:T(8,128)(2,1)}), bf16[512,1024]{1,0:T(8,128)(2,1)}) %all-gather.4.cloned.1.call-update) | async-done | bytes 1048592 | tf_op jit(solution)/shard_map/all_gather | solution.py:77
  33.0 4.5 %collective-permute-start = (bf16[2,256]{1,0:T(2,128)(2,1)S(1)}, bf16[2,256]{1,0:T(2,128)(2,1)S(1)}, u32[]{:S(2)}, u32[]{:S(2)}) collective-permute-start(bf16[2,256]{1,0:T(2,128)(2,1)S(1)} %get-tuple-element.40), channel_id=1, source_target_pairs={{0,4},{4,8},{8,12},{12,16},{16,20},{20,24},{24,28},{1,5},{5,9},{9,... | collective-permute-start | bytes 3080 | tf_op jit(solution)/shard_map/ppermute | solution.py:18
  40.4 4.9 %collective-permute-start.2 = (bf16[16,256]{1,0:T(8,128)(2,1)S(1)}, bf16[16,256]{1,0:T(8,128)(2,1)S(1)}, u32[]{:S(2)}, u32[]{:S(2)}) collective-permute-start(bf16[16,256]{1,0:T(8,128)(2,1)S(1)} %get-tuple-element.38), channel_id=1, source_target_pairs={{0,4},{4,8},{8,12},{12,16},{16,20},{20,24},{24,28},{1,5},{5,9},{9,... | collective-permute-start | bytes 24584 | tf_op jit(solution)/shard_map/ppermute | solution.py:18
  48.1 5.7 %collective-permute-start.4 = (bf16[128,256]{1,0:T(8,128)(2,1)S(1)}, bf16[128,256]{1,0:T(8,128)(2,1)S(1)}, u32[]{:S(2)}, u32[]{:S(2)}) collective-permute-start(bf16[128,256]{1,0:T(8,128)(2,1)S(1)} %get-tuple-element.36), channel_id=1, source_target_pairs={{0,4},{4,8},{8,12},{12,16},{16,20},{20,24},{24,28},{1,5},{5,9},{9,... | collective-permute-start | bytes 196616 | tf_op jit(solution)/shard_map/ppermute | solution.py:18
  57.5 20.6 %all-gather.6.cloned.1.call-done = bf16[512,1024]{1,0:T(8,128)(2,1)} async-done(((bf16[512,256]{1,0:T(8,128)(2,1)}), bf16[512,1024]{1,0:T(8,128)(2,1)}) %all-gather.6.cloned.1.call-update) | async-done | bytes 1048592 | tf_op jit(solution)/shard_map/all_gather | solution.py:89
  79.6 24.0 %collective-permute-done.6 = bf16[512,1024]{1,0:T(8,128)(2,1)S(1)} collective-permute-done((bf16[512,1024]{1,0:T(8,128)(2,1)}, bf16[512,1024]{1,0:T(8,128)(2,1)S(1)}, u32[]{:S(2)}, u32[]{:S(2)}) %collective-permute-start.6) | collective-permute-done | bytes 1048608 | tf_op jit(solution)/shard_map/ppermute | solution.py:34
  106.7 21.6 %collective-permute-done.7 = bf16[512,1024]{1,0:T(8,128)(2,1)} collective-permute-done((bf16[512,1024]{1,0:T(8,128)(2,1)S(1)}, bf16[512,1024]{1,0:T(8,128)(2,1)}, u32[]{:S(2)}, u32[]{:S(2)}) %collective-permute-start.7) | collective-permute-done | bytes 1048608 | tf_op jit(solution)/shard_map/ppermute | solution.py:34
  128.2 2.4 collective-permute-start.8
  132.5 42.9 %collective-permute-done.8 = bf16[512,1024]{1,0:T(8,128)(2,1)S(1)} collective-permute-done((bf16[512,1024]{1,0:T(8,128)(2,1)}, bf16[512,1024]{1,0:T(8,128)(2,1)S(1)}, u32[]{:S(2)}, u32[]{:S(2)}) %collective-permute-start.8) | collective-permute-done | bytes 1048608 | tf_op jit(solution)/shard_map/ppermute | solution.py:34
  177.2 4.0 gather_fusion
  186.4 6.4 %psum.35 = f32[512]{0:T(512)} all-reduce(f32[512]{0:T(512)} %multiply_reduce_fusion.1), channel_id=1, replica_groups=mesh['seq'=8,'ch'=4] {'ch'}, use_global_device_ids=true, to_apply=%region_3.4 | all-reduce | flops 512 | bytes 4096 | tf_op jit(solution)/shard_map/psum | solution.py:112
  195.3 5.0 %scatter_custom_fusion = s32[1024]{0:T(1024)} fusion(s32[1024]{0:T(1024)} %get-tuple-element.54, s32[1024]{0:T(1024)} %iota.7, s32[]{:T(128)} %constant.18.clone.1), kind=kCustom, calls=%fused_computation.138 | custom fusion | bytes 4608 | tf_op jit(solution)/shard_map/scatter | solution.py:116
  202.2 10.6 %all-gather.8.cloned.1.call-done = bf16[512,1024]{1,0:T(8,128)(2,1)} async-done(((bf16[512,256]{1,0:T(8,128)(2,1)}), bf16[512,1024]{1,0:T(8,128)(2,1)}) %all-gather.8.cloned.1.call-update) | async-done | bytes 1048592 | tf_op jit(solution)/shard_map/all_gather | solution.py:114
  215.1 3.4 gather_fusion.1
  222.8 7.0 %collective-permute-done.9 = bf16[512,256]{1,0:T(8,128)(2,1)S(1)} collective-permute-done((bf16[512,256]{1,0:T(8,128)(2,1)S(1)}, bf16[512,256]{1,0:T(8,128)(2,1)S(1)}, u32[]{:S(2)}, u32[]{:S(2)}) %collective-permute-start.9) | collective-permute-done | bytes 262176 | tf_op jit(solution)/shard_map/ppermute | solution.py:34
  232.8 4.6 %collective-permute-done.10 = bf16[512,256]{1,0:T(8,128)(2,1)S(1)} collective-permute-done((bf16[512,256]{1,0:T(8,128)(2,1)S(1)}, bf16[512,256]{1,0:T(8,128)(2,1)S(1)}, u32[]{:S(2)}, u32[]{:S(2)}) %collective-permute-start.10) | collective-permute-done | bytes 262176 | tf_op jit(solution)/shard_map/ppermute | solution.py:34
  241.0 9.7 %collective-permute-done.11 = bf16[512,256]{1,0:T(8,128)(2,1)} collective-permute-done((bf16[512,256]{1,0:T(8,128)(2,1)S(1)}, bf16[512,256]{1,0:T(8,128)(2,1)}, u32[]{:S(2)}, u32[]{:S(2)}) %collective-permute-start.11) | collective-permute-done | bytes 262176 | tf_op jit(solution)/shard_map/ppermute | solution.py:34
  250.8 3.2 rev.7
  255.4 3.4 collective-permute-start.13
  262.5 2.5 collective-permute-done.12
  265.3 3.2 collective-permute-start.15
  269.9 4.2 %collective-permute-done.14 = bf16[16,256]{1,0:T(8,128)(2,1)S(1)} collective-permute-done((bf16[16,256]{1,0:T(8,128)(2,1)S(1)}, bf16[16,256]{1,0:T(8,128)(2,1)S(1)}, u32[]{:S(2)}, u32[]{:S(2)}) %collective-permute-start.14) | collective-permute-done | bytes 8224 | tf_op jit(solution)/shard_map/ppermute | solution.py:20
  275.8 4.5 %collective-permute-start.17 = (bf16[2,256]{1,0:T(2,128)(2,1)S(1)}, bf16[2,256]{1,0:T(2,128)(2,1)S(1)}, u32[]{:S(2)}, u32[]{:S(2)}) collective-permute-start(bf16[2,256]{1,0:T(2,128)(2,1)S(1)} %get-tuple-element.30), channel_id=1, source_target_pairs={{0,4},{4,8},{8,12},{12,16},{16,20},{20,24},{24,28},{1,5},{5,9},{9,... | collective-permute-start | bytes 3080 | tf_op jit(solution)/shard_map/ppermute | solution.py:18
  283.4 127.9 %all-reduce.2 = (bf16[1024,256]{1,0:T(8,128)(2,1)}, bf16[1024,256]{1,0:T(8,128)(2,1)}, bf16[1024,256]{1,0:T(8,128)(2,1)}, f32[3,4,256]{2,1,0:T(4,128)}) all-reduce(f32[1024,256]{1,0:T(8,128)} %fusion.46, f32[1024,256]{1,0:T(8,128)S(1)} %fusion.48, f32[1024,256]{1,0:T(8,128)S(1)} %copy-done.1, ...), channel_id=1, replica_groups=mesh['seq'=8,'ch'=4] {'seq'}, use_global_device_ids=true, to_apply=%region_5.6 | all-reduce | flops 789504 | bytes 4743168 | tf_op jit(solution)/shard_map/psum | solution.py:147
  (157 shorter events, 56.6 us)
Async XLA Ops:
  7.2 97.9 %copy-start = (bf16[1024,256]{1,0:T(8,128)(2,1)S(1)}, bf16[1024,256]{1,0:T(8,128)(2,1)}, u32[]{:S(2)}) copy-start(bf16[1024,256]{1,0:T(8,128)(2,1)} %param.18) | copy-start | bytes 1572868
  7.2 22.5 %all-gather.4.cloned.1.call-start = ((), (), s32[]{:S(2)}) async-start(), calls=%async_computation.1 | async-start | bytes 1310720 | tf_op jit(solution)/shard_map/all_gather | solution.py:77
  9.3 68.8 %all-gather.6.cloned.1.call-start = ((), (), s32[]{:S(2)}) async-start(), calls=%async_computation.2 | async-start | bytes 1310720 | tf_op jit(solution)/shard_map/all_gather | solution.py:89
  31.7 6.0 %collective-permute-start.1 = (bf16[2,256]{1,0:T(2,128)(2,1)S(1)}, bf16[2,256]{1,0:T(2,128)(2,1)S(1)}, u32[]{:S(2)}, u32[]{:S(2)}) collective-permute-start(bf16[2,256]{1,0:T(2,128)(2,1)S(1)} %get-tuple-element.41), channel_id=1, source_target_pairs={{4,0},{8,4},{12,8},{16,12},{20,16},{24,20},{28,24},{5,1},{9,5},{13... | collective-permute-start | bytes 3080 | tf_op jit(solution)/shard_map/ppermute | solution.py:20
  33.0 5.8 %collective-permute-start = (bf16[2,256]{1,0:T(2,128)(2,1)S(1)}, bf16[2,256]{1,0:T(2,128)(2,1)S(1)}, u32[]{:S(2)}, u32[]{:S(2)}) collective-permute-start(bf16[2,256]{1,0:T(2,128)(2,1)S(1)} %get-tuple-element.40), channel_id=1, source_target_pairs={{0,4},{4,8},{8,12},{12,16},{16,20},{20,24},{24,28},{1,5},{5,9},{9,... | collective-permute-start | bytes 3080 | tf_op jit(solution)/shard_map/ppermute | solution.py:18
  39.1 6.2 %collective-permute-start.3 = (bf16[16,256]{1,0:T(8,128)(2,1)S(1)}, bf16[16,256]{1,0:T(8,128)(2,1)S(1)}, u32[]{:S(2)}, u32[]{:S(2)}) collective-permute-start(bf16[16,256]{1,0:T(8,128)(2,1)S(1)} %get-tuple-element.39), channel_id=1, source_target_pairs={{4,0},{8,4},{12,8},{16,12},{20,16},{24,20},{28,24},{5,1},{9,5},{13... | collective-permute-start | bytes 24584 | tf_op jit(solution)/shard_map/ppermute | solution.py:20
  40.4 6.3 %collective-permute-start.2 = (bf16[16,256]{1,0:T(8,128)(2,1)S(1)}, bf16[16,256]{1,0:T(8,128)(2,1)S(1)}, u32[]{:S(2)}, u32[]{:S(2)}) collective-permute-start(bf16[16,256]{1,0:T(8,128)(2,1)S(1)} %get-tuple-element.38), channel_id=1, source_target_pairs={{0,4},{4,8},{8,12},{12,16},{16,20},{20,24},{24,28},{1,5},{5,9},{9,... | collective-permute-start | bytes 24584 | tf_op jit(solution)/shard_map/ppermute | solution.py:18
  46.8 7.3 %collective-permute-start.5 = (bf16[128,256]{1,0:T(8,128)(2,1)S(1)}, bf16[128,256]{1,0:T(8,128)(2,1)S(1)}, u32[]{:S(2)}, u32[]{:S(2)}) collective-permute-start(bf16[128,256]{1,0:T(8,128)(2,1)S(1)} %get-tuple-element.37), channel_id=1, source_target_pairs={{4,0},{8,4},{12,8},{16,12},{20,16},{24,20},{28,24},{5,1},{9,5},{13... | collective-permute-start | bytes 196616 | tf_op jit(solution)/shard_map/ppermute | solution.py:20
  48.1 7.6 %collective-permute-start.4 = (bf16[128,256]{1,0:T(8,128)(2,1)S(1)}, bf16[128,256]{1,0:T(8,128)(2,1)S(1)}, u32[]{:S(2)}, u32[]{:S(2)}) collective-permute-start(bf16[128,256]{1,0:T(8,128)(2,1)S(1)} %get-tuple-element.36), channel_id=1, source_target_pairs={{0,4},{4,8},{8,12},{12,16},{16,20},{20,24},{24,28},{1,5},{5,9},{9,... | collective-permute-start | bytes 196616 | tf_op jit(solution)/shard_map/ppermute | solution.py:18
  57.4 73.9 %copy-start.10 = (s32[1024]{0:T(1024)S(1)}, s32[1024]{0:T(1024)}, u32[]{:S(2)}) copy-start(s32[1024]{0:T(1024)} %param.16) | copy-start | bytes 12292
  57.4 127.2 %reduce-scatter.2.cloned.1.call-start = ((), (), s32[]{:S(2)}) async-start(), calls=%async_computation.3 | async-start | bytes 1310720 | tf_op jit(solution)/shard_map/reduce_scatter | solution.py:106
  78.1 25.5 %collective-permute-start.6 = (bf16[512,1024]{1,0:T(8,128)(2,1)}, bf16[512,1024]{1,0:T(8,128)(2,1)S(1)}, u32[]{:S(2)}, u32[]{:S(2)}) collective-permute-start(bf16[512,1024]{1,0:T(8,128)(2,1)} %all-gather.6.cloned.1.call-done), channel_id=1, source_target_pairs={{0,4},{4,0},{8,12},{12,8},{16,20},{20,16},{24,28},{28,24},{1,5},{5... | collective-permute-start | bytes 3145736 | tf_op jit(solution)/shard_map/ppermute | solution.py:34
  103.6 24.6 %collective-permute-start.7 = (bf16[512,1024]{1,0:T(8,128)(2,1)S(1)}, bf16[512,1024]{1,0:T(8,128)(2,1)}, u32[]{:S(2)}, u32[]{:S(2)}) collective-permute-start(bf16[512,1024]{1,0:T(8,128)(2,1)S(1)} %collective-permute-done.6), channel_id=1, source_target_pairs={{0,8},{8,0},{4,12},{12,4},{16,24},{24,16},{20,28},{28,20},{1,9},{9... | collective-permute-start | bytes 3145736 | tf_op jit(solution)/shard_map/ppermute | solution.py:34
  106.6 106.2 %all-gather.8.cloned.1.call-start = ((), (), s32[]{:S(2)}) async-start(), calls=%async_computation.4 | async-start | bytes 1310720 | tf_op jit(solution)/shard_map/all_gather | solution.py:114
  128.2 47.2 %collective-permute-start.8 = (bf16[512,1024]{1,0:T(8,128)(2,1)}, bf16[512,1024]{1,0:T(8,128)(2,1)S(1)}, u32[]{:S(2)}, u32[]{:S(2)}) collective-permute-start(bf16[512,1024]{1,0:T(8,128)(2,1)} %collective-permute-done.7), channel_id=1, source_target_pairs={{0,16},{16,0},{4,20},{20,4},{8,24},{24,8},{12,28},{28,12},{1,17},{... | collective-permute-start | bytes 3145736 | tf_op jit(solution)/shard_map/ppermute | solution.py:34
  221.3 8.5 %collective-permute-start.9 = (bf16[512,256]{1,0:T(8,128)(2,1)S(1)}, bf16[512,256]{1,0:T(8,128)(2,1)S(1)}, u32[]{:S(2)}, u32[]{:S(2)}) collective-permute-start(bf16[512,256]{1,0:T(8,128)(2,1)S(1)} %select_bitcast_fusion), channel_id=1, source_target_pairs={{0,4},{4,0},{8,12},{12,8},{16,20},{20,16},{24,28},{28,24},{1,5},{5... | collective-permute-start | bytes 786440 | tf_op jit(solution)/shard_map/ppermute | solution.py:34
  229.8 7.6 %collective-permute-start.10 = (bf16[512,256]{1,0:T(8,128)(2,1)S(1)}, bf16[512,256]{1,0:T(8,128)(2,1)S(1)}, u32[]{:S(2)}, u32[]{:S(2)}) collective-permute-start(bf16[512,256]{1,0:T(8,128)(2,1)S(1)} %collective-permute-done.9), channel_id=1, source_target_pairs={{0,8},{8,0},{4,12},{12,4},{16,24},{24,16},{20,28},{28,20},{1,9},{9... | collective-permute-start | bytes 786440 | tf_op jit(solution)/shard_map/ppermute | solution.py:34
  237.4 13.3 %collective-permute-start.11 = (bf16[512,256]{1,0:T(8,128)(2,1)S(1)}, bf16[512,256]{1,0:T(8,128)(2,1)}, u32[]{:S(2)}, u32[]{:S(2)}) collective-permute-start(bf16[512,256]{1,0:T(8,128)(2,1)S(1)} %collective-permute-done.10), channel_id=1, source_target_pairs={{0,16},{16,0},{4,20},{20,4},{8,24},{24,8},{12,28},{28,12},{1,17},{... | collective-permute-start | bytes 786440 | tf_op jit(solution)/shard_map/ppermute | solution.py:34
  255.4 7.1 %collective-permute-start.13 = (bf16[128,256]{1,0:T(8,128)(2,1)S(1)}, bf16[128,256]{1,0:T(8,128)(2,1)S(1)}, u32[]{:S(2)}, u32[]{:S(2)}) collective-permute-start(bf16[128,256]{1,0:T(8,128)(2,1)S(1)} %get-tuple-element.35), channel_id=1, source_target_pairs={{0,4},{4,8},{8,12},{12,16},{16,20},{20,24},{24,28},{1,5},{5,9},{9,... | collective-permute-start | bytes 196616 | tf_op jit(solution)/shard_map/ppermute | solution.py:18
  258.8 6.2 %collective-permute-start.12 = (bf16[128,256]{1,0:T(8,128)(2,1)S(1)}, bf16[128,256]{1,0:T(8,128)(2,1)S(1)}, u32[]{:S(2)}, u32[]{:S(2)}) collective-permute-start(bf16[128,256]{1,0:T(8,128)(2,1)S(1)} %get-tuple-element.34), channel_id=1, source_target_pairs={{4,0},{8,4},{12,8},{16,12},{20,16},{24,20},{28,24},{5,1},{9,5},{13... | collective-permute-start | bytes 196616 | tf_op jit(solution)/shard_map/ppermute | solution.py:20
  265.3 4.5 %collective-permute-start.15 = (bf16[16,256]{1,0:T(8,128)(2,1)S(1)}, bf16[16,256]{1,0:T(8,128)(2,1)S(1)}, u32[]{:S(2)}, u32[]{:S(2)}) collective-permute-start(bf16[16,256]{1,0:T(8,128)(2,1)S(1)} %get-tuple-element.33), channel_id=1, source_target_pairs={{0,4},{4,8},{8,12},{12,16},{16,20},{20,24},{24,28},{1,5},{5,9},{9,... | collective-permute-start | bytes 24584 | tf_op jit(solution)/shard_map/ppermute | solution.py:18
  268.5 5.5 %collective-permute-start.14 = (bf16[16,256]{1,0:T(8,128)(2,1)S(1)}, bf16[16,256]{1,0:T(8,128)(2,1)S(1)}, u32[]{:S(2)}, u32[]{:S(2)}) collective-permute-start(bf16[16,256]{1,0:T(8,128)(2,1)S(1)} %get-tuple-element.32), channel_id=1, source_target_pairs={{4,0},{8,4},{12,8},{16,12},{20,16},{24,20},{28,24},{5,1},{9,5},{13... | collective-permute-start | bytes 24584 | tf_op jit(solution)/shard_map/ppermute | solution.py:20
  274.5 5.9 %collective-permute-start.16 = (bf16[2,256]{1,0:T(2,128)(2,1)S(1)}, bf16[2,256]{1,0:T(2,128)(2,1)S(1)}, u32[]{:S(2)}, u32[]{:S(2)}) collective-permute-start(bf16[2,256]{1,0:T(2,128)(2,1)S(1)} %get-tuple-element.31), channel_id=1, source_target_pairs={{4,0},{8,4},{12,8},{16,12},{20,16},{24,20},{28,24},{5,1},{9,5},{13... | collective-permute-start | bytes 3080 | tf_op jit(solution)/shard_map/ppermute | solution.py:20
  275.8 5.8 %collective-permute-start.17 = (bf16[2,256]{1,0:T(2,128)(2,1)S(1)}, bf16[2,256]{1,0:T(2,128)(2,1)S(1)}, u32[]{:S(2)}, u32[]{:S(2)}) collective-permute-start(bf16[2,256]{1,0:T(2,128)(2,1)S(1)} %get-tuple-element.30), channel_id=1, source_target_pairs={{0,4},{4,8},{8,12},{12,16},{16,20},{20,24},{24,28},{1,5},{5,9},{9,... | collective-permute-start | bytes 3080 | tf_op jit(solution)/shard_map/ppermute | solution.py:18
  (42 other events, 804.8 us)
Sparse Core Ops, SparseCore 0:
  10.2 19.5 all-gather.3
  57.5 20.5 all-gather.5
  106.7 23.9 reduce-scatter.1
  194.9 17.8 all-gather.7
where the time goes:
time: 419 us; the launch traced here: 418 us
  waiting for transfers between devices  174 us (42%)
  blocking collectives  134 us (32%)
  starting transfers between devices  45 us (11%)
  local copies, waits for them, and re-layouts  24.3 us (6%)
  between operations  14.5 us (3%)
  matrix products  13.5 us (3%)
  other arithmetic  12.3 us (3%)
    psum x1, blocking collectives, local(): lax.psum((local_in, local_gate, local_out, jnp.stack(tap_grads)), 'seq')  128 us
    ppermute x6, waiting for transfers between devices, partner(): return lax.ppermute(block, axis, route)  110 us
    ppermute x6, starting transfers between devices, extended(): lax.ppermute(tail, axis, [(i, (i + 1) % count) for i in range(ends)])  26.3 us
    all_gather x1, waiting for transfers between devices, local(): gated_full = lax.all_gather(gated, 'ch', axis=1, tiled=True)  20.6 us
    all_gather x1, waiting for transfers between devices, local(): full_input = lax.all_gather(local_input, 'ch', axis=1, tiled=True)  20.4 us
    ppermute x6, starting transfers between devices, partner(): return lax.ppermute(block, axis, route)  10.8 us
    all_gather x1, waiting for transfers between devices, local(): grad_full = lax.all_gather(grad_comb, 'ch', axis=1, tiled=True)  10.6 us
  transfers between devices with their start and end apart: 22, of which 16 were waited for; matrix products, arithmetic and copies ran while one was open for 6% of the time, Pallas kernels for 0%

commit v1 on v0

v1 whole, which is shorter than its diff:
```python
import jax
import jax.numpy as jnp
from jax import lax
from jax.sharding import PartitionSpec as P

DILATIONS = (1, 8, 64)
EPSILON = 1e-06
REACH_BACK = 2 * sum(DILATIONS)
REACH_AHEAD = sum(DILATIONS)
BACK = -(-REACH_BACK // 16) * 16
AHEAD = -(-REACH_AHEAD // 16) * 16


def swap(block, distance):
    count = lax.axis_size("ch")
    return lax.ppermute(block, "ch", [(i, i ^ distance) for i in range(count)])


def gather_relative(block):
    blocks = {0: block}
    distance = lax.axis_size("ch") // 2
    while distance:
        for j in list(blocks):
            blocks[j ^ distance] = swap(blocks[j], distance)
        distance //= 2
    return [blocks[j] for j in range(len(blocks))]


def reorder(array, width, axis=0):
    me = lax.axis_index("ch")
    count = lax.axis_size("ch")
    return jnp.concatenate(
        [lax.dynamic_slice_in_dim(array, (me ^ j) * width, width, axis) for j in range(count)], axis=axis
    )


def mirror(block):
    count = lax.axis_size("seq")
    return lax.ppermute(block, "seq", [(i, count - 1 - i) for i in range(count)])


def with_halo(block, before, after):
    count = lax.axis_size("seq")
    left = lax.ppermute(block[block.shape[0] - before :], "seq", [(i, i + 1) for i in range(count - 1)])
    right = lax.ppermute(block[:after], "seq", [(i + 1, i) for i in range(count - 1)])
    return jnp.concatenate([left, block, right], axis=0)


def flip(block):
    rows = block.shape[0]
    index = jnp.arange(rows, dtype=jnp.int32)
    anti = (index[:, None] + index[None, :] == rows - 1).astype(block.dtype)
    return jnp.dot(anti, block, preferred_element_type=jnp.float32).astype(block.dtype)


def inside(before, rows, after):
    place = lax.axis_index("seq") * rows + jnp.arange(-before, rows + after, dtype=jnp.int32)
    return ((place >= 0) & (place < lax.axis_size("seq") * rows))[:, None]


def local(tokens, hidden, embedding, w_in, w_gate, conv_w, channel_order, gain, w_out, cotangent):
    rows, width = hidden.shape
    full = gain.shape[0]
    bf16, f32 = jnp.bfloat16, jnp.float32
    shift = jnp.zeros((rows, width), f32)
    for base in range(embedding.shape[0]):
        shift = jnp.where((tokens == base)[:, None], embedding[base].astype(f32)[None, :], shift)
    local_input = (hidden.astype(f32) + shift).astype(bf16)
    full_input = jnp.concatenate(gather_relative(local_input), axis=1)

    w_in_r = reorder(w_in, width)
    w_gate_r = reorder(w_gate, width)
    w_out_r = reorder(w_out, width)
    gain_r = reorder(gain, width)
    order_r = reorder(channel_order, width)
    index_r = reorder(jnp.arange(full, dtype=jnp.int32), width)
    choose = (index_r[:, None] == order_r[None, :]).astype(bf16)
    choose_inverse = (order_r[:, None] == index_r[None, :width]).astype(bf16)

    grad_terms = lax.dot_general(cotangent, w_out, (((1,), (1,)), ((), ())), preferred_element_type=f32)
    grad_own = lax.psum_scatter(grad_terms.astype(bf16), "ch", scatter_dimension=1, tiled=True)
    grad_norm = reorder(lax.all_gather(grad_own, "ch", axis=1, tiled=True), width, 1).astype(f32)

    projected = jnp.dot(full_input, w_in_r, preferred_element_type=f32).astype(bf16)
    level = with_halo(projected, BACK, AHEAD)
    gate_pre = jnp.dot(full_input, w_gate_r, preferred_element_type=f32)
    before, after = BACK, AHEAD
    saved = []
    for number, dilation in enumerate(DILATIONS):
        saved.append((level, before))
        last = number == len(DILATIONS) - 1
        next_before = 0 if last else before - 2 * dilation
        next_after = 0 if last else after - dilation
        total = 0.0
        for tap in range(4):
            begin = before - next_before + (tap - 2) * dilation
            total = total + conv_w[number, tap][None, :] * level[
                begin : begin + next_before + rows + next_after
            ].astype(f32)
        if not last:
            total = jnp.where(inside(next_before, rows, next_after), total, 0.0)
        level = total.astype(bf16)
        before, after = next_before, next_after
    level_3 = level
    sigmoid = jax.nn.sigmoid(gate_pre)
    gate_act = gate_pre * sigmoid
    gated = (level_3.astype(f32) * gate_act).astype(bf16)
    mirrored = mirror(flip(gated))
    gated_full = jnp.concatenate(gather_relative(gated), axis=1)
    mirrored_full = jnp.concatenate(gather_relative(mirrored), axis=1)
    combined = gated_full.astype(f32) + jnp.dot(mirrored_full, choose, preferred_element_type=f32)
    inv_scale = lax.rsqrt(jnp.mean(combined * combined, axis=1, keepdims=True) + EPSILON)
    hat = combined * inv_scale
    scaled = grad_norm * gain_r[None, :]
    row_total = jnp.sum(scaled * hat, axis=1, keepdims=True)
    grad_comb = (inv_scale * (scaled - hat * row_total / full)).astype(bf16)
    chosen = jnp.dot(grad_comb, choose_inverse, preferred_element_type=f32).astype(bf16)
    grad_mirror = mirror(flip(chosen))

    normalized = (hat * gain_r[None, :]).astype(bf16)
    output = (
        local_input.astype(f32) + jnp.dot(normalized, w_out_r, preferred_element_type=f32)
    ).astype(bf16)

    contract_rows = (((0,), (0,)), ((), ()))

    def weight_grad(left, right):
        product = lax.dot_general(left, right, contract_rows, preferred_element_type=f32)
        return reorder(product.astype(bf16), width)

    def sum_early(part):
        own = lax.psum_scatter(part, "seq", scatter_dimension=0, tiled=True)
        return lax.all_gather(own, "seq", axis=0, tiled=True)

    grad_out = sum_early(weight_grad(normalized, cotangent))

    grad_gated = grad_comb[:, :width].astype(f32) + grad_mirror.astype(f32)
    upstream = (grad_gated * gate_act).astype(bf16)
    grad_gate_pre = (
        grad_gated * level_3.astype(f32) * sigmoid * (1.0 + gate_pre * (1.0 - sigmoid))
    ).astype(bf16)
    before, after = AHEAD, BACK
    extended = with_halo(upstream, before, after)
    grad_gate = sum_early(weight_grad(full_input, grad_gate_pre))
    tap_grads = []
    for number in reversed(range(len(DILATIONS))):
        dilation = DILATIONS[number]
        source, source_before = saved[number]
        own = extended[before : before + rows].astype(f32)
        for tap in range(4):
            begin = source_before + (tap - 2) * dilation
            tap_grads.append(jnp.sum(own * source[begin : begin + rows].astype(f32), axis=0))
        last = number == 0
        next_before = 0 if last else before - dilation
        next_after = 0 if last else after - 2 * dilation
        total = 0.0
        for tap in range(4):
            begin = before - next_before - (tap - 2) * dilation
            total = total + conv_w[number, tap][None, :] * extended[
                begin : begin + next_before + rows + next_after
            ].astype(f32)
        if not last:
            total = jnp.where(inside(next_before, rows, next_after), total, 0.0)
        extended = total.astype(bf16)
        before, after = next_before, next_after
    taps = jnp.stack([jnp.stack(tap_grads[4 * (2 - number) : 4 * (3 - number)]) for number in range(3)])
    grad_conv = lax.psum(taps, "seq")
    grad_in = lax.psum(weight_grad(full_input, extended), "seq")
    return output, grad_in, grad_gate, grad_out, grad_conv


def solution(mesh):
    placed = (
        P("seq"),
        P("seq", "ch"),
        P(None, "ch"),
        P(None, "ch"),
        P(None, "ch"),
        P(None, None, "ch"),
        P(),
        P(),
        P(None, "ch"),
        P("seq", "ch"),
    )
    return jax.shard_map(
        local,
        mesh=mesh,
        in_specs=placed,
        out_specs=(
            P("seq", "ch"),
            P(None, "ch"),
            P(None, "ch"),
            P(None, "ch"),
            P(None, None, "ch"),
        ),
        check_vma=False,
    )
```

time: 419 us -> 324 us (0.77)
  blocking collectives: 134 us -> 97.7 us
  waiting for transfers between devices: 174 us -> 146 us
  starting transfers between devices: 45 us -> 24.8 us
  local copies, waits for them, and re-layouts: 24.3 us -> 6.4 us
  matrix products: 13.5 us -> 20 us
    ppermute x18 -> x15, waiting for transfers between devices: 122 us -> 18.7 us  [the longest x9 8.67 us: swap(): return lax.ppermute(block, 'ch', [(i, i ^ distance) for i in range(count)])]
    psum x2 -> x1, blocking collectives: 134 us -> 33.8 us  [local(): grad_conv = lax.psum(taps, 'seq')]
    reduce_scatter x1 -> x3, waiting for transfers between devices: 0.02 us -> 73.4 us  [the longest x2 73.4 us: sum_early(): own = lax.psum_scatter(part, 'seq', scatter_dimension=0, tiled=True)]
    all_gather x0 -> x2, blocking collectives: none -> 63.8 us  [sum_early(): return lax.all_gather(own, 'seq', axis=0, tiled=True)]
    psum x0 -> x1, waiting for transfers between devices: none -> 44.7 us  [local(): grad_in = lax.psum(weight_grad(full_input, extended), 'seq')]
    all_gather x3 -> x1, waiting for transfers between devices: 51.6 us -> 9.51 us  [local(): lax.all_gather(grad_own, 'ch', axis=1, tiled=True)]
    ppermute x18 -> x15, starting transfers between devices: 44.8 us -> 24.5 us  [the longest x2 8.23 us: with_halo(): lax.ppermute(block[block.shape[0] - before:], 'seq', [(i, i + 1) for i in...]
    gather x4 -> x0, local copies, waits for them, and re-layouts: 10.5 us -> none  [the longest x2 5.3 us: local(): jnp.take(mirror_full, channel_order, axis=1).astype(jnp.float32)]
  transfers between devices with their start and end apart: 22 -> 20, of which waited for: 16 -> 9; matrix products, arithmetic and copies ran while one was open for 6% -> 9% of each run, Pallas kernels for 0% -> 0%
where the time goes in v1:
time: 324 us
  waiting for transfers between devices  146 us (45%)
  blocking collectives  97.7 us (30%)
  starting transfers between devices  24.8 us (8%)
  matrix products  20 us (6%)
  between operations  16.3 us (5%)
  other arithmetic  12 us (4%)
  local copies, waits for them, and re-layouts  6.4 us (2%)
    reduce_scatter x2, waiting for transfers between devices, sum_early(): own = lax.psum_scatter(part, 'seq', scatter_dimension=0, tiled=True)  73.4 us
    all_gather x2, blocking collectives, sum_early(): return lax.all_gather(own, 'seq', axis=0, tiled=True)  63.8 us
    psum x1, waiting for transfers between devices, local(): grad_in = lax.psum(weight_grad(full_input, extended), 'seq')  44.7 us
    psum x1, blocking collectives, local(): grad_conv = lax.psum(taps, 'seq')  33.8 us
    all_gather x1, waiting for transfers between devices, local(): lax.all_gather(grad_own, 'ch', axis=1, tiled=True)  9.51 us
    ppermute x9, waiting for transfers between devices, swap(): return lax.ppermute(block, 'ch', [(i, i ^ distance) for i in range(count)])  8.67 us
    ppermute x2, starting transfers between devices, with_halo(): lax.ppermute(block[block.shape[0] - before:], 'seq', [(i, i + 1) for i in...  8.23 us
    ppermute x2, starting transfers between devices, mirror(): lax.ppermute(block, 'seq', [(i, count - 1 - i) for i in range(count)])  7.06 us
  transfers between devices with their start and end apart: 20, of which 9 were waited for; matrix products, arithmetic and copies ran while one was open for 9% of the time, Pallas kernels for 0%

profile of v1, /device:TPU:0, one launch (start us, length us, event | category | flops | bytes accessed | tf_op | source)
XLA Modules:
  0.0 323.6 jit_solution(18250509434335412357)
XLA Ops:
  10.9 3.0 collective-permute-start.1
  13.9 2.5 convolution_convert_fusion
  16.6 3.7 %collective-permute-done.1 = bf16[512,256]{1,0:T(8,128)(2,1)S(1)} collective-permute-done((bf16[512,256]{1,0:T(8,128)(2,1)S(1)}, bf16[512,256]{1,0:T(8,128)(2,1)S(1)}, u32[]{:S(2)}, u32[]{:S(2)}) %collective-permute-start.1) | collective-permute-done | bytes 262176 | tf_op jit(solution)/shard_map/ppermute | solution.py:16
  23.3 3.7 %collective-permute-start.3 = (bf16[160,256]{1,0:T(8,128)(2,1)S(1)}, bf16[160,256]{1,0:T(8,128)(2,1)S(1)}, u32[]{:S(2)}, u32[]{:S(2)}) collective-permute-start(bf16[160,256]{1,0:T(8,128)(2,1)S(1)} %slice.235), channel_id=1, source_target_pairs={{0,4},{4,8},{8,12},{12,16},{16,20},{20,24},{24,28},{1,5},{5,9},{9,... | collective-permute-start | bytes 245768 | tf_op jit(solution)/shard_map/ppermute | solution.py:44
  28.3 4.6 %collective-permute-done.4 = bf16[80,256]{1,0:T(8,128)(2,1)S(1)} collective-permute-done((bf16[80,256]{1,0:T(8,128)(2,1)S(1)}, bf16[80,256]{1,0:T(8,128)(2,1)S(1)}, u32[]{:S(2)}, u32[]{:S(2)}) %collective-permute-start.4) | collective-permute-done | bytes 40992 | tf_op jit(solution)/shard_map/ppermute | solution.py:45
  33.7 2.7 fusion.20
  37.7 2.8 collective-permute-start.8
  42.1 5.4 %collective-permute-done.8 = bf16[512,256]{1,0:T(8,128)(2,1)S(1)} collective-permute-done((bf16[512,256]{1,0:T(8,128)(2,1)S(1)}, bf16[512,256]{1,0:T(8,128)(2,1)S(1)}, u32[]{:S(2)}, u32[]{:S(2)}) %collective-permute-start.8) | collective-permute-done | bytes 262176 | tf_op jit(solution)/shard_map/ppermute | solution.py:39
  50.3 3.5 %collective-permute-done.10 = bf16[512,256]{1,0:T(8,128)(2,1)S(1)} collective-permute-done((bf16[512,256]{1,0:T(8,128)(2,1)S(1)}, bf16[512,256]{1,0:T(8,128)(2,1)S(1)}, u32[]{:S(2)}, u32[]{:S(2)}) %collective-permute-start.10) | collective-permute-done | bytes 262176 | tf_op jit(solution)/shard_map/ppermute | solution.py:16
  55.7 2.7 multiply_reduce_fusion.1
  60.0 9.5 %all-gather.2.cloned.1.call-done = bf16[512,1024]{1,0:T(8,128)(2,1)} async-done(((bf16[512,256]{1,0:T(8,128)(2,1)}), bf16[512,1024]{1,0:T(8,128)(2,1)}) %all-gather.2.cloned.1.call-update) | async-done | bytes 1048592 | tf_op jit(solution)/shard_map/all_gather | solution.py:82
  72.9 2.9 convolution_convert_fusion.4
  75.8 4.3 %collective-permute-start.12 = (bf16[512,256]{1,0:T(8,128)(2,1)}, bf16[512,256]{1,0:T(8,128)(2,1)}, u32[]{:S(2)}, u32[]{:S(2)}) collective-permute-start(bf16[512,256]{1,0:T(8,128)(2,1)} %convolution_convert_fusion.4), channel_id=1, source_target_pairs={{0,28},{4,24},{8,20},{12,16},{16,12},{20,8},{24,4},{28,0},{1,29},{... | collective-permute-start | bytes 786440 | tf_op jit(solution)/shard_map/ppermute | solution.py:39
  80.0 2.4 fusion.6
  82.4 51.3 %reduce-scatter.8.cloned.1.call-done = bf16[128,256]{1,0:T(8,128)(2,1)} async-done(((bf16[1024,256]{1,0:T(8,128)(2,1)}), bf16[128,256]{1,0:T(8,128)(2,1)}) %reduce-scatter.8.cloned.1.call-update) | async-done | bytes 65552 | tf_op jit(solution)/shard_map/reduce_scatter | solution.py:132
  133.8 31.8 %all_gather.11 = bf16[1024,256]{1,0:T(8,128)(2,1)S(1)} all-gather(bf16[128,256]{1,0:T(8,128)(2,1)} %reduce-scatter.8.cloned.1.call-done), channel_id=1, replica_groups=mesh['seq'=8,'ch'=4] {'seq'}, dimensions={0}, use_global_device_ids=true | all-gather | bytes 589824 | tf_op jit(solution)/shard_map/all_gather | solution.py:133
  168.6 4.5 %collective-permute-start.14 = (bf16[80,256]{1,0:T(8,128)(2,1)S(1)}, bf16[80,256]{1,0:T(8,128)(2,1)S(1)}, u32[]{:S(2)}, u32[]{:S(2)}) collective-permute-start(bf16[80,256]{1,0:T(8,128)(2,1)S(1)} %slice.253), channel_id=1, source_target_pairs={{0,4},{4,8},{8,12},{12,16},{16,20},{20,24},{24,28},{1,5},{5,9},{9,... | collective-permute-start | bytes 122888 | tf_op jit(solution)/shard_map/ppermute | solution.py:44
  173.2 1.8 convolution_convert_fusion.2
  176.7 1.7 convolution_convert_fusion.3
  179.9 33.8 %psum.15 = f32[3,4,256]{2,1,0:T(4,128)} all-reduce(f32[3,4,256]{2,1,0:T(4,128)S(1)} %pad_maximum_fusion.12), channel_id=1, replica_groups=mesh['seq'=8,'ch'=4] {'seq'}, use_global_device_ids=true, to_apply=%region_18.19 | all-reduce | flops 3072 | bytes 24576 | tf_op jit(solution)/shard_map/psum | solution.py:167
  213.8 22.1 %reduce-scatter.6.cloned.1.call-done = bf16[128,256]{1,0:T(8,128)(2,1)} async-done(((bf16[1024,256]{1,0:T(8,128)(2,1)}), bf16[128,256]{1,0:T(8,128)(2,1)}) %reduce-scatter.6.cloned.1.call-update) | async-done | bytes 65552 | tf_op jit(solution)/shard_map/reduce_scatter | solution.py:132
  235.8 32.0 %all_gather.10 = bf16[1024,256]{1,0:T(8,128)(2,1)S(1)} all-gather(bf16[128,256]{1,0:T(8,128)(2,1)} %reduce-scatter.6.cloned.1.call-done), channel_id=1, replica_groups=mesh['seq'=8,'ch'=4] {'seq'}, dimensions={0}, use_global_device_ids=true | all-gather | bytes 589824 | tf_op jit(solution)/shard_map/all_gather | solution.py:133
  267.8 44.7 %all-reduce.2.cloned.1.call-done = bf16[1024,256]{1,0:T(8,128)(2,1)} async-done(((bf16[1024,256]{1,0:T(8,128)(2,1)}), bf16[1024,256]{1,0:T(8,128)(2,1)}) %all-reduce.2.cloned.1.call-update) | async-done | bytes 524304 | tf_op jit(solution)/shard_map/psum | solution.py:168
  312.5 1.9 copy.18
  (134 shorter events, 28.0 us)
Async XLA Ops:
  8.0 41.0 %reduce-scatter.4.cloned.1.call-start = ((), (), s32[]{:S(2)}) async-start(), calls=%async_computation.3 | async-start | bytes 1310720 | tf_op jit(solution)/shard_map/reduce_scatter | solution.py:81
  10.9 9.3 %collective-permute-start.1 = (bf16[512,256]{1,0:T(8,128)(2,1)S(1)}, bf16[512,256]{1,0:T(8,128)(2,1)S(1)}, u32[]{:S(2)}, u32[]{:S(2)}) collective-permute-start(bf16[512,256]{1,0:T(8,128)(2,1)S(1)} %add_convert_fusion), channel_id=1, source_target_pairs={{0,2},{1,3},{2,0},{3,1},{4,6},{5,7},{6,4},{7,5},{8,10},{9,11},{10,... | collective-permute-start | bytes 786440 | tf_op jit(solution)/shard_map/ppermute | solution.py:16
  13.9 6.5 %collective-permute-start = (bf16[512,256]{1,0:T(8,128)(2,1)S(1)}, bf16[512,256]{1,0:T(8,128)(2,1)S(1)}, u32[]{:S(2)}, u32[]{:S(2)}) collective-permute-start(bf16[512,256]{1,0:T(8,128)(2,1)S(1)} %add_convert_fusion), channel_id=1, source_target_pairs={{0,1},{1,0},{2,3},{3,2},{4,5},{5,4},{6,7},{7,6},{8,9},{9,8},{10,11... | collective-permute-start | bytes 786440 | tf_op jit(solution)/shard_map/ppermute | solution.py:16
  16.4 53.1 %all-gather.2.cloned.1.call-start = ((), (), s32[]{:S(2)}) async-start(), calls=%async_computation.4 | async-start | bytes 1310720 | tf_op jit(solution)/shard_map/all_gather | solution.py:82
  20.2 1.7 collective-permute-start.2
  23.3 9.6 %collective-permute-start.3 = (bf16[160,256]{1,0:T(8,128)(2,1)S(1)}, bf16[160,256]{1,0:T(8,128)(2,1)S(1)}, u32[]{:S(2)}, u32[]{:S(2)}) collective-permute-start(bf16[160,256]{1,0:T(8,128)(2,1)S(1)} %slice.235), channel_id=1, source_target_pairs={{0,4},{4,8},{8,12},{12,16},{16,20},{20,24},{24,28},{1,5},{5,9},{9,... | collective-permute-start | bytes 245768 | tf_op jit(solution)/shard_map/ppermute | solution.py:44
  27.0 5.9 %collective-permute-start.4 = (bf16[80,256]{1,0:T(8,128)(2,1)S(1)}, bf16[80,256]{1,0:T(8,128)(2,1)S(1)}, u32[]{:S(2)}, u32[]{:S(2)}) collective-permute-start(bf16[80,256]{1,0:T(8,128)(2,1)S(1)} %slice.236), channel_id=1, source_target_pairs={{4,0},{8,4},{12,8},{16,12},{20,16},{24,20},{28,24},{5,1},{9,5},{13... | collective-permute-start | bytes 122888 | tf_op jit(solution)/shard_map/ppermute | solution.py:45
  37.7 9.8 %collective-permute-start.8 = (bf16[512,256]{1,0:T(8,128)(2,1)S(1)}, bf16[512,256]{1,0:T(8,128)(2,1)S(1)}, u32[]{:S(2)}, u32[]{:S(2)}) collective-permute-start(bf16[512,256]{1,0:T(8,128)(2,1)S(1)} %convolution_convert_fusion.6), channel_id=1, source_target_pairs={{0,28},{4,24},{8,20},{12,16},{16,12},{20,8},{24,4},{28,0},{1,29},{... | collective-permute-start | bytes 786440 | tf_op jit(solution)/shard_map/ppermute | solution.py:39
  40.6 9.7 %collective-permute-start.6 = (bf16[512,256]{1,0:T(8,128)(2,1)}, bf16[512,256]{1,0:T(8,128)(2,1)S(1)}, u32[]{:S(2)}, u32[]{:S(2)}) collective-permute-start(bf16[512,256]{1,0:T(8,128)(2,1)} %get-tuple-element.18), channel_id=1, source_target_pairs={{0,2},{1,3},{2,0},{3,1},{4,6},{5,7},{6,4},{7,5},{8,10},{9,11},{10,... | collective-permute-start | bytes 786440 | tf_op jit(solution)/shard_map/ppermute | solution.py:16
  47.5 6.4 %collective-permute-start.10 = (bf16[512,256]{1,0:T(8,128)(2,1)S(1)}, bf16[512,256]{1,0:T(8,128)(2,1)S(1)}, u32[]{:S(2)}, u32[]{:S(2)}) collective-permute-start(bf16[512,256]{1,0:T(8,128)(2,1)S(1)} %collective-permute-done.8), channel_id=1, source_target_pairs={{0,2},{1,3},{2,0},{3,1},{4,6},{5,7},{6,4},{7,5},{8,10},{9,11},{10,... | collective-permute-start | bytes 786440 | tf_op jit(solution)/shard_map/ppermute | solution.py:16
  49.1 84.7 %reduce-scatter.8.cloned.1.call-start = ((), (), s32[]{:S(2)}) async-start(), calls=%async_computation.7 | async-start | bytes 589824 | tf_op jit(solution)/shard_map/reduce_scatter | solution.py:132
  49.8 5.9 %collective-permute-start.5 = (bf16[512,256]{1,0:T(8,128)(2,1)}, bf16[512,256]{1,0:T(8,128)(2,1)S(1)}, u32[]{:S(2)}, u32[]{:S(2)}) collective-permute-start(bf16[512,256]{1,0:T(8,128)(2,1)} %get-tuple-element.18), channel_id=1, source_target_pairs={{0,1},{1,0},{2,3},{3,2},{4,5},{5,4},{6,7},{7,6},{8,9},{9,8},{10,11... | collective-permute-start | bytes 786440 | tf_op jit(solution)/shard_map/ppermute | solution.py:16
  49.8 5.9 %collective-permute-start.9 = (bf16[512,256]{1,0:T(8,128)(2,1)S(1)}, bf16[512,256]{1,0:T(8,128)(2,1)S(1)}, u32[]{:S(2)}, u32[]{:S(2)}) collective-permute-start(bf16[512,256]{1,0:T(8,128)(2,1)S(1)} %collective-permute-done.8), channel_id=1, source_target_pairs={{0,1},{1,0},{2,3},{3,2},{4,5},{5,4},{6,7},{7,6},{8,9},{9,8},{10,11... | collective-permute-start | bytes 786440 | tf_op jit(solution)/shard_map/ppermute | solution.py:16
  50.3 5.4 %collective-permute-start.7 = (bf16[512,256]{1,0:T(8,128)(2,1)S(1)}, bf16[512,256]{1,0:T(8,128)(2,1)S(1)}, u32[]{:S(2)}, u32[]{:S(2)}) collective-permute-start(bf16[512,256]{1,0:T(8,128)(2,1)S(1)} %collective-permute-done.6), channel_id=1, source_target_pairs={{0,1},{1,0},{2,3},{3,2},{4,5},{5,4},{6,7},{7,6},{8,9},{9,8},{10,11... | collective-permute-start | bytes 786440 | tf_op jit(solution)/shard_map/ppermute | solution.py:16
  53.8 1.8 collective-permute-start.11
  60.0 175.9 %reduce-scatter.6.cloned.1.call-start = ((), (), s32[]{:S(2)}) async-start(), calls=%async_computation.6 | async-start | bytes 589824 | tf_op jit(solution)/shard_map/reduce_scatter | solution.py:132
  75.8 89.9 %collective-permute-start.12 = (bf16[512,256]{1,0:T(8,128)(2,1)}, bf16[512,256]{1,0:T(8,128)(2,1)}, u32[]{:S(2)}, u32[]{:S(2)}) collective-permute-start(bf16[512,256]{1,0:T(8,128)(2,1)} %convolution_convert_fusion.4), channel_id=1, source_target_pairs={{0,28},{4,24},{8,20},{12,16},{16,12},{20,8},{24,4},{28,0},{1,29},{... | collective-permute-start | bytes 786440 | tf_op jit(solution)/shard_map/ppermute | solution.py:39
  82.4 90.7 %copy-start.4 = (f32[512,256]{1,0:T(8,128)S(1)}, f32[512,256]{1,0:T(8,128)}, u32[]{:S(2)}) copy-start(f32[512,256]{1,0:T(8,128)} %get-tuple-element.76) | copy-start | bytes 1572868
  82.4 90.8 %copy-start.6 = (bf16[512,256]{1,0:T(8,128)(2,1)S(1)}, bf16[512,256]{1,0:T(8,128)(2,1)}, u32[]{:S(2)}) copy-start(bf16[512,256]{1,0:T(8,128)(2,1)} %copy-done.5) | copy-start | bytes 786436
  82.4 90.8 %copy-start.17 = (bf16[512,256]{1,0:T(8,128)(2,1)S(1)}, bf16[512,256]{1,0:T(8,128)(2,1)}, u32[]{:S(2)}) copy-start(bf16[512,256]{1,0:T(8,128)(2,1)} %copy-done.16) | copy-start | bytes 786436
  133.8 39.4 %copy-start.23 = (bf16[512,256]{1,0:T(8,128)(2,1)S(1)}, bf16[512,256]{1,0:T(8,128)(2,1)}, u32[]{:S(2)}) copy-start(bf16[512,256]{1,0:T(8,128)(2,1)} %get-tuple-element.19) | copy-start | bytes 786436
  167.3 8.9 %collective-permute-start.13 = (bf16[160,256]{1,0:T(8,128)(2,1)S(1)}, bf16[160,256]{1,0:T(8,128)(2,1)S(1)}, u32[]{:S(2)}, u32[]{:S(2)}) collective-permute-start(bf16[160,256]{1,0:T(8,128)(2,1)S(1)} %slice.250), channel_id=1, source_target_pairs={{4,0},{8,4},{12,8},{16,12},{20,16},{24,20},{28,24},{5,1},{9,5},{13... | collective-permute-start | bytes 245768 | tf_op jit(solution)/shard_map/ppermute | solution.py:45
  168.6 7.6 %collective-permute-start.14 = (bf16[80,256]{1,0:T(8,128)(2,1)S(1)}, bf16[80,256]{1,0:T(8,128)(2,1)S(1)}, u32[]{:S(2)}, u32[]{:S(2)}) collective-permute-start(bf16[80,256]{1,0:T(8,128)(2,1)S(1)} %slice.253), channel_id=1, source_target_pairs={{0,4},{4,8},{8,12},{12,16},{16,20},{20,24},{24,28},{1,5},{5,9},{9,... | collective-permute-start | bytes 122888 | tf_op jit(solution)/shard_map/ppermute | solution.py:44
  176.0 136.6 %all-reduce.2.cloned.1.call-start = ((), (), s32[]{:S(2)}) async-start(), calls=%async_computation.5 | async-start | bytes 1048576 | tf_op jit(solution)/shard_map/psum | solution.py:168
  (20 other events, 209.3 us)
Sparse Core Ops, SparseCore 0:
  16.6 25.3 reduce-scatter.3
  49.2 20.2 all-gather.1
Sparse Core Ops, SparseCore 1:
  60.0 73.7 reduce-scatter.7
  176.1 59.7 reduce-scatter.5
  240.1 72.4 all-reduce.1

commit v2 on v1

--- a/solution.py
+++ b/solution.py
@@ -9,21 +9,71 @@
 REACH_AHEAD = sum(DILATIONS)
 BACK = -(-REACH_BACK // 16) * 16
 AHEAD = -(-REACH_AHEAD // 16) * 16
-
-
-def swap(block, distance):
-    count = lax.axis_size("ch")
-    return lax.ppermute(block, "ch", [(i, i ^ distance) for i in range(count)])
+CHUNKS = 2
+
+
+def exchange(block, axis, distance):
+    count = lax.axis_size(axis)
+    return lax.ppermute(block, axis, [(i, i ^ distance) for i in range(count)])
+
+
+def distances(axis):
+    return [1 << bit for bit in range(lax.axis_size(axis).bit_length() - 1)]
 
 
 def gather_relative(block):
     blocks = {0: block}
-    distance = lax.axis_size("ch") // 2
-    while distance:
+    for distance in reversed(distances("ch")):
         for j in list(blocks):
-            blocks[j ^ distance] = swap(blocks[j], distance)
-        distance //= 2
+            blocks[j ^ distance] = exchange(blocks[j], "ch", distance)
     return [blocks[j] for j in range(len(blocks))]
+
+
+def sum_relative(blocks):
+    blocks = dict(enumerate(blocks))
+    width = blocks[0].shape[1]
+    for distance in distances("ch"):
+        sent = [j for j in blocks if j & distance]
+        other = exchange(
+            jnp.concatenate([blocks[j].astype(jnp.bfloat16) for j in sent], axis=1), "ch", distance
+        )
+        for place, j in enumerate(sent):
+            part = other[:, place * width : (place + 1) * width]
+            blocks[j ^ distance] = blocks[j ^ distance] + part.astype(jnp.float32)
+            del blocks[j]
+    return blocks[0].astype(jnp.bfloat16)
+
+
+def sum_over_seq(part, order):
+    me = lax.axis_index("seq")
+    for distance in order:
+        half = part.shape[0] // 2
+        bit = (me & distance) // distance
+        sent = lax.dynamic_slice_in_dim(part, (1 - bit) * half, half, 0).astype(jnp.bfloat16)
+        kept = lax.dynamic_slice_in_dim(part, bit * half, half, 0)
+        part = kept.astype(jnp.float32) + exchange(sent, "seq", distance).astype(jnp.float32)
+    part = part.astype(jnp.bfloat16)
+    for distance in reversed(order):
+        bit = (me & distance) // distance
+        other = exchange(part, "seq", distance)
+        part = jnp.where(
+            bit == 0, jnp.concatenate([part, other], axis=0), jnp.concatenate([other, part], axis=0)
+        )
+    return part
+
+
+def sum_gradient(part):
+    order = distances("seq")
+    half = part.shape[0] // 2
+    return jnp.concatenate(
+        [sum_over_seq(part[:half], order), sum_over_seq(part[half:], order[1:] + order[:1])], axis=0
+    )
+
+
+def sum_small(part):
+    for distance in distances("seq"):
+        part = part + exchange(part, "seq", distance)
+    return part
 
 
 def reorder(array, width, axis=0):
@@ -39,11 +89,28 @@
     return lax.ppermute(block, "seq", [(i, count - 1 - i) for i in range(count)])
 
 
-def with_halo(block, before, after):
+def pair_routes(turn):
     count = lax.axis_size("seq")
-    left = lax.ppermute(block[block.shape[0] - before :], "seq", [(i, i + 1) for i in range(count - 1)])
-    right = lax.ppermute(block[:after], "seq", [(i + 1, i) for i in range(count - 1)])
-    return jnp.concatenate([left, block, right], axis=0)
+    return [(low, low + 1) for low in range(turn, count - 1, 2)]
+
+
+def halo(block, before, after, far=0):
+    reach = max(before, after)
+    odd = lax.axis_index("seq") % 2 == 1
+    head, tail = block[:reach], block[block.shape[0] - reach :]
+    received = []
+    for turn in range(2):
+        channels = lax.axis_size("ch")
+        route = []
+        for low, high in pair_routes(turn):
+            for c in range(channels):
+                route.append((low * channels + c, high * channels + (c ^ far)))
+                route.append((high * channels + c, low * channels + (c ^ far)))
+        sent = jnp.where(odd, head, tail) if turn == 0 else jnp.where(odd, tail, head)
+        received.append(lax.ppermute(sent, ("seq", "ch"), route))
+    left = jnp.where(odd, received[0], received[1])
+    right = jnp.where(odd, received[1], received[0])
+    return left[reach - before :], right[:after]
 
 
 def flip(block):
@@ -61,12 +128,22 @@
 def local(tokens, hidden, embedding, w_in, w_gate, conv_w, channel_order, gain, w_out, cotangent):
     rows, width = hidden.shape
     full = gain.shape[0]
+    channels = full // width
     bf16, f32 = jnp.bfloat16, jnp.float32
-    shift = jnp.zeros((rows, width), f32)
-    for base in range(embedding.shape[0]):
-        shift = jnp.where((tokens == base)[:, None], embedding[base].astype(f32)[None, :], shift)
+    bases = jnp.arange(embedding.shape[0], dtype=jnp.int32)
+    one_hot = (bases[:, None] == tokens[None, :]).astype(bf16)
+    shift = lax.dot_general(one_hot, embedding, (((0,), (0,)), ((), ())), preferred_element_type=f32)
     local_input = (hidden.astype(f32) + shift).astype(bf16)
-    full_input = jnp.concatenate(gather_relative(local_input), axis=1)
+
+    edges = [jnp.concatenate(halo(local_input, BACK, AHEAD, far), axis=0) for far in range(0, channels, 2)]
+    mains = gather_relative(local_input)
+    edge_blocks = {}
+    packed = exchange(jnp.concatenate(edges, axis=0), "ch", 1)
+    for place, far in enumerate(range(0, channels, 2)):
+        edge_blocks[far] = edges[place]
+        edge_blocks[far ^ 1] = packed[place * (BACK + AHEAD) : (place + 1) * (BACK + AHEAD)]
+    full_input = jnp.concatenate(mains, axis=1)
+    edge_input = jnp.concatenate([edge_blocks[j] for j in range(channels)], axis=1)
 
     w_in_r = reorder(w_in, width)
     w_gate_r = reorder(w_gate, width)
@@ -77,12 +154,17 @@
     choose = (index_r[:, None] == order_r[None, :]).astype(bf16)
     choose_inverse = (order_r[:, None] == index_r[None, :width]).astype(bf16)
 
-    grad_terms = lax.dot_general(cotangent, w_out, (((1,), (1,)), ((), ())), preferred_element_type=f32)
-    grad_own = lax.psum_scatter(grad_terms.astype(bf16), "ch", scatter_dimension=1, tiled=True)
-    grad_norm = reorder(lax.all_gather(grad_own, "ch", axis=1, tiled=True), width, 1).astype(f32)
+    grad_terms = lax.dot_general(
+        cotangent, w_out_r, (((1,), (1,)), ((), ())), preferred_element_type=f32
+    ).astype(bf16)
+    grad_own = sum_relative(
+        [grad_terms[:, j * width : (j + 1) * width].astype(f32) for j in range(channels)]
+    )
+    grad_norm = jnp.concatenate(gather_relative(grad_own), axis=1)
 
     projected = jnp.dot(full_input, w_in_r, preferred_element_type=f32).astype(bf16)
-    level = with_halo(projected, BACK, AHEAD)
+    projected_edge = jnp.dot(edge_input, w_in_r, preferred_element_type=f32).astype(bf16)
+    level = jnp.concatenate([projected_edge[:BACK], projected, projected_edge[BACK:]], axis=0)
     gate_pre = jnp.dot(full_input, w_gate_r, preferred_element_type=f32)
     before, after = BACK, AHEAD
     saved = []
@@ -105,19 +187,31 @@
     sigmoid = jax.nn.sigmoid(gate_pre)
     gate_act = gate_pre * sigmoid
     gated = (level_3.astype(f32) * gate_act).astype(bf16)
-    mirrored = mirror(flip(gated))
+
+    flipped = flip(gated)
+    size = rows // CHUNKS
+    chunks = [slice(k * size, (k + 1) * size) for k in range(CHUNKS)]
+    mirrored = [mirror(flipped[chunk]) for chunk in chunks]
     gated_full = jnp.concatenate(gather_relative(gated), axis=1)
-    mirrored_full = jnp.concatenate(gather_relative(mirrored), axis=1)
-    combined = gated_full.astype(f32) + jnp.dot(mirrored_full, choose, preferred_element_type=f32)
-    inv_scale = lax.rsqrt(jnp.mean(combined * combined, axis=1, keepdims=True) + EPSILON)
-    hat = combined * inv_scale
-    scaled = grad_norm * gain_r[None, :]
-    row_total = jnp.sum(scaled * hat, axis=1, keepdims=True)
-    grad_comb = (inv_scale * (scaled - hat * row_total / full)).astype(bf16)
-    chosen = jnp.dot(grad_comb, choose_inverse, preferred_element_type=f32).astype(bf16)
-    grad_mirror = mirror(flip(chosen))
-
-    normalized = (hat * gain_r[None, :]).astype(bf16)
+    grad_comb, grad_mirror, normalized = [], [], []
+    for chunk, part in zip(chunks, mirrored):
+        mirrored_full = jnp.concatenate(gather_relative(part), axis=1)
+        combined = gated_full[chunk].astype(f32) + jnp.dot(
+            mirrored_full, choose, preferred_element_type=f32
+        )
+        inv_scale = lax.rsqrt(jnp.mean(combined * combined, axis=1, keepdims=True) + EPSILON)
+        hat = combined * inv_scale
+        scaled = grad_norm[chunk].astype(f32) * gain_r[None, :]
+        row_total = jnp.sum(scaled * hat, axis=1, keepdims=True)
+        grad_here = (inv_scale * (scaled - hat * row_total / full)).astype(bf16)
+        chosen = jnp.dot(grad_here, choose_inverse, preferred_element_type=f32).astype(bf16)
+        grad_mirror.append(mirror(flip(chosen)))
+        grad_comb.append(grad_here[:, :width])
+        normalized.append((hat * gain_r[None, :]).astype(bf16))
+    normalized = jnp.concatenate(normalized, axis=0)
+    grad_comb = jnp.concatenate(grad_comb, axis=0)
+    grad_mirror = jnp.concatenate(grad_mirror[::-1], axis=0)
+
     output = (
         local_input.astype(f32) + jnp.dot(normalized, w_out_r, preferred_element_type=f32)
     ).astype(bf16)
@@ -128,20 +222,17 @@
         product = lax.dot_general(left, right, contract_rows, preferred_element_type=f32)
         return reorder(product.astype(bf16), width)
 
-    def sum_early(part):
-        own = lax.psum_scatter(part, "seq", scatter_dimension=0, tiled=True)
-        return lax.all_gather(own, "seq", axis=0, tiled=True)
-
-    grad_out = sum_early(weight_grad(normalized, cotangent))
-
-    grad_gated = grad_comb[:, :width].astype(f32) + grad_mirror.astype(f32)
+    grad_out = sum_gradient(weight_grad(normalized, cotangent))
+
+    grad_gated = grad_comb.astype(f32) + grad_mirror.astype(f32)
     upstream = (grad_gated * gate_act).astype(bf16)
     grad_gate_pre = (
         grad_gated * level_3.astype(f32) * sigmoid * (1.0 + gate_pre * (1.0 - sigmoid))
     ).astype(bf16)
     before, after = AHEAD, BACK
-    extended = with_halo(upstream, before, after)
-    grad_gate = sum_early(weight_grad(full_input, grad_gate_pre))
+    left, right = halo(upstream, before, after)
+    extended = jnp.concatenate([left, upstream, right], axis=0)
+    grad_gate = sum_gradient(weight_grad(full_input, grad_gate_pre))
     tap_grads = []
     for number in reversed(range(len(DILATIONS))):
         dilation = DILATIONS[number]
@@ -164,8 +255,8 @@
         extended = total.astype(bf16)
         before, after = next_before, next_after
     taps = jnp.stack([jnp.stack(tap_grads[4 * (2 - number) : 4 * (3 - number)]) for number in range(3)])
-    grad_conv = lax.psum(taps, "seq")
-    grad_in = lax.psum(weight_grad(full_input, extended), "seq")
+    grad_conv = sum_small(taps)
+    grad_in = sum_gradient(weight_grad(full_input, extended))
     return output, grad_in, grad_gate, grad_out, grad_conv
 
 

time: 324 us -> 173 us (0.53)
  waiting for transfers between devices: 146 us -> 46.8 us
  blocking collectives: 97.7 us -> 0 us
  starting transfers between devices: 24.8 us -> 92.7 us
  between operations: 16.3 us -> 1.88 us
  matrix products: 20 us -> 13 us
  local copies, waits for them, and re-layouts: 6.4 us -> 3.08 us
    reduce_scatter x3 -> x0, waiting for transfers between devices: 73.4 us -> none  [the longest x2 73.4 us: sum_early(): own = lax.psum_scatter(part, 'seq', scatter_dimension=0, tiled=True)]
    ppermute x13 -> x63, starting transfers between devices: 17.4 us -> 81.3 us  [the longest x57 68.4 us: exchange(): return lax.ppermute(block, axis, [(i, i ^ distance) for i in range(count)])]
    all_gather x2 -> x0, blocking collectives: 63.8 us -> none  [sum_early(): return lax.all_gather(own, 'seq', axis=0, tiled=True)]
    psum x1 -> x0, waiting for transfers between devices: 44.7 us -> none  [local(): grad_in = lax.psum(weight_grad(full_input, extended), 'seq')]
    psum x1 -> x0, blocking collectives: 33.8 us -> none  [local(): grad_conv = lax.psum(taps, 'seq')]
    ppermute x13 -> x63, waiting for transfers between devices: 13.3 us -> 43.6 us  [the longest x57 43.6 us: exchange(): return lax.ppermute(block, axis, [(i, i ^ distance) for i in range(count)])]
    all_gather x1 -> x0, waiting for transfers between devices: 9.51 us -> none  [local(): lax.all_gather(grad_own, 'ch', axis=1, tiled=True)]
    ppermute x2 -> x4, starting transfers between devices: 7.06 us -> 11.4 us  [mirror(): lax.ppermute(block, 'seq', [(i, count - 1 - i) for i in range(count)])]
  transfers between devices with their start and end apart: 20 -> 67, of which waited for: 9 -> 21; matrix products, arithmetic and copies ran while one was open for 9% -> 12% of each run, Pallas kernels for 0% -> 0%
where the time goes in v2:
time: 173 us
  starting transfers between devices  92.7 us (54%)
  waiting for transfers between devices  46.8 us (27%)
  other arithmetic  15.1 us (9%)
  matrix products  13 us (8%)
  local copies, waits for them, and re-layouts  3.08 us (2%)
  between operations  1.88 us (1%)
    ppermute x57, starting transfers between devices, exchange(): return lax.ppermute(block, axis, [(i, i ^ distance) for i in range(count)])  68.4 us
    ppermute x57, waiting for transfers between devices, exchange(): return lax.ppermute(block, axis, [(i, i ^ distance) for i in range(count)])  43.6 us
    ppermute x6, starting transfers between devices, halo(): received.append(lax.ppermute(sent, ('seq', 'ch'), route))  12.9 us
    ppermute x4, starting transfers between devices, mirror(): lax.ppermute(block, 'seq', [(i, count - 1 - i) for i in range(count)])  11.4 us
    dot_general x3, matrix products, flip(): jnp.dot(anti, block, preferred_element_type=jnp.float32).astype(block.dtype)  3.59 us
  transfers between devices with their start and end apart: 67, of which 21 were waited for; matrix products, arithmetic and copies ran while one was open for 12% of the time, Pallas kernels for 0%

profile of v2, /device:TPU:0, one launch (start us, length us, event | category | flops | bytes accessed | tf_op | source)
XLA Modules:
  0.0 172.6 jit_solution(6747961866439705488)
XLA Ops:
  2.7 3.0 %collective-permute-start = (bf16[160,256]{1,0:T(8,128)(2,1)}, bf16[160,256]{1,0:T(8,128)(2,1)S(1)}, u32[]{:S(2)}, u32[]{:S(2)}) collective-permute-start(bf16[160,256]{1,0:T(8,128)(2,1)} %get-tuple-element.59), channel_id=1, source_target_pairs={{0,4},{4,0},{1,5},{5,1},{2,6},{6,2},{3,7},{7,3},{8,12},{12,8},{9,1... | collective-permute-start | bytes 245768 | tf_op jit(solution)/shard_map/ppermute | solution.py:110
  12.1 3.9 %collective-permute-done.6 = bf16[512,256]{1,0:T(8,128)(2,1)S(1)} collective-permute-done((bf16[512,256]{1,0:T(8,128)(2,1)S(1)}, bf16[512,256]{1,0:T(8,128)(2,1)S(1)}, u32[]{:S(2)}, u32[]{:S(2)}) %collective-permute-start.6) | collective-permute-done | bytes 262176 | tf_op jit(solution)/shard_map/ppermute | solution.py:17
  20.4 2.1 %collective-permute-start.9 = (bf16[512,256]{1,0:T(8,128)(2,1)S(1)}, bf16[512,256]{1,0:T(8,128)(2,1)}, u32[]{:S(2)}, u32[]{:S(2)}) collective-permute-start(bf16[512,256]{1,0:T(8,128)(2,1)S(1)} %get-tuple-element.20), channel_id=1, source_target_pairs={{0,2},{1,3},{2,0},{3,1},{4,6},{5,7},{6,4},{7,5},{8,10},{9,11},{10,... | collective-permute-start | bytes 786440 | tf_op jit(solution)/shard_map/ppermute | solution.py:17
  23.0 5.7 %collective-permute-start.11 = (bf16[256,256]{1,0:T(8,128)(2,1)S(1)}, bf16[256,256]{1,0:T(8,128)(2,1)S(1)}, u32[]{:S(2)}, u32[]{:S(2)}) collective-permute-start(bf16[256,256]{1,0:T(8,128)(2,1)S(1)} %get-tuple-element.56), channel_id=1, source_target_pairs={{0,28},{4,24},{8,20},{12,16},{16,12},{20,8},{24,4},{28,0},{1,29},{... | collective-permute-start | bytes 393224 | tf_op jit(solution)/shard_map/ppermute | solution.py:89
  29.3 3.2 %collective-permute-done.11 = bf16[256,256]{1,0:T(8,128)(2,1)S(1)} collective-permute-done((bf16[256,256]{1,0:T(8,128)(2,1)S(1)}, bf16[256,256]{1,0:T(8,128)(2,1)S(1)}, u32[]{:S(2)}, u32[]{:S(2)}) %collective-permute-start.11) | collective-permute-done | bytes 131104 | tf_op jit(solution)/shard_map/ppermute | solution.py:89
  35.3 2.1 %collective-permute-start.22 = (bf16[512,256]{1,0:T(8,128)(2,1)S(1)}, bf16[512,256]{1,0:T(8,128)(2,1)S(1)}, u32[]{:S(2)}, u32[]{:S(2)}) collective-permute-start(bf16[512,256]{1,0:T(8,128)(2,1)S(1)} %add_convert_fusion), channel_id=1, source_target_pairs={{0,2},{1,3},{2,0},{3,1},{4,6},{5,7},{6,4},{7,5},{8,10},{9,11},{10,... | collective-permute-start | bytes 786440 | tf_op jit(solution)/shard_map/ppermute | solution.py:17
  42.0 4.0 %collective-permute-done.17 = bf16[256,256]{1,0:T(8,128)(2,1)S(1)} collective-permute-done((bf16[256,256]{1,0:T(8,128)(2,1)S(1)}, bf16[256,256]{1,0:T(8,128)(2,1)S(1)}, u32[]{:S(2)}, u32[]{:S(2)}) %collective-permute-start.17) | collective-permute-done | bytes 131104 | tf_op jit(solution)/shard_map/ppermute | solution.py:17
  54.1 5.6 %collective-permute-start.24 = (bf16[256,256]{1,0:T(8,128)(2,1)}, bf16[256,256]{1,0:T(8,128)(2,1)S(1)}, u32[]{:S(2)}, u32[]{:S(2)}) collective-permute-start(bf16[256,256]{1,0:T(8,128)(2,1)} %convolution_convert_fusion.7), channel_id=1, source_target_pairs={{0,28},{4,24},{8,20},{12,16},{16,12},{20,8},{24,4},{28,0},{1,29},{... | collective-permute-start | bytes 393224 | tf_op jit(solution)/shard_map/ppermute | solution.py:89
  60.7 5.1 %collective-permute-start.52 = (bf16[256,256]{1,0:T(8,128)(2,1)S(1)}, bf16[256,256]{1,0:T(8,128)(2,1)S(1)}, u32[]{:S(2)}, u32[]{:S(2)}) collective-permute-start(bf16[256,256]{1,0:T(8,128)(2,1)S(1)} %fusion.112), channel_id=1, source_target_pairs={{0,4},{4,0},{8,12},{12,8},{16,20},{20,16},{24,28},{28,24},{1,5},{5... | collective-permute-start | bytes 393224 | tf_op jit(solution)/shard_map/ppermute | solution.py:17
  66.1 3.4 %collective-permute-start.58 = (bf16[256,256]{1,0:T(8,128)(2,1)S(1)}, bf16[256,256]{1,0:T(8,128)(2,1)S(1)}, u32[]{:S(2)}, u32[]{:S(2)}) collective-permute-start(bf16[256,256]{1,0:T(8,128)(2,1)S(1)} %fusion.110), channel_id=1, source_target_pairs={{0,8},{4,12},{8,0},{12,4},{16,24},{20,28},{24,16},{28,20},{1,9},{5... | collective-permute-start | bytes 393224 | tf_op jit(solution)/shard_map/ppermute | solution.py:17
  72.2 6.2 %collective-permute-start.27 = (bf16[160,256]{1,0:T(8,128)(2,1)S(1)}, bf16[160,256]{1,0:T(8,128)(2,1)S(1)}, u32[]{:S(2)}, u32[]{:S(2)}) collective-permute-start(bf16[160,256]{1,0:T(8,128)(2,1)S(1)} %get-tuple-element.54), channel_id=1, source_target_pairs={{0,4},{4,0},{1,5},{5,1},{2,6},{6,2},{3,7},{7,3},{8,12},{12,8},{9,1... | collective-permute-start | bytes 245768 | tf_op jit(solution)/shard_map/ppermute | solution.py:110
  78.7 4.7 %collective-permute-start.53 = (bf16[128,256]{1,0:T(8,128)(2,1)S(1)}, bf16[128,256]{1,0:T(8,128)(2,1)S(1)}, u32[]{:S(2)}, u32[]{:S(2)}) collective-permute-start(bf16[128,256]{1,0:T(8,128)(2,1)S(1)} %dynamic-slice_convert_fusion.1), channel_id=1, source_target_pairs={{0,8},{4,12},{8,0},{12,4},{16,24},{20,28},{24,16},{28,20},{1,9},{5... | collective-permute-start | bytes 196616 | tf_op jit(solution)/shard_map/ppermute | solution.py:17
  97.8 2.5 %collective-permute-done.65 = f32[3,4,256]{2,1,0:T(4,128)S(1)} collective-permute-done((f32[3,4,256]{2,1,0:T(4,128)S(1)}, f32[3,4,256]{2,1,0:T(4,128)S(1)}, u32[]{:S(2)}, u32[]{:S(2)}) %collective-permute-start.65) | collective-permute-done | bytes 12320 | tf_op jit(solution)/shard_map/ppermute | solution.py:17
  103.2 2.9 %collective-permute-done.66 = f32[3,4,256]{2,1,0:T(4,128)S(1)} collective-permute-done((f32[3,4,256]{2,1,0:T(4,128)S(1)}, f32[3,4,256]{2,1,0:T(4,128)S(1)}, u32[]{:S(2)}, u32[]{:S(2)}) %collective-permute-start.66) | collective-permute-done | bytes 12320 | tf_op jit(solution)/shard_map/ppermute | solution.py:17
  114.8 2.5 %collective-permute-done.56 = bf16[128,256]{1,0:T(8,128)(2,1)S(1)} collective-permute-done((bf16[128,256]{1,0:T(8,128)(2,1)S(1)}, bf16[128,256]{1,0:T(8,128)(2,1)S(1)}, u32[]{:S(2)}, u32[]{:S(2)}) %collective-permute-start.56) | collective-permute-done | bytes 65568 | tf_op jit(solution)/shard_map/ppermute | solution.py:17
  119.2 3.2 %collective-permute-done.62 = bf16[128,256]{1,0:T(8,128)(2,1)S(1)} collective-permute-done((bf16[128,256]{1,0:T(8,128)(2,1)S(1)}, bf16[128,256]{1,0:T(8,128)(2,1)S(1)}, u32[]{:S(2)}, u32[]{:S(2)}) %collective-permute-start.62) | collective-permute-done | bytes 65568 | tf_op jit(solution)/shard_map/ppermute | solution.py:17
  122.5 4.5 %collective-permute-start.57 = (bf16[256,256]{1,0:T(8,128)(2,1)S(1)}, bf16[256,256]{1,0:T(8,128)(2,1)S(1)}, u32[]{:S(2)}, u32[]{:S(2)}) collective-permute-start(bf16[256,256]{1,0:T(8,128)(2,1)S(1)} %maximum_select_fusion.10), channel_id=1, source_target_pairs={{0,4},{4,0},{8,12},{12,8},{16,20},{20,16},{24,28},{28,24},{1,5},{5... | collective-permute-start | bytes 393224 | tf_op jit(solution)/shard_map/ppermute | solution.py:17
  128.7 2.1 %collective-permute-start.48 = (bf16[64,256]{1,0:T(8,128)(2,1)S(1)}, bf16[64,256]{1,0:T(8,128)(2,1)S(1)}, u32[]{:S(2)}, u32[]{:S(2)}) collective-permute-start(bf16[64,256]{1,0:T(8,128)(2,1)S(1)} %dynamic-slice_convert_fusion.8), channel_id=1, source_target_pairs={{0,4},{4,0},{8,12},{12,8},{16,20},{20,16},{24,28},{28,24},{1,5},{5... | collective-permute-start | bytes 98312 | tf_op jit(solution)/shard_map/ppermute | solution.py:17
  135.2 4.3 %collective-permute-done.43 = bf16[64,256]{1,0:T(8,128)(2,1)S(1)} collective-permute-done((bf16[64,256]{1,0:T(8,128)(2,1)S(1)}, bf16[64,256]{1,0:T(8,128)(2,1)S(1)}, u32[]{:S(2)}, u32[]{:S(2)}) %collective-permute-start.43) | collective-permute-done | bytes 32800 | tf_op jit(solution)/shard_map/ppermute | solution.py:17
  140.4 3.1 %collective-permute-done.49 = bf16[64,256]{1,0:T(8,128)(2,1)S(1)} collective-permute-done((bf16[64,256]{1,0:T(8,128)(2,1)S(1)}, bf16[64,256]{1,0:T(8,128)(2,1)S(1)}, u32[]{:S(2)}, u32[]{:S(2)}) %collective-permute-start.49) | collective-permute-done | bytes 32800 | tf_op jit(solution)/shard_map/ppermute | solution.py:17
  143.8 2.5 %collective-permute-start.50 = (bf16[128,256]{1,0:T(8,128)(2,1)S(1)}, bf16[128,256]{1,0:T(8,128)(2,1)S(1)}, u32[]{:S(2)}, u32[]{:S(2)}) collective-permute-start(bf16[128,256]{1,0:T(8,128)(2,1)S(1)} %maximum_select_fusion.15), channel_id=1, source_target_pairs={{0,16},{4,20},{8,24},{12,28},{16,0},{20,4},{24,8},{28,12},{1,17},{... | collective-permute-start | bytes 196616 | tf_op jit(solution)/shard_map/ppermute | solution.py:17
  147.0 4.4 %collective-permute-done.30 = bf16[64,256]{1,0:T(8,128)(2,1)S(1)} collective-permute-done((bf16[64,256]{1,0:T(8,128)(2,1)S(1)}, bf16[64,256]{1,0:T(8,128)(2,1)S(1)}, u32[]{:S(2)}, u32[]{:S(2)}) %collective-permute-start.30) | collective-permute-done | bytes 32800 | tf_op jit(solution)/shard_map/ppermute | solution.py:17
  152.2 3.1 %collective-permute-done.36 = bf16[64,256]{1,0:T(8,128)(2,1)S(1)} collective-permute-done((bf16[64,256]{1,0:T(8,128)(2,1)S(1)}, bf16[64,256]{1,0:T(8,128)(2,1)S(1)}, u32[]{:S(2)}, u32[]{:S(2)}) %collective-permute-start.36) | collective-permute-done | bytes 32800 | tf_op jit(solution)/shard_map/ppermute | solution.py:17
  161.3 2.5 %collective-permute-start.38 = (bf16[128,256]{1,0:T(8,128)(2,1)S(1)}, bf16[128,256]{1,0:T(8,128)(2,1)S(1)}, u32[]{:S(2)}, u32[]{:S(2)}) collective-permute-start(bf16[128,256]{1,0:T(8,128)(2,1)S(1)} %maximum_select_fusion.13), channel_id=1, source_target_pairs={{0,16},{4,20},{8,24},{12,28},{16,0},{20,4},{24,8},{28,12},{1,17},{... | collective-permute-start | bytes 196616 | tf_op jit(solution)/shard_map/ppermute | solution.py:17
  (296 shorter events, 84.1 us)
Async XLA Ops:
  11.4 11.4 %collective-permute-start.19 = (bf16[512,512]{1,0:T(8,128)(2,1)S(1)}, bf16[512,512]{1,0:T(8,128)(2,1)S(1)}, u32[]{:S(2)}, u32[]{:S(2)}) collective-permute-start(bf16[512,512]{1,0:T(8,128)(2,1)S(1)} %pad_maximum_fusion.8), channel_id=1, source_target_pairs={{0,1},{1,0},{2,3},{3,2},{4,5},{5,4},{6,7},{7,6},{8,9},{9,8},{10,11... | collective-permute-start | bytes 1572872 | tf_op jit(solution)/shard_map/ppermute | solution.py:17
  20.4 13.9 %collective-permute-start.9 = (bf16[512,256]{1,0:T(8,128)(2,1)S(1)}, bf16[512,256]{1,0:T(8,128)(2,1)}, u32[]{:S(2)}, u32[]{:S(2)}) collective-permute-start(bf16[512,256]{1,0:T(8,128)(2,1)S(1)} %get-tuple-element.20), channel_id=1, source_target_pairs={{0,2},{1,3},{2,0},{3,1},{4,6},{5,7},{6,4},{7,5},{8,10},{9,11},{10,... | collective-permute-start | bytes 786440 | tf_op jit(solution)/shard_map/ppermute | solution.py:17
  22.9 12.3 %collective-permute-start.20 = (bf16[512,256]{1,0:T(8,128)(2,1)S(1)}, bf16[512,256]{1,0:T(8,128)(2,1)S(1)}, u32[]{:S(2)}, u32[]{:S(2)}) collective-permute-start(bf16[512,256]{1,0:T(8,128)(2,1)S(1)} %add_convert_fusion.1), channel_id=1, source_target_pairs={{0,2},{1,3},{2,0},{3,1},{4,6},{5,7},{6,4},{7,5},{8,10},{9,11},{10,... | collective-permute-start | bytes 786440 | tf_op jit(solution)/shard_map/ppermute | solution.py:17
  35.3 10.7 %collective-permute-start.22 = (bf16[512,256]{1,0:T(8,128)(2,1)S(1)}, bf16[512,256]{1,0:T(8,128)(2,1)S(1)}, u32[]{:S(2)}, u32[]{:S(2)}) collective-permute-start(bf16[512,256]{1,0:T(8,128)(2,1)S(1)} %add_convert_fusion), channel_id=1, source_target_pairs={{0,2},{1,3},{2,0},{3,1},{4,6},{5,7},{6,4},{7,5},{8,10},{9,11},{10,... | collective-permute-start | bytes 786440 | tf_op jit(solution)/shard_map/ppermute | solution.py:17
  54.1 16.5 %collective-permute-start.24 = (bf16[256,256]{1,0:T(8,128)(2,1)}, bf16[256,256]{1,0:T(8,128)(2,1)S(1)}, u32[]{:S(2)}, u32[]{:S(2)}) collective-permute-start(bf16[256,256]{1,0:T(8,128)(2,1)} %convolution_convert_fusion.7), channel_id=1, source_target_pairs={{0,28},{4,24},{8,20},{12,16},{16,12},{20,8},{24,4},{28,0},{1,29},{... | collective-permute-start | bytes 393224 | tf_op jit(solution)/shard_map/ppermute | solution.py:89
  59.8 10.9 %collective-permute-start.25 = (bf16[256,256]{1,0:T(8,128)(2,1)}, bf16[256,256]{1,0:T(8,128)(2,1)S(1)}, u32[]{:S(2)}, u32[]{:S(2)}) collective-permute-start(bf16[256,256]{1,0:T(8,128)(2,1)} %convolution_convert_fusion.6), channel_id=1, source_target_pairs={{0,28},{4,24},{8,20},{12,16},{16,12},{20,8},{24,4},{28,0},{1,29},{... | collective-permute-start | bytes 393224 | tf_op jit(solution)/shard_map/ppermute | solution.py:89
  60.7 17.7 %collective-permute-start.52 = (bf16[256,256]{1,0:T(8,128)(2,1)S(1)}, bf16[256,256]{1,0:T(8,128)(2,1)S(1)}, u32[]{:S(2)}, u32[]{:S(2)}) collective-permute-start(bf16[256,256]{1,0:T(8,128)(2,1)S(1)} %fusion.112), channel_id=1, source_target_pairs={{0,4},{4,0},{8,12},{12,8},{16,20},{20,16},{24,28},{28,24},{1,5},{5... | collective-permute-start | bytes 393224 | tf_op jit(solution)/shard_map/ppermute | solution.py:17
  66.1 17.3 %collective-permute-start.58 = (bf16[256,256]{1,0:T(8,128)(2,1)S(1)}, bf16[256,256]{1,0:T(8,128)(2,1)S(1)}, u32[]{:S(2)}, u32[]{:S(2)}) collective-permute-start(bf16[256,256]{1,0:T(8,128)(2,1)S(1)} %fusion.110), channel_id=1, source_target_pairs={{0,8},{4,12},{8,0},{12,4},{16,24},{20,28},{24,16},{28,20},{1,9},{5... | collective-permute-start | bytes 393224 | tf_op jit(solution)/shard_map/ppermute | solution.py:17
  71.2 18.1 %collective-permute-start.26 = (bf16[160,256]{1,0:T(8,128)(2,1)S(1)}, bf16[160,256]{1,0:T(8,128)(2,1)S(1)}, u32[]{:S(2)}, u32[]{:S(2)}) collective-permute-start(bf16[160,256]{1,0:T(8,128)(2,1)S(1)} %get-tuple-element.55), channel_id=1, source_target_pairs={{4,8},{8,4},{5,9},{9,5},{6,10},{10,6},{7,11},{11,7},{12,16},{16,12... | collective-permute-start | bytes 245768 | tf_op jit(solution)/shard_map/ppermute | solution.py:110
  72.2 18.4 %collective-permute-start.27 = (bf16[160,256]{1,0:T(8,128)(2,1)S(1)}, bf16[160,256]{1,0:T(8,128)(2,1)S(1)}, u32[]{:S(2)}, u32[]{:S(2)}) collective-permute-start(bf16[160,256]{1,0:T(8,128)(2,1)S(1)} %get-tuple-element.54), channel_id=1, source_target_pairs={{0,4},{4,0},{1,5},{5,1},{2,6},{6,2},{3,7},{7,3},{8,12},{12,8},{9,1... | collective-permute-start | bytes 245768 | tf_op jit(solution)/shard_map/ppermute | solution.py:110
  84.9 23.5 %collective-permute-start.40 = (bf16[256,256]{1,0:T(8,128)(2,1)S(1)}, bf16[256,256]{1,0:T(8,128)(2,1)S(1)}, u32[]{:S(2)}, u32[]{:S(2)}) collective-permute-start(bf16[256,256]{1,0:T(8,128)(2,1)S(1)} %fusion.116), channel_id=1, source_target_pairs={{0,4},{4,0},{8,12},{12,8},{16,20},{20,16},{24,28},{28,24},{1,5},{5... | collective-permute-start | bytes 393224 | tf_op jit(solution)/shard_map/ppermute | solution.py:17
  85.6 24.7 %collective-permute-start.46 = (bf16[256,256]{1,0:T(8,128)(2,1)S(1)}, bf16[256,256]{1,0:T(8,128)(2,1)S(1)}, u32[]{:S(2)}, u32[]{:S(2)}) collective-permute-start(bf16[256,256]{1,0:T(8,128)(2,1)S(1)} %fusion.114), channel_id=1, source_target_pairs={{0,8},{4,12},{8,0},{12,4},{16,24},{20,28},{24,16},{28,20},{1,9},{5... | collective-permute-start | bytes 393224 | tf_op jit(solution)/shard_map/ppermute | solution.py:17
  89.3 12.2 %collective-permute-start.60 = (bf16[64,256]{1,0:T(8,128)(2,1)S(1)}, bf16[64,256]{1,0:T(8,128)(2,1)S(1)}, u32[]{:S(2)}, u32[]{:S(2)}) collective-permute-start(bf16[64,256]{1,0:T(8,128)(2,1)S(1)} %dynamic-slice_convert_fusion.6), channel_id=1, source_target_pairs={{0,4},{4,0},{8,12},{12,8},{16,20},{20,16},{24,28},{28,24},{1,5},{5... | collective-permute-start | bytes 98312 | tf_op jit(solution)/shard_map/ppermute | solution.py:17
  95.6 33.1 %collective-permute-start.28 = (bf16[256,256]{1,0:T(8,128)(2,1)S(1)}, bf16[256,256]{1,0:T(8,128)(2,1)S(1)}, u32[]{:S(2)}, u32[]{:S(2)}) collective-permute-start(bf16[256,256]{1,0:T(8,128)(2,1)S(1)} %fusion.120), channel_id=1, source_target_pairs={{0,4},{4,0},{8,12},{12,8},{16,20},{20,16},{24,28},{28,24},{1,5},{5... | collective-permute-start | bytes 393224 | tf_op jit(solution)/shard_map/ppermute | solution.py:17
  100.3 30.8 %collective-permute-start.34 = (bf16[256,256]{1,0:T(8,128)(2,1)S(1)}, bf16[256,256]{1,0:T(8,128)(2,1)S(1)}, u32[]{:S(2)}, u32[]{:S(2)}) collective-permute-start(bf16[256,256]{1,0:T(8,128)(2,1)S(1)} %fusion.118), channel_id=1, source_target_pairs={{0,8},{4,12},{8,0},{12,4},{16,24},{20,28},{24,16},{28,20},{1,9},{5... | collective-permute-start | bytes 393224 | tf_op jit(solution)/shard_map/ppermute | solution.py:17
  110.4 16.6 %collective-permute-start.41 = (bf16[128,256]{1,0:T(8,128)(2,1)S(1)}, bf16[128,256]{1,0:T(8,128)(2,1)S(1)}, u32[]{:S(2)}, u32[]{:S(2)}) collective-permute-start(bf16[128,256]{1,0:T(8,128)(2,1)S(1)} %dynamic-slice_convert_fusion.3), channel_id=1, source_target_pairs={{0,8},{4,12},{8,0},{12,4},{16,24},{20,28},{24,16},{28,20},{1,9},{5... | collective-permute-start | bytes 196616 | tf_op jit(solution)/shard_map/ppermute | solution.py:17
  111.3 15.9 %collective-permute-start.47 = (bf16[128,256]{1,0:T(8,128)(2,1)S(1)}, bf16[128,256]{1,0:T(8,128)(2,1)S(1)}, u32[]{:S(2)}, u32[]{:S(2)}) collective-permute-start(bf16[128,256]{1,0:T(8,128)(2,1)S(1)} %dynamic-slice_convert_fusion.2), channel_id=1, source_target_pairs={{0,16},{4,20},{8,24},{12,28},{16,0},{20,4},{24,8},{28,12},{1,17},{... | collective-permute-start | bytes 196616 | tf_op jit(solution)/shard_map/ppermute | solution.py:17
  122.5 35.6 %collective-permute-start.57 = (bf16[256,256]{1,0:T(8,128)(2,1)S(1)}, bf16[256,256]{1,0:T(8,128)(2,1)S(1)}, u32[]{:S(2)}, u32[]{:S(2)}) collective-permute-start(bf16[256,256]{1,0:T(8,128)(2,1)S(1)} %maximum_select_fusion.10), channel_id=1, source_target_pairs={{0,4},{4,0},{8,12},{12,8},{16,20},{20,16},{24,28},{28,24},{1,5},{5... | collective-permute-start | bytes 393224 | tf_op jit(solution)/shard_map/ppermute | solution.py:17
  127.0 33.1 %collective-permute-start.63 = (bf16[256,256]{1,0:T(8,128)(2,1)S(1)}, bf16[256,256]{1,0:T(8,128)(2,1)S(1)}, u32[]{:S(2)}, u32[]{:S(2)}) collective-permute-start(bf16[256,256]{1,0:T(8,128)(2,1)S(1)} %maximum_select_fusion.11), channel_id=1, source_target_pairs={{0,8},{4,12},{8,0},{12,4},{16,24},{20,28},{24,16},{28,20},{1,9},{5... | collective-permute-start | bytes 393224 | tf_op jit(solution)/shard_map/ppermute | solution.py:17
  131.1 12.7 %collective-permute-start.29 = (bf16[128,256]{1,0:T(8,128)(2,1)S(1)}, bf16[128,256]{1,0:T(8,128)(2,1)S(1)}, u32[]{:S(2)}, u32[]{:S(2)}) collective-permute-start(bf16[128,256]{1,0:T(8,128)(2,1)S(1)} %dynamic-slice_convert_fusion.5), channel_id=1, source_target_pairs={{0,8},{4,12},{8,0},{12,4},{16,24},{20,28},{24,16},{28,20},{1,9},{5... | collective-permute-start | bytes 196616 | tf_op jit(solution)/shard_map/ppermute | solution.py:17
  132.1 14.3 %collective-permute-start.35 = (bf16[128,256]{1,0:T(8,128)(2,1)S(1)}, bf16[128,256]{1,0:T(8,128)(2,1)S(1)}, u32[]{:S(2)}, u32[]{:S(2)}) collective-permute-start(bf16[128,256]{1,0:T(8,128)(2,1)S(1)} %dynamic-slice_convert_fusion.4), channel_id=1, source_target_pairs={{0,16},{4,20},{8,24},{12,28},{16,0},{20,4},{24,8},{28,12},{1,17},{... | collective-permute-start | bytes 196616 | tf_op jit(solution)/shard_map/ppermute | solution.py:17
  143.5 12.3 %collective-permute-start.44 = (bf16[128,256]{1,0:T(8,128)(2,1)S(1)}, bf16[128,256]{1,0:T(8,128)(2,1)S(1)}, u32[]{:S(2)}, u32[]{:S(2)}) collective-permute-start(bf16[128,256]{1,0:T(8,128)(2,1)S(1)} %maximum_select_fusion.14), channel_id=1, source_target_pairs={{0,8},{4,12},{8,0},{12,4},{16,24},{20,28},{24,16},{28,20},{1,9},{5... | collective-permute-start | bytes 196616 | tf_op jit(solution)/shard_map/ppermute | solution.py:17
  143.8 12.9 %collective-permute-start.50 = (bf16[128,256]{1,0:T(8,128)(2,1)S(1)}, bf16[128,256]{1,0:T(8,128)(2,1)S(1)}, u32[]{:S(2)}, u32[]{:S(2)}) collective-permute-start(bf16[128,256]{1,0:T(8,128)(2,1)S(1)} %maximum_select_fusion.15), channel_id=1, source_target_pairs={{0,16},{4,20},{8,24},{12,28},{16,0},{20,4},{24,8},{28,12},{1,17},{... | collective-permute-start | bytes 196616 | tf_op jit(solution)/shard_map/ppermute | solution.py:17
  156.7 11.8 %collective-permute-start.45 = (bf16[256,256]{1,0:T(8,128)(2,1)S(1)}, bf16[256,256]{1,0:T(8,128)(2,1)S(1)}, u32[]{:S(2)}, u32[]{:S(2)}) collective-permute-start(bf16[256,256]{1,0:T(8,128)(2,1)S(1)} %maximum_select_fusion.8), channel_id=1, source_target_pairs={{0,4},{4,0},{8,12},{12,8},{16,20},{20,16},{24,28},{28,24},{1,5},{5... | collective-permute-start | bytes 393224 | tf_op jit(solution)/shard_map/ppermute | solution.py:17
  (69 other events, 384.3 us)

commit v3 on v2

--- a/solution.py
+++ b/solution.py
@@ -9,9 +9,6 @@
 REACH_AHEAD = sum(DILATIONS)
 BACK = -(-REACH_BACK // 16) * 16
 AHEAD = -(-REACH_AHEAD // 16) * 16
-CHUNKS = 2
-
-
 def exchange(block, axis, distance):
     count = lax.axis_size(axis)
     return lax.ppermute(block, axis, [(i, i ^ distance) for i in range(count)])
@@ -34,9 +31,8 @@
     width = blocks[0].shape[1]
     for distance in distances("ch"):
         sent = [j for j in blocks if j & distance]
-        other = exchange(
-            jnp.concatenate([blocks[j].astype(jnp.bfloat16) for j in sent], axis=1), "ch", distance
-        )
+        packed = jnp.concatenate([blocks[j].astype(jnp.bfloat16) for j in sent], axis=1)
+        other = exchange(packed, "ch", distance)
         for place, j in enumerate(sent):
             part = other[:, place * width : (place + 1) * width]
             blocks[j ^ distance] = blocks[j ^ distance] + part.astype(jnp.float32)
@@ -44,36 +40,21 @@
     return blocks[0].astype(jnp.bfloat16)
 
 
-def sum_over_seq(part, order):
-    me = lax.axis_index("seq")
-    for distance in order:
-        half = part.shape[0] // 2
-        bit = (me & distance) // distance
-        sent = lax.dynamic_slice_in_dim(part, (1 - bit) * half, half, 0).astype(jnp.bfloat16)
-        kept = lax.dynamic_slice_in_dim(part, bit * half, half, 0)
-        part = kept.astype(jnp.float32) + exchange(sent, "seq", distance).astype(jnp.float32)
+def halve(part, distance):
+    half = part.shape[0] // 2
+    bit = (lax.axis_index("seq") & distance) // distance
+    sent = lax.dynamic_slice_in_dim(part, (1 - bit) * half, half, 0).astype(jnp.bfloat16)
+    kept = lax.dynamic_slice_in_dim(part, bit * half, half, 0)
+    return kept.astype(jnp.float32) + exchange(sent, "seq", distance).astype(jnp.float32)
+
+
+def double(part, distance):
     part = part.astype(jnp.bfloat16)
-    for distance in reversed(order):
-        bit = (me & distance) // distance
-        other = exchange(part, "seq", distance)
-        part = jnp.where(
-            bit == 0, jnp.concatenate([part, other], axis=0), jnp.concatenate([other, part], axis=0)
-        )
-    return part
-
-
-def sum_gradient(part):
-    order = distances("seq")
-    half = part.shape[0] // 2
-    return jnp.concatenate(
-        [sum_over_seq(part[:half], order), sum_over_seq(part[half:], order[1:] + order[:1])], axis=0
-    )
-
-
-def sum_small(part):
-    for distance in distances("seq"):
-        part = part + exchange(part, "seq", distance)
-    return part
+    bit = (lax.axis_index("seq") & distance) // distance
+    other = exchange(part, "seq", distance)
+    return jnp.where(
+        bit == 0, jnp.concatenate([part, other], axis=0), jnp.concatenate([other, part], axis=0)
+    )
 
 
 def reorder(array, width, axis=0):
@@ -135,15 +116,10 @@
     shift = lax.dot_general(one_hot, embedding, (((0,), (0,)), ((), ())), preferred_element_type=f32)
     local_input = (hidden.astype(f32) + shift).astype(bf16)
 
-    edges = [jnp.concatenate(halo(local_input, BACK, AHEAD, far), axis=0) for far in range(0, channels, 2)]
     mains = gather_relative(local_input)
-    edge_blocks = {}
-    packed = exchange(jnp.concatenate(edges, axis=0), "ch", 1)
-    for place, far in enumerate(range(0, channels, 2)):
-        edge_blocks[far] = edges[place]
-        edge_blocks[far ^ 1] = packed[place * (BACK + AHEAD) : (place + 1) * (BACK + AHEAD)]
+    edge_source, mains[1] = lax.optimization_barrier((local_input, mains[1]))
+    edges = [jnp.concatenate(halo(edge_source, BACK, AHEAD, far), axis=0) for far in range(0, channels, 2)]
     full_input = jnp.concatenate(mains, axis=1)
-    edge_input = jnp.concatenate([edge_blocks[j] for j in range(channels)], axis=1)
 
     w_in_r = reorder(w_in, width)
     w_gate_r = reorder(w_gate, width)
@@ -154,14 +130,20 @@
     choose = (index_r[:, None] == order_r[None, :]).astype(bf16)
     choose_inverse = (order_r[:, None] == index_r[None, :width]).astype(bf16)
 
+    early_cotangent, edges[0] = lax.optimization_barrier((cotangent, edges[0]))
     grad_terms = lax.dot_general(
-        cotangent, w_out_r, (((1,), (1,)), ((), ())), preferred_element_type=f32
+        early_cotangent, w_out_r, (((1,), (1,)), ((), ())), preferred_element_type=f32
     ).astype(bf16)
     grad_own = sum_relative(
         [grad_terms[:, j * width : (j + 1) * width].astype(f32) for j in range(channels)]
     )
-    grad_norm = jnp.concatenate(gather_relative(grad_own), axis=1)
-
+
+    edge_blocks = {}
+    packed = exchange(jnp.concatenate(edges, axis=0), "ch", 1)
+    for place, far in enumerate(range(0, channels, 2)):
+        edge_blocks[far] = edges[place]
+        edge_blocks[far ^ 1] = packed[place * (BACK + AHEAD) : (place + 1) * (BACK + AHEAD)]
+    edge_input = jnp.concatenate([edge_blocks[j] for j in range(channels)], axis=1)
     projected = jnp.dot(full_input, w_in_r, preferred_element_type=f32).astype(bf16)
     projected_edge = jnp.dot(edge_input, w_in_r, preferred_element_type=f32).astype(bf16)
     level = jnp.concatenate([projected_edge[:BACK], projected, projected_edge[BACK:]], axis=0)
@@ -188,29 +170,24 @@
     gate_act = gate_pre * sigmoid
     gated = (level_3.astype(f32) * gate_act).astype(bf16)
 
-    flipped = flip(gated)
-    size = rows // CHUNKS
-    chunks = [slice(k * size, (k + 1) * size) for k in range(CHUNKS)]
-    mirrored = [mirror(flipped[chunk]) for chunk in chunks]
+    mirrored = mirror(flip(gated))
     gated_full = jnp.concatenate(gather_relative(gated), axis=1)
-    grad_comb, grad_mirror, normalized = [], [], []
-    for chunk, part in zip(chunks, mirrored):
-        mirrored_full = jnp.concatenate(gather_relative(part), axis=1)
-        combined = gated_full[chunk].astype(f32) + jnp.dot(
-            mirrored_full, choose, preferred_element_type=f32
-        )
-        inv_scale = lax.rsqrt(jnp.mean(combined * combined, axis=1, keepdims=True) + EPSILON)
-        hat = combined * inv_scale
-        scaled = grad_norm[chunk].astype(f32) * gain_r[None, :]
-        row_total = jnp.sum(scaled * hat, axis=1, keepdims=True)
-        grad_here = (inv_scale * (scaled - hat * row_total / full)).astype(bf16)
-        chosen = jnp.dot(grad_here, choose_inverse, preferred_element_type=f32).astype(bf16)
-        grad_mirror.append(mirror(flip(chosen)))
-        grad_comb.append(grad_here[:, :width])
-        normalized.append((hat * gain_r[None, :]).astype(bf16))
-    normalized = jnp.concatenate(normalized, axis=0)
-    grad_comb = jnp.concatenate(grad_comb, axis=0)
-    grad_mirror = jnp.concatenate(grad_mirror[::-1], axis=0)
+    grad_blocks = gather_relative(grad_own)
+    mirrored, grad_blocks[channels // 2] = lax.optimization_barrier((mirrored, grad_blocks[channels // 2]))
+    grad_norm = jnp.concatenate(grad_blocks, axis=1).astype(f32)
+    mirrored_full = jnp.concatenate(gather_relative(mirrored), axis=1)
+    combined = gated_full.astype(f32) + jnp.dot(mirrored_full, choose, preferred_element_type=f32)
+    inv_scale = lax.rsqrt(jnp.mean(combined * combined, axis=1, keepdims=True) + EPSILON)
+    hat = combined * inv_scale
+    scaled = grad_norm * gain_r[None, :]
+    row_total = jnp.sum(scaled * hat, axis=1, keepdims=True)
+    grad_full = (inv_scale * (scaled - hat * row_total / full)).astype(bf16)
+    grad_comb = grad_full[:, :width]
+    chosen = jnp.dot(grad_full, choose_inverse, preferred_element_type=f32).astype(bf16)
+    flipped = flip(chosen)
+    normalized = (hat * gain_r[None, :]).astype(bf16)
+    normalized, flipped = lax.optimization_barrier((normalized, flipped))
+    grad_mirror = mirror(flipped)
 
     output = (
         local_input.astype(f32) + jnp.dot(normalized, w_out_r, preferred_element_type=f32)
@@ -222,7 +199,11 @@
         product = lax.dot_general(left, right, contract_rows, preferred_element_type=f32)
         return reorder(product.astype(bf16), width)
 
-    grad_out = sum_gradient(weight_grad(normalized, cotangent))
+    steps = distances("seq")
+    turned = steps[1:] + steps[:1]
+    sum_out = weight_grad(normalized, cotangent)
+    sum_out = halve(sum_out, steps[0])
+    grad_comb, sum_out = lax.optimization_barrier((grad_comb, sum_out))
 
     grad_gated = grad_comb.astype(f32) + grad_mirror.astype(f32)
     upstream = (grad_gated * gate_act).astype(bf16)
@@ -231,8 +212,10 @@
     ).astype(bf16)
     before, after = AHEAD, BACK
     left, right = halo(upstream, before, after)
+    sum_out = halve(sum_out, steps[1])
     extended = jnp.concatenate([left, upstream, right], axis=0)
-    grad_gate = sum_gradient(weight_grad(full_input, grad_gate_pre))
+    extended, sum_out = lax.optimization_barrier((extended, sum_out))
+    rest = [(halve, distance) for distance in steps[2:]] + [(double, distance) for distance in steps[::-1]]
     tap_grads = []
     for number in reversed(range(len(DILATIONS))):
         dilation = DILATIONS[number]
@@ -254,10 +237,34 @@
             total = jnp.where(inside(next_before, rows, next_after), total, 0.0)
         extended = total.astype(bf16)
         before, after = next_before, next_after
-    taps = jnp.stack([jnp.stack(tap_grads[4 * (2 - number) : 4 * (3 - number)]) for number in range(3)])
-    grad_conv = sum_small(taps)
-    grad_in = sum_gradient(weight_grad(full_input, extended))
-    return output, grad_in, grad_gate, grad_out, grad_conv
+    taps = jnp.stack([tap_grads[4 * (2 - number) + tap] for number in range(3) for tap in range(4)])
+    spare = -taps.shape[0] % 128
+    product = jnp.concatenate(
+        [
+            weight_grad(full_input, extended),
+            jnp.pad(taps, ((0, spare), (0, 0))).astype(bf16),
+        ],
+        axis=0,
+    )
+    sum_in, sum_gate = product, weight_grad(full_input, grad_gate_pre)
+    for place in range(len(steps)):
+        sum_in, sum_gate, sum_out = lax.optimization_barrier((sum_in, sum_gate, sum_out))
+        sum_in = halve(sum_in, steps[place])
+        sum_gate = halve(sum_gate, turned[place])
+        move, distance = rest.pop(0)
+        sum_out = move(sum_out, distance)
+    for place in reversed(range(len(steps))):
+        sum_in, sum_gate, sum_out = lax.optimization_barrier((sum_in, sum_gate, sum_out))
+        sum_in = double(sum_in, steps[place])
+        sum_gate = double(sum_gate, turned[place])
+        if rest:
+            move, distance = rest.pop(0)
+            sum_out = move(sum_out, distance)
+    for move, distance in rest:
+        sum_out = move(sum_out, distance)
+    grad_in = sum_in[:full]
+    grad_conv = sum_in[full : full + taps.shape[0]].astype(f32).reshape(conv_w.shape)
+    return output, grad_in, sum_gate, sum_out, grad_conv
 
 
 def solution(mesh):

time: 173 us -> 162 us (0.936)
  starting transfers between devices: 92.7 us -> 55.4 us
  waiting for transfers between devices: 46.8 us -> 61 us
  local copies, waits for them, and re-layouts: 3.08 us -> 9.82 us
  matrix products: 13 us -> 18.1 us
    ppermute x57 -> x33, starting transfers between devices: 68.4 us -> 37 us  [exchange(): return lax.ppermute(block, axis, [(i, i ^ distance) for i in range(count)])]
    ppermute x57 -> x33, waiting for transfers between devices: 43.6 us -> 51.4 us  [exchange(): return lax.ppermute(block, axis, [(i, i ^ distance) for i in range(count)])]
    ppermute x6, waiting for transfers between devices: 0.02 us -> 5.19 us  [halo(): received.append(lax.ppermute(sent, ('seq', 'ch'), route))]
    ppermute x6, starting transfers between devices: 12.9 us -> 9.31 us  [halo(): received.append(lax.ppermute(sent, ('seq', 'ch'), route))]
    concatenate x5 -> x2, other arithmetic: 3.78 us -> 0.29 us  [the longest x1 0.2 us: local(): extended = jnp.concatenate([left, upstream, right], axis=0)]
    dynamic_slice x12 -> x11, local copies, waits for them, and re-layouts: 0.74 us -> 3.44 us  [reorder(): lax.dynamic_slice_in_dim(array, (me ^ j) * width, width, axis)]
    dot_general x3, matrix products: 1.89 us -> 4.31 us  [weight_grad(): lax.dot_general(left, right, contract_rows, preferred_element_type=f32)]
    ppermute x4 -> x2, starting transfers between devices: 11.4 us -> 9.15 us  [mirror(): lax.ppermute(block, 'seq', [(i, count - 1 - i) for i in range(count)])]
  transfers between devices with their start and end apart: 67 -> 41, of which waited for: 21 -> 20; matrix products, arithmetic and copies ran while one was open for 12% -> 14% of each run, Pallas kernels for 0% -> 0%
where the time goes in v3:
time: 162 us; the launch traced here: 161 us
  waiting for transfers between devices  61 us (38%)
  starting transfers between devices  55.4 us (34%)
  matrix products  18.1 us (11%)
  other arithmetic  15.1 us (9%)
  local copies, waits for them, and re-layouts  9.82 us (6%)
  between operations  2 us (1%)
    ppermute x33, waiting for transfers between devices, exchange(): return lax.ppermute(block, axis, [(i, i ^ distance) for i in range(count)])  51.4 us
    ppermute x33, starting transfers between devices, exchange(): return lax.ppermute(block, axis, [(i, i ^ distance) for i in range(count)])  37 us
    ppermute x6, starting transfers between devices, halo(): received.append(lax.ppermute(sent, ('seq', 'ch'), route))  9.31 us
    ppermute x2, starting transfers between devices, mirror(): lax.ppermute(block, 'seq', [(i, count - 1 - i) for i in range(count)])  9.15 us
    ppermute x6, waiting for transfers between devices, halo(): received.append(lax.ppermute(sent, ('seq', 'ch'), route))  5.19 us
    ppermute x2, waiting for transfers between devices, mirror(): lax.ppermute(block, 'seq', [(i, count - 1 - i) for i in range(count)])  4.35 us
    dot_general x3, matrix products, weight_grad(): lax.dot_general(left, right, contract_rows, preferred_element_type=f32)  4.31 us
    dynamic_slice x11, local copies, waits for them, and re-layouts, reorder(): lax.dynamic_slice_in_dim(array, (me ^ j) * width, width, axis)  3.44 us
  transfers between devices with their start and end apart: 41, of which 20 were waited for; matrix products, arithmetic and copies ran while one was open for 14% of the time, Pallas kernels for 0%

profile of v3, /device:TPU:0, one launch (start us, length us, event | category | flops | bytes accessed | tf_op | source)
XLA Modules:
  0.0 161.5 jit_solution(8300791643426633650)
XLA Ops:
  11.4 4.3 %collective-permute-start.3 = (bf16[160,256]{0,1:T(8,128)(2,1)S(1)}, bf16[160,256]{0,1:T(8,128)(2,1)S(1)}, u32[]{:S(2)}, u32[]{:S(2)}) collective-permute-start(bf16[160,256]{0,1:T(8,128)(2,1)S(1)} %get-tuple-element.113), channel_id=1, source_target_pairs={{0,6},{4,2},{1,7},{5,3},{2,4},{6,0},{3,5},{7,1},{8,14},{12,10},{9,... | collective-permute-start | bytes 245768 | tf_op jit(solution)/shard_map/ppermute | solution.py:91
  25.8 4.1 %collective-permute-start.13 = (bf16[512,256]{0,1:T(8,128)(2,1)S(1)}, bf16[512,256]{0,1:T(8,128)(2,1)S(1)}, u32[]{:S(2)}, u32[]{:S(2)}) collective-permute-start(bf16[512,256]{0,1:T(8,128)(2,1)S(1)} %add_convert_fusion.1), channel_id=1, source_target_pairs={{0,2},{1,3},{2,0},{3,1},{4,6},{5,7},{6,4},{7,5},{8,10},{9,11},{10,... | collective-permute-start | bytes 786440 | tf_op jit(solution)/shard_map/ppermute | solution.py:14
  32.8 4.6 %collective-permute-start.11 = (bf16[512,256]{1,0:T(8,128)(2,1)S(1)}, bf16[512,256]{1,0:T(8,128)(2,1)S(1)}, u32[]{:S(2)}, u32[]{:S(2)}) collective-permute-start(bf16[512,256]{1,0:T(8,128)(2,1)S(1)} %convolution_convert_fusion.6), channel_id=1, source_target_pairs={{0,28},{4,24},{8,20},{12,16},{16,12},{20,8},{24,4},{28,0},{1,29},{... | collective-permute-start | bytes 786440 | tf_op jit(solution)/shard_map/ppermute | solution.py:70
  39.5 4.3 %collective-permute-done.11 = bf16[512,256]{1,0:T(8,128)(2,1)S(1)} collective-permute-done((bf16[512,256]{1,0:T(8,128)(2,1)S(1)}, bf16[512,256]{1,0:T(8,128)(2,1)S(1)}, u32[]{:S(2)}, u32[]{:S(2)}) %collective-permute-start.11) | collective-permute-done | bytes 262176 | tf_op jit(solution)/shard_map/ppermute | solution.py:70
  43.9 2.8 %collective-permute-done.14 = bf16[512,256]{0,1:T(8,128)(2,1)S(1)} collective-permute-done((bf16[512,256]{0,1:T(8,128)(2,1)S(1)}, bf16[512,256]{0,1:T(8,128)(2,1)S(1)}, u32[]{:S(2)}, u32[]{:S(2)}) %collective-permute-start.14) | collective-permute-done | bytes 262176 | tf_op jit(solution)/shard_map/ppermute | solution.py:14
  47.9 4.5 %collective-permute-done.9 = bf16[512,256]{0,1:T(8,128)(2,1)S(1)} collective-permute-done((bf16[512,256]{0,1:T(8,128)(2,1)S(1)}, bf16[512,256]{0,1:T(8,128)(2,1)S(1)}, u32[]{:S(2)}, u32[]{:S(2)}) %collective-permute-start.9) | collective-permute-done | bytes 262176 | tf_op jit(solution)/shard_map/ppermute | solution.py:14
  52.9 3.8 %collective-permute-done.16 = bf16[512,256]{1,0:T(8,128)(2,1)S(1)} collective-permute-done((bf16[512,256]{1,0:T(8,128)(2,1)S(1)}, bf16[512,256]{1,0:T(8,128)(2,1)S(1)}, u32[]{:S(2)}, u32[]{:S(2)}) %collective-permute-start.16) | collective-permute-done | bytes 262176 | tf_op jit(solution)/shard_map/ppermute | solution.py:14
  58.3 2.8 %multiply_reduce_fusion.1 = (f32[512]{0:T(512)S(1)}, f32[512,1024]{0,1:T(8,128)S(1)}) fusion(s32[1024]{0:T(1024)S(1)} %pad_add_fusion.1, s32[1024]{0:T(1024)S(1)} %pad_add_fusion, bf16[512,256]{1,0:T(8,128)(2,1)} %collective-permute-done.17, bf16[512,256]{1,0:T(8,128)(2,1)S(1)} %collective-permute-done.16, bf16[512,256]{1,0:T(8,128)(2,1)} %collective-permute-done.15, ...), kind=kOutput, calls=%fused_computation.6 | convolution fusion | flops 1084751360 | bytes 4204544 | tf_op jit(solution)/shard_map/dot_general | solution.py:179
  67.0 2.6 %collective-permute-start.20 = (bf16[512,256]{1,0:T(8,128)(2,1)}, bf16[512,256]{1,0:T(8,128)(2,1)}, u32[]{:S(2)}, u32[]{:S(2)}) collective-permute-start(bf16[512,256]{1,0:T(8,128)(2,1)} %constant_dynamic-slice_fusion.6), channel_id=1, source_target_pairs={{0,4},{4,0},{8,12},{12,8},{16,20},{20,16},{24,28},{28,24},{1,5},{5... | collective-permute-start | bytes 786440 | tf_op jit(solution)/shard_map/ppermute | solution.py:14
  70.1 4.6 %collective-permute-start.21 = (bf16[512,256]{0,1:T(8,128)(2,1)}, bf16[512,256]{0,1:T(8,128)(2,1)}, u32[]{:S(2)}, u32[]{:S(2)}) collective-permute-start(bf16[512,256]{0,1:T(8,128)(2,1)} %convolution_convert_fusion.4), channel_id=1, source_target_pairs={{0,28},{4,24},{8,20},{12,16},{16,12},{20,8},{24,4},{28,0},{1,29},{... | collective-permute-start | bytes 786440 | tf_op jit(solution)/shard_map/ppermute | solution.py:70
  76.2 5.9 %collective-permute-done.20 = bf16[512,256]{1,0:T(8,128)(2,1)} collective-permute-done((bf16[512,256]{1,0:T(8,128)(2,1)}, bf16[512,256]{1,0:T(8,128)(2,1)}, u32[]{:S(2)}, u32[]{:S(2)}) %collective-permute-start.20) | collective-permute-done | bytes 262176 | tf_op jit(solution)/shard_map/ppermute | solution.py:14
  85.2 3.5 %collective-permute-start.24 = (bf16[256,256]{1,0:T(8,128)(2,1)S(1)}, bf16[256,256]{1,0:T(8,128)(2,1)S(1)}, u32[]{:S(2)}, u32[]{:S(2)}) collective-permute-start(bf16[256,256]{1,0:T(8,128)(2,1)S(1)} %dynamic-slice_convert_fusion.2), channel_id=1, source_target_pairs={{0,8},{4,12},{8,0},{12,4},{16,24},{20,28},{24,16},{28,20},{1,9},{5... | collective-permute-start | bytes 393224 | tf_op jit(solution)/shard_map/ppermute | solution.py:14
  92.2 2.8 %collective-permute-done.22 = bf16[160,256]{0,1:T(8,128)(2,1)S(1)} collective-permute-done((bf16[160,256]{0,1:T(8,128)(2,1)S(1)}, bf16[160,256]{0,1:T(8,128)(2,1)S(1)}, u32[]{:S(2)}, u32[]{:S(2)}) %collective-permute-start.22) | collective-permute-done | bytes 81952 | tf_op jit(solution)/shard_map/ppermute | solution.py:91
  102.0 5.4 %collective-permute-start.27 = (bf16[128,256]{1,0:T(8,128)(2,1)S(1)}, bf16[128,256]{1,0:T(8,128)(2,1)S(1)}, u32[]{:S(2)}, u32[]{:S(2)}) collective-permute-start(bf16[128,256]{1,0:T(8,128)(2,1)S(1)} %dynamic-slice_convert_fusion.5), channel_id=1, source_target_pairs={{0,16},{4,20},{8,24},{12,28},{16,0},{20,4},{24,8},{28,12},{1,17},{... | collective-permute-start | bytes 196616 | tf_op jit(solution)/shard_map/ppermute | solution.py:14
  110.0 3.9 %collective-permute-done.26 = bf16[512,256]{1,0:T(8,128)(2,1)S(1)} collective-permute-done((bf16[512,256]{1,0:T(8,128)(2,1)S(1)}, bf16[512,256]{1,0:T(8,128)(2,1)S(1)}, u32[]{:S(2)}, u32[]{:S(2)}) %collective-permute-start.26) | collective-permute-done | bytes 262176 | tf_op jit(solution)/shard_map/ppermute | solution.py:14
  116.7 2.8 %collective-permute-start.29 = (bf16[256,256]{1,0:T(8,128)(2,1)S(1)}, bf16[256,256]{1,0:T(8,128)(2,1)S(1)}, u32[]{:S(2)}, u32[]{:S(2)}) collective-permute-start(bf16[256,256]{1,0:T(8,128)(2,1)S(1)} %dynamic-slice_convert_fusion.1), channel_id=1, source_target_pairs={{0,16},{4,20},{8,24},{12,28},{16,0},{20,4},{24,8},{28,12},{1,17},{... | collective-permute-start | bytes 393224 | tf_op jit(solution)/shard_map/ppermute | solution.py:14
  119.6 2.7 %collective-permute-done.30 = bf16[128,256]{1,0:T(8,128)(2,1)S(1)} collective-permute-done((bf16[128,256]{1,0:T(8,128)(2,1)S(1)}, bf16[128,256]{1,0:T(8,128)(2,1)S(1)}, u32[]{:S(2)}, u32[]{:S(2)}) %collective-permute-start.30) | collective-permute-done | bytes 65568 | tf_op jit(solution)/shard_map/ppermute | solution.py:14
  122.4 2.7 %collective-permute-done.29 = bf16[256,256]{1,0:T(8,128)(2,1)S(1)} collective-permute-done((bf16[256,256]{1,0:T(8,128)(2,1)S(1)}, bf16[256,256]{1,0:T(8,128)(2,1)S(1)}, u32[]{:S(2)}, u32[]{:S(2)}) %collective-permute-start.29) | collective-permute-done | bytes 131104 | tf_op jit(solution)/shard_map/ppermute | solution.py:14
  125.0 2.8 %collective-permute-done.28 = bf16[288,256]{1,0:T(8,128)(2,1)S(1)} collective-permute-done((bf16[288,256]{1,0:T(8,128)(2,1)S(1)}, bf16[288,256]{1,0:T(8,128)(2,1)S(1)}, u32[]{:S(2)}, u32[]{:S(2)}) %collective-permute-start.28) | collective-permute-done | bytes 147488 | tf_op jit(solution)/shard_map/ppermute | solution.py:14
  129.9 3.1 %collective-permute-done.32 = bf16[128,256]{1,0:T(8,128)(2,1)S(1)} collective-permute-done((bf16[128,256]{1,0:T(8,128)(2,1)S(1)}, bf16[128,256]{1,0:T(8,128)(2,1)S(1)}, u32[]{:S(2)}, u32[]{:S(2)}) %collective-permute-start.32) | collective-permute-done | bytes 65568 | tf_op jit(solution)/shard_map/ppermute | solution.py:14
  133.0 2.7 %collective-permute-done.31 = bf16[144,256]{1,0:T(8,128)(2,1)S(1)} collective-permute-done((bf16[144,256]{1,0:T(8,128)(2,1)S(1)}, bf16[144,256]{1,0:T(8,128)(2,1)S(1)}, u32[]{:S(2)}, u32[]{:S(2)}) %collective-permute-start.31) | collective-permute-done | bytes 73760 | tf_op jit(solution)/shard_map/ppermute | solution.py:14
  140.3 3.6 %collective-permute-done.34 = bf16[144,256]{1,0:T(8,128)(2,1)S(1)} collective-permute-done((bf16[144,256]{1,0:T(8,128)(2,1)S(1)}, bf16[144,256]{1,0:T(8,128)(2,1)S(1)}, u32[]{:S(2)}, u32[]{:S(2)}) %collective-permute-start.34) | collective-permute-done | bytes 73760 | tf_op jit(solution)/shard_map/ppermute | solution.py:14
  147.6 4.5 %collective-permute-done.38 = bf16[256,256]{1,0:T(8,128)(2,1)S(1)} collective-permute-done((bf16[256,256]{1,0:T(8,128)(2,1)S(1)}, bf16[256,256]{1,0:T(8,128)(2,1)S(1)}, u32[]{:S(2)}, u32[]{:S(2)}) %collective-permute-start.38) | collective-permute-done | bytes 131104 | tf_op jit(solution)/shard_map/ppermute | solution.py:14
  155.9 2.8 %collective-permute-done.40 = bf16[512,256]{1,0:T(8,128)(2,1)S(1)} collective-permute-done((bf16[512,256]{1,0:T(8,128)(2,1)S(1)}, bf16[512,256]{1,0:T(8,128)(2,1)S(1)}, u32[]{:S(2)}, u32[]{:S(2)}) %collective-permute-start.40) | collective-permute-done | bytes 262176 | tf_op jit(solution)/shard_map/ppermute | solution.py:14
  (281 shorter events, 71.8 us)
Async XLA Ops:
  3.4 13.0 %collective-permute-start.6 = (bf16[512,256]{0,1:T(8,128)(2,1)S(1)}, bf16[512,256]{0,1:T(8,128)(2,1)}, u32[]{:S(2)}, u32[]{:S(2)}) collective-permute-start(bf16[512,256]{0,1:T(8,128)(2,1)S(1)} %fusion.7), channel_id=1, source_target_pairs={{0,2},{1,3},{2,0},{3,1},{4,6},{5,7},{6,4},{7,5},{8,10},{9,11},{10,... | collective-permute-start | bytes 786440 | tf_op jit(solution)/shard_map/ppermute | solution.py:14
  9.1 7.3 %collective-permute-start.1 = (bf16[160,256]{0,1:T(8,128)(2,1)S(1)}, bf16[160,256]{0,1:T(8,128)(2,1)S(1)}, u32[]{:S(2)}, u32[]{:S(2)}) collective-permute-start(bf16[160,256]{0,1:T(8,128)(2,1)S(1)} %get-tuple-element.113), channel_id=1, source_target_pairs={{0,4},{4,0},{1,5},{5,1},{2,6},{6,2},{3,7},{7,3},{8,12},{12,8},{9,1... | collective-permute-start | bytes 245768 | tf_op jit(solution)/shard_map/ppermute | solution.py:91
  11.4 7.6 %collective-permute-start.3 = (bf16[160,256]{0,1:T(8,128)(2,1)S(1)}, bf16[160,256]{0,1:T(8,128)(2,1)S(1)}, u32[]{:S(2)}, u32[]{:S(2)}) collective-permute-start(bf16[160,256]{0,1:T(8,128)(2,1)S(1)} %get-tuple-element.113), channel_id=1, source_target_pairs={{0,6},{4,2},{1,7},{5,3},{2,4},{6,0},{3,5},{7,1},{8,14},{12,10},{9,... | collective-permute-start | bytes 245768 | tf_op jit(solution)/shard_map/ppermute | solution.py:91
  25.8 11.6 %collective-permute-start.13 = (bf16[512,256]{0,1:T(8,128)(2,1)S(1)}, bf16[512,256]{0,1:T(8,128)(2,1)S(1)}, u32[]{:S(2)}, u32[]{:S(2)}) collective-permute-start(bf16[512,256]{0,1:T(8,128)(2,1)S(1)} %add_convert_fusion.1), channel_id=1, source_target_pairs={{0,2},{1,3},{2,0},{3,1},{4,6},{5,7},{6,4},{7,5},{8,10},{9,11},{10,... | collective-permute-start | bytes 786440 | tf_op jit(solution)/shard_map/ppermute | solution.py:14
  32.8 11.1 %collective-permute-start.11 = (bf16[512,256]{1,0:T(8,128)(2,1)S(1)}, bf16[512,256]{1,0:T(8,128)(2,1)S(1)}, u32[]{:S(2)}, u32[]{:S(2)}) collective-permute-start(bf16[512,256]{1,0:T(8,128)(2,1)S(1)} %convolution_convert_fusion.6), channel_id=1, source_target_pairs={{0,28},{4,24},{8,20},{12,16},{16,12},{20,8},{24,4},{28,0},{1,29},{... | collective-permute-start | bytes 786440 | tf_op jit(solution)/shard_map/ppermute | solution.py:70
  37.5 9.3 %collective-permute-start.14 = (bf16[512,256]{0,1:T(8,128)(2,1)S(1)}, bf16[512,256]{0,1:T(8,128)(2,1)S(1)}, u32[]{:S(2)}, u32[]{:S(2)}) collective-permute-start(bf16[512,256]{0,1:T(8,128)(2,1)S(1)} %add_convert_fusion), channel_id=1, source_target_pairs={{0,2},{1,3},{2,0},{3,1},{4,6},{5,7},{6,4},{7,5},{8,10},{9,11},{10,... | collective-permute-start | bytes 786440 | tf_op jit(solution)/shard_map/ppermute | solution.py:14
  38.5 13.9 %collective-permute-start.9 = (bf16[512,256]{0,1:T(8,128)(2,1)S(1)}, bf16[512,256]{0,1:T(8,128)(2,1)S(1)}, u32[]{:S(2)}, u32[]{:S(2)}) collective-permute-start(bf16[512,256]{0,1:T(8,128)(2,1)S(1)} %get-tuple-element.82), channel_id=1, source_target_pairs={{0,2},{1,3},{2,0},{3,1},{4,6},{5,7},{6,4},{7,5},{8,10},{9,11},{10,... | collective-permute-start | bytes 786440 | tf_op jit(solution)/shard_map/ppermute | solution.py:14
  46.7 9.9 %collective-permute-start.16 = (bf16[512,256]{1,0:T(8,128)(2,1)S(1)}, bf16[512,256]{1,0:T(8,128)(2,1)S(1)}, u32[]{:S(2)}, u32[]{:S(2)}) collective-permute-start(bf16[512,256]{1,0:T(8,128)(2,1)S(1)} %collective-permute-done.11), channel_id=1, source_target_pairs={{0,2},{1,3},{2,0},{3,1},{4,6},{5,7},{6,4},{7,5},{8,10},{9,11},{10,... | collective-permute-start | bytes 786440 | tf_op jit(solution)/shard_map/ppermute | solution.py:14
  47.9 9.7 %collective-permute-start.8 = (bf16[512,256]{0,1:T(8,128)(2,1)S(1)}, bf16[512,256]{0,1:T(8,128)(2,1)S(1)}, u32[]{:S(2)}, u32[]{:S(2)}) collective-permute-start(bf16[512,256]{0,1:T(8,128)(2,1)S(1)} %get-tuple-element.82), channel_id=1, source_target_pairs={{0,1},{1,0},{2,3},{3,2},{4,5},{5,4},{6,7},{7,6},{8,9},{9,8},{10,11... | collective-permute-start | bytes 786440 | tf_op jit(solution)/shard_map/ppermute | solution.py:14
  67.0 15.2 %collective-permute-start.20 = (bf16[512,256]{1,0:T(8,128)(2,1)}, bf16[512,256]{1,0:T(8,128)(2,1)}, u32[]{:S(2)}, u32[]{:S(2)}) collective-permute-start(bf16[512,256]{1,0:T(8,128)(2,1)} %constant_dynamic-slice_fusion.6), channel_id=1, source_target_pairs={{0,4},{4,0},{8,12},{12,8},{16,20},{20,16},{24,28},{28,24},{1,5},{5... | collective-permute-start | bytes 786440 | tf_op jit(solution)/shard_map/ppermute | solution.py:14
  70.1 13.0 %collective-permute-start.21 = (bf16[512,256]{0,1:T(8,128)(2,1)}, bf16[512,256]{0,1:T(8,128)(2,1)}, u32[]{:S(2)}, u32[]{:S(2)}) collective-permute-start(bf16[512,256]{0,1:T(8,128)(2,1)} %convolution_convert_fusion.4), channel_id=1, source_target_pairs={{0,28},{4,24},{8,20},{12,16},{16,12},{20,8},{24,4},{28,0},{1,29},{... | collective-permute-start | bytes 786440 | tf_op jit(solution)/shard_map/ppermute | solution.py:70
  85.2 10.1 %collective-permute-start.24 = (bf16[256,256]{1,0:T(8,128)(2,1)S(1)}, bf16[256,256]{1,0:T(8,128)(2,1)S(1)}, u32[]{:S(2)}, u32[]{:S(2)}) collective-permute-start(bf16[256,256]{1,0:T(8,128)(2,1)S(1)} %dynamic-slice_convert_fusion.2), channel_id=1, source_target_pairs={{0,8},{4,12},{8,0},{12,4},{16,24},{20,28},{24,16},{28,20},{1,9},{5... | collective-permute-start | bytes 393224 | tf_op jit(solution)/shard_map/ppermute | solution.py:14
  102.0 8.0 %collective-permute-start.27 = (bf16[128,256]{1,0:T(8,128)(2,1)S(1)}, bf16[128,256]{1,0:T(8,128)(2,1)S(1)}, u32[]{:S(2)}, u32[]{:S(2)}) collective-permute-start(bf16[128,256]{1,0:T(8,128)(2,1)S(1)} %dynamic-slice_convert_fusion.5), channel_id=1, source_target_pairs={{0,16},{4,20},{8,24},{12,28},{16,0},{20,4},{24,8},{28,12},{1,17},{... | collective-permute-start | bytes 196616 | tf_op jit(solution)/shard_map/ppermute | solution.py:14
  107.4 6.4 %collective-permute-start.26 = (bf16[512,256]{1,0:T(8,128)(2,1)S(1)}, bf16[512,256]{1,0:T(8,128)(2,1)S(1)}, u32[]{:S(2)}, u32[]{:S(2)}) collective-permute-start(bf16[512,256]{1,0:T(8,128)(2,1)S(1)} %constant_dynamic-slice_fusion), channel_id=1, source_target_pairs={{0,8},{4,12},{8,0},{12,4},{16,24},{20,28},{24,16},{28,20},{1,9},{5... | collective-permute-start | bytes 786440 | tf_op jit(solution)/shard_map/ppermute | solution.py:14
  109.5 6.8 %collective-permute-start.25 = (bf16[576,256]{1,0:T(8,128)(2,1)S(1)}, bf16[576,256]{1,0:T(8,128)(2,1)S(1)}, u32[]{:S(2)}, u32[]{:S(2)}) collective-permute-start(bf16[576,256]{1,0:T(8,128)(2,1)S(1)} %constant_dynamic-slice_fusion.1), channel_id=1, source_target_pairs={{0,4},{4,0},{8,12},{12,8},{16,20},{20,16},{24,28},{28,24},{1,5},{5... | collective-permute-start | bytes 884744 | tf_op jit(solution)/shard_map/ppermute | solution.py:14
  116.7 8.3 %collective-permute-start.29 = (bf16[256,256]{1,0:T(8,128)(2,1)S(1)}, bf16[256,256]{1,0:T(8,128)(2,1)S(1)}, u32[]{:S(2)}, u32[]{:S(2)}) collective-permute-start(bf16[256,256]{1,0:T(8,128)(2,1)S(1)} %dynamic-slice_convert_fusion.1), channel_id=1, source_target_pairs={{0,16},{4,20},{8,24},{12,28},{16,0},{20,4},{24,8},{28,12},{1,17},{... | collective-permute-start | bytes 393224 | tf_op jit(solution)/shard_map/ppermute | solution.py:14
  119.5 8.4 %collective-permute-start.28 = (bf16[288,256]{1,0:T(8,128)(2,1)S(1)}, bf16[288,256]{1,0:T(8,128)(2,1)S(1)}, u32[]{:S(2)}, u32[]{:S(2)}) collective-permute-start(bf16[288,256]{1,0:T(8,128)(2,1)S(1)} %dynamic-slice_convert_fusion), channel_id=1, source_target_pairs={{0,8},{4,12},{8,0},{12,4},{16,24},{20,28},{24,16},{28,20},{1,9},{5... | collective-permute-start | bytes 442376 | tf_op jit(solution)/shard_map/ppermute | solution.py:14
  127.9 7.9 %collective-permute-start.33 = (bf16[256,256]{1,0:T(8,128)(2,1)S(1)}, bf16[256,256]{1,0:T(8,128)(2,1)S(1)}, u32[]{:S(2)}, u32[]{:S(2)}) collective-permute-start(bf16[256,256]{1,0:T(8,128)(2,1)S(1)} %maximum_select_fusion.7), channel_id=1, source_target_pairs={{0,8},{4,12},{8,0},{12,4},{16,24},{20,28},{24,16},{28,20},{1,9},{5... | collective-permute-start | bytes 393224 | tf_op jit(solution)/shard_map/ppermute | solution.py:14
  128.1 7.6 %collective-permute-start.31 = (bf16[144,256]{1,0:T(8,128)(2,1)S(1)}, bf16[144,256]{1,0:T(8,128)(2,1)S(1)}, u32[]{:S(2)}, u32[]{:S(2)}) collective-permute-start(bf16[144,256]{1,0:T(8,128)(2,1)S(1)} %dynamic-slice_convert_fusion.3), channel_id=1, source_target_pairs={{0,16},{4,20},{8,24},{12,28},{16,0},{20,4},{24,8},{28,12},{1,17},{... | collective-permute-start | bytes 221192 | tf_op jit(solution)/shard_map/ppermute | solution.py:14
  136.0 7.9 %collective-permute-start.36 = (bf16[512,256]{1,0:T(8,128)(2,1)S(1)}, bf16[512,256]{1,0:T(8,128)(2,1)S(1)}, u32[]{:S(2)}, u32[]{:S(2)}) collective-permute-start(bf16[512,256]{1,0:T(8,128)(2,1)S(1)} %maximum_select_fusion.4), channel_id=1, source_target_pairs={{0,4},{4,0},{8,12},{12,8},{16,20},{20,16},{24,28},{28,24},{1,5},{5... | collective-permute-start | bytes 786440 | tf_op jit(solution)/shard_map/ppermute | solution.py:14
  144.9 7.1 %collective-permute-start.38 = (bf16[256,256]{1,0:T(8,128)(2,1)S(1)}, bf16[256,256]{1,0:T(8,128)(2,1)S(1)}, u32[]{:S(2)}, u32[]{:S(2)}) collective-permute-start(bf16[256,256]{1,0:T(8,128)(2,1)S(1)} %maximum_select_fusion.8), channel_id=1, source_target_pairs={{0,16},{4,20},{8,24},{12,28},{16,0},{20,4},{24,8},{28,12},{1,17},{... | collective-permute-start | bytes 393224 | tf_op jit(solution)/shard_map/ppermute | solution.py:14
  145.2 6.9 %collective-permute-start.37 = (bf16[288,256]{1,0:T(8,128)(2,1)S(1)}, bf16[288,256]{1,0:T(8,128)(2,1)S(1)}, u32[]{:S(2)}, u32[]{:S(2)}) collective-permute-start(bf16[288,256]{1,0:T(8,128)(2,1)S(1)} %maximum_select_fusion.6), channel_id=1, source_target_pairs={{0,8},{4,12},{8,0},{12,4},{16,24},{20,28},{24,16},{28,20},{1,9},{5... | collective-permute-start | bytes 442376 | tf_op jit(solution)/shard_map/ppermute | solution.py:14
  152.3 6.4 %collective-permute-start.40 = (bf16[512,256]{1,0:T(8,128)(2,1)S(1)}, bf16[512,256]{1,0:T(8,128)(2,1)S(1)}, u32[]{:S(2)}, u32[]{:S(2)}) collective-permute-start(bf16[512,256]{1,0:T(8,128)(2,1)S(1)} %maximum_select_fusion.5), channel_id=1, source_target_pairs={{0,8},{4,12},{8,0},{12,4},{16,24},{20,28},{24,16},{28,20},{1,9},{5... | collective-permute-start | bytes 786440 | tf_op jit(solution)/shard_map/ppermute | solution.py:14
  152.9 6.8 %collective-permute-start.39 = (bf16[576,256]{1,0:T(8,128)(2,1)S(1)}, bf16[576,256]{1,0:T(8,128)(2,1)S(1)}, u32[]{:S(2)}, u32[]{:S(2)}) collective-permute-start(bf16[576,256]{1,0:T(8,128)(2,1)S(1)} %maximum_select_fusion.3), channel_id=1, source_target_pairs={{0,4},{4,0},{8,12},{12,8},{16,20},{20,16},{24,28},{28,24},{1,5},{5... | collective-permute-start | bytes 884744 | tf_op jit(solution)/shard_map/ppermute | solution.py:14
  (70 other events, 602.6 us)

commit v4 on v3

--- a/solution.py
+++ b/solution.py
@@ -24,20 +24,6 @@
         for j in list(blocks):
             blocks[j ^ distance] = exchange(blocks[j], "ch", distance)
     return [blocks[j] for j in range(len(blocks))]
-
-
-def sum_relative(blocks):
-    blocks = dict(enumerate(blocks))
-    width = blocks[0].shape[1]
-    for distance in distances("ch"):
-        sent = [j for j in blocks if j & distance]
-        packed = jnp.concatenate([blocks[j].astype(jnp.bfloat16) for j in sent], axis=1)
-        other = exchange(packed, "ch", distance)
-        for place, j in enumerate(sent):
-            part = other[:, place * width : (place + 1) * width]
-            blocks[j ^ distance] = blocks[j ^ distance] + part.astype(jnp.float32)
-            del blocks[j]
-    return blocks[0].astype(jnp.bfloat16)
 
 
 def halve(part, distance):
@@ -130,13 +116,26 @@
     choose = (index_r[:, None] == order_r[None, :]).astype(bf16)
     choose_inverse = (order_r[:, None] == index_r[None, :width]).astype(bf16)
 
-    early_cotangent, edges[0] = lax.optimization_barrier((cotangent, edges[0]))
-    grad_terms = lax.dot_general(
-        early_cotangent, w_out_r, (((1,), (1,)), ((), ())), preferred_element_type=f32
+    mirrored_cotangent = mirror(flip(cotangent))
+    w_out_r, mains[channels // 2] = lax.optimization_barrier((w_out_r, mains[channels // 2]))
+    w_out_blocks = gather_relative(w_out_r)
+    both_cotangent = jnp.concatenate([cotangent, mirrored_cotangent], axis=0)
+    send_cotangent, w_out_blocks[channels // 2] = lax.optimization_barrier(
+        (both_cotangent, w_out_blocks[channels // 2])
+    )
+    all_cotangent = jnp.concatenate(gather_relative(send_cotangent), axis=1)
+    all_w_out = jnp.concatenate(
+        [
+            jnp.concatenate(
+                [w_out_blocks[j][(i ^ j) * width : ((i ^ j) + 1) * width] for i in range(channels)], axis=0
+            )
+            for j in range(channels)
+        ],
+        axis=1,
+    )
+    grad_norm = lax.dot_general(
+        all_cotangent, all_w_out, (((1,), (1,)), ((), ())), preferred_element_type=f32
     ).astype(bf16)
-    grad_own = sum_relative(
-        [grad_terms[:, j * width : (j + 1) * width].astype(f32) for j in range(channels)]
-    )
 
     edge_blocks = {}
     packed = exchange(jnp.concatenate(edges, axis=0), "ch", 1)
@@ -172,22 +171,20 @@
 
     mirrored = mirror(flip(gated))
     gated_full = jnp.concatenate(gather_relative(gated), axis=1)
-    grad_blocks = gather_relative(grad_own)
-    mirrored, grad_blocks[channels // 2] = lax.optimization_barrier((mirrored, grad_blocks[channels // 2]))
-    grad_norm = jnp.concatenate(grad_blocks, axis=1).astype(f32)
     mirrored_full = jnp.concatenate(gather_relative(mirrored), axis=1)
-    combined = gated_full.astype(f32) + jnp.dot(mirrored_full, choose, preferred_element_type=f32)
+    combined = jnp.concatenate([gated_full, mirrored_full], axis=0).astype(f32) + jnp.dot(
+        jnp.concatenate([mirrored_full, gated_full], axis=0), choose, preferred_element_type=f32
+    )
     inv_scale = lax.rsqrt(jnp.mean(combined * combined, axis=1, keepdims=True) + EPSILON)
     hat = combined * inv_scale
-    scaled = grad_norm * gain_r[None, :]
+    scaled = grad_norm.astype(f32) * gain_r[None, :]
     row_total = jnp.sum(scaled * hat, axis=1, keepdims=True)
-    grad_full = (inv_scale * (scaled - hat * row_total / full)).astype(bf16)
-    grad_comb = grad_full[:, :width]
-    chosen = jnp.dot(grad_full, choose_inverse, preferred_element_type=f32).astype(bf16)
-    flipped = flip(chosen)
-    normalized = (hat * gain_r[None, :]).astype(bf16)
-    normalized, flipped = lax.optimization_barrier((normalized, flipped))
-    grad_mirror = mirror(flipped)
+    grad_comb = (inv_scale * (scaled - hat * row_total / full)).astype(bf16)
+    grad_gated = grad_comb[:rows, :width].astype(f32) + jnp.dot(
+        grad_comb[rows:], choose_inverse, preferred_element_type=f32
+    )
+    both_normalized = (hat * gain_r[None, :]).astype(bf16)
+    normalized = both_normalized[:rows]
 
     output = (
         local_input.astype(f32) + jnp.dot(normalized, w_out_r, preferred_element_type=f32)
@@ -201,21 +198,32 @@
 
     steps = distances("seq")
     turned = steps[1:] + steps[:1]
-    sum_out = weight_grad(normalized, cotangent)
-    sum_out = halve(sum_out, steps[0])
-    grad_comb, sum_out = lax.optimization_barrier((grad_comb, sum_out))
-
-    grad_gated = grad_comb.astype(f32) + grad_mirror.astype(f32)
+    side = lax.axis_index("seq") % 2
+    picked = jnp.concatenate(
+        [
+            lax.dynamic_slice_in_dim(
+                both_normalized, ((side * (channels // 2) + j) ^ lax.axis_index("ch")) * width, width, 1
+            )
+            for j in range(channels // 2)
+        ],
+        axis=1,
+    )
+    sum_out = lax.dot_general(picked, both_cotangent, contract_rows, preferred_element_type=f32)
+
     upstream = (grad_gated * gate_act).astype(bf16)
     grad_gate_pre = (
         grad_gated * level_3.astype(f32) * sigmoid * (1.0 + gate_pre * (1.0 - sigmoid))
     ).astype(bf16)
     before, after = AHEAD, BACK
     left, right = halo(upstream, before, after)
-    sum_out = halve(sum_out, steps[1])
+    sum_gate = halve(weight_grad(full_input, grad_gate_pre), turned[0])
+    sum_out = halve(sum_out, turned[0])
     extended = jnp.concatenate([left, upstream, right], axis=0)
-    extended, sum_out = lax.optimization_barrier((extended, sum_out))
-    rest = [(halve, distance) for distance in steps[2:]] + [(double, distance) for distance in steps[::-1]]
+    extended, sum_gate, sum_out = lax.optimization_barrier((extended, sum_gate, sum_out))
+    rest_gate = [(halve, distance) for distance in turned[1:]] + [(double, distance) for distance in turned[::-1]]
+    rest_out = [(halve, distance) for distance in turned[1:-1]] + [
+        (double, distance) for distance in steps[::-1]
+    ]
     tap_grads = []
     for number in reversed(range(len(DILATIONS))):
         dilation = DILATIONS[number]
@@ -246,22 +254,17 @@
         ],
         axis=0,
     )
-    sum_in, sum_gate = product, weight_grad(full_input, grad_gate_pre)
-    for place in range(len(steps)):
+    sum_in = product
+    rest_in = [(halve, distance) for distance in steps] + [(double, distance) for distance in steps[::-1]]
+    for place, (move, distance) in enumerate(rest_in):
         sum_in, sum_gate, sum_out = lax.optimization_barrier((sum_in, sum_gate, sum_out))
-        sum_in = halve(sum_in, steps[place])
-        sum_gate = halve(sum_gate, turned[place])
-        move, distance = rest.pop(0)
-        sum_out = move(sum_out, distance)
-    for place in reversed(range(len(steps))):
-        sum_in, sum_gate, sum_out = lax.optimization_barrier((sum_in, sum_gate, sum_out))
-        sum_in = double(sum_in, steps[place])
-        sum_gate = double(sum_gate, turned[place])
-        if rest:
-            move, distance = rest.pop(0)
+        sum_in = move(sum_in, distance)
+        if place < len(rest_gate):
+            move, distance = rest_gate[place]
+            sum_gate = move(sum_gate, distance)
+        if place < len(rest_out):
+            move, distance = rest_out[place]
             sum_out = move(sum_out, distance)
-    for move, distance in rest:
-        sum_out = move(sum_out, distance)
     grad_in = sum_in[:full]
     grad_conv = sum_in[full : full + taps.shape[0]].astype(f32).reshape(conv_w.shape)
     return output, grad_in, sum_gate, sum_out, grad_conv

time: 162 us -> 159 us (0.981)
  waiting for transfers between devices: 61 us -> 71.8 us
  starting transfers between devices: 55.4 us -> 47.4 us
  other arithmetic: 15.1 us -> 12.5 us
  local copies, waits for them, and re-layouts: 9.82 us -> 7.52 us
    ppermute x33, waiting for transfers between devices: 51.4 us -> 59.2 us  [exchange(): return lax.ppermute(block, axis, [(i, i ^ distance) for i in range(count)])]
    ppermute x33, starting transfers between devices: 37 us -> 33 us  [exchange(): return lax.ppermute(block, axis, [(i, i ^ distance) for i in range(count)])]
    ppermute x6, waiting for transfers between devices: 5.19 us -> 9.17 us  [halo(): received.append(lax.ppermute(sent, ('seq', 'ch'), route))]
    dot_general x2 -> x4, matrix products: 3.23 us -> 6.53 us  [the longest x1 2.84 us: local(): jnp.dot(jnp.concatenate([mirrored_full, gated_full], axis=0), choose, pre...]
    ppermute x6, starting transfers between devices: 9.31 us -> 6.2 us  [halo(): received.append(lax.ppermute(sent, ('seq', 'ch'), route))]
    dynamic_slice x11 -> x10, local copies, waits for them, and re-layouts: 3.44 us -> 1.34 us  [reorder(): lax.dynamic_slice_in_dim(array, (me ^ j) * width, width, axis)]
    dot_general x3 -> x2, matrix products: 4.31 us -> 3.78 us  [weight_grad(): lax.dot_general(left, right, contract_rows, preferred_element_type=f32)]
  transfers between devices with their start and end apart: 41 -> 41, of which waited for: 20 -> 20; matrix products, arithmetic and copies ran while one was open for 14% -> 13% of each run, Pallas kernels for 0% -> 0%
where the time goes in v4:
time: 159 us; the launch traced here: 158 us
  waiting for transfers between devices  71.8 us (45%)
  starting transfers between devices  47.4 us (30%)
  matrix products  17.8 us (11%)
  other arithmetic  12.5 us (8%)
  local copies, waits for them, and re-layouts  7.52 us (5%)
    ppermute x33, waiting for transfers between devices, exchange(): return lax.ppermute(block, axis, [(i, i ^ distance) for i in range(count)])  59.2 us
    ppermute x33, starting transfers between devices, exchange(): return lax.ppermute(block, axis, [(i, i ^ distance) for i in range(count)])  33 us
    ppermute x6, waiting for transfers between devices, halo(): received.append(lax.ppermute(sent, ('seq', 'ch'), route))  9.17 us
    ppermute x2, starting transfers between devices, mirror(): lax.ppermute(block, 'seq', [(i, count - 1 - i) for i in range(count)])  8.17 us
    ppermute x6, starting transfers between devices, halo(): received.append(lax.ppermute(sent, ('seq', 'ch'), route))  6.2 us
    dot_general x2, matrix products, weight_grad(): lax.dot_general(left, right, contract_rows, preferred_element_type=f32)  3.78 us
    ppermute x2, waiting for transfers between devices, mirror(): lax.ppermute(block, 'seq', [(i, count - 1 - i) for i in range(count)])  3.39 us
  transfers between devices with their start and end apart: 41, of which 20 were waited for; matrix products, arithmetic and copies ran while one was open for 13% of the time, Pallas kernels for 0%

profile of v4, /device:TPU:0, one launch (start us, length us, event | category | flops | bytes accessed | tf_op | source)
XLA Modules:
  0.0 158.5 jit_solution(6283559288021251147)
XLA Ops:
  3.4 2.6 %collective-permute-start.6 = (bf16[512,256]{0,1:T(8,128)(2,1)S(1)}, bf16[512,256]{0,1:T(8,128)(2,1)}, u32[]{:S(2)}, u32[]{:S(2)}) collective-permute-start(bf16[512,256]{0,1:T(8,128)(2,1)S(1)} %fusion.48), channel_id=1, source_target_pairs={{0,2},{1,3},{2,0},{3,1},{4,6},{5,7},{6,4},{7,5},{8,10},{9,11},{10,... | collective-permute-start | bytes 786440 | tf_op jit(solution)/shard_map/ppermute | solution.py:14
  6.0 2.0 %convolution_convert_fusion.2 = bf16[512,256]{1,0:T(8,128)(2,1)} fusion(bf16[512,256]{1,0:T(8,128)(2,1)} %param.19), kind=kOutput, calls=%fused_computation.55 | convolution fusion | flops 134873088 | bytes 524288 | tf_op jit(solution)/shard_map/dot_general | solution.py:87
  8.0 4.6 %collective-permute-start.15 = (bf16[512,256]{1,0:T(8,128)(2,1)}, bf16[512,256]{1,0:T(8,128)(2,1)S(1)}, u32[]{:S(2)}, u32[]{:S(2)}) collective-permute-start(bf16[512,256]{1,0:T(8,128)(2,1)} %convolution_convert_fusion.2), channel_id=1, source_target_pairs={{0,28},{4,24},{8,20},{12,16},{16,12},{20,8},{24,4},{28,0},{1,29},{... | collective-permute-start | bytes 786440 | tf_op jit(solution)/shard_map/ppermute | solution.py:56
  17.0 2.8 %collective-permute-start.3 = (bf16[160,256]{0,1:T(8,128)(2,1)S(1)}, bf16[160,256]{0,1:T(8,128)(2,1)S(1)}, u32[]{:S(2)}, u32[]{:S(2)}) collective-permute-start(bf16[160,256]{0,1:T(8,128)(2,1)S(1)} %get-tuple-element.111), channel_id=1, source_target_pairs={{0,6},{4,2},{1,7},{5,3},{2,4},{6,0},{3,5},{7,1},{8,14},{12,10},{9,... | collective-permute-start | bytes 245768 | tf_op jit(solution)/shard_map/ppermute | solution.py:77
  20.5 9.2 %collective-permute-done.1 = bf16[160,256]{0,1:T(8,128)(2,1)S(1)} collective-permute-done((bf16[160,256]{0,1:T(8,128)(2,1)S(1)}, bf16[160,256]{0,1:T(8,128)(2,1)S(1)}, u32[]{:S(2)}, u32[]{:S(2)}) %collective-permute-start.1) | collective-permute-done | bytes 81952 | tf_op jit(solution)/shard_map/ppermute | solution.py:77
  37.4 3.6 %collective-permute-start.11 = (bf16[512,256]{0,1:T(8,128)(2,1)S(1)}, bf16[512,256]{0,1:T(8,128)(2,1)S(1)}, u32[]{:S(2)}, u32[]{:S(2)}) collective-permute-start(bf16[512,256]{0,1:T(8,128)(2,1)S(1)} %convolution_convert_fusion.3), channel_id=1, source_target_pairs={{0,28},{4,24},{8,20},{12,16},{16,12},{20,8},{24,4},{28,0},{1,29},{... | collective-permute-start | bytes 786440 | tf_op jit(solution)/shard_map/ppermute | solution.py:56
  42.3 2.9 %collective-permute-done.16 = bf16[1024,256]{1,0:T(8,128)(2,1)S(1)} collective-permute-done((bf16[1024,256]{1,0:T(8,128)(2,1)S(1)}, bf16[1024,256]{1,0:T(8,128)(2,1)S(1)}, u32[]{:S(2)}, u32[]{:S(2)}) %collective-permute-start.16) | collective-permute-done | bytes 524320 | tf_op jit(solution)/shard_map/ppermute | solution.py:14
  45.2 3.4 %collective-permute-done.11 = bf16[512,256]{0,1:T(8,128)(2,1)S(1)} collective-permute-done((bf16[512,256]{0,1:T(8,128)(2,1)S(1)}, bf16[512,256]{0,1:T(8,128)(2,1)S(1)}, u32[]{:S(2)}, u32[]{:S(2)}) %collective-permute-start.11) | collective-permute-done | bytes 262176 | tf_op jit(solution)/shard_map/ppermute | solution.py:56
  50.5 16.4 %collective-permute-done.13 = bf16[512,256]{0,1:T(8,128)(2,1)S(1)} collective-permute-done((bf16[512,256]{0,1:T(8,128)(2,1)S(1)}, bf16[512,256]{0,1:T(8,128)(2,1)S(1)}, u32[]{:S(2)}, u32[]{:S(2)}) %collective-permute-start.13) | collective-permute-done | bytes 262176 | tf_op jit(solution)/shard_map/ppermute | solution.py:14
  69.6 2.8 %multiply_reduce_fusion.1 = (f32[1024]{0:T(1024)S(1)}, f32[1024,1024]{0,1:T(8,128)S(1)}) fusion(s32[1024]{0:T(1024)S(1)} %get-tuple-element.140, s32[1024]{0:T(1024)S(1)} %get-tuple-element.139, bf16[512,256]{0,1:T(8,128)(2,1)S(1)} %collective-permute-done.10, bf16[512,256]{0,1:T(8,128)(2,1)S(1)} %collective-permute-done.9, ...), kind=kOutput, calls=%fused_computation.4 | convolution fusion | flops 2172648448 | bytes 6303744 | tf_op jit(solution)/shard_map/dot_general | solution.py:175
  72.4 2.5 %multiply_reduce_fusion = (f32[1024]{0:T(1024)S(1)}, bf16[1024,1024]{0,1:T(8,128)(2,1)S(1)}) fusion(f32[1024,1024]{0,1:T(8,128)S(1)} %get-tuple-element.134, f32[1024]{0:T(1024)S(1)} %pad_maximum_fusion.11, f32[1024]{0:T(1024)S(1)} %add_rsqrt_fusion, bf16[256,256]{1,0:T(8,128)(2,1)S(1)} %get-tuple-element.91, bf16[256,256]{1,0:T(8,128)(2,1)S(1)} %get-tuple-element.92, ...), kind=kOutput, calls=%fused_computation.1 | convolution fusion | flops 2185231360 | bytes 10498048 | tf_op jit(solution)/shard_map/dot_general | solution.py:136
  76.8 4.1 %collective-permute-start.25 = (bf16[256,256]{1,0:T(8,128)(2,1)S(1)}, bf16[256,256]{1,0:T(8,128)(2,1)S(1)}, u32[]{:S(2)}, u32[]{:S(2)}) collective-permute-start(bf16[256,256]{1,0:T(8,128)(2,1)S(1)} %dynamic-slice_convert_fusion.2), channel_id=1, source_target_pairs={{0,8},{4,12},{8,0},{12,4},{16,24},{20,28},{24,16},{28,20},{1,9},{5... | collective-permute-start | bytes 393224 | tf_op jit(solution)/shard_map/ppermute | solution.py:14
  85.3 4.0 %collective-permute-start.24 = (bf16[512,256]{1,0:T(8,128)(2,1)S(1)}, bf16[512,256]{1,0:T(8,128)(2,1)S(1)}, u32[]{:S(2)}, u32[]{:S(2)}) collective-permute-start(bf16[512,256]{1,0:T(8,128)(2,1)S(1)} %constant_dynamic-slice_fusion.3), channel_id=1, source_target_pairs={{0,8},{4,12},{8,0},{12,4},{16,24},{20,28},{24,16},{28,20},{1,9},{5... | collective-permute-start | bytes 786440 | tf_op jit(solution)/shard_map/ppermute | solution.py:14
  90.4 7.4 %collective-permute-done.24 = bf16[512,256]{1,0:T(8,128)(2,1)S(1)} collective-permute-done((bf16[512,256]{1,0:T(8,128)(2,1)S(1)}, bf16[512,256]{1,0:T(8,128)(2,1)S(1)}, u32[]{:S(2)}, u32[]{:S(2)}) %collective-permute-start.24) | collective-permute-done | bytes 262176 | tf_op jit(solution)/shard_map/ppermute | solution.py:14
  101.5 1.9 %convolution_convert_fusion = bf16[1024,256]{1,0:T(8,128)(2,1)S(1)} fusion(bf16[536,256]{0,1:T(8,128)(2,1)S(1)} %select_convert_fusion.2, f32[256]{0:T(256)S(1)} %bitcast.29, f32[256]{0:T(256)S(1)} %bitcast.31, f32[256]{0:T(256)S(1)} %bitcast.33, f32[256]{0:T(256)S(1)} %bitcast.35, bf16[512,256]{0,1:T(8,128)(2,1)S(1)} %collective-permute-done.7, ...), kind=kOutput, calls=%fused_computation.49 | convolution fusion | flops 274464768 | bytes 2625536 | tf_op jit(solution)/shard_map/dot_general | solution.py:196
  107.7 4.2 %collective-permute-done.28 = bf16[128,256]{1,0:T(8,128)(2,1)S(1)} collective-permute-done((bf16[128,256]{1,0:T(8,128)(2,1)S(1)}, bf16[128,256]{1,0:T(8,128)(2,1)S(1)}, u32[]{:S(2)}, u32[]{:S(2)}) %collective-permute-start.28) | collective-permute-done | bytes 65568 | tf_op jit(solution)/shard_map/ppermute | solution.py:14
  117.9 2.5 %collective-permute-done.30 = bf16[128,256]{1,0:T(8,128)(2,1)S(1)} collective-permute-done((bf16[128,256]{1,0:T(8,128)(2,1)S(1)}, bf16[128,256]{1,0:T(8,128)(2,1)S(1)}, u32[]{:S(2)}, u32[]{:S(2)}) %collective-permute-start.30) | collective-permute-done | bytes 65568 | tf_op jit(solution)/shard_map/ppermute | solution.py:14
  127.6 4.0 %collective-permute-done.32 = bf16[144,256]{1,0:T(8,128)(2,1)S(1)} collective-permute-done((bf16[144,256]{1,0:T(8,128)(2,1)S(1)}, bf16[144,256]{1,0:T(8,128)(2,1)S(1)}, u32[]{:S(2)}, u32[]{:S(2)}) %collective-permute-start.32) | collective-permute-done | bytes 73760 | tf_op jit(solution)/shard_map/ppermute | solution.py:14
  132.4 2.3 %collective-permute-start.36 = (bf16[256,256]{1,0:T(8,128)(2,1)S(1)}, bf16[256,256]{1,0:T(8,128)(2,1)S(1)}, u32[]{:S(2)}, u32[]{:S(2)}) collective-permute-start(bf16[256,256]{1,0:T(8,128)(2,1)S(1)} %maximum_select_fusion.8), channel_id=1, source_target_pairs={{0,16},{4,20},{8,24},{12,28},{16,0},{20,4},{24,8},{28,12},{1,17},{... | collective-permute-start | bytes 393224 | tf_op jit(solution)/shard_map/ppermute | solution.py:14
  134.7 2.3 %collective-permute-done.35 = bf16[144,256]{1,0:T(8,128)(2,1)S(1)} collective-permute-done((bf16[144,256]{1,0:T(8,128)(2,1)S(1)}, bf16[144,256]{1,0:T(8,128)(2,1)S(1)}, u32[]{:S(2)}, u32[]{:S(2)}) %collective-permute-start.35) | collective-permute-done | bytes 73760 | tf_op jit(solution)/shard_map/ppermute | solution.py:14
  137.1 2.9 %collective-permute-done.36 = bf16[256,256]{1,0:T(8,128)(2,1)S(1)} collective-permute-done((bf16[256,256]{1,0:T(8,128)(2,1)S(1)}, bf16[256,256]{1,0:T(8,128)(2,1)S(1)}, u32[]{:S(2)}, u32[]{:S(2)}) %collective-permute-start.36) | collective-permute-done | bytes 131104 | tf_op jit(solution)/shard_map/ppermute | solution.py:14
  143.1 3.1 %collective-permute-done.38 = bf16[288,256]{1,0:T(8,128)(2,1)S(1)} collective-permute-done((bf16[288,256]{1,0:T(8,128)(2,1)S(1)}, bf16[288,256]{1,0:T(8,128)(2,1)S(1)}, u32[]{:S(2)}, u32[]{:S(2)}) %collective-permute-start.38) | collective-permute-done | bytes 147488 | tf_op jit(solution)/shard_map/ppermute | solution.py:14
  146.4 2.7 %collective-permute-done.39 = bf16[512,256]{1,0:T(8,128)(2,1)S(1)} collective-permute-done((bf16[512,256]{1,0:T(8,128)(2,1)S(1)}, bf16[512,256]{1,0:T(8,128)(2,1)S(1)}, u32[]{:S(2)}, u32[]{:S(2)}) %collective-permute-start.39) | collective-permute-done | bytes 262176 | tf_op jit(solution)/shard_map/ppermute | solution.py:14
  153.0 3.8 %collective-permute-done.40 = bf16[576,256]{1,0:T(8,128)(2,1)S(1)} collective-permute-done((bf16[576,256]{1,0:T(8,128)(2,1)S(1)}, bf16[576,256]{1,0:T(8,128)(2,1)S(1)}, u32[]{:S(2)}, u32[]{:S(2)}) %collective-permute-start.40) | collective-permute-done | bytes 294944 | tf_op jit(solution)/shard_map/ppermute | solution.py:14
  (200 shorter events, 59.0 us)
Async XLA Ops:
  2.9 12.7 %collective-permute-start = (bf16[512,256]{0,1:T(8,128)(2,1)S(1)}, bf16[512,256]{0,1:T(8,128)(2,1)}, u32[]{:S(2)}, u32[]{:S(2)}) collective-permute-start(bf16[512,256]{0,1:T(8,128)(2,1)S(1)} %fusion.48), channel_id=1, source_target_pairs={{0,1},{1,0},{2,3},{3,2},{4,5},{5,4},{6,7},{7,6},{8,9},{9,8},{10,11... | collective-permute-start | bytes 786440 | tf_op jit(solution)/shard_map/ppermute | solution.py:14
  3.4 16.4 %collective-permute-start.6 = (bf16[512,256]{0,1:T(8,128)(2,1)S(1)}, bf16[512,256]{0,1:T(8,128)(2,1)}, u32[]{:S(2)}, u32[]{:S(2)}) collective-permute-start(bf16[512,256]{0,1:T(8,128)(2,1)S(1)} %fusion.48), channel_id=1, source_target_pairs={{0,2},{1,3},{2,0},{3,1},{4,6},{5,7},{6,4},{7,5},{8,10},{9,11},{10,... | collective-permute-start | bytes 786440 | tf_op jit(solution)/shard_map/ppermute | solution.py:14
  8.0 33.0 %collective-permute-start.15 = (bf16[512,256]{1,0:T(8,128)(2,1)}, bf16[512,256]{1,0:T(8,128)(2,1)S(1)}, u32[]{:S(2)}, u32[]{:S(2)}) collective-permute-start(bf16[512,256]{1,0:T(8,128)(2,1)} %convolution_convert_fusion.2), channel_id=1, source_target_pairs={{0,28},{4,24},{8,20},{12,16},{16,12},{20,8},{24,4},{28,0},{1,29},{... | collective-permute-start | bytes 786440 | tf_op jit(solution)/shard_map/ppermute | solution.py:56
  15.7 13.9 %collective-permute-start.1 = (bf16[160,256]{0,1:T(8,128)(2,1)S(1)}, bf16[160,256]{0,1:T(8,128)(2,1)S(1)}, u32[]{:S(2)}, u32[]{:S(2)}) collective-permute-start(bf16[160,256]{0,1:T(8,128)(2,1)S(1)} %get-tuple-element.111), channel_id=1, source_target_pairs={{0,4},{4,0},{1,5},{5,1},{2,6},{6,2},{3,7},{7,3},{8,12},{12,8},{9,1... | collective-permute-start | bytes 245768 | tf_op jit(solution)/shard_map/ppermute | solution.py:77
  16.3 13.3 %collective-permute-start.2 = (bf16[160,256]{0,1:T(8,128)(2,1)S(1)}, bf16[160,256]{0,1:T(8,128)(2,1)S(1)}, u32[]{:S(2)}, u32[]{:S(2)}) collective-permute-start(bf16[160,256]{0,1:T(8,128)(2,1)S(1)} %get-tuple-element.110), channel_id=1, source_target_pairs={{4,8},{8,4},{5,9},{9,5},{6,10},{10,6},{7,11},{11,7},{12,16},{16,12... | collective-permute-start | bytes 245768 | tf_op jit(solution)/shard_map/ppermute | solution.py:77
  17.0 12.7 %collective-permute-start.3 = (bf16[160,256]{0,1:T(8,128)(2,1)S(1)}, bf16[160,256]{0,1:T(8,128)(2,1)S(1)}, u32[]{:S(2)}, u32[]{:S(2)}) collective-permute-start(bf16[160,256]{0,1:T(8,128)(2,1)S(1)} %get-tuple-element.111), channel_id=1, source_target_pairs={{0,6},{4,2},{1,7},{5,3},{2,4},{6,0},{3,5},{7,1},{8,14},{12,10},{9,... | collective-permute-start | bytes 245768 | tf_op jit(solution)/shard_map/ppermute | solution.py:77
  19.8 9.9 %collective-permute-start.4 = (bf16[160,256]{0,1:T(8,128)(2,1)S(1)}, bf16[160,256]{0,1:T(8,128)(2,1)S(1)}, u32[]{:S(2)}, u32[]{:S(2)}) collective-permute-start(bf16[160,256]{0,1:T(8,128)(2,1)S(1)} %get-tuple-element.110), channel_id=1, source_target_pairs={{4,10},{8,6},{5,11},{9,7},{6,8},{10,4},{7,9},{11,5},{12,18},{16,14... | collective-permute-start | bytes 245768 | tf_op jit(solution)/shard_map/ppermute | solution.py:77
  30.5 14.7 %collective-permute-start.16 = (bf16[1024,256]{1,0:T(8,128)(2,1)S(1)}, bf16[1024,256]{1,0:T(8,128)(2,1)S(1)}, u32[]{:S(2)}, u32[]{:S(2)}) collective-permute-start(bf16[1024,256]{1,0:T(8,128)(2,1)S(1)} %pad_maximum_fusion.2), channel_id=1, source_target_pairs={{0,2},{1,3},{2,0},{3,1},{4,6},{5,7},{6,4},{7,5},{8,10},{9,11},{10,... | collective-permute-start | bytes 1572872 | tf_op jit(solution)/shard_map/ppermute | solution.py:14
  31.0 17.6 %collective-permute-start.20 = (bf16[1024,256]{1,0:T(8,128)(2,1)S(1)}, bf16[1024,256]{1,0:T(8,128)(2,1)S(1)}, u32[]{:S(2)}, u32[]{:S(2)}) collective-permute-start(bf16[1024,256]{1,0:T(8,128)(2,1)S(1)} %pad_maximum_fusion.2), channel_id=1, source_target_pairs={{0,1},{1,0},{2,3},{3,2},{4,5},{5,4},{6,7},{7,6},{8,9},{9,8},{10,11... | collective-permute-start | bytes 1572872 | tf_op jit(solution)/shard_map/ppermute | solution.py:14
  37.4 11.3 %collective-permute-start.11 = (bf16[512,256]{0,1:T(8,128)(2,1)S(1)}, bf16[512,256]{0,1:T(8,128)(2,1)S(1)}, u32[]{:S(2)}, u32[]{:S(2)}) collective-permute-start(bf16[512,256]{0,1:T(8,128)(2,1)S(1)} %convolution_convert_fusion.3), channel_id=1, source_target_pairs={{0,28},{4,24},{8,20},{12,16},{16,12},{20,8},{24,4},{28,0},{1,29},{... | collective-permute-start | bytes 786440 | tf_op jit(solution)/shard_map/ppermute | solution.py:56
  41.0 25.9 %collective-permute-start.9 = (bf16[512,256]{0,1:T(8,128)(2,1)S(1)}, bf16[512,256]{0,1:T(8,128)(2,1)S(1)}, u32[]{:S(2)}, u32[]{:S(2)}) collective-permute-start(bf16[512,256]{0,1:T(8,128)(2,1)S(1)} %get-tuple-element.74), channel_id=1, source_target_pairs={{0,2},{1,3},{2,0},{3,1},{4,6},{5,7},{6,4},{7,5},{8,10},{9,11},{10,... | collective-permute-start | bytes 786440 | tf_op jit(solution)/shard_map/ppermute | solution.py:14
  45.2 22.3 %collective-permute-start.18 = (bf16[1024,256]{1,0:T(8,128)(2,1)S(1)}, bf16[1024,256]{1,0:T(8,128)(2,1)S(1)}, u32[]{:S(2)}, u32[]{:S(2)}) collective-permute-start(bf16[1024,256]{1,0:T(8,128)(2,1)S(1)} %constant_dynamic-update-slice_fusion.4), channel_id=1, source_target_pairs={{0,2},{1,3},{2,0},{3,1},{4,6},{5,7},{6,4},{7,5},{8,10},{9,11},{10,... | collective-permute-start | bytes 1572872 | tf_op jit(solution)/shard_map/ppermute | solution.py:14
  45.2 22.4 %collective-permute-start.21 = (bf16[1024,256]{1,0:T(8,128)(2,1)S(1)}, bf16[1024,256]{1,0:T(8,128)(2,1)S(1)}, u32[]{:S(2)}, u32[]{:S(2)}) collective-permute-start(bf16[1024,256]{1,0:T(8,128)(2,1)S(1)} %collective-permute-done.16), channel_id=1, source_target_pairs={{0,1},{1,0},{2,3},{3,2},{4,5},{5,4},{6,7},{7,6},{8,9},{9,8},{10,11... | collective-permute-start | bytes 1572872 | tf_op jit(solution)/shard_map/ppermute | solution.py:14
  48.6 18.3 %collective-permute-start.13 = (bf16[512,256]{0,1:T(8,128)(2,1)S(1)}, bf16[512,256]{0,1:T(8,128)(2,1)S(1)}, u32[]{:S(2)}, u32[]{:S(2)}) collective-permute-start(bf16[512,256]{0,1:T(8,128)(2,1)S(1)} %collective-permute-done.11), channel_id=1, source_target_pairs={{0,2},{1,3},{2,0},{3,1},{4,6},{5,7},{6,4},{7,5},{8,10},{9,11},{10,... | collective-permute-start | bytes 786440 | tf_op jit(solution)/shard_map/ppermute | solution.py:14
  50.2 18.2 %collective-permute-start.8 = (bf16[512,256]{0,1:T(8,128)(2,1)S(1)}, bf16[512,256]{0,1:T(8,128)(2,1)S(1)}, u32[]{:S(2)}, u32[]{:S(2)}) collective-permute-start(bf16[512,256]{0,1:T(8,128)(2,1)S(1)} %get-tuple-element.74), channel_id=1, source_target_pairs={{0,1},{1,0},{2,3},{3,2},{4,5},{5,4},{6,7},{7,6},{8,9},{9,8},{10,11... | collective-permute-start | bytes 786440 | tf_op jit(solution)/shard_map/ppermute | solution.py:14
  76.8 12.9 %collective-permute-start.25 = (bf16[256,256]{1,0:T(8,128)(2,1)S(1)}, bf16[256,256]{1,0:T(8,128)(2,1)S(1)}, u32[]{:S(2)}, u32[]{:S(2)}) collective-permute-start(bf16[256,256]{1,0:T(8,128)(2,1)S(1)} %dynamic-slice_convert_fusion.2), channel_id=1, source_target_pairs={{0,8},{4,12},{8,0},{12,4},{16,24},{20,28},{24,16},{28,20},{1,9},{5... | collective-permute-start | bytes 393224 | tf_op jit(solution)/shard_map/ppermute | solution.py:14
  85.3 12.5 %collective-permute-start.24 = (bf16[512,256]{1,0:T(8,128)(2,1)S(1)}, bf16[512,256]{1,0:T(8,128)(2,1)S(1)}, u32[]{:S(2)}, u32[]{:S(2)}) collective-permute-start(bf16[512,256]{1,0:T(8,128)(2,1)S(1)} %constant_dynamic-slice_fusion.3), channel_id=1, source_target_pairs={{0,8},{4,12},{8,0},{12,4},{16,24},{20,28},{24,16},{28,20},{1,9},{5... | collective-permute-start | bytes 786440 | tf_op jit(solution)/shard_map/ppermute | solution.py:14
  104.5 7.3 %collective-permute-start.28 = (bf16[128,256]{1,0:T(8,128)(2,1)S(1)}, bf16[128,256]{1,0:T(8,128)(2,1)S(1)}, u32[]{:S(2)}, u32[]{:S(2)}) collective-permute-start(bf16[128,256]{1,0:T(8,128)(2,1)S(1)} %dynamic-slice_convert_fusion.5), channel_id=1, source_target_pairs={{0,16},{4,20},{8,24},{12,28},{16,0},{20,4},{24,8},{28,12},{1,17},{... | collective-permute-start | bytes 196616 | tf_op jit(solution)/shard_map/ppermute | solution.py:14
  105.7 8.8 %collective-permute-start.27 = (bf16[256,256]{1,0:T(8,128)(2,1)S(1)}, bf16[256,256]{1,0:T(8,128)(2,1)S(1)}, u32[]{:S(2)}, u32[]{:S(2)}) collective-permute-start(bf16[256,256]{1,0:T(8,128)(2,1)S(1)} %dynamic-slice_convert_fusion.1), channel_id=1, source_target_pairs={{0,16},{4,20},{8,24},{12,28},{16,0},{20,4},{24,8},{28,12},{1,17},{... | collective-permute-start | bytes 393224 | tf_op jit(solution)/shard_map/ppermute | solution.py:14
  107.6 7.2 %collective-permute-start.26 = (bf16[576,256]{1,0:T(8,128)(2,1)S(1)}, bf16[576,256]{1,0:T(8,128)(2,1)S(1)}, u32[]{:S(2)}, u32[]{:S(2)}) collective-permute-start(bf16[576,256]{1,0:T(8,128)(2,1)S(1)} %constant_dynamic-slice_fusion), channel_id=1, source_target_pairs={{0,4},{4,0},{8,12},{12,8},{16,20},{20,16},{24,28},{28,24},{1,5},{5... | collective-permute-start | bytes 884744 | tf_op jit(solution)/shard_map/ppermute | solution.py:14
  122.2 9.4 %collective-permute-start.34 = (bf16[256,256]{1,0:T(8,128)(2,1)S(1)}, bf16[256,256]{1,0:T(8,128)(2,1)S(1)}, u32[]{:S(2)}, u32[]{:S(2)}) collective-permute-start(bf16[256,256]{1,0:T(8,128)(2,1)S(1)} %maximum_select_fusion.7), channel_id=1, source_target_pairs={{0,8},{4,12},{8,0},{12,4},{16,24},{20,28},{24,16},{28,20},{1,9},{5... | collective-permute-start | bytes 393224 | tf_op jit(solution)/shard_map/ppermute | solution.py:14
  131.8 8.3 %collective-permute-start.37 = (bf16[512,256]{1,0:T(8,128)(2,1)S(1)}, bf16[512,256]{1,0:T(8,128)(2,1)S(1)}, u32[]{:S(2)}, u32[]{:S(2)}) collective-permute-start(bf16[512,256]{1,0:T(8,128)(2,1)S(1)} %maximum_select_fusion.4), channel_id=1, source_target_pairs={{0,4},{4,0},{8,12},{12,8},{16,20},{20,16},{24,28},{28,24},{1,5},{5... | collective-permute-start | bytes 786440 | tf_op jit(solution)/shard_map/ppermute | solution.py:14
  132.4 7.6 %collective-permute-start.36 = (bf16[256,256]{1,0:T(8,128)(2,1)S(1)}, bf16[256,256]{1,0:T(8,128)(2,1)S(1)}, u32[]{:S(2)}, u32[]{:S(2)}) collective-permute-start(bf16[256,256]{1,0:T(8,128)(2,1)S(1)} %maximum_select_fusion.8), channel_id=1, source_target_pairs={{0,16},{4,20},{8,24},{12,28},{16,0},{20,4},{24,8},{28,12},{1,17},{... | collective-permute-start | bytes 393224 | tf_op jit(solution)/shard_map/ppermute | solution.py:14
  141.7 7.3 %collective-permute-start.39 = (bf16[512,256]{1,0:T(8,128)(2,1)S(1)}, bf16[512,256]{1,0:T(8,128)(2,1)S(1)}, u32[]{:S(2)}, u32[]{:S(2)}) collective-permute-start(bf16[512,256]{1,0:T(8,128)(2,1)S(1)} %maximum_select_fusion.5), channel_id=1, source_target_pairs={{0,8},{4,12},{8,0},{12,4},{16,24},{20,28},{24,16},{28,20},{1,9},{5... | collective-permute-start | bytes 786440 | tf_op jit(solution)/shard_map/ppermute | solution.py:14
  (30 other events, 277.9 us)

commit v5 on v4

--- a/solution.py
+++ b/solution.py
@@ -116,14 +116,15 @@
     choose = (index_r[:, None] == order_r[None, :]).astype(bf16)
     choose_inverse = (order_r[:, None] == index_r[None, :width]).astype(bf16)
 
-    mirrored_cotangent = mirror(flip(cotangent))
+    early_cotangent, edges[0] = lax.optimization_barrier((flip(cotangent), edges[0]))
+    mirrored_cotangent = mirror(early_cotangent)
     w_out_r, mains[channels // 2] = lax.optimization_barrier((w_out_r, mains[channels // 2]))
     w_out_blocks = gather_relative(w_out_r)
     both_cotangent = jnp.concatenate([cotangent, mirrored_cotangent], axis=0)
     send_cotangent, w_out_blocks[channels // 2] = lax.optimization_barrier(
         (both_cotangent, w_out_blocks[channels // 2])
     )
-    all_cotangent = jnp.concatenate(gather_relative(send_cotangent), axis=1)
+    cotangent_blocks = gather_relative(send_cotangent)
     all_w_out = jnp.concatenate(
         [
             jnp.concatenate(
@@ -133,10 +134,6 @@
         ],
         axis=1,
     )
-    grad_norm = lax.dot_general(
-        all_cotangent, all_w_out, (((1,), (1,)), ((), ())), preferred_element_type=f32
-    ).astype(bf16)
-
     edge_blocks = {}
     packed = exchange(jnp.concatenate(edges, axis=0), "ch", 1)
     for place, far in enumerate(range(0, channels, 2)):
@@ -171,7 +168,14 @@
 
     mirrored = mirror(flip(gated))
     gated_full = jnp.concatenate(gather_relative(gated), axis=1)
+    mirrored, cotangent_blocks[channels // 2] = lax.optimization_barrier(
+        (mirrored, cotangent_blocks[channels // 2])
+    )
     mirrored_full = jnp.concatenate(gather_relative(mirrored), axis=1)
+    all_cotangent = jnp.concatenate(cotangent_blocks, axis=1)
+    grad_norm = lax.dot_general(
+        all_cotangent, all_w_out, (((1,), (1,)), ((), ())), preferred_element_type=f32
+    ).astype(bf16)
     combined = jnp.concatenate([gated_full, mirrored_full], axis=0).astype(f32) + jnp.dot(
         jnp.concatenate([mirrored_full, gated_full], axis=0), choose, preferred_element_type=f32
     )
@@ -216,11 +220,10 @@
     ).astype(bf16)
     before, after = AHEAD, BACK
     left, right = halo(upstream, before, after)
-    sum_gate = halve(weight_grad(full_input, grad_gate_pre), turned[0])
+    sum_gate = halve(weight_grad(full_input, grad_gate_pre), steps[0])
     sum_out = halve(sum_out, turned[0])
     extended = jnp.concatenate([left, upstream, right], axis=0)
-    extended, sum_gate, sum_out = lax.optimization_barrier((extended, sum_gate, sum_out))
-    rest_gate = [(halve, distance) for distance in turned[1:]] + [(double, distance) for distance in turned[::-1]]
+    rest_gate = [(halve, distance) for distance in turned[:-1]] + [(double, distance) for distance in steps[::-1]]
     rest_out = [(halve, distance) for distance in turned[1:-1]] + [
         (double, distance) for distance in steps[::-1]
     ]

time: 159 us -> 173 us (1.088)
  waiting for transfers between devices: 71.8 us -> 51.1 us
  local copies, waits for them, and re-layouts: 7.52 us -> 20.4 us
  starting transfers between devices: 47.4 us -> 59.9 us
  other arithmetic: 12.5 us -> 17.6 us
  matrix products: 17.8 us -> 20.8 us
    ppermute x33, waiting for transfers between devices: 59.2 us -> 40.1 us  [exchange(): return lax.ppermute(block, axis, [(i, i ^ distance) for i in range(count)])]
    ppermute x33, starting transfers between devices: 33 us -> 39.4 us  [exchange(): return lax.ppermute(block, axis, [(i, i ^ distance) for i in range(count)])]
    ppermute x6, starting transfers between devices: 6.2 us -> 11.5 us  [halo(): received.append(lax.ppermute(sent, ('seq', 'ch'), route))]
    unnamed x36 -> x118, local copies, waits for them, and re-layouts: 2.26 us -> 6.95 us
    ppermute x6, waiting for transfers between devices: 9.17 us -> 5.86 us  [halo(): received.append(lax.ppermute(sent, ('seq', 'ch'), route))]
    select_n x9, other arithmetic: 2.73 us -> 5.71 us  [double(): jnp.where(bit == 0, jnp.concatenate([part, other], axis=0), jnp.concatena...]
    another operation x13, local copies, waits for them, and re-layouts: 0.12 us -> 2.29 us  [local(): jnp.stack([tap_grads[4 * (2 - number) + tap] for number in range(3) for t...]
    dot_general x1, matrix products: 0.44 us -> 2.36 us  [local(): lax.dot_general(picked, both_cotangent, contract_rows, preferred_element_...]
  transfers between devices with their start and end apart: 41 -> 41, of which waited for: 20 -> 19; matrix products, arithmetic and copies ran while one was open for 13% -> 23% of each run, Pallas kernels for 0% -> 0%
where the time goes in v5:
time: 173 us; the launch traced here: 172 us
  starting transfers between devices  59.9 us (35%)
  waiting for transfers between devices  51.1 us (30%)
  matrix products  20.8 us (12%)
  local copies, waits for them, and re-layouts  20.4 us (12%)
  other arithmetic  17.6 us (10%)
  between operations  1.91 us (1%)
    ppermute x33, waiting for transfers between devices, exchange(): return lax.ppermute(block, axis, [(i, i ^ distance) for i in range(count)])  40.1 us
    ppermute x33, starting transfers between devices, exchange(): return lax.ppermute(block, axis, [(i, i ^ distance) for i in range(count)])  39.4 us
    ppermute x6, starting transfers between devices, halo(): received.append(lax.ppermute(sent, ('seq', 'ch'), route))  11.5 us
    ppermute x2, starting transfers between devices, mirror(): lax.ppermute(block, 'seq', [(i, count - 1 - i) for i in range(count)])  9.05 us
    unnamed x118, local copies, waits for them, and re-layouts  6.95 us
    ppermute x6, waiting for transfers between devices, halo(): received.append(lax.ppermute(sent, ('seq', 'ch'), route))  5.86 us
    select_n x9, other arithmetic, double(): jnp.where(bit == 0, jnp.concatenate([part, other], axis=0), jnp.concatena...  5.71 us
    ppermute x2, waiting for transfers between devices, mirror(): lax.ppermute(block, 'seq', [(i, count - 1 - i) for i in range(count)])  5.13 us
  transfers between devices with their start and end apart: 41, of which 19 were waited for; matrix products, arithmetic and copies ran while one was open for 23% of the time, Pallas kernels for 0%

profile of v5, /device:TPU:0, one launch (start us, length us, event | category | flops | bytes accessed | tf_op | source)
XLA Modules:
  0.0 171.8 jit_solution(1984388674400773988)
XLA Ops:
  3.4 2.6 %collective-permute-start.6 = (bf16[512,256]{0,1:T(8,128)(2,1)S(1)}, bf16[512,256]{0,1:T(8,128)(2,1)}, u32[]{:S(2)}, u32[]{:S(2)}) collective-permute-start(bf16[512,256]{0,1:T(8,128)(2,1)S(1)} %fusion.48), channel_id=1, source_target_pairs={{0,2},{1,3},{2,0},{3,1},{4,6},{5,7},{6,4},{7,5},{8,10},{9,11},{10,... | collective-permute-start | bytes 786440 | tf_op jit(solution)/shard_map/ppermute | solution.py:14
  15.2 4.3 %collective-permute-start.3 = (bf16[160,256]{0,1:T(8,128)(2,1)S(1)}, bf16[160,256]{0,1:T(8,128)(2,1)S(1)}, u32[]{:S(2)}, u32[]{:S(2)}) collective-permute-start(bf16[160,256]{0,1:T(8,128)(2,1)S(1)} %get-tuple-element.114), channel_id=1, source_target_pairs={{0,6},{4,2},{1,7},{5,3},{2,4},{6,0},{3,5},{7,1},{8,14},{12,10},{9,... | collective-permute-start | bytes 245768 | tf_op jit(solution)/shard_map/ppermute | solution.py:77
  20.4 2.4 %collective-permute-done.3 = bf16[160,256]{0,1:T(8,128)(2,1)S(1)} collective-permute-done((bf16[160,256]{0,1:T(8,128)(2,1)S(1)}, bf16[160,256]{0,1:T(8,128)(2,1)S(1)}, u32[]{:S(2)}, u32[]{:S(2)}) %collective-permute-start.3) | collective-permute-done | bytes 81952 | tf_op jit(solution)/shard_map/ppermute | solution.py:77
  23.7 4.0 %collective-permute-start.13 = (bf16[1024,256]{1,0:T(8,128)(2,1)S(1)}, bf16[1024,256]{1,0:T(8,128)(2,1)S(1)}, u32[]{:S(2)}, u32[]{:S(2)}) collective-permute-start(bf16[1024,256]{1,0:T(8,128)(2,1)S(1)} %pad_maximum_fusion.2), channel_id=1, source_target_pairs={{0,2},{1,3},{2,0},{3,1},{4,6},{5,7},{6,4},{7,5},{8,10},{9,11},{10,... | collective-permute-start | bytes 1572872 | tf_op jit(solution)/shard_map/ppermute | solution.py:14
  27.9 4.5 %collective-permute-start.12 = (bf16[512,256]{1,0:T(8,128)(2,1)S(1)}, bf16[512,256]{1,0:T(8,128)(2,1)S(1)}, u32[]{:S(2)}, u32[]{:S(2)}) collective-permute-start(bf16[512,256]{1,0:T(8,128)(2,1)S(1)} %convolution_convert_fusion.4), channel_id=1, source_target_pairs={{0,28},{4,24},{8,20},{12,16},{16,12},{20,8},{24,4},{28,0},{1,29},{... | collective-permute-start | bytes 786440 | tf_op jit(solution)/shard_map/ppermute | solution.py:56
  36.9 2.4 %fusion.65 = (bf16[512,256]{0,1:T(8,128)(2,1)S(1)}, bf16[512,256]{0,1:T(8,128)(2,1)}, f32[512,256]{0,1:T(8,128)}) fusion(bf16[725,256]{0,1:T(8,128)(2,1)S(1)} %select_convert_fusion, f32[256]{0:T(256)S(1)} %bitcast.40, f32[256]{0:T(256)S(1)} %bitcast.42, f32[256]{0:T(256)S(1)} %bitcast.38, f32[256]{0:T(256)S(1)} %bitcast.36, ...), kind=kOutput, calls=%fused_computation.98 | convolution fusion | flops 277217280 | bytes 3674112 | tf_op jit(solution)/shard_map/dot_general | solution.py:146
  43.0 4.5 %collective-permute-start.11 = (bf16[512,256]{0,1:T(8,128)(2,1)}, bf16[512,256]{0,1:T(8,128)(2,1)}, u32[]{:S(2)}, u32[]{:S(2)}) collective-permute-start(bf16[512,256]{0,1:T(8,128)(2,1)} %convolution_convert_fusion.2), channel_id=1, source_target_pairs={{0,28},{4,24},{8,20},{12,16},{16,12},{20,8},{24,4},{28,0},{1,29},{... | collective-permute-start | bytes 786440 | tf_op jit(solution)/shard_map/ppermute | solution.py:56
  48.8 5.1 %collective-permute-done.11 = bf16[512,256]{0,1:T(8,128)(2,1)} collective-permute-done((bf16[512,256]{0,1:T(8,128)(2,1)}, bf16[512,256]{0,1:T(8,128)(2,1)}, u32[]{:S(2)}, u32[]{:S(2)}) %collective-permute-start.11) | collective-permute-done | bytes 262176 | tf_op jit(solution)/shard_map/ppermute | solution.py:56
  57.2 3.7 %collective-permute-done.9 = bf16[512,256]{0,1:T(8,128)(2,1)S(1)} collective-permute-done((bf16[512,256]{0,1:T(8,128)(2,1)}, bf16[512,256]{0,1:T(8,128)(2,1)S(1)}, u32[]{:S(2)}, u32[]{:S(2)}) %collective-permute-start.9) | collective-permute-done | bytes 262176 | tf_op jit(solution)/shard_map/ppermute | solution.py:14
  61.5 4.0 %collective-permute-done.16 = bf16[512,256]{0,1:T(8,128)(2,1)S(1)} collective-permute-done((bf16[512,256]{0,1:T(8,128)(2,1)}, bf16[512,256]{0,1:T(8,128)(2,1)S(1)}, u32[]{:S(2)}, u32[]{:S(2)}) %collective-permute-start.16) | collective-permute-done | bytes 262176 | tf_op jit(solution)/shard_map/ppermute | solution.py:14
  67.2 2.8 %multiply_reduce_fusion.1 = (f32[1024]{0:T(1024)S(1)}, f32[1024,1024]{0,1:T(8,128)S(1)}) fusion(s32[1024]{0:T(1024)S(1)} %copy-done.36, s32[1024]{0:T(1024)S(1)} %copy-done.37, bf16[512,256]{0,1:T(8,128)(2,1)S(1)} %collective-permute-done.10, bf16[512,256]{0,1:T(8,128)(2,1)S(1)} %collective-permute-done.9, bf16[512,256]{0,1:T(8,128)(2,1)S(1)} %collective-permute-done.8, ...), kind=kOutput, calls=%fused_computation.4 | convolution fusion | flops 2172648448 | bytes 6303744 | tf_op jit(solution)/shard_map/dot_general | solution.py:179
  70.0 3.7 %multiply_reduce_fusion = (f32[1024]{0:T(1024)S(1)}, bf16[1024,1024]{0,1:T(8,128)(2,1)S(1)}) fusion(f32[1024,1024]{0,1:T(8,128)S(1)} %get-tuple-element.137, f32[1024]{0:T(1024)S(1)} %pad_maximum_fusion.15, f32[1024]{0:T(1024)S(1)} %add_rsqrt_fusion, bf16[256,256]{1,0:T(8,128)(2,1)S(1)} %get-tuple-element.94, bf16[256,256]{1,0:T(8,128)(2,1)S(1)} %get-tuple-element.95, ...), kind=kOutput, calls=%fused_computation.1 | convolution fusion | flops 2185231360 | bytes 10498048 | tf_op jit(solution)/shard_map/dot_general | solution.py:176
  75.1 2.4 %fusion.56 = f32[512,256]{1,0:T(8,128)} fusion(bf16[1024,256]{1,0:T(8,128)(2,1)} %constant_dynamic-update-slice_fusion, bf16[1024,256]{0,1:T(8,128)(2,1)S(1)} %get-tuple-element.82, bf16[1024,256]{0,1:T(8,128)(2,1)S(1)} %get-tuple-element.81), kind=kOutput, calls=%fused_computation.63 | convolution fusion | flops 270532608 | bytes 2097152 | tf_op jit(solution)/shard_map/dot_general | solution.py:215
  79.1 6.0 %collective-permute-start.25 = (bf16[256,256]{1,0:T(8,128)(2,1)}, bf16[256,256]{1,0:T(8,128)(2,1)}, u32[]{:S(2)}, u32[]{:S(2)}) collective-permute-start(bf16[256,256]{1,0:T(8,128)(2,1)} %dynamic-slice_convert_fusion.2), channel_id=1, source_target_pairs={{0,8},{4,12},{8,0},{12,4},{16,24},{20,28},{24,16},{28,20},{1,9},{5... | collective-permute-start | bytes 393224 | tf_op jit(solution)/shard_map/ppermute | solution.py:14
  89.0 3.6 %collective-permute-start.23 = (bf16[160,256]{0,1:T(8,128)(2,1)S(1)}, bf16[160,256]{0,1:T(8,128)(2,1)S(1)}, u32[]{:S(2)}, u32[]{:S(2)}) collective-permute-start(bf16[160,256]{0,1:T(8,128)(2,1)S(1)} %get-tuple-element.109), channel_id=1, source_target_pairs={{0,4},{4,0},{1,5},{5,1},{2,6},{6,2},{3,7},{7,3},{8,12},{12,8},{9,1... | collective-permute-start | bytes 245768 | tf_op jit(solution)/shard_map/ppermute | solution.py:77
  95.6 3.4 %collective-permute-done.23 = bf16[160,256]{0,1:T(8,128)(2,1)S(1)} collective-permute-done((bf16[160,256]{0,1:T(8,128)(2,1)S(1)}, bf16[160,256]{0,1:T(8,128)(2,1)S(1)}, u32[]{:S(2)}, u32[]{:S(2)}) %collective-permute-start.23) | collective-permute-done | bytes 81952 | tf_op jit(solution)/shard_map/ppermute | solution.py:77
  109.5 3.0 %collective-permute-start.28 = (bf16[128,256]{1,0:T(8,128)(2,1)S(1)}, bf16[128,256]{1,0:T(8,128)(2,1)S(1)}, u32[]{:S(2)}, u32[]{:S(2)}) collective-permute-start(bf16[128,256]{1,0:T(8,128)(2,1)S(1)} %dynamic-slice_convert_fusion.5), channel_id=1, source_target_pairs={{0,16},{4,20},{8,24},{12,28},{16,0},{20,4},{24,8},{28,12},{1,17},{... | collective-permute-start | bytes 196616 | tf_op jit(solution)/shard_map/ppermute | solution.py:14
  115.6 2.6 %collective-permute-done.27 = bf16[256,256]{1,0:T(8,128)(2,1)S(1)} collective-permute-done((bf16[256,256]{1,0:T(8,128)(2,1)S(1)}, bf16[256,256]{1,0:T(8,128)(2,1)S(1)}, u32[]{:S(2)}, u32[]{:S(2)}) %collective-permute-start.27) | collective-permute-done | bytes 131104 | tf_op jit(solution)/shard_map/ppermute | solution.py:14
  118.3 4.0 %collective-permute-done.26 = bf16[576,256]{1,0:T(8,128)(2,1)S(1)} collective-permute-done((bf16[576,256]{1,0:T(8,128)(2,1)S(1)}, bf16[576,256]{1,0:T(8,128)(2,1)S(1)}, u32[]{:S(2)}, u32[]{:S(2)}) %collective-permute-start.26) | collective-permute-done | bytes 294944 | tf_op jit(solution)/shard_map/ppermute | solution.py:14
  136.4 2.6 %collective-permute-done.33 = bf16[128,256]{1,0:T(8,128)(2,1)S(1)} collective-permute-done((bf16[128,256]{1,0:T(8,128)(2,1)S(1)}, bf16[128,256]{1,0:T(8,128)(2,1)S(1)}, u32[]{:S(2)}, u32[]{:S(2)}) %collective-permute-start.33) | collective-permute-done | bytes 65568 | tf_op jit(solution)/shard_map/ppermute | solution.py:14
  139.0 3.0 %collective-permute-done.32 = bf16[144,256]{1,0:T(8,128)(2,1)S(1)} collective-permute-done((bf16[144,256]{1,0:T(8,128)(2,1)S(1)}, bf16[144,256]{1,0:T(8,128)(2,1)S(1)}, u32[]{:S(2)}, u32[]{:S(2)}) %collective-permute-start.32) | collective-permute-done | bytes 73760 | tf_op jit(solution)/shard_map/ppermute | solution.py:14
  144.8 2.8 %collective-permute-done.35 = bf16[144,256]{1,0:T(8,128)(2,1)} collective-permute-done((bf16[144,256]{1,0:T(8,128)(2,1)S(1)}, bf16[144,256]{1,0:T(8,128)(2,1)}, u32[]{:S(2)}, u32[]{:S(2)}) %collective-permute-start.35) | collective-permute-done | bytes 73760 | tf_op jit(solution)/shard_map/ppermute | solution.py:14
  156.3 4.9 %collective-permute-done.39 = bf16[512,256]{1,0:T(8,128)(2,1)S(1)} collective-permute-done((bf16[512,256]{1,0:T(8,128)(2,1)S(1)}, bf16[512,256]{1,0:T(8,128)(2,1)S(1)}, u32[]{:S(2)}, u32[]{:S(2)}) %collective-permute-start.39) | collective-permute-done | bytes 262176 | tf_op jit(solution)/shard_map/ppermute | solution.py:14
  164.4 4.8 %collective-permute-done.40 = bf16[576,256]{1,0:T(8,128)(2,1)} collective-permute-done((bf16[576,256]{1,0:T(8,128)(2,1)S(1)}, bf16[576,256]{1,0:T(8,128)(2,1)}, u32[]{:S(2)}, u32[]{:S(2)}) %collective-permute-start.40) | collective-permute-done | bytes 294944 | tf_op jit(solution)/shard_map/ppermute | solution.py:14
  (281 shorter events, 82.8 us)
Async XLA Ops:
  2.9 10.0 %collective-permute-start = (bf16[512,256]{0,1:T(8,128)(2,1)S(1)}, bf16[512,256]{0,1:T(8,128)(2,1)S(1)}, u32[]{:S(2)}, u32[]{:S(2)}) collective-permute-start(bf16[512,256]{0,1:T(8,128)(2,1)S(1)} %fusion.48), channel_id=1, source_target_pairs={{0,1},{1,0},{2,3},{3,2},{4,5},{5,4},{6,7},{7,6},{8,9},{9,8},{10,11... | collective-permute-start | bytes 786440 | tf_op jit(solution)/shard_map/ppermute | solution.py:14
  3.4 16.8 %collective-permute-start.6 = (bf16[512,256]{0,1:T(8,128)(2,1)S(1)}, bf16[512,256]{0,1:T(8,128)(2,1)}, u32[]{:S(2)}, u32[]{:S(2)}) collective-permute-start(bf16[512,256]{0,1:T(8,128)(2,1)S(1)} %fusion.48), channel_id=1, source_target_pairs={{0,2},{1,3},{2,0},{3,1},{4,6},{5,7},{6,4},{7,5},{8,10},{9,11},{10,... | collective-permute-start | bytes 786440 | tf_op jit(solution)/shard_map/ppermute | solution.py:14
  13.0 7.3 %collective-permute-start.1 = (bf16[160,256]{0,1:T(8,128)(2,1)S(1)}, bf16[160,256]{0,1:T(8,128)(2,1)S(1)}, u32[]{:S(2)}, u32[]{:S(2)}) collective-permute-start(bf16[160,256]{0,1:T(8,128)(2,1)S(1)} %get-tuple-element.114), channel_id=1, source_target_pairs={{0,4},{4,0},{1,5},{5,1},{2,6},{6,2},{3,7},{7,3},{8,12},{12,8},{9,1... | collective-permute-start | bytes 245768 | tf_op jit(solution)/shard_map/ppermute | solution.py:77
  15.2 7.6 %collective-permute-start.3 = (bf16[160,256]{0,1:T(8,128)(2,1)S(1)}, bf16[160,256]{0,1:T(8,128)(2,1)S(1)}, u32[]{:S(2)}, u32[]{:S(2)}) collective-permute-start(bf16[160,256]{0,1:T(8,128)(2,1)S(1)} %get-tuple-element.114), channel_id=1, source_target_pairs={{0,6},{4,2},{1,7},{5,3},{2,4},{6,0},{3,5},{7,1},{8,14},{12,10},{9,... | collective-permute-start | bytes 245768 | tf_op jit(solution)/shard_map/ppermute | solution.py:77
  20.2 12.2 %collective-permute-start.7 = (bf16[512,256]{0,1:T(8,128)(2,1)}, bf16[512,256]{0,1:T(8,128)(2,1)S(1)}, u32[]{:S(2)}, u32[]{:S(2)}) collective-permute-start(bf16[512,256]{0,1:T(8,128)(2,1)} %collective-permute-done.6), channel_id=1, source_target_pairs={{0,1},{1,0},{2,3},{3,2},{4,5},{5,4},{6,7},{7,6},{8,9},{9,8},{10,11... | collective-permute-start | bytes 786440 | tf_op jit(solution)/shard_map/ppermute | solution.py:14
  23.1 11.0 %collective-permute-start.5 = (bf16[480,256]{0,1:T(8,128)(2,1)S(1)}, bf16[480,256]{0,1:T(8,128)(2,1)S(1)}, u32[]{:S(2)}, u32[]{:S(2)}) collective-permute-start(bf16[480,256]{0,1:T(8,128)(2,1)S(1)} %pad_maximum_fusion.11), channel_id=1, source_target_pairs={{0,1},{1,0},{2,3},{3,2},{4,5},{5,4},{6,7},{7,6},{8,9},{9,8},{10,11... | collective-permute-start | bytes 737288 | tf_op jit(solution)/shard_map/ppermute | solution.py:14
  23.7 16.6 %collective-permute-start.13 = (bf16[1024,256]{1,0:T(8,128)(2,1)S(1)}, bf16[1024,256]{1,0:T(8,128)(2,1)S(1)}, u32[]{:S(2)}, u32[]{:S(2)}) collective-permute-start(bf16[1024,256]{1,0:T(8,128)(2,1)S(1)} %pad_maximum_fusion.2), channel_id=1, source_target_pairs={{0,2},{1,3},{2,0},{3,1},{4,6},{5,7},{6,4},{7,5},{8,10},{9,11},{10,... | collective-permute-start | bytes 1572872 | tf_op jit(solution)/shard_map/ppermute | solution.py:14
  27.7 27.7 %collective-permute-start.20 = (bf16[1024,256]{1,0:T(8,128)(2,1)S(1)}, bf16[1024,256]{1,0:T(8,128)(2,1)S(1)}, u32[]{:S(2)}, u32[]{:S(2)}) collective-permute-start(bf16[1024,256]{1,0:T(8,128)(2,1)S(1)} %pad_maximum_fusion.2), channel_id=1, source_target_pairs={{0,1},{1,0},{2,3},{3,2},{4,5},{5,4},{6,7},{7,6},{8,9},{9,8},{10,11... | collective-permute-start | bytes 1572872 | tf_op jit(solution)/shard_map/ppermute | solution.py:14
  27.9 11.5 %collective-permute-start.12 = (bf16[512,256]{1,0:T(8,128)(2,1)S(1)}, bf16[512,256]{1,0:T(8,128)(2,1)S(1)}, u32[]{:S(2)}, u32[]{:S(2)}) collective-permute-start(bf16[512,256]{1,0:T(8,128)(2,1)S(1)} %convolution_convert_fusion.4), channel_id=1, source_target_pairs={{0,28},{4,24},{8,20},{12,16},{16,12},{20,8},{24,4},{28,0},{1,29},{... | collective-permute-start | bytes 786440 | tf_op jit(solution)/shard_map/ppermute | solution.py:56
  40.3 15.1 %collective-permute-start.14 = (bf16[1024,256]{1,0:T(8,128)(2,1)}, bf16[1024,256]{1,0:T(8,128)(2,1)}, u32[]{:S(2)}, u32[]{:S(2)}) collective-permute-start(bf16[1024,256]{1,0:T(8,128)(2,1)} %constant_dynamic-update-slice_fusion), channel_id=1, source_target_pairs={{0,2},{1,3},{2,0},{3,1},{4,6},{5,7},{6,4},{7,5},{8,10},{9,11},{10,... | collective-permute-start | bytes 1572872 | tf_op jit(solution)/shard_map/ppermute | solution.py:14
  43.0 10.8 %collective-permute-start.11 = (bf16[512,256]{0,1:T(8,128)(2,1)}, bf16[512,256]{0,1:T(8,128)(2,1)}, u32[]{:S(2)}, u32[]{:S(2)}) collective-permute-start(bf16[512,256]{0,1:T(8,128)(2,1)} %convolution_convert_fusion.2), channel_id=1, source_target_pairs={{0,28},{4,24},{8,20},{12,16},{16,12},{20,8},{24,4},{28,0},{1,29},{... | collective-permute-start | bytes 786440 | tf_op jit(solution)/shard_map/ppermute | solution.py:56
  47.6 13.3 %collective-permute-start.21 = (bf16[1024,256]{1,0:T(8,128)(2,1)S(1)}, bf16[1024,256]{1,0:T(8,128)(2,1)S(1)}, u32[]{:S(2)}, u32[]{:S(2)}) collective-permute-start(bf16[1024,256]{1,0:T(8,128)(2,1)S(1)} %collective-permute-done.13), channel_id=1, source_target_pairs={{0,1},{1,0},{2,3},{3,2},{4,5},{5,4},{6,7},{7,6},{8,9},{9,8},{10,11... | collective-permute-start | bytes 1572872 | tf_op jit(solution)/shard_map/ppermute | solution.py:14
  48.1 12.8 %collective-permute-start.9 = (bf16[512,256]{0,1:T(8,128)(2,1)}, bf16[512,256]{0,1:T(8,128)(2,1)S(1)}, u32[]{:S(2)}, u32[]{:S(2)}) collective-permute-start(bf16[512,256]{0,1:T(8,128)(2,1)} %copy-done.50), channel_id=1, source_target_pairs={{0,2},{1,3},{2,0},{3,1},{4,6},{5,7},{6,4},{7,5},{8,10},{9,11},{10,... | collective-permute-start | bytes 786440 | tf_op jit(solution)/shard_map/ppermute | solution.py:14
  53.9 13.2 %collective-permute-start.8 = (bf16[512,256]{0,1:T(8,128)(2,1)}, bf16[512,256]{0,1:T(8,128)(2,1)S(1)}, u32[]{:S(2)}, u32[]{:S(2)}) collective-permute-start(bf16[512,256]{0,1:T(8,128)(2,1)} %copy-done.50), channel_id=1, source_target_pairs={{0,1},{1,0},{2,3},{3,2},{4,5},{5,4},{6,7},{7,6},{8,9},{9,8},{10,11... | collective-permute-start | bytes 786440 | tf_op jit(solution)/shard_map/ppermute | solution.py:14
  55.4 14.6 %collective-permute-start.18 = (bf16[1024,256]{1,0:T(8,128)(2,1)}, bf16[1024,256]{1,0:T(8,128)(2,1)S(1)}, u32[]{:S(2)}, u32[]{:S(2)}) collective-permute-start(bf16[1024,256]{1,0:T(8,128)(2,1)} %constant_dynamic-update-slice_fusion), channel_id=1, source_target_pairs={{0,1},{1,0},{2,3},{3,2},{4,5},{5,4},{6,7},{7,6},{8,9},{9,8},{10,11... | collective-permute-start | bytes 1572872 | tf_op jit(solution)/shard_map/ppermute | solution.py:14
  55.4 10.1 %collective-permute-start.16 = (bf16[512,256]{0,1:T(8,128)(2,1)}, bf16[512,256]{0,1:T(8,128)(2,1)S(1)}, u32[]{:S(2)}, u32[]{:S(2)}) collective-permute-start(bf16[512,256]{0,1:T(8,128)(2,1)} %collective-permute-done.11), channel_id=1, source_target_pairs={{0,2},{1,3},{2,0},{3,1},{4,6},{5,7},{6,4},{7,5},{8,10},{9,11},{10,... | collective-permute-start | bytes 786440 | tf_op jit(solution)/shard_map/ppermute | solution.py:14
  79.1 28.3 %collective-permute-start.25 = (bf16[256,256]{1,0:T(8,128)(2,1)}, bf16[256,256]{1,0:T(8,128)(2,1)}, u32[]{:S(2)}, u32[]{:S(2)}) collective-permute-start(bf16[256,256]{1,0:T(8,128)(2,1)} %dynamic-slice_convert_fusion.2), channel_id=1, source_target_pairs={{0,8},{4,12},{8,0},{12,4},{16,24},{20,28},{24,16},{28,20},{1,9},{5... | collective-permute-start | bytes 393224 | tf_op jit(solution)/shard_map/ppermute | solution.py:14
  88.3 7.3 %collective-permute-start.22 = (bf16[160,256]{0,1:T(8,128)(2,1)S(1)}, bf16[160,256]{0,1:T(8,128)(2,1)S(1)}, u32[]{:S(2)}, u32[]{:S(2)}) collective-permute-start(bf16[160,256]{0,1:T(8,128)(2,1)S(1)} %get-tuple-element.110), channel_id=1, source_target_pairs={{4,8},{8,4},{5,9},{9,5},{6,10},{10,6},{7,11},{11,7},{12,16},{16,12... | collective-permute-start | bytes 245768 | tf_op jit(solution)/shard_map/ppermute | solution.py:77
  89.0 10.0 %collective-permute-start.23 = (bf16[160,256]{0,1:T(8,128)(2,1)S(1)}, bf16[160,256]{0,1:T(8,128)(2,1)S(1)}, u32[]{:S(2)}, u32[]{:S(2)}) collective-permute-start(bf16[160,256]{0,1:T(8,128)(2,1)S(1)} %get-tuple-element.109), channel_id=1, source_target_pairs={{0,4},{4,0},{1,5},{5,1},{2,6},{6,2},{3,7},{7,3},{8,12},{12,8},{9,1... | collective-permute-start | bytes 245768 | tf_op jit(solution)/shard_map/ppermute | solution.py:77
  93.3 15.1 %collective-permute-start.24 = (bf16[512,256]{1,0:T(8,128)(2,1)}, bf16[512,256]{1,0:T(8,128)(2,1)}, u32[]{:S(2)}, u32[]{:S(2)}) collective-permute-start(bf16[512,256]{1,0:T(8,128)(2,1)} %constant_dynamic-slice_fusion.3), channel_id=1, source_target_pairs={{0,4},{4,0},{8,12},{12,8},{16,20},{20,16},{24,28},{28,24},{1,5},{5... | collective-permute-start | bytes 786440 | tf_op jit(solution)/shard_map/ppermute | solution.py:14
  115.4 6.9 %collective-permute-start.26 = (bf16[576,256]{1,0:T(8,128)(2,1)S(1)}, bf16[576,256]{1,0:T(8,128)(2,1)S(1)}, u32[]{:S(2)}, u32[]{:S(2)}) collective-permute-start(bf16[576,256]{1,0:T(8,128)(2,1)S(1)} %constant_dynamic-slice_fusion), channel_id=1, source_target_pairs={{0,4},{4,0},{8,12},{12,8},{16,20},{20,16},{24,28},{28,24},{1,5},{5... | collective-permute-start | bytes 884744 | tf_op jit(solution)/shard_map/ppermute | solution.py:14
  131.6 10.4 %collective-permute-start.34 = (bf16[256,256]{1,0:T(8,128)(2,1)S(1)}, bf16[256,256]{1,0:T(8,128)(2,1)S(1)}, u32[]{:S(2)}, u32[]{:S(2)}) collective-permute-start(bf16[256,256]{1,0:T(8,128)(2,1)S(1)} %maximum_select_fusion.7), channel_id=1, source_target_pairs={{0,8},{4,12},{8,0},{12,4},{16,24},{20,28},{24,16},{28,20},{1,9},{5... | collective-permute-start | bytes 393224 | tf_op jit(solution)/shard_map/ppermute | solution.py:14
  134.4 7.6 %collective-permute-start.32 = (bf16[144,256]{1,0:T(8,128)(2,1)S(1)}, bf16[144,256]{1,0:T(8,128)(2,1)S(1)}, u32[]{:S(2)}, u32[]{:S(2)}) collective-permute-start(bf16[144,256]{1,0:T(8,128)(2,1)S(1)} %dynamic-slice_convert_fusion.3), channel_id=1, source_target_pairs={{0,16},{4,20},{8,24},{12,28},{16,0},{20,4},{24,8},{28,12},{1,17},{... | collective-permute-start | bytes 221192 | tf_op jit(solution)/shard_map/ppermute | solution.py:14
  152.4 8.9 %collective-permute-start.39 = (bf16[512,256]{1,0:T(8,128)(2,1)S(1)}, bf16[512,256]{1,0:T(8,128)(2,1)S(1)}, u32[]{:S(2)}, u32[]{:S(2)}) collective-permute-start(bf16[512,256]{1,0:T(8,128)(2,1)S(1)} %maximum_select_fusion.5), channel_id=1, source_target_pairs={{0,4},{4,0},{8,12},{12,8},{16,20},{20,16},{24,28},{28,24},{1,5},{5... | collective-permute-start | bytes 786440 | tf_op jit(solution)/shard_map/ppermute | solution.py:14
  (71 other events, 488.1 us)

commit v6 on v0

v6 whole, which is shorter than its diff:
```python
import functools

import jax
import jax.numpy as jnp
from jax import lax
from jax.experimental import pallas as pl
from jax.experimental.pallas import tpu as pltpu
from jax.sharding import PartitionSpec as P

DILATIONS = (1, 8, 64)
EPSILON = 1e-06
FORE = (160, 144, 128, 0)
AFT = (80, 72, 64, 0)
BACK_FORE = (0, 8, 16, 80)
BACK_AFT = (0, 8, 24, 160)
EDGE = 160
SPARE = 64

BF16, F32 = jnp.bfloat16, jnp.float32
ROWS_DOT = (((0,), (0,)), ((), ()))
LAST_DOT = (((1,), (1,)), ((), ()))


def dot(left, right, dims=(((1,), (0,)), ((), ()))):
    return lax.dot_general(left, right, dims, preferred_element_type=F32)


def run(body, place, operands, outs, scratch=(), megabytes=16, gflop=0.1):
    moved = sum(x.size * x.dtype.itemsize for x in operands)
    return pl.pallas_call(
        body,
        out_shape=[jax.ShapeDtypeStruct(shape, dtype) for shape, dtype in outs],
        in_specs=[pl.BlockSpec(memory_space=pltpu.SMEM)]
        + [pl.BlockSpec(memory_space=pltpu.VMEM)] * len(operands),
        out_specs=[pl.BlockSpec(memory_space=pltpu.VMEM)] * len(outs),
        scratch_shapes=list(scratch),
        compiler_params=pltpu.CompilerParams(vmem_limit_bytes=megabytes << 20),
        cost_estimate=pl.CostEstimate(flops=int(gflop * 1e9), bytes_accessed=moved, transcendentals=0),
    )(place, *operands)


def part(index, size, multiple=None):
    return pl.ds(pl.multiple_of(index * size, multiple or size), size)


def anti_identity(rows):
    down = lax.broadcasted_iota(jnp.int32, (rows, rows), 0)
    across = lax.broadcasted_iota(jnp.int32, (rows, rows), 1)
    return (down + across == rows - 1).astype(F32).astype(BF16)


def input_kernel(place, tokens, hidden, embedding, block_in, first, second, padded):
    bases, rows = embedding.shape[0], hidden.shape[0]
    padded[...] = jnp.zeros_like(padded)
    padded[:bases] = embedding[...].astype(F32)
    base = lax.broadcasted_iota(jnp.int32, (padded.shape[0], rows), 0)
    one_hot = (base == tokens[...]).astype(F32).astype(BF16)
    shift = dot(one_hot, padded[...].astype(BF16), ROWS_DOT)
    block_in[...] = (hidden[...].astype(F32) + shift).astype(BF16)
    odd = place[0] % 2
    far = rows - EDGE
    first[...] = block_in[pl.ds(pl.multiple_of((1 - odd) * far, 16), EDGE), :]
    second[...] = block_in[pl.ds(pl.multiple_of(odd * far, 16), EDGE), :]


def setup_kernel(place, cotangent, order, flipped, choose):
    flipped[...] = dot(anti_identity(cotangent.shape[0]), cotangent[...]).astype(BF16)
    me, width = place[1], cotangent.shape[1]
    down = lax.broadcasted_iota(jnp.int32, (width, width), 0)
    for j in range(order.shape[1] // width):
        for i in range(order.shape[1] // width):
            wanted = order[:, part(me ^ i, width)]
            choose[j * width : (j + 1) * width, i * width : (i + 1) * width] = (
                (down + (me ^ j) * width == wanted).astype(F32).astype(BF16)
            )


def project_kernel(channels, place, *refs):
    mains, (w_in, w_gate, projected, gate_pre) = refs[:channels], refs[channels:]
    me, width = place[1], mains[0].shape[1]
    for weight, out in ((w_in, projected), (w_gate, gate_pre)):
        total = dot(mains[0][...], weight[part(me, width), :])
        for j in range(1, channels):
            total += dot(mains[j][...], weight[part(me ^ j, width), :])
        out[...] = total


def keep_inside(total, place, before, rows):
    position = lax.broadcasted_iota(jnp.int32, total.shape, 0) + (place[0] * rows - before)
    return jnp.where((position >= 0) & (position < place[2] * rows), total, 0.0)


def forward_kernel(channels, place, edges, edges_core, w_in, projected, gate_pre, conv_w, *outs):
    level_0, level_1, level_2, level_3, gated, flipped = outs
    me, odd = place[1], place[0] % 2
    rows, width = projected.shape
    left = jnp.zeros((EDGE, width), F32)
    right = jnp.zeros((AFT[0], width), F32)
    for j in range(channels):
        source = edges_core if j % 2 else edges
        base = (j // 2) * 2 * EDGE
        weight = w_in[part(me ^ j, width), :]
        left += dot(source[pl.ds(pl.multiple_of(base + (1 - odd) * EDGE, 16), EDGE), :], weight)
        right += dot(source[pl.ds(pl.multiple_of(base + odd * EDGE, 16), AFT[0]), :], weight)
    level_0[:EDGE] = left
    level_0[EDGE : EDGE + rows] = projected[...]
    level_0[EDGE + rows :] = right
    source = level_0
    for number, (dilation, target) in enumerate(zip(DILATIONS, (level_1, level_2, level_3))):
        shift = FORE[number] - FORE[number + 1]
        count = target.shape[0]
        total = jnp.zeros((count, width), F32)
        for tap in range(4):
            begin = shift + (tap - 2) * dilation
            total += conv_w[number, tap : tap + 1, :] * source[begin : begin + count]
        if FORE[number + 1]:
            total = keep_inside(total, place, FORE[number + 1], rows)
        target[...] = total
        source = target
    gate = gate_pre[...]
    gated[...] = (level_3[...] * (gate / (1.0 + jnp.exp(-gate)))).astype(BF16)
    flipped[...] = dot(anti_identity(rows), gated[...]).astype(BF16)


def norm_grad_kernel(channels, place, *refs):
    own, mirrored = refs[:channels], refs[channels : 2 * channels]
    near, near_core, far_mine, far_other, far_core_mine, far_core_other, out, far, far_core = refs[2 * channels :]
    me, side = place[1], place[0] % 2
    half = far_mine.shape[0]
    for whole, mine, other in ((far, far_mine, far_other), (far_core, far_core_mine, far_core_other)):
        whole[part(side, half), :] = mine[...]
        whole[part(1 - side, half), :] = other[...]
    weights = (near, near_core, far, far_core)
    rows, width = own[0].shape
    for block, cotangents in enumerate((own, mirrored)):
        for i in range(channels):
            total = jnp.zeros((rows, width), F32)
            for j in range(channels):
                total += dot(cotangents[j][...], weights[j][part(i ^ me, width), :], LAST_DOT)
            out[block * rows : (block + 1) * rows, i * width : (i + 1) * width] = total.astype(BF16)


def combine_kernel(channels, place, *refs):
    own, mirrored = refs[:channels], refs[channels : 2 * channels]
    grad_norm, choose, gain, gate_pre, level_3 = refs[2 * channels : 2 * channels + 5]
    normalized, upstream, grad_gate_pre, first, second, gains, grad_gated = refs[2 * channels + 5 :]
    me = place[1]
    rows, width = own[0].shape
    full = channels * width
    tile = rows // 4
    for j in range(channels):
        gains[:, j * width : (j + 1) * width] = gain[:, part(me ^ j, width)]
    for block, (here, there) in enumerate(((own, mirrored), (mirrored, own))):

        def step(k, carry, block=block, here=here, there=there):
            at = part(k, tile)
            mine = jnp.concatenate([ref[at, :].astype(F32) for ref in here], axis=1)
            other = jnp.concatenate([ref[at, :] for ref in there], axis=1)
            combined = mine + dot(other, choose[...])
            mean = jnp.sum(combined * combined, axis=1, keepdims=True) * (1.0 / full)
            inv_scale = lax.rsqrt(mean + EPSILON)
            hat = combined * inv_scale
            at_both = pl.ds(pl.multiple_of(block * rows + k * tile, tile), tile)
            normalized[at_both, :] = (hat * gains[...]).astype(BF16)
            scaled = grad_norm[at_both, :].astype(F32) * gains[...]
            row_total = jnp.sum(scaled * hat, axis=1, keepdims=True) * (1.0 / full)
            if block == 0:
                grad_gated[at, :] = inv_scale * (scaled[:, :width] - hat[:, :width] * row_total)
            else:
                grad_comb = (inv_scale * (scaled - hat * row_total)).astype(BF16)
                grad_gated[at, :] += dot(grad_comb, choose[:width, :], LAST_DOT)
            return carry

        lax.fori_loop(0, rows // tile, step, 0)
    gate = gate_pre[...]
    sigmoid = 1.0 / (1.0 + jnp.exp(-gate))
    total = grad_gated[...]
    upstream[...] = (total * (gate * sigmoid)).astype(BF16)
    grad_gate_pre[...] = (total * level_3[...] * sigmoid * (1.0 + gate * (1.0 - sigmoid))).astype(BF16)
    odd, far = place[0] % 2, rows - EDGE
    first[...] = upstream[pl.ds(pl.multiple_of((1 - odd) * far, 16), EDGE), :]
    second[...] = upstream[pl.ds(pl.multiple_of(odd * far, 16), EDGE), :]


def output_kernel(channels, place, normalized, w_out, block_in, output):
    me = place[1]
    rows, width = block_in.shape
    total = block_in[...].astype(F32)
    for j in range(channels):
        total += dot(normalized[:rows, j * width : (j + 1) * width], w_out[part(me ^ j, width), :])
    output[...] = total.astype(BF16)


def products_kernel(channels, place, normalized, cotangent, mirrored_cotangent, grad_gate_pre, *refs):
    mains = refs[:channels]
    out_sent, out_kept, gate_sent, gate_kept, whole_out, whole_gate = refs[channels:]
    me, side = place[1], place[0] % 2
    rows, width = cotangent.shape
    for j in range(channels // 2):
        block = (side * (channels // 2) + j) ^ me
        columns = part(block, width)
        whole_out[j * width : (j + 1) * width, :] = dot(
            normalized[:rows, columns], cotangent[...], ROWS_DOT
        ) + dot(normalized[rows:, columns], mirrored_cotangent[...], ROWS_DOT)
    half = whole_out.shape[0] // 2
    bit = (place[0] // 2) % 2
    out_sent[...] = whole_out[part(1 - bit, half), :].astype(BF16)
    out_kept[...] = whole_out[part(bit, half), :]
    for j in range(channels):
        whole_gate[part(me ^ j, width), :] = dot(mains[j][...], grad_gate_pre[...], ROWS_DOT)
    half = whole_gate.shape[0] // 2
    gate_sent[...] = whole_gate[part(1 - side, half), :].astype(BF16)
    gate_kept[...] = whole_gate[part(side, half), :]


def backward_kernel(channels, place, upstream, first, second, level_0, level_1, level_2, conv_w, *refs):
    mains = refs[:channels]
    sent, kept, whole, grad_3, grad_2, grad_1 = refs[channels:]
    me, odd = place[1], place[0] % 2
    rows, width = upstream.shape
    fore = BACK_FORE[3]
    even = (odd == 0).astype(F32)
    early, late = first[...].astype(F32), second[...].astype(F32)
    grad_3[:fore] = (early * (1.0 - even) + late * even)[EDGE - fore :]
    grad_3[fore : fore + rows] = upstream[...].astype(F32)
    grad_3[fore + rows :] = early * even + late * (1.0 - even)
    half = whole.shape[0] // 2
    for top in (half - SPARE, 2 * half - SPARE):
        whole[top : top + SPARE, :] = jnp.zeros((SPARE, width), F32)
    levels = (level_0, level_1, level_2)
    grads = (None, grad_1, grad_2, grad_3)
    grad_0 = None
    for number in (2, 1, 0):
        dilation, source, level = DILATIONS[number], grads[number + 1], levels[number]
        fore = BACK_FORE[number + 1]
        here = source[fore : fore + rows]
        for tap in range(4):
            begin = FORE[number] + (tap - 2) * dilation
            row = half - SPARE + 4 * number + tap
            whole[row : row + 1, :] = jnp.sum(here * level[begin : begin + rows], axis=0, keepdims=True)
        count = BACK_FORE[number] + rows + BACK_AFT[number]
        total = jnp.zeros((count, width), F32)
        for tap in range(4):
            begin = fore - BACK_FORE[number] - (tap - 2) * dilation
            total += conv_w[number, tap : tap + 1, :] * source[begin : begin + count]
        if number:
            grads[number][...] = keep_inside(total, place, BACK_FORE[number], rows)
        else:
            grad_0 = total.astype(BF16)
    for j in range(channels):
        block = me ^ j
        start = (block // (channels // 2)) * half + (block % (channels // 2)) * width
        whole[pl.ds(pl.multiple_of(start, SPARE), width), :] = dot(mains[j][...], grad_0, ROWS_DOT)
    sent[...] = whole[part(1 - odd, half), :].astype(BF16)
    kept[...] = whole[part(odd, half), :]


def exchange(block, axis, distance):
    count = lax.axis_size(axis)
    return lax.ppermute(block, axis, [(i, i ^ distance) for i in range(count)])


def distances(axis):
    return [1 << bit for bit in range(lax.axis_size(axis).bit_length() - 1)]


def mirror(block):
    count = lax.axis_size("seq")
    return lax.ppermute(block, "seq", [(i, count - 1 - i) for i in range(count)])


def swap_edges(first, second, far=0):
    count, channels = lax.axis_size("seq"), lax.axis_size("ch")
    received = []
    for turn, block in enumerate((first, second)):
        route = []
        for low in range(turn, count - 1, 2):
            for c in range(channels):
                route.append((low * channels + c, (low + 1) * channels + (c ^ far)))
                route.append(((low + 1) * channels + c, low * channels + (c ^ far)))
        received.append(lax.ppermute(block, ("seq", "ch"), route))
    return received


def together(*values):
    return lax.optimization_barrier(values)


def seq_bit(distance):
    return (lax.axis_index("seq") & distance) // distance


def halve(total, distance):
    half = total.shape[0] // 2
    bit = seq_bit(distance)
    sent = lax.dynamic_slice_in_dim(total, (1 - bit) * half, half, 0).astype(BF16)
    kept = lax.dynamic_slice_in_dim(total, bit * half, half, 0)
    return kept.astype(F32) + exchange(sent, "seq", distance).astype(F32)


def double(total, distance):
    return jnp.concatenate(both_halves(total, distance), axis=0)


def both_halves(total, distance):
    total = total.astype(BF16)
    other = exchange(total, "seq", distance)
    first = seq_bit(distance) == 0
    return jnp.where(first, total, other), jnp.where(first, other, total)


def local(tokens, hidden, embedding, w_in, w_gate, conv_w, channel_order, gain, w_out, cotangent):
    rows, width = hidden.shape
    full = gain.shape[0]
    channels = full // width
    cross = channels // 2
    taps = conv_w.shape[0] * conv_w.shape[1]
    steps = distances("seq")
    block = ((rows, width), BF16)
    place = jnp.stack([lax.axis_index("seq"), lax.axis_index("ch"), lax.axis_size("seq")]).astype(jnp.int32)

    local_input, first, second = run(
        input_kernel,
        place,
        (tokens.reshape(1, rows), hidden, embedding),
        [block, ((EDGE, width), BF16), ((EDGE, width), BF16)],
        [pltpu.VMEM((16, width), F32)],
    )
    input_x = exchange(local_input, "ch", cross)
    input_core = exchange(local_input, "ch", 1)
    near = swap_edges(first, second)
    far = swap_edges(first, second, cross)
    flipped_cotangent, choose = run(
        setup_kernel,
        place,
        (cotangent, channel_order.reshape(1, full)),
        [block, ((full, full), BF16)],
    )
    w_half = lax.dynamic_slice_in_dim(w_out, seq_bit(1) * (full // 2), full // 2, 0)
    w_half, input_x = together(w_half, input_x)
    w_x_mine = exchange(w_half, "ch", cross)
    mains = [local_input, input_core, input_x, exchange(input_x, "ch", 1)]
    edges = jnp.concatenate(near + far, axis=0)
    edges_core = exchange(edges, "ch", 1)
    edges, flipped_cotangent = together(edges, flipped_cotangent)
    mirrored_cotangent = mirror(flipped_cotangent)
    early_cotangent, w_x_mine = together(cotangent, w_x_mine)
    cotangent_x = exchange(early_cotangent, "ch", cross)
    w_x_other = exchange(w_x_mine, "seq", 1)
    late_cotangent, cotangent_x = together(mirrored_cotangent, cotangent_x)
    mirrored_cotangent_x = exchange(late_cotangent, "ch", cross)

    projected, gate_pre = run(
        functools.partial(project_kernel, channels),
        place,
        (*mains, w_in, w_gate),
        [((rows, width), F32)] * 2,
        gflop=0.6,
    )
    level_0, level_1, level_2, level_3, gated, flipped = run(
        functools.partial(forward_kernel, channels),
        place,
        (edges, edges_core, w_in, projected, gate_pre, conv_w),
        [((fore + rows + aft, width), F32) for fore, aft in zip(FORE, AFT)] + [block, block],
        megabytes=24,
        gflop=0.4,
    )
    mirrored = mirror(flipped)
    gated_x = exchange(gated, "ch", cross)
    gated_all = [gated, exchange(gated, "ch", 1), gated_x, exchange(gated_x, "ch", 1)]
    mirrored, mirrored_cotangent_x = together(mirrored, mirrored_cotangent_x)
    mirrored_x = exchange(mirrored, "ch", cross)
    cotangent_all = [cotangent, exchange(cotangent, "ch", 1), cotangent_x, exchange(cotangent_x, "ch", 1)]
    mirrored_cotangent_all = [
        mirrored_cotangent,
        exchange(mirrored_cotangent, "ch", 1),
        mirrored_cotangent_x,
        exchange(mirrored_cotangent_x, "ch", 1),
    ]
    grad_norm = run(
        functools.partial(norm_grad_kernel, channels),
        place,
        (
            *cotangent_all,
            *mirrored_cotangent_all,
            w_out,
            exchange(w_out, "ch", 1),
            w_x_mine,
            w_x_other,
            exchange(w_x_mine, "ch", 1),
            exchange(w_x_other, "ch", 1),
        ),
        [((2 * rows, full), BF16)],
        [pltpu.VMEM((full, width), BF16)] * 2,
        megabytes=24,
        gflop=2.1,
    )[0]
    mirrored_all = [mirrored, exchange(mirrored, "ch", 1), mirrored_x, exchange(mirrored_x, "ch", 1)]

    normalized, upstream, grad_gate_pre, first, second = run(
        functools.partial(combine_kernel, channels),
        place,
        (*gated_all, *mirrored_all, grad_norm, choose, gain.reshape(1, full), gate_pre, level_3),
        [((2 * rows, full), BF16), block, block, ((EDGE, width), BF16), ((EDGE, width), BF16)],
        [pltpu.VMEM((1, full), F32), pltpu.VMEM((rows, width), F32)],
        megabytes=32,
        gflop=2.5,
    )
    first, second = swap_edges(first, second)
    out_sent, out_kept, gate_sent, gate_kept = run(
        functools.partial(products_kernel, channels),
        place,
        (normalized, cotangent, mirrored_cotangent, grad_gate_pre, *mains),
        [
            ((full // 4, width), BF16),
            ((full // 4, width), F32),
            ((full // 2, width), BF16),
            ((full // 2, width), F32),
        ],
        [pltpu.VMEM((full // 2, width), F32), pltpu.VMEM((full, width), F32)],
        megabytes=24,
        gflop=0.8,
    )
    out_other = exchange(out_sent, "seq", steps[1])
    gate_other = exchange(gate_sent, "seq", steps[0])
    half = full // 2 + SPARE
    in_sent, in_kept = run(
        functools.partial(backward_kernel, channels),
        place,
        (upstream, first, second, level_0, level_1, level_2, conv_w, *mains),
        [((half, width), BF16), ((half, width), F32)],
        [pltpu.VMEM((2 * half, width), F32)]
        + [pltpu.VMEM((BACK_FORE[k] + rows + BACK_AFT[k], width), F32) for k in (3, 2, 1)],
        megabytes=24,
        gflop=0.5,
    )
    output = run(
        functools.partial(output_kernel, channels),
        place,
        (normalized, w_out, local_input),
        [block],
        gflop=0.3,
    )[0]

    sum_out = out_kept + out_other.astype(F32)
    sum_gate = gate_kept + gate_other.astype(F32)
    in_sent, sum_gate, sum_out = together(in_sent, sum_gate, sum_out)
    sum_in = in_kept + exchange(in_sent, "seq", steps[0]).astype(F32)
    undo = [(double, distance) for distance in steps[::-1]]
    rest_gate = [(halve, distance) for distance in steps[1:]] + undo
    rest_out = [(halve, distance) for distance in steps[2:]] + undo
    rest_in = [(halve, distance) for distance in steps[1:]] + undo[:-1]
    for number in range(len(rest_in) + 1):
        if number:
            sum_in, sum_gate, sum_out = together(sum_in, sum_gate, sum_out)
            move, distance = rest_in[number - 1]
            sum_in = move(sum_in, distance)
        if number < len(rest_gate):
            move, distance = rest_gate[number]
            sum_gate = move(sum_gate, distance)
        if number < len(rest_out):
            move, distance = rest_out[number]
            sum_out = move(sum_out, distance)
    low, high = both_halves(sum_in, steps[0])
    grad_in = jnp.concatenate([low[: full // 2], high[: full // 2]], axis=0)
    grad_conv = low[full // 2 : full // 2 + taps].astype(F32).reshape(conv_w.shape)
    return output, grad_in, sum_gate, sum_out, grad_conv


def solution(mesh):
    placed = (
        P("seq"),
        P("seq", "ch"),
        P(None, "ch"),
        P(None, "ch"),
        P(None, "ch"),
        P(None, None, "ch"),
        P(),
        P(),
        P(None, "ch"),
        P("seq", "ch"),
    )
    return jax.shard_map(
        local,
        mesh=mesh,
        in_specs=placed,
        out_specs=(
            P("seq", "ch"),
            P(None, "ch"),
            P(None, "ch"),
            P(None, "ch"),
            P(None, None, "ch"),
        ),
        check_vma=False,
    )
```

time: 419 us -> 159 us (0.38)
  blocking collectives: 134 us -> 0 us
  waiting for transfers between devices: 174 us -> 55 us
  Pallas kernels: 0 us -> 23.9 us
  matrix products: 13.5 us -> 0 us
  between operations: 14.5 us -> 1.13 us
  starting transfers between devices: 45 us -> 56.9 us
  other arithmetic: 12.3 us -> 4.19 us
  local copies, waits for them, and re-layouts: 24.3 us -> 16.9 us
    psum x2 -> x0, blocking collectives: 134 us -> none  [the longest x1 128 us: local(): lax.psum((local_in, local_gate, local_out, jnp.stack(tap_grads)), 'seq')]
    ppermute x18 -> x46, waiting for transfers between devices: 122 us -> 55 us  [the longest x38 49 us: exchange(): return lax.ppermute(block, axis, [(i, i ^ distance) for i in range(count)])]
    all_gather x3 -> x0, waiting for transfers between devices: 51.6 us -> none  [the longest x1 20.6 us: local(): gated_full = lax.all_gather(gated, 'ch', axis=1, tiled=True)]
    pallas_call x0 -> x9, Pallas kernels: none -> 23.9 us  [run(): pl.pallas_call(body, out_shape=[jax.ShapeDtypeStruct(shape, dtype) for sh...]
    unnamed x88 -> x53, local copies, waits for them, and re-layouts: 0.2 us -> 15.3 us
    dot_general x8 -> x0, matrix products: 13.5 us -> none  [the longest x1 2.19 us: local(): lax.dot_general(full_input, grad_gate_pre, contract_rows, preferred_eleme...]
    ppermute x18 -> x46, starting transfers between devices: 44.8 us -> 56.9 us  [the longest x38 38.3 us: exchange(): return lax.ppermute(block, axis, [(i, i ^ distance) for i in range(count)])]
    gather x4 -> x0, local copies, waits for them, and re-layouts: 10.5 us -> none  [the longest x2 5.3 us: local(): jnp.take(mirror_full, channel_order, axis=1).astype(jnp.float32)]
  transfers between devices with their start and end apart: 22 -> 46, of which waited for: 16 -> 19; matrix products, arithmetic and copies ran while one was open for 6% -> 2% of each run, Pallas kernels for 0% -> 8%
where the time goes in v6:
time: 159 us; the launch traced here: 158 us
  starting transfers between devices  56.9 us (36%)
  waiting for transfers between devices  55 us (35%)
  Pallas kernels  23.9 us (15%)
  local copies, waits for them, and re-layouts  16.9 us (11%)
  other arithmetic  4.19 us (3%)
    ppermute x38, waiting for transfers between devices, exchange(): return lax.ppermute(block, axis, [(i, i ^ distance) for i in range(count)])  49 us
    ppermute x38, starting transfers between devices, exchange(): return lax.ppermute(block, axis, [(i, i ^ distance) for i in range(count)])  38.3 us
    pallas_call x9, Pallas kernels, run(): pl.pallas_call(body, out_shape=[jax.ShapeDtypeStruct(shape, dtype) for sh...  23.9 us
    unnamed x53, local copies, waits for them, and re-layouts  15.3 us
    ppermute x6, starting transfers between devices, swap_edges(): received.append(lax.ppermute(block, ('seq', 'ch'), route))  10.5 us
    ppermute x2, starting transfers between devices, mirror(): lax.ppermute(block, 'seq', [(i, count - 1 - i) for i in range(count)])  8.02 us
    ppermute x2, waiting for transfers between devices, mirror(): lax.ppermute(block, 'seq', [(i, count - 1 - i) for i in range(count)])  4.64 us
  transfers between devices with their start and end apart: 46, of which 19 were waited for; matrix products, arithmetic and copies ran while one was open for 2% of the time, Pallas kernels for 8%

profile of v6, /device:TPU:0, one launch (start us, length us, event | category | flops | bytes accessed | tf_op | source)
XLA Modules:
  0.0 158.0 jit_solution(15904964604097960678)
XLA Ops:
  3.9 3.0 %collective-permute-start = (bf16[160,256]{1,0:T(8,128)(2,1)S(1)}, bf16[160,256]{1,0:T(8,128)(2,1)S(1)}, u32[]{:S(2)}, u32[]{:S(2)}) collective-permute-start(bf16[160,256]{1,0:T(8,128)(2,1)S(1)} %get-tuple-element.54), channel_id=1, source_target_pairs={{0,4},{4,0},{1,5},{5,1},{2,6},{6,2},{3,7},{7,3},{8,12},{12,8},{9,1... | collective-permute-start | bytes 245768 | tf_op jit(solution)/shard_map/ppermute | solution.py:281
  12.3 5.9 %collective-permute-done.6.refs_2_ = bf16[512,256]{1,0:T(8,128)(2,1)S(1)} collective-permute-done((bf16[512,256]{1,0:T(8,128)(2,1)S(1)}, bf16[512,256]{1,0:T(8,128)(2,1)S(1)}, u32[]{:S(2)}, u32[]{:S(2)}) %collective-permute-start.6) | collective-permute-done | bytes 262176 | tf_op jit(solution)/shard_map/ppermute | solution.py:260
  22.3 5.5 %collective-permute-start.12 = (bf16[512,256]{1,0:T(8,128)(2,1)S(1)}, bf16[512,256]{1,0:T(8,128)(2,1)S(1)}, u32[]{:S(2)}, u32[]{:S(2)}) collective-permute-start(bf16[512,256]{1,0:T(8,128)(2,1)S(1)} %get-tuple-element.64), channel_id=1, source_target_pairs={{0,28},{4,24},{8,20},{12,16},{16,12},{20,8},{24,4},{28,0},{1,29},{... | collective-permute-start | bytes 786440 | tf_op jit(solution)/shard_map/ppermute | solution.py:269
  36.8 2.5 %collective-permute-start.11 = (bf16[512,256]{1,0:T(8,128)(2,1)S(1)}, bf16[512,256]{1,0:T(8,128)(2,1)S(1)}, u32[]{:S(2)}, u32[]{:S(2)}) collective-permute-start(bf16[512,256]{1,0:T(8,128)(2,1)S(1)} %get-tuple-element.63), channel_id=1, source_target_pairs={{0,28},{4,24},{8,20},{12,16},{16,12},{20,8},{24,4},{28,0},{1,29},{... | collective-permute-start | bytes 786440 | tf_op jit(solution)/shard_map/ppermute | solution.py:269
  40.2 3.6 %collective-permute-start.24 = (bf16[512,256]{1,0:T(8,128)(2,1)S(1)}, bf16[512,256]{1,0:T(8,128)(2,1)S(1)}, u32[]{:S(2)}, u32[]{:S(2)}) collective-permute-start(bf16[512,256]{1,0:T(8,128)(2,1)S(1)} %collective-permute-done.13.refs_10_), channel_id=1, source_target_pairs={{0,4},{4,0},{8,12},{12,8},{16,20},{20,16},{24,28},{28,24},{1,5},{5... | collective-permute-start | bytes 786440 | tf_op jit(solution)/shard_map/ppermute | solution.py:260
  43.8 4.6 %collective-permute-done.11.refs_4_ = bf16[512,256]{1,0:T(8,128)(2,1)S(1)} collective-permute-done((bf16[512,256]{1,0:T(8,128)(2,1)S(1)}, bf16[512,256]{1,0:T(8,128)(2,1)S(1)}, u32[]{:S(2)}, u32[]{:S(2)}) %collective-permute-start.11) | collective-permute-done | bytes 262176 | tf_op jit(solution)/shard_map/ppermute | solution.py:269
  50.1 5.0 %collective-permute-done.24.refs_11_ = bf16[512,256]{1,0:T(8,128)(2,1)S(1)} collective-permute-done((bf16[512,256]{1,0:T(8,128)(2,1)S(1)}, bf16[512,256]{1,0:T(8,128)(2,1)S(1)}, u32[]{:S(2)}, u32[]{:S(2)}) %collective-permute-start.24) | collective-permute-done | bytes 262176 | tf_op jit(solution)/shard_map/ppermute | solution.py:260
  57.8 6.0 %collective-permute-done.17.refs_6_ = bf16[512,256]{1,0:T(8,128)(2,1)S(1)} collective-permute-done((bf16[512,256]{1,0:T(8,128)(2,1)S(1)}, bf16[512,256]{1,0:T(8,128)(2,1)S(1)}, u32[]{:S(2)}, u32[]{:S(2)}) %collective-permute-start.17) | collective-permute-done | bytes 262176 | tf_op jit(solution)/shard_map/ppermute | solution.py:260
  63.8 3.3 %shard_map.141.refs_8_ = bf16[1024,1024]{1,0:T(8,128)(2,1)S(1)} custom-call(s32[3]{0:T(128)S(1)} %pad_add_fusion.place, bf16[512,256]{1,0:T(8,128)(2,1)} %cotangent.3, bf16[512,256]{1,0:T(8,128)(2,1)S(1)} %collective-permute-done.19.refs_1_, bf16[512,256]{1,0:T(8,128)(2,1)S(1)} %collective-permute-done.14.refs_2_, ...), custom_call_target="tpu_custom_call" | custom-call | flops 2100000000 | bytes 4194304 | tf_op jit(solution)/shard_map/pallas_call | solution.py:30
  67.2 7.9 %shard_map.142 = (bf16[1024,1024]{1,0:T(8,128)(2,1)S(1)}, bf16[512,256]{1,0:T(8,128)(2,1)S(1)}, bf16[512,256]{1,0:T(8,128)(2,1)S(1)}, bf16[160,256]{1,0:T(8,128)(2,1)}, bf16[160,256]{1,0:T(8,128)(2,1)}) custom-call(s32[3]{0:T(128)S(1)} %pad_add_fusion.place, bf16[512,256]{1,0:T(8,128)(2,1)S(1)} %get-tuple-element.62.refs_0_, ...), custom_call_target="tpu_custom_call" | custom-call | flops 2500000000 | bytes 7344128 | tf_op jit(solution)/shard_map/pallas_call | solution.py:30
  75.1 2.4 %shard_map.145 = (bf16[256,256]{1,0:T(8,128)(2,1)}, f32[256,256]{1,0:T(8,128)S(1)}, bf16[512,256]{1,0:T(8,128)(2,1)S(1)}, f32[512,256]{1,0:T(8,128)S(1)}) custom-call(s32[3]{0:T(128)S(1)} %pad_add_fusion.place, bf16[1024,1024]{1,0:T(8,128)(2,1)S(1)} %get-tuple-element.74.normalized, bf16[512,256]{1,0:T(8,128)(2,1)} %cotangent.3, ...), custom_call_target="tpu_custom_call" | custom-call | flops 800000000 | bytes 3932160 | tf_op jit(solution)/shard_map/pallas_call | solution.py:30
  79.7 5.2 %collective-permute-start.30 = (bf16[256,256]{1,0:T(8,128)(2,1)}, bf16[256,256]{1,0:T(8,128)(2,1)}, u32[]{:S(2)}, u32[]{:S(2)}) collective-permute-start(bf16[256,256]{1,0:T(8,128)(2,1)} %get-tuple-element.87), channel_id=1, source_target_pairs={{0,8},{4,12},{8,0},{12,4},{16,24},{20,28},{24,16},{28,20},{1,9},{5... | collective-permute-start | bytes 393224 | tf_op jit(solution)/shard_map/ppermute | solution.py:260
  84.9 3.4 %collective-permute-start.27 = (bf16[160,256]{1,0:T(8,128)(2,1)}, bf16[160,256]{1,0:T(8,128)(2,1)S(1)}, u32[]{:S(2)}, u32[]{:S(2)}) collective-permute-start(bf16[160,256]{1,0:T(8,128)(2,1)} %get-tuple-element.76), channel_id=1, source_target_pairs={{0,4},{4,0},{1,5},{5,1},{2,6},{6,2},{3,7},{7,3},{8,12},{12,8},{9,1... | collective-permute-start | bytes 245768 | tf_op jit(solution)/shard_map/ppermute | solution.py:281
  89.6 2.4 %collective-permute-start.29 = (bf16[512,256]{1,0:T(8,128)(2,1)}, bf16[512,256]{1,0:T(8,128)(2,1)S(1)}, u32[]{:S(2)}, u32[]{:S(2)}) collective-permute-start(bf16[512,256]{1,0:T(8,128)(2,1)} %copy-done.20), channel_id=1, source_target_pairs={{0,4},{4,0},{8,12},{12,8},{16,20},{20,16},{24,28},{28,24},{1,5},{5... | collective-permute-start | bytes 786440 | tf_op jit(solution)/shard_map/ppermute | solution.py:260
  97.2 2.8 %shard_map.144 = (bf16[576,256]{1,0:T(8,128)(2,1)S(1)}, f32[576,256]{1,0:T(8,128)S(1)}) custom-call(s32[3]{0:T(128)S(1)} %pad_add_fusion.place, bf16[512,256]{1,0:T(8,128)(2,1)S(1)} %copy-done.14, bf16[160,256]{1,0:T(8,128)(2,1)S(1)} %collective-permute-done.27.first, bf16[160,256]{1,0:T(8,128)(2,1)} %collective-permute-done.28.second, ...), custom_call_target="tpu_custom_call" | custom-call | flops 500000000 | bytes 3723264 | tf_op jit(solution)/shard_map/pallas_call | solution.py:30
  101.2 4.4 %collective-permute-start.33 = (bf16[128,256]{1,0:T(8,128)(2,1)S(1)}, bf16[128,256]{1,0:T(8,128)(2,1)S(1)}, u32[]{:S(2)}, u32[]{:S(2)}) collective-permute-start(bf16[128,256]{1,0:T(8,128)(2,1)S(1)} %dynamic-slice_convert_fusion.4), channel_id=1, source_target_pairs={{0,16},{4,20},{8,24},{12,28},{16,0},{20,4},{24,8},{28,12},{1,17},{... | collective-permute-start | bytes 196616 | tf_op jit(solution)/shard_map/ppermute | solution.py:260
  110.7 4.3 %collective-permute-done.31 = bf16[576,256]{1,0:T(8,128)(2,1)S(1)} collective-permute-done((bf16[576,256]{1,0:T(8,128)(2,1)S(1)}, bf16[576,256]{1,0:T(8,128)(2,1)S(1)}, u32[]{:S(2)}, u32[]{:S(2)}) %collective-permute-start.31) | collective-permute-done | bytes 294944 | tf_op jit(solution)/shard_map/ppermute | solution.py:260
  118.9 2.9 %collective-permute-done.36 = bf16[128,256]{1,0:T(8,128)(2,1)S(1)} collective-permute-done((bf16[128,256]{1,0:T(8,128)(2,1)S(1)}, bf16[128,256]{1,0:T(8,128)(2,1)S(1)}, u32[]{:S(2)}, u32[]{:S(2)}) %collective-permute-start.36) | collective-permute-done | bytes 65568 | tf_op jit(solution)/shard_map/ppermute | solution.py:260
  129.6 4.3 %collective-permute-done.37 = bf16[144,256]{1,0:T(8,128)(2,1)S(1)} collective-permute-done((bf16[144,256]{1,0:T(8,128)(2,1)S(1)}, bf16[144,256]{1,0:T(8,128)(2,1)S(1)}, u32[]{:S(2)}, u32[]{:S(2)}) %collective-permute-start.37) | collective-permute-done | bytes 73760 | tf_op jit(solution)/shard_map/ppermute | solution.py:260
  136.8 2.5 %collective-permute-done.40 = bf16[144,256]{1,0:T(8,128)(2,1)S(1)} collective-permute-done((bf16[144,256]{1,0:T(8,128)(2,1)S(1)}, bf16[144,256]{1,0:T(8,128)(2,1)S(1)}, u32[]{:S(2)}, u32[]{:S(2)}) %collective-permute-start.40) | collective-permute-done | bytes 73760 | tf_op jit(solution)/shard_map/ppermute | solution.py:260
  139.4 2.4 %collective-permute-done.41 = bf16[256,256]{1,0:T(8,128)(2,1)S(1)} collective-permute-done((bf16[256,256]{1,0:T(8,128)(2,1)S(1)}, bf16[256,256]{1,0:T(8,128)(2,1)S(1)}, u32[]{:S(2)}, u32[]{:S(2)}) %collective-permute-start.41) | collective-permute-done | bytes 131104 | tf_op jit(solution)/shard_map/ppermute | solution.py:260
  142.7 2.4 %collective-permute-start.43 = (bf16[288,256]{1,0:T(8,128)(2,1)S(1)}, bf16[288,256]{1,0:T(8,128)(2,1)S(1)}, u32[]{:S(2)}, u32[]{:S(2)}) collective-permute-start(bf16[288,256]{1,0:T(8,128)(2,1)S(1)} %pad_maximum_fusion.6), channel_id=1, source_target_pairs={{0,8},{4,12},{8,0},{12,4},{16,24},{20,28},{24,16},{28,20},{1,9},{5... | collective-permute-start | bytes 442376 | tf_op jit(solution)/shard_map/ppermute | solution.py:260
  149.4 3.9 %collective-permute-done.45 = bf16[512,256]{1,0:T(8,128)(2,1)S(1)} collective-permute-done((bf16[512,256]{1,0:T(8,128)(2,1)S(1)}, bf16[512,256]{1,0:T(8,128)(2,1)S(1)}, u32[]{:S(2)}, u32[]{:S(2)}) %collective-permute-start.45) | collective-permute-done | bytes 262176 | tf_op jit(solution)/shard_map/ppermute | solution.py:260
  154.1 2.3 %collective-permute-done.44 = bf16[576,256]{1,0:T(8,128)(2,1)S(1)} collective-permute-done((bf16[576,256]{1,0:T(8,128)(2,1)S(1)}, bf16[576,256]{1,0:T(8,128)(2,1)S(1)}, u32[]{:S(2)}, u32[]{:S(2)}) %collective-permute-start.44) | collective-permute-done | bytes 294944 | tf_op jit(solution)/shard_map/ppermute | solution.py:260
  (168 shorter events, 63.9 us)
Async XLA Ops:
  9.1 10.3 %collective-permute-start.3 = (bf16[160,256]{1,0:T(8,128)(2,1)S(1)}, bf16[160,256]{1,0:T(8,128)(2,1)S(1)}, u32[]{:S(2)}, u32[]{:S(2)}) collective-permute-start(bf16[160,256]{1,0:T(8,128)(2,1)S(1)} %get-tuple-element.55), channel_id=1, source_target_pairs={{4,10},{8,6},{5,11},{9,7},{6,8},{10,4},{7,9},{11,5},{12,18},{16,14... | collective-permute-start | bytes 245768 | tf_op jit(solution)/shard_map/ppermute | solution.py:281
  9.7 8.4 %collective-permute-start.6 = (bf16[512,256]{1,0:T(8,128)(2,1)S(1)}, bf16[512,256]{1,0:T(8,128)(2,1)S(1)}, u32[]{:S(2)}, u32[]{:S(2)}) collective-permute-start(bf16[512,256]{1,0:T(8,128)(2,1)S(1)} %get-tuple-element.58.refs_0_.block_in), channel_id=1, source_target_pairs={{0,2},{1,3},{2,0},{3,1},{4,6},{5,7},{6,4},{7,5},{8,10},{9,11},{10,... | collective-permute-start | bytes 786440 | tf_op jit(solution)/shard_map/ppermute | solution.py:260
  18.2 9.6 %collective-permute-start.13 = (bf16[512,256]{1,0:T(8,128)(2,1)S(1)}, bf16[512,256]{1,0:T(8,128)(2,1)S(1)}, u32[]{:S(2)}, u32[]{:S(2)}) collective-permute-start(bf16[512,256]{1,0:T(8,128)(2,1)S(1)} %constant_dynamic-slice_fusion), channel_id=1, source_target_pairs={{0,2},{1,3},{2,0},{3,1},{4,6},{5,7},{6,4},{7,5},{8,10},{9,11},{10,... | collective-permute-start | bytes 786440 | tf_op jit(solution)/shard_map/ppermute | solution.py:260
  19.4 12.6 %collective-permute-start.4 = (bf16[640,256]{1,0:T(8,128)(2,1)S(1)}, bf16[640,256]{1,0:T(8,128)(2,1)S(1)}, u32[]{:S(2)}, u32[]{:S(2)}) collective-permute-start(bf16[640,256]{1,0:T(8,128)(2,1)S(1)} %constant_dynamic-update-slice_fusion.edges), channel_id=1, source_target_pairs={{0,1},{1,0},{2,3},{3,2},{4,5},{5,4},{6,7},{7,6},{8,9},{9,8},{10,11... | collective-permute-start | bytes 983048 | tf_op jit(solution)/shard_map/ppermute | solution.py:260
  19.4 9.2 %collective-permute-start.5 = (bf16[512,256]{1,0:T(8,128)(2,1)S(1)}, bf16[512,256]{1,0:T(8,128)(2,1)S(1)}, u32[]{:S(2)}, u32[]{:S(2)}) collective-permute-start(bf16[512,256]{1,0:T(8,128)(2,1)S(1)} %get-tuple-element.58.refs_0_.block_in), channel_id=1, source_target_pairs={{0,1},{1,0},{2,3},{3,2},{4,5},{5,4},{6,7},{7,6},{8,9},{9,8},{10,11... | collective-permute-start | bytes 786440 | tf_op jit(solution)/shard_map/ppermute | solution.py:260
  19.9 8.7 %collective-permute-start.7 = (bf16[512,256]{1,0:T(8,128)(2,1)S(1)}, bf16[512,256]{1,0:T(8,128)(2,1)S(1)}, u32[]{:S(2)}, u32[]{:S(2)}) collective-permute-start(bf16[512,256]{1,0:T(8,128)(2,1)S(1)} %collective-permute-done.6.refs_2_), channel_id=1, source_target_pairs={{0,1},{1,0},{2,3},{3,2},{4,5},{5,4},{6,7},{7,6},{8,9},{9,8},{10,11... | collective-permute-start | bytes 786440 | tf_op jit(solution)/shard_map/ppermute | solution.py:260
  22.3 17.1 %collective-permute-start.12 = (bf16[512,256]{1,0:T(8,128)(2,1)S(1)}, bf16[512,256]{1,0:T(8,128)(2,1)S(1)}, u32[]{:S(2)}, u32[]{:S(2)}) collective-permute-start(bf16[512,256]{1,0:T(8,128)(2,1)S(1)} %get-tuple-element.64), channel_id=1, source_target_pairs={{0,28},{4,24},{8,20},{12,16},{16,12},{20,8},{24,4},{28,0},{1,29},{... | collective-permute-start | bytes 786440 | tf_op jit(solution)/shard_map/ppermute | solution.py:269
  27.8 11.6 %collective-permute-start.14 = (bf16[512,256]{1,0:T(8,128)(2,1)}, bf16[512,256]{1,0:T(8,128)(2,1)S(1)}, u32[]{:S(2)}, u32[]{:S(2)}) collective-permute-start(bf16[512,256]{1,0:T(8,128)(2,1)} %cotangent.3), channel_id=1, source_target_pairs={{0,2},{1,3},{2,0},{3,1},{4,6},{5,7},{6,4},{7,5},{8,10},{9,11},{10,... | collective-permute-start | bytes 786440 | tf_op jit(solution)/shard_map/ppermute | solution.py:260
  28.6 21.5 %collective-permute-start.23 = (bf16[1024,256]{1,0:T(8,128)(2,1)}, bf16[1024,256]{1,0:T(8,128)(2,1)S(1)}, u32[]{:S(2)}, u32[]{:S(2)}) collective-permute-start(bf16[1024,256]{1,0:T(8,128)(2,1)} %w_out.1), channel_id=1, source_target_pairs={{0,1},{1,0},{2,3},{3,2},{4,5},{5,4},{6,7},{7,6},{8,9},{9,8},{10,11... | collective-permute-start | bytes 1572872 | tf_op jit(solution)/shard_map/ppermute | solution.py:260
  36.8 11.6 %collective-permute-start.11 = (bf16[512,256]{1,0:T(8,128)(2,1)S(1)}, bf16[512,256]{1,0:T(8,128)(2,1)S(1)}, u32[]{:S(2)}, u32[]{:S(2)}) collective-permute-start(bf16[512,256]{1,0:T(8,128)(2,1)S(1)} %get-tuple-element.63), channel_id=1, source_target_pairs={{0,28},{4,24},{8,20},{12,16},{16,12},{20,8},{24,4},{28,0},{1,29},{... | collective-permute-start | bytes 786440 | tf_op jit(solution)/shard_map/ppermute | solution.py:269
  39.3 9.1 %collective-permute-start.15 = (bf16[512,256]{1,0:T(8,128)(2,1)S(1)}, bf16[512,256]{1,0:T(8,128)(2,1)S(1)}, u32[]{:S(2)}, u32[]{:S(2)}) collective-permute-start(bf16[512,256]{1,0:T(8,128)(2,1)S(1)} %collective-permute-done.12.refs_4_.mirrored_cotangent), channel_id=1, source_target_pairs={{0,2},{1,3},{2,0},{3,1},{4,6},{5,7},{6,4},{7,5},{8,10},{9,11},{10,... | collective-permute-start | bytes 786440 | tf_op jit(solution)/shard_map/ppermute | solution.py:260
  40.2 8.7 %collective-permute-start.19 = (bf16[512,256]{1,0:T(8,128)(2,1)}, bf16[512,256]{1,0:T(8,128)(2,1)S(1)}, u32[]{:S(2)}, u32[]{:S(2)}) collective-permute-start(bf16[512,256]{1,0:T(8,128)(2,1)} %cotangent.3), channel_id=1, source_target_pairs={{0,1},{1,0},{2,3},{3,2},{4,5},{5,4},{6,7},{7,6},{8,9},{9,8},{10,11... | collective-permute-start | bytes 786440 | tf_op jit(solution)/shard_map/ppermute | solution.py:260
  40.2 14.9 %collective-permute-start.24 = (bf16[512,256]{1,0:T(8,128)(2,1)S(1)}, bf16[512,256]{1,0:T(8,128)(2,1)S(1)}, u32[]{:S(2)}, u32[]{:S(2)}) collective-permute-start(bf16[512,256]{1,0:T(8,128)(2,1)S(1)} %collective-permute-done.13.refs_10_), channel_id=1, source_target_pairs={{0,4},{4,0},{8,12},{12,8},{16,20},{20,16},{24,28},{28,24},{1,5},{5... | collective-permute-start | bytes 786440 | tf_op jit(solution)/shard_map/ppermute | solution.py:260
  48.4 8.2 %collective-permute-start.25 = (bf16[512,256]{1,0:T(8,128)(2,1)S(1)}, bf16[512,256]{1,0:T(8,128)(2,1)S(1)}, u32[]{:S(2)}, u32[]{:S(2)}) collective-permute-start(bf16[512,256]{1,0:T(8,128)(2,1)S(1)} %collective-permute-done.13.refs_10_), channel_id=1, source_target_pairs={{0,1},{1,0},{2,3},{3,2},{4,5},{5,4},{6,7},{7,6},{8,9},{9,8},{10,11... | collective-permute-start | bytes 786440 | tf_op jit(solution)/shard_map/ppermute | solution.py:260
  48.9 8.3 %collective-permute-start.9 = (bf16[512,256]{1,0:T(8,128)(2,1)S(1)}, bf16[512,256]{1,0:T(8,128)(2,1)S(1)}, u32[]{:S(2)}, u32[]{:S(2)}) collective-permute-start(bf16[512,256]{1,0:T(8,128)(2,1)S(1)} %get-tuple-element.62.refs_0_), channel_id=1, source_target_pairs={{0,2},{1,3},{2,0},{3,1},{4,6},{5,7},{6,4},{7,5},{8,10},{9,11},{10,... | collective-permute-start | bytes 786440 | tf_op jit(solution)/shard_map/ppermute | solution.py:260
  55.1 8.7 %collective-permute-start.17 = (bf16[512,256]{1,0:T(8,128)(2,1)S(1)}, bf16[512,256]{1,0:T(8,128)(2,1)S(1)}, u32[]{:S(2)}, u32[]{:S(2)}) collective-permute-start(bf16[512,256]{1,0:T(8,128)(2,1)S(1)} %collective-permute-done.11.refs_4_), channel_id=1, source_target_pairs={{0,2},{1,3},{2,0},{3,1},{4,6},{5,7},{6,4},{7,5},{8,10},{9,11},{10,... | collective-permute-start | bytes 786440 | tf_op jit(solution)/shard_map/ppermute | solution.py:260
  57.2 10.0 %collective-permute-start.8 = (bf16[512,256]{1,0:T(8,128)(2,1)S(1)}, bf16[512,256]{1,0:T(8,128)(2,1)S(1)}, u32[]{:S(2)}, u32[]{:S(2)}) collective-permute-start(bf16[512,256]{1,0:T(8,128)(2,1)S(1)} %get-tuple-element.62.refs_0_), channel_id=1, source_target_pairs={{0,1},{1,0},{2,3},{3,2},{4,5},{5,4},{6,7},{7,6},{8,9},{9,8},{10,11... | collective-permute-start | bytes 786440 | tf_op jit(solution)/shard_map/ppermute | solution.py:260
  57.2 10.0 %collective-permute-start.10 = (bf16[512,256]{1,0:T(8,128)(2,1)S(1)}, bf16[512,256]{1,0:T(8,128)(2,1)S(1)}, u32[]{:S(2)}, u32[]{:S(2)}) collective-permute-start(bf16[512,256]{1,0:T(8,128)(2,1)S(1)} %collective-permute-done.9.refs_2_), channel_id=1, source_target_pairs={{0,1},{1,0},{2,3},{3,2},{4,5},{5,4},{6,7},{7,6},{8,9},{9,8},{10,11... | collective-permute-start | bytes 786440 | tf_op jit(solution)/shard_map/ppermute | solution.py:260
  57.7 9.5 %collective-permute-start.16 = (bf16[512,256]{1,0:T(8,128)(2,1)S(1)}, bf16[512,256]{1,0:T(8,128)(2,1)S(1)}, u32[]{:S(2)}, u32[]{:S(2)}) collective-permute-start(bf16[512,256]{1,0:T(8,128)(2,1)S(1)} %collective-permute-done.11.refs_4_), channel_id=1, source_target_pairs={{0,1},{1,0},{2,3},{3,2},{4,5},{5,4},{6,7},{7,6},{8,9},{9,8},{10,11... | collective-permute-start | bytes 786440 | tf_op jit(solution)/shard_map/ppermute | solution.py:260
  79.7 20.4 %collective-permute-start.30 = (bf16[256,256]{1,0:T(8,128)(2,1)}, bf16[256,256]{1,0:T(8,128)(2,1)}, u32[]{:S(2)}, u32[]{:S(2)}) collective-permute-start(bf16[256,256]{1,0:T(8,128)(2,1)} %get-tuple-element.87), channel_id=1, source_target_pairs={{0,8},{4,12},{8,0},{12,4},{16,24},{20,28},{24,16},{28,20},{1,9},{5... | collective-permute-start | bytes 393224 | tf_op jit(solution)/shard_map/ppermute | solution.py:260
  89.6 11.5 %collective-permute-start.29 = (bf16[512,256]{1,0:T(8,128)(2,1)}, bf16[512,256]{1,0:T(8,128)(2,1)S(1)}, u32[]{:S(2)}, u32[]{:S(2)}) collective-permute-start(bf16[512,256]{1,0:T(8,128)(2,1)} %copy-done.20), channel_id=1, source_target_pairs={{0,4},{4,0},{8,12},{12,8},{16,20},{20,16},{24,28},{28,24},{1,5},{5... | collective-permute-start | bytes 786440 | tf_op jit(solution)/shard_map/ppermute | solution.py:260
  124.1 9.8 %collective-permute-start.39 = (bf16[256,256]{1,0:T(8,128)(2,1)S(1)}, bf16[256,256]{1,0:T(8,128)(2,1)S(1)}, u32[]{:S(2)}, u32[]{:S(2)}) collective-permute-start(bf16[256,256]{1,0:T(8,128)(2,1)S(1)} %pad_maximum_fusion.7), channel_id=1, source_target_pairs={{0,8},{4,12},{8,0},{12,4},{16,24},{20,28},{24,16},{28,20},{1,9},{5... | collective-permute-start | bytes 393224 | tf_op jit(solution)/shard_map/ppermute | solution.py:260
  125.6 8.3 %collective-permute-start.37 = (bf16[144,256]{1,0:T(8,128)(2,1)S(1)}, bf16[144,256]{1,0:T(8,128)(2,1)S(1)}, u32[]{:S(2)}, u32[]{:S(2)}) collective-permute-start(bf16[144,256]{1,0:T(8,128)(2,1)S(1)} %dynamic-slice_convert_fusion.2), channel_id=1, source_target_pairs={{0,16},{4,20},{8,24},{12,28},{16,0},{20,4},{24,8},{28,12},{1,17},{... | collective-permute-start | bytes 221192 | tf_op jit(solution)/shard_map/ppermute | solution.py:260
  148.3 8.1 %collective-permute-start.44 = (bf16[576,256]{1,0:T(8,128)(2,1)S(1)}, bf16[576,256]{1,0:T(8,128)(2,1)S(1)}, u32[]{:S(2)}, u32[]{:S(2)}) collective-permute-start(bf16[576,256]{1,0:T(8,128)(2,1)S(1)} %pad_maximum_fusion.3), channel_id=1, source_target_pairs={{0,4},{4,0},{8,12},{12,8},{16,20},{20,16},{24,28},{28,24},{1,5},{5... | collective-permute-start | bytes 884744 | tf_op jit(solution)/shard_map/ppermute | solution.py:260
  (47 other events, 320.1 us)

commit v7 on v6

--- a/solution.py
+++ b/solution.py
@@ -25,7 +25,7 @@
     return lax.dot_general(left, right, dims, preferred_element_type=F32)
 
 
-def run(body, place, operands, outs, scratch=(), megabytes=16, gflop=0.1):
+def run(body, place, operands, outs, scratch=(), megabytes=8, gflop=0.1):
     moved = sum(x.size * x.dtype.itemsize for x in operands)
     return pl.pallas_call(
         body,
@@ -49,7 +49,7 @@
     return (down + across == rows - 1).astype(F32).astype(BF16)
 
 
-def input_kernel(place, tokens, hidden, embedding, block_in, first, second, padded):
+def input_kernel(place, tokens, hidden, embedding, block_in, padded):
     bases, rows = embedding.shape[0], hidden.shape[0]
     padded[...] = jnp.zeros_like(padded)
     padded[:bases] = embedding[...].astype(F32)
@@ -57,13 +57,13 @@
     one_hot = (base == tokens[...]).astype(F32).astype(BF16)
     shift = dot(one_hot, padded[...].astype(BF16), ROWS_DOT)
     block_in[...] = (hidden[...].astype(F32) + shift).astype(BF16)
+
+
+def setup_kernel(place, block_in, cotangent, order, first, second, flipped, choose):
     odd = place[0] % 2
-    far = rows - EDGE
+    far = block_in.shape[0] - EDGE
     first[...] = block_in[pl.ds(pl.multiple_of((1 - odd) * far, 16), EDGE), :]
     second[...] = block_in[pl.ds(pl.multiple_of(odd * far, 16), EDGE), :]
-
-
-def setup_kernel(place, cotangent, order, flipped, choose):
     flipped[...] = dot(anti_identity(cotangent.shape[0]), cotangent[...]).astype(BF16)
     me, width = place[1], cotangent.shape[1]
     down = lax.broadcasted_iota(jnp.int32, (width, width), 0)
@@ -91,7 +91,7 @@
 
 
 def forward_kernel(channels, place, edges, edges_core, w_in, projected, gate_pre, conv_w, *outs):
-    level_0, level_1, level_2, level_3, gated, flipped = outs
+    level_0, level_1, level_2, level_3, gated = outs
     me, odd = place[1], place[0] % 2
     rows, width = projected.shape
     left = jnp.zeros((EDGE, width), F32)
@@ -119,7 +119,10 @@
         source = target
     gate = gate_pre[...]
     gated[...] = (level_3[...] * (gate / (1.0 + jnp.exp(-gate)))).astype(BF16)
-    flipped[...] = dot(anti_identity(rows), gated[...]).astype(BF16)
+
+
+def flip_kernel(place, block, flipped):
+    flipped[...] = dot(anti_identity(block.shape[0]), block[...]).astype(BF16)
 
 
 def norm_grad_kernel(channels, place, *refs):
@@ -319,32 +322,31 @@
     block = ((rows, width), BF16)
     place = jnp.stack([lax.axis_index("seq"), lax.axis_index("ch"), lax.axis_size("seq")]).astype(jnp.int32)
 
-    local_input, first, second = run(
+    local_input = run(
         input_kernel,
         place,
         (tokens.reshape(1, rows), hidden, embedding),
-        [block, ((EDGE, width), BF16), ((EDGE, width), BF16)],
+        [block],
         [pltpu.VMEM((16, width), F32)],
-    )
+    )[0]
     input_x = exchange(local_input, "ch", cross)
     input_core = exchange(local_input, "ch", 1)
+    first, second, flipped_cotangent, choose = run(
+        setup_kernel,
+        place,
+        (local_input, cotangent, channel_order.reshape(1, full)),
+        [((EDGE, width), BF16), ((EDGE, width), BF16), block, ((full, full), BF16)],
+    )
     near = swap_edges(first, second)
     far = swap_edges(first, second, cross)
-    flipped_cotangent, choose = run(
-        setup_kernel,
-        place,
-        (cotangent, channel_order.reshape(1, full)),
-        [block, ((full, full), BF16)],
-    )
+    flipped_cotangent, *near = together(flipped_cotangent, *near)
+    mirrored_cotangent = mirror(flipped_cotangent)
     w_half = lax.dynamic_slice_in_dim(w_out, seq_bit(1) * (full // 2), full // 2, 0)
-    w_half, input_x = together(w_half, input_x)
+    w_half, early_cotangent, input_x = together(w_half, cotangent, input_x)
     w_x_mine = exchange(w_half, "ch", cross)
     mains = [local_input, input_core, input_x, exchange(input_x, "ch", 1)]
     edges = jnp.concatenate(near + far, axis=0)
     edges_core = exchange(edges, "ch", 1)
-    edges, flipped_cotangent = together(edges, flipped_cotangent)
-    mirrored_cotangent = mirror(flipped_cotangent)
-    early_cotangent, w_x_mine = together(cotangent, w_x_mine)
     cotangent_x = exchange(early_cotangent, "ch", cross)
     w_x_other = exchange(w_x_mine, "seq", 1)
     late_cotangent, cotangent_x = together(mirrored_cotangent, cotangent_x)
@@ -355,21 +357,22 @@
         place,
         (*mains, w_in, w_gate),
         [((rows, width), F32)] * 2,
-        gflop=0.6,
-    )
-    level_0, level_1, level_2, level_3, gated, flipped = run(
+        gflop=6.0,
+    )
+    level_0, level_1, level_2, level_3, gated = run(
         functools.partial(forward_kernel, channels),
         place,
         (edges, edges_core, w_in, projected, gate_pre, conv_w),
-        [((fore + rows + aft, width), F32) for fore, aft in zip(FORE, AFT)] + [block, block],
-        megabytes=24,
+        [((fore + rows + aft, width), F32) for fore, aft in zip(FORE, AFT)] + [block],
         gflop=0.4,
     )
-    mirrored = mirror(flipped)
-    gated_x = exchange(gated, "ch", cross)
+    mirrored, w_x_other = together(mirror(gated), w_x_other)
+    mirrored = run(flip_kernel, place, (mirrored,), [block], gflop=12.0)[0]
+    late_gated, mirrored_cotangent = together(gated, mirrored_cotangent)
+    gated_x = exchange(late_gated, "ch", cross)
+    mirrored, mirrored_cotangent_x, gated_x = together(mirrored, mirrored_cotangent_x, gated_x)
+    mirrored_x = exchange(mirrored, "ch", cross)
     gated_all = [gated, exchange(gated, "ch", 1), gated_x, exchange(gated_x, "ch", 1)]
-    mirrored, mirrored_cotangent_x = together(mirrored, mirrored_cotangent_x)
-    mirrored_x = exchange(mirrored, "ch", cross)
     cotangent_all = [cotangent, exchange(cotangent, "ch", 1), cotangent_x, exchange(cotangent_x, "ch", 1)]
     mirrored_cotangent_all = [
         mirrored_cotangent,
@@ -392,9 +395,9 @@
         ),
         [((2 * rows, full), BF16)],
         [pltpu.VMEM((full, width), BF16)] * 2,
-        megabytes=24,
-        gflop=2.1,
+        gflop=6.0,
     )[0]
+    mirrored_x, grad_norm = together(mirrored_x, grad_norm)
     mirrored_all = [mirrored, exchange(mirrored, "ch", 1), mirrored_x, exchange(mirrored_x, "ch", 1)]
 
     normalized, upstream, grad_gate_pre, first, second = run(
@@ -403,7 +406,6 @@
         (*gated_all, *mirrored_all, grad_norm, choose, gain.reshape(1, full), gate_pre, level_3),
         [((2 * rows, full), BF16), block, block, ((EDGE, width), BF16), ((EDGE, width), BF16)],
         [pltpu.VMEM((1, full), F32), pltpu.VMEM((rows, width), F32)],
-        megabytes=32,
         gflop=2.5,
     )
     first, second = swap_edges(first, second)
@@ -418,9 +420,9 @@
             ((full // 2, width), F32),
         ],
         [pltpu.VMEM((full // 2, width), F32), pltpu.VMEM((full, width), F32)],
-        megabytes=24,
         gflop=0.8,
     )
+    out_sent, gate_sent, first, second = together(out_sent, gate_sent, first, second)
     out_other = exchange(out_sent, "seq", steps[1])
     gate_other = exchange(gate_sent, "seq", steps[0])
     half = full // 2 + SPARE
@@ -431,7 +433,6 @@
         [((half, width), BF16), ((half, width), F32)],
         [pltpu.VMEM((2 * half, width), F32)]
         + [pltpu.VMEM((BACK_FORE[k] + rows + BACK_AFT[k], width), F32) for k in (3, 2, 1)],
-        megabytes=24,
         gflop=0.5,
     )
     output = run(

time: 159 us -> 155 us (0.975)
  waiting for transfers between devices: 55 us -> 45.4 us
  starting transfers between devices: 56.9 us -> 61.6 us
    ppermute x38, starting transfers between devices: 38.3 us -> 49.4 us  [exchange(): return lax.ppermute(block, axis, [(i, i ^ distance) for i in range(count)])]
    ppermute x38, waiting for transfers between devices: 49 us -> 42.8 us  [exchange(): return lax.ppermute(block, axis, [(i, i ^ distance) for i in range(count)])]
    ppermute x2, waiting for transfers between devices: 4.64 us -> 0.01 us  [mirror(): lax.ppermute(block, 'seq', [(i, count - 1 - i) for i in range(count)])]
    ppermute x6, starting transfers between devices: 10.5 us -> 7.3 us  [swap_edges(): received.append(lax.ppermute(block, ('seq', 'ch'), route))]
    ppermute x2, starting transfers between devices: 8.02 us -> 4.85 us  [mirror(): lax.ppermute(block, 'seq', [(i, count - 1 - i) for i in range(count)])]
    unnamed x53 -> x67, local copies, waits for them, and re-layouts: 15.3 us -> 16.4 us
    pallas_call x9 -> x10, Pallas kernels: 23.9 us -> 23.1 us  [run(): pl.pallas_call(body, out_shape=[jax.ShapeDtypeStruct(shape, dtype) for sh...]
  transfers between devices with their start and end apart: 46 -> 46, of which waited for: 19 -> 20; matrix products, arithmetic and copies ran while one was open for 2% -> 3% of each run, Pallas kernels for 8% -> 10%
where the time goes in v7:
time: 155 us; the launch traced here: 154 us
  starting transfers between devices  61.6 us (40%)
  waiting for transfers between devices  45.4 us (29%)
  Pallas kernels  23.1 us (15%)
  local copies, waits for them, and re-layouts  18 us (12%)
  other arithmetic  5.05 us (3%)
    ppermute x38, starting transfers between devices, exchange(): return lax.ppermute(block, axis, [(i, i ^ distance) for i in range(count)])  49.4 us
    ppermute x38, waiting for transfers between devices, exchange(): return lax.ppermute(block, axis, [(i, i ^ distance) for i in range(count)])  42.8 us
    pallas_call x10, Pallas kernels, run(): pl.pallas_call(body, out_shape=[jax.ShapeDtypeStruct(shape, dtype) for sh...  23.1 us
    unnamed x67, local copies, waits for them, and re-layouts  16.4 us
    ppermute x6, starting transfers between devices, swap_edges(): received.append(lax.ppermute(block, ('seq', 'ch'), route))  7.3 us
    ppermute x2, starting transfers between devices, mirror(): lax.ppermute(block, 'seq', [(i, count - 1 - i) for i in range(count)])  4.85 us
  transfers between devices with their start and end apart: 46, of which 20 were waited for; matrix products, arithmetic and copies ran while one was open for 3% of the time, Pallas kernels for 10%

profile of v7, /device:TPU:0, one launch (start us, length us, event | category | flops | bytes accessed | tf_op | source)
XLA Modules:
  0.0 154.4 jit_solution(6880976733997024978)
XLA Ops:
  3.8 3.0 %collective-permute-start.6 = (bf16[512,256]{1,0:T(8,128)(2,1)S(1)}, bf16[512,256]{1,0:T(8,128)(2,1)S(1)}, u32[]{:S(2)}, u32[]{:S(2)}) collective-permute-start(bf16[512,256]{1,0:T(8,128)(2,1)S(1)} %shard_map.137.block_in.refs_0_), channel_id=1, source_target_pairs={{0,2},{1,3},{2,0},{3,1},{4,6},{5,7},{6,4},{7,5},{8,10},{9,11},{10,... | collective-permute-start | bytes 786440 | tf_op jit(solution)/shard_map/ppermute | solution.py:263
  8.5 1.9 %shard_map.138 = (bf16[160,256]{1,0:T(8,128)(2,1)}, bf16[160,256]{1,0:T(8,128)(2,1)S(1)}, bf16[512,256]{1,0:T(8,128)(2,1)}, bf16[1024,1024]{1,0:T(8,128)(2,1)S(1)}) custom-call(s32[3]{0:T(128)S(1)} %pad_add_fusion.place, bf16[512,256]{1,0:T(8,128)(2,1)S(1)} %shard_map.137.block_in.refs_0_, bf16[512,256]{1,0:T(8,128)(2,1)S(1)} %copy-done.3, s32[1,1024]{1,0:T(1,128)S(1)} %bitcast.5), custom_call_target="tpu_custom_call" | custom-call | flops 100000000 | bytes 528384 | tf_op jit(solution)/shard_map/pallas_call | solution.py:30
  18.8 3.7 %collective-permute-start.12 = (bf16[512,256]{1,0:T(8,128)(2,1)}, bf16[512,256]{1,0:T(8,128)(2,1)S(1)}, u32[]{:S(2)}, u32[]{:S(2)}) collective-permute-start(bf16[512,256]{1,0:T(8,128)(2,1)} %get-tuple-element.74), channel_id=1, source_target_pairs={{0,28},{4,24},{8,20},{12,16},{16,12},{20,8},{24,4},{28,0},{1,29},{... | collective-permute-start | bytes 786440 | tf_op jit(solution)/shard_map/ppermute | solution.py:272
  27.9 2.0 %shard_map.140 = (f32[752,256]{1,0:T(8,128)S(1)}, f32[728,256]{1,0:T(8,128)S(1)}, f32[704,256]{1,0:T(8,128)S(1)}, f32[512,256]{1,0:T(8,128)S(1)}, bf16[512,256]{1,0:T(8,128)(2,1)S(1)}) custom-call(s32[3]{0:T(128)S(1)} %pad_add_fusion.place, bf16[640,256]{1,0:T(8,128)(2,1)S(1)} %constant_dynamic-update-slice_fusion.edges, ...), custom_call_target="tpu_custom_call" | custom-call | flops 400000000 | bytes 2240512 | tf_op jit(solution)/shard_map/pallas_call | solution.py:30
  31.7 7.9 %collective-permute-start.11 = (bf16[512,256]{1,0:T(8,128)(2,1)S(1)}, bf16[512,256]{1,0:T(8,128)(2,1)S(1)}, u32[]{:S(2)}, u32[]{:S(2)}) collective-permute-start(bf16[512,256]{1,0:T(8,128)(2,1)S(1)} %collective-permute-done.10.refs_10_), channel_id=1, source_target_pairs={{0,4},{4,0},{8,12},{12,8},{16,20},{20,16},{24,28},{28,24},{1,5},{5... | collective-permute-start | bytes 786440 | tf_op jit(solution)/shard_map/ppermute | solution.py:263
  42.1 7.7 %collective-permute-done.11.refs_11_ = bf16[512,256]{1,0:T(8,128)(2,1)S(1)} collective-permute-done((bf16[512,256]{1,0:T(8,128)(2,1)S(1)}, bf16[512,256]{1,0:T(8,128)(2,1)S(1)}, u32[]{:S(2)}, u32[]{:S(2)}) %collective-permute-start.11) | collective-permute-done | bytes 262176 | tf_op jit(solution)/shard_map/ppermute | solution.py:263
  51.3 2.7 %collective-permute-done.14.refs_6_ = bf16[512,256]{1,0:T(8,128)(2,1)S(1)} collective-permute-done((bf16[512,256]{1,0:T(8,128)(2,1)S(1)}, bf16[512,256]{1,0:T(8,128)(2,1)S(1)}, u32[]{:S(2)}, u32[]{:S(2)}) %collective-permute-start.14) | collective-permute-done | bytes 262176 | tf_op jit(solution)/shard_map/ppermute | solution.py:263
  57.0 2.9 %shard_map.142.refs_8_ = bf16[1024,1024]{1,0:T(8,128)(2,1)S(1)} custom-call(s32[3]{0:T(128)S(1)} %pad_add_fusion.place, bf16[512,256]{1,0:T(8,128)(2,1)S(1)} %copy-done.4, bf16[512,256]{1,0:T(8,128)(2,1)S(1)} %collective-permute-done.19.refs_1_, bf16[512,256]{1,0:T(8,128)(2,1)S(1)} %collective-permute-done.13.refs_2_, ...), custom_call_target="tpu_custom_call" | custom-call | flops 6000000000 | bytes 4194304 | tf_op jit(solution)/shard_map/pallas_call | solution.py:30
  60.0 3.3 %collective-permute-done.18.refs_6_ = bf16[512,256]{1,0:T(8,128)(2,1)S(1)} collective-permute-done((bf16[512,256]{1,0:T(8,128)(2,1)S(1)}, bf16[512,256]{1,0:T(8,128)(2,1)S(1)}, u32[]{:S(2)}, u32[]{:S(2)}) %collective-permute-start.18) | collective-permute-done | bytes 262176 | tf_op jit(solution)/shard_map/ppermute | solution.py:263
  64.9 7.4 %shard_map.143 = (bf16[1024,1024]{1,0:T(8,128)(2,1)S(1)}, bf16[512,256]{1,0:T(8,128)(2,1)S(1)}, bf16[512,256]{1,0:T(8,128)(2,1)S(1)}, bf16[160,256]{1,0:T(8,128)(2,1)S(1)}, bf16[160,256]{1,0:T(8,128)(2,1)S(1)}) custom-call(s32[3]{0:T(128)S(1)} %pad_add_fusion.place, bf16[512,256]{1,0:T(8,128)(2,1)S(1)} %get-tuple-element.77.refs_0_, ...), custom_call_target="tpu_custom_call" | custom-call | flops 2500000000 | bytes 7344128 | tf_op jit(solution)/shard_map/pallas_call | solution.py:30
  72.3 3.6 %collective-permute-start.27 = (bf16[160,256]{1,0:T(8,128)(2,1)S(1)}, bf16[160,256]{1,0:T(8,128)(2,1)S(1)}, u32[]{:S(2)}, u32[]{:S(2)}) collective-permute-start(bf16[160,256]{1,0:T(8,128)(2,1)S(1)} %get-tuple-element.93), channel_id=1, source_target_pairs={{0,4},{4,0},{1,5},{5,1},{2,6},{6,2},{3,7},{7,3},{8,12},{12,8},{9,1... | collective-permute-start | bytes 245768 | tf_op jit(solution)/shard_map/ppermute | solution.py:284
  76.8 1.9 %shard_map.145 = (bf16[256,256]{1,0:T(8,128)(2,1)}, f32[256,256]{1,0:T(8,128)S(1)}, bf16[512,256]{1,0:T(8,128)(2,1)S(1)}, f32[512,256]{1,0:T(8,128)S(1)}) custom-call(s32[3]{0:T(128)S(1)} %pad_add_fusion.place, bf16[1024,1024]{1,0:T(8,128)(2,1)S(1)} %get-tuple-element.88.normalized, bf16[512,256]{1,0:T(8,128)(2,1)S(1)} %copy-done.5, ...), custom_call_target="tpu_custom_call" | custom-call | flops 800000000 | bytes 3932160 | tf_op jit(solution)/shard_map/pallas_call | solution.py:30
  81.5 9.0 %collective-permute-start.30 = (bf16[256,256]{1,0:T(8,128)(2,1)}, bf16[256,256]{1,0:T(8,128)(2,1)}, u32[]{:S(2)}, u32[]{:S(2)}) collective-permute-start(bf16[256,256]{1,0:T(8,128)(2,1)} %get-tuple-element.105), channel_id=1, source_target_pairs={{0,8},{4,12},{8,0},{12,4},{16,24},{20,28},{24,16},{28,20},{1,9},{5... | collective-permute-start | bytes 393224 | tf_op jit(solution)/shard_map/ppermute | solution.py:263
  97.1 2.4 %shard_map.146 = (bf16[576,256]{1,0:T(8,128)(2,1)S(1)}, f32[576,256]{1,0:T(8,128)S(1)}) custom-call(s32[3]{0:T(128)S(1)} %pad_add_fusion.place, bf16[512,256]{1,0:T(8,128)(2,1)S(1)} %copy-done.17, bf16[160,256]{1,0:T(8,128)(2,1)S(1)} %collective-permute-done.27.first, bf16[160,256]{1,0:T(8,128)(2,1)S(1)} %copy-done.22, f32[752,256]{1,0:T(8,128)S(1)} %copy-done.7, ...), custom_call_target="tpu_custom_call" | custom-call | flops 500000000 | bytes 3723264 | tf_op jit(solution)/shard_map/pallas_call | solution.py:30
  104.3 1.9 %collective-permute-done.33 = bf16[128,256]{1,0:T(8,128)(2,1)S(1)} collective-permute-done((bf16[128,256]{1,0:T(8,128)(2,1)S(1)}, bf16[128,256]{1,0:T(8,128)(2,1)S(1)}, u32[]{:S(2)}, u32[]{:S(2)}) %collective-permute-start.33) | collective-permute-done | bytes 65568 | tf_op jit(solution)/shard_map/ppermute | solution.py:263
  107.7 2.8 %collective-permute-done.31 = bf16[576,256]{1,0:T(8,128)(2,1)S(1)} collective-permute-done((bf16[576,256]{1,0:T(8,128)(2,1)S(1)}, bf16[576,256]{1,0:T(8,128)(2,1)S(1)}, u32[]{:S(2)}, u32[]{:S(2)}) %collective-permute-start.31) | collective-permute-done | bytes 294944 | tf_op jit(solution)/shard_map/ppermute | solution.py:263
  110.5 2.7 %collective-permute-start.36 = (bf16[128,256]{1,0:T(8,128)(2,1)S(1)}, bf16[128,256]{1,0:T(8,128)(2,1)S(1)}, u32[]{:S(2)}, u32[]{:S(2)}) collective-permute-start(bf16[128,256]{1,0:T(8,128)(2,1)S(1)} %convert_add_fusion.7), channel_id=1, source_target_pairs={{0,16},{4,20},{8,24},{12,28},{16,0},{20,4},{24,8},{28,12},{1,17},{... | collective-permute-start | bytes 196616 | tf_op jit(solution)/shard_map/ppermute | solution.py:263
  116.5 2.6 %collective-permute-done.35 = bf16[128,256]{1,0:T(8,128)(2,1)S(1)} collective-permute-done((bf16[128,256]{1,0:T(8,128)(2,1)S(1)}, bf16[128,256]{1,0:T(8,128)(2,1)S(1)}, u32[]{:S(2)}, u32[]{:S(2)}) %collective-permute-start.35) | collective-permute-done | bytes 65568 | tf_op jit(solution)/shard_map/ppermute | solution.py:263
  124.2 2.2 %collective-permute-done.38 = bf16[128,256]{1,0:T(8,128)(2,1)S(1)} collective-permute-done((bf16[128,256]{1,0:T(8,128)(2,1)S(1)}, bf16[128,256]{1,0:T(8,128)(2,1)S(1)}, u32[]{:S(2)}, u32[]{:S(2)}) %collective-permute-start.38) | collective-permute-done | bytes 65568 | tf_op jit(solution)/shard_map/ppermute | solution.py:263
  126.4 4.1 %collective-permute-done.37 = bf16[144,256]{1,0:T(8,128)(2,1)S(1)} collective-permute-done((bf16[144,256]{1,0:T(8,128)(2,1)S(1)}, bf16[144,256]{1,0:T(8,128)(2,1)S(1)}, u32[]{:S(2)}, u32[]{:S(2)}) %collective-permute-start.37) | collective-permute-done | bytes 73760 | tf_op jit(solution)/shard_map/ppermute | solution.py:263
  131.8 2.6 %collective-permute-start.41 = (bf16[256,256]{1,0:T(8,128)(2,1)S(1)}, bf16[256,256]{1,0:T(8,128)(2,1)S(1)}, u32[]{:S(2)}, u32[]{:S(2)}) collective-permute-start(bf16[256,256]{1,0:T(8,128)(2,1)S(1)} %pad_maximum_fusion.8), channel_id=1, source_target_pairs={{0,8},{4,12},{8,0},{12,4},{16,24},{20,28},{24,16},{28,20},{1,9},{5... | collective-permute-start | bytes 393224 | tf_op jit(solution)/shard_map/ppermute | solution.py:263
  139.8 1.8 %collective-permute-start.43 = (bf16[288,256]{1,0:T(8,128)(2,1)S(1)}, bf16[288,256]{1,0:T(8,128)(2,1)S(1)}, u32[]{:S(2)}, u32[]{:S(2)}) collective-permute-start(bf16[288,256]{1,0:T(8,128)(2,1)S(1)} %pad_maximum_fusion.6), channel_id=1, source_target_pairs={{0,8},{4,12},{8,0},{12,4},{16,24},{20,28},{24,16},{28,20},{1,9},{5... | collective-permute-start | bytes 442376 | tf_op jit(solution)/shard_map/ppermute | solution.py:263
  146.1 3.6 %collective-permute-done.45 = bf16[512,256]{1,0:T(8,128)(2,1)S(1)} collective-permute-done((bf16[512,256]{1,0:T(8,128)(2,1)S(1)}, bf16[512,256]{1,0:T(8,128)(2,1)S(1)}, u32[]{:S(2)}, u32[]{:S(2)}) %collective-permute-start.45) | collective-permute-done | bytes 262176 | tf_op jit(solution)/shard_map/ppermute | solution.py:263
  150.5 2.3 %collective-permute-done.44 = bf16[576,256]{1,0:T(8,128)(2,1)S(1)} collective-permute-done((bf16[576,256]{1,0:T(8,128)(2,1)S(1)}, bf16[576,256]{1,0:T(8,128)(2,1)S(1)}, u32[]{:S(2)}, u32[]{:S(2)}) %collective-permute-start.44) | collective-permute-done | bytes 294944 | tf_op jit(solution)/shard_map/ppermute | solution.py:263
  (183 shorter events, 67.4 us)
Async XLA Ops:
  3.8 13.4 %collective-permute-start.6 = (bf16[512,256]{1,0:T(8,128)(2,1)S(1)}, bf16[512,256]{1,0:T(8,128)(2,1)S(1)}, u32[]{:S(2)}, u32[]{:S(2)}) collective-permute-start(bf16[512,256]{1,0:T(8,128)(2,1)S(1)} %shard_map.137.block_in.refs_0_), channel_id=1, source_target_pairs={{0,2},{1,3},{2,0},{3,1},{4,6},{5,7},{6,4},{7,5},{8,10},{9,11},{10,... | collective-permute-start | bytes 786440 | tf_op jit(solution)/shard_map/ppermute | solution.py:263
  17.2 7.3 %collective-permute-start.7 = (bf16[512,256]{1,0:T(8,128)(2,1)S(1)}, bf16[512,256]{1,0:T(8,128)(2,1)S(1)}, u32[]{:S(2)}, u32[]{:S(2)}) collective-permute-start(bf16[512,256]{1,0:T(8,128)(2,1)S(1)} %collective-permute-done.6.refs_2_), channel_id=1, source_target_pairs={{0,1},{1,0},{2,3},{3,2},{4,5},{5,4},{6,7},{7,6},{8,9},{9,8},{10,11... | collective-permute-start | bytes 786440 | tf_op jit(solution)/shard_map/ppermute | solution.py:263
  18.8 9.1 %collective-permute-start.4 = (bf16[640,256]{1,0:T(8,128)(2,1)S(1)}, bf16[640,256]{1,0:T(8,128)(2,1)S(1)}, u32[]{:S(2)}, u32[]{:S(2)}) collective-permute-start(bf16[640,256]{1,0:T(8,128)(2,1)S(1)} %constant_dynamic-update-slice_fusion.edges), channel_id=1, source_target_pairs={{0,1},{1,0},{2,3},{3,2},{4,5},{5,4},{6,7},{7,6},{8,9},{9,8},{10,11... | collective-permute-start | bytes 983048 | tf_op jit(solution)/shard_map/ppermute | solution.py:263
  18.8 20.7 %collective-permute-start.12 = (bf16[512,256]{1,0:T(8,128)(2,1)}, bf16[512,256]{1,0:T(8,128)(2,1)S(1)}, u32[]{:S(2)}, u32[]{:S(2)}) collective-permute-start(bf16[512,256]{1,0:T(8,128)(2,1)} %get-tuple-element.74), channel_id=1, source_target_pairs={{0,28},{4,24},{8,20},{12,16},{16,12},{20,8},{24,4},{28,0},{1,29},{... | collective-permute-start | bytes 786440 | tf_op jit(solution)/shard_map/ppermute | solution.py:272
  22.5 9.2 %collective-permute-start.10 = (bf16[512,256]{1,0:T(8,128)(2,1)S(1)}, bf16[512,256]{1,0:T(8,128)(2,1)S(1)}, u32[]{:S(2)}, u32[]{:S(2)}) collective-permute-start(bf16[512,256]{1,0:T(8,128)(2,1)S(1)} %constant_dynamic-slice_fusion), channel_id=1, source_target_pairs={{0,2},{1,3},{2,0},{3,1},{4,6},{5,7},{6,4},{7,5},{8,10},{9,11},{10,... | collective-permute-start | bytes 786440 | tf_op jit(solution)/shard_map/ppermute | solution.py:263
  23.1 17.0 %collective-permute-start.13 = (bf16[512,256]{1,0:T(8,128)(2,1)S(1)}, bf16[512,256]{1,0:T(8,128)(2,1)S(1)}, u32[]{:S(2)}, u32[]{:S(2)}) collective-permute-start(bf16[512,256]{1,0:T(8,128)(2,1)S(1)} %copy-done.4), channel_id=1, source_target_pairs={{0,2},{1,3},{2,0},{3,1},{4,6},{5,7},{6,4},{7,5},{8,10},{9,11},{10,... | collective-permute-start | bytes 786440 | tf_op jit(solution)/shard_map/ppermute | solution.py:263
  30.0 11.6 %collective-permute-start.9 = (bf16[512,256]{1,0:T(8,128)(2,1)S(1)}, bf16[512,256]{1,0:T(8,128)(2,1)S(1)}, u32[]{:S(2)}, u32[]{:S(2)}) collective-permute-start(bf16[512,256]{1,0:T(8,128)(2,1)S(1)} %get-tuple-element.77.refs_0_), channel_id=1, source_target_pairs={{0,28},{4,24},{8,20},{12,16},{16,12},{20,8},{24,4},{28,0},{1,29},{... | collective-permute-start | bytes 786440 | tf_op jit(solution)/shard_map/ppermute | solution.py:272
  31.7 18.2 %collective-permute-start.11 = (bf16[512,256]{1,0:T(8,128)(2,1)S(1)}, bf16[512,256]{1,0:T(8,128)(2,1)S(1)}, u32[]{:S(2)}, u32[]{:S(2)}) collective-permute-start(bf16[512,256]{1,0:T(8,128)(2,1)S(1)} %collective-permute-done.10.refs_10_), channel_id=1, source_target_pairs={{0,4},{4,0},{8,12},{12,8},{16,20},{20,16},{24,28},{28,24},{1,5},{5... | collective-permute-start | bytes 786440 | tf_op jit(solution)/shard_map/ppermute | solution.py:263
  39.6 14.9 %collective-permute-start.23 = (bf16[1024,256]{1,0:T(8,128)(2,1)S(1)}, bf16[1024,256]{1,0:T(8,128)(2,1)S(1)}, u32[]{:S(2)}, u32[]{:S(2)}) collective-permute-start(bf16[1024,256]{1,0:T(8,128)(2,1)S(1)} %copy-done), channel_id=1, source_target_pairs={{0,1},{1,0},{2,3},{3,2},{4,5},{5,4},{6,7},{7,6},{8,9},{9,8},{10,11... | collective-permute-start | bytes 1572872 | tf_op jit(solution)/shard_map/ppermute | solution.py:263
  39.6 14.4 %collective-permute-start.19 = (bf16[512,256]{1,0:T(8,128)(2,1)S(1)}, bf16[512,256]{1,0:T(8,128)(2,1)S(1)}, u32[]{:S(2)}, u32[]{:S(2)}) collective-permute-start(bf16[512,256]{1,0:T(8,128)(2,1)S(1)} %copy-done.4), channel_id=1, source_target_pairs={{0,1},{1,0},{2,3},{3,2},{4,5},{5,4},{6,7},{7,6},{8,9},{9,8},{10,11... | collective-permute-start | bytes 786440 | tf_op jit(solution)/shard_map/ppermute | solution.py:263
  40.1 10.7 %collective-permute-start.15 = (bf16[512,256]{1,0:T(8,128)(2,1)S(1)}, bf16[512,256]{1,0:T(8,128)(2,1)S(1)}, u32[]{:S(2)}, u32[]{:S(2)}) collective-permute-start(bf16[512,256]{1,0:T(8,128)(2,1)S(1)} %get-tuple-element.77.refs_0_), channel_id=1, source_target_pairs={{0,2},{1,3},{2,0},{3,1},{4,6},{5,7},{6,4},{7,5},{8,10},{9,11},{10,... | collective-permute-start | bytes 786440 | tf_op jit(solution)/shard_map/ppermute | solution.py:263
  41.6 12.4 %collective-permute-start.14 = (bf16[512,256]{1,0:T(8,128)(2,1)S(1)}, bf16[512,256]{1,0:T(8,128)(2,1)S(1)}, u32[]{:S(2)}, u32[]{:S(2)}) collective-permute-start(bf16[512,256]{1,0:T(8,128)(2,1)S(1)} %collective-permute-done.12.refs_4_.mirrored_cotangent), channel_id=1, source_target_pairs={{0,2},{1,3},{2,0},{3,1},{4,6},{5,7},{6,4},{7,5},{8,10},{9,11},{10,... | collective-permute-start | bytes 786440 | tf_op jit(solution)/shard_map/ppermute | solution.py:263
  54.6 8.7 %collective-permute-start.8 = (bf16[512,256]{1,0:T(8,128)(2,1)S(1)}, bf16[512,256]{1,0:T(8,128)(2,1)S(1)}, u32[]{:S(2)}, u32[]{:S(2)}) collective-permute-start(bf16[512,256]{1,0:T(8,128)(2,1)S(1)} %get-tuple-element.77.refs_0_), channel_id=1, source_target_pairs={{0,1},{1,0},{2,3},{3,2},{4,5},{5,4},{6,7},{7,6},{8,9},{9,8},{10,11... | collective-permute-start | bytes 786440 | tf_op jit(solution)/shard_map/ppermute | solution.py:263
  55.0 8.3 %collective-permute-start.18 = (bf16[512,256]{1,0:T(8,128)(2,1)S(1)}, bf16[512,256]{1,0:T(8,128)(2,1)S(1)}, u32[]{:S(2)}, u32[]{:S(2)}) collective-permute-start(bf16[512,256]{1,0:T(8,128)(2,1)S(1)} %shard_map.141.refs_4_), channel_id=1, source_target_pairs={{0,2},{1,3},{2,0},{3,1},{4,6},{5,7},{6,4},{7,5},{8,10},{9,11},{10,... | collective-permute-start | bytes 786440 | tf_op jit(solution)/shard_map/ppermute | solution.py:263
  56.5 6.8 %collective-permute-start.17 = (bf16[512,256]{1,0:T(8,128)(2,1)S(1)}, bf16[512,256]{1,0:T(8,128)(2,1)S(1)}, u32[]{:S(2)}, u32[]{:S(2)}) collective-permute-start(bf16[512,256]{1,0:T(8,128)(2,1)S(1)} %shard_map.141.refs_4_), channel_id=1, source_target_pairs={{0,1},{1,0},{2,3},{3,2},{4,5},{5,4},{6,7},{7,6},{8,9},{9,8},{10,11... | collective-permute-start | bytes 786440 | tf_op jit(solution)/shard_map/ppermute | solution.py:263
  56.5 6.8 %collective-permute-start.16 = (bf16[512,256]{1,0:T(8,128)(2,1)S(1)}, bf16[512,256]{1,0:T(8,128)(2,1)S(1)}, u32[]{:S(2)}, u32[]{:S(2)}) collective-permute-start(bf16[512,256]{1,0:T(8,128)(2,1)S(1)} %collective-permute-done.15.refs_2_), channel_id=1, source_target_pairs={{0,1},{1,0},{2,3},{3,2},{4,5},{5,4},{6,7},{7,6},{8,9},{9,8},{10,11... | collective-permute-start | bytes 786440 | tf_op jit(solution)/shard_map/ppermute | solution.py:263
  72.3 8.6 %collective-permute-start.27 = (bf16[160,256]{1,0:T(8,128)(2,1)S(1)}, bf16[160,256]{1,0:T(8,128)(2,1)S(1)}, u32[]{:S(2)}, u32[]{:S(2)}) collective-permute-start(bf16[160,256]{1,0:T(8,128)(2,1)S(1)} %get-tuple-element.93), channel_id=1, source_target_pairs={{0,4},{4,0},{1,5},{5,1},{2,6},{6,2},{3,7},{7,3},{8,12},{12,8},{9,1... | collective-permute-start | bytes 245768 | tf_op jit(solution)/shard_map/ppermute | solution.py:284
  81.5 18.0 %collective-permute-start.30 = (bf16[256,256]{1,0:T(8,128)(2,1)}, bf16[256,256]{1,0:T(8,128)(2,1)}, u32[]{:S(2)}, u32[]{:S(2)}) collective-permute-start(bf16[256,256]{1,0:T(8,128)(2,1)} %get-tuple-element.105), channel_id=1, source_target_pairs={{0,8},{4,12},{8,0},{12,4},{16,24},{20,28},{24,16},{28,20},{1,9},{5... | collective-permute-start | bytes 393224 | tf_op jit(solution)/shard_map/ppermute | solution.py:263
  90.5 10.0 %collective-permute-start.29 = (bf16[512,256]{1,0:T(8,128)(2,1)}, bf16[512,256]{1,0:T(8,128)(2,1)S(1)}, u32[]{:S(2)}, u32[]{:S(2)}) collective-permute-start(bf16[512,256]{1,0:T(8,128)(2,1)} %copy-done.30), channel_id=1, source_target_pairs={{0,4},{4,0},{8,12},{12,8},{16,20},{20,16},{24,28},{28,24},{1,5},{5... | collective-permute-start | bytes 786440 | tf_op jit(solution)/shard_map/ppermute | solution.py:263
  119.9 10.6 %collective-permute-start.39 = (bf16[256,256]{1,0:T(8,128)(2,1)S(1)}, bf16[256,256]{1,0:T(8,128)(2,1)S(1)}, u32[]{:S(2)}, u32[]{:S(2)}) collective-permute-start(bf16[256,256]{1,0:T(8,128)(2,1)S(1)} %pad_maximum_fusion.7), channel_id=1, source_target_pairs={{0,8},{4,12},{8,0},{12,4},{16,24},{20,28},{24,16},{28,20},{1,9},{5... | collective-permute-start | bytes 393224 | tf_op jit(solution)/shard_map/ppermute | solution.py:263
  122.9 7.6 %collective-permute-start.37 = (bf16[144,256]{1,0:T(8,128)(2,1)S(1)}, bf16[144,256]{1,0:T(8,128)(2,1)S(1)}, u32[]{:S(2)}, u32[]{:S(2)}) collective-permute-start(bf16[144,256]{1,0:T(8,128)(2,1)S(1)} %dynamic-slice_convert_fusion.2), channel_id=1, source_target_pairs={{0,16},{4,20},{8,24},{12,28},{16,0},{20,4},{24,8},{28,12},{1,17},{... | collective-permute-start | bytes 221192 | tf_op jit(solution)/shard_map/ppermute | solution.py:263
  130.7 8.2 %collective-permute-start.42 = (bf16[512,256]{1,0:T(8,128)(2,1)S(1)}, bf16[512,256]{1,0:T(8,128)(2,1)S(1)}, u32[]{:S(2)}, u32[]{:S(2)}) collective-permute-start(bf16[512,256]{1,0:T(8,128)(2,1)S(1)} %pad_maximum_fusion.4), channel_id=1, source_target_pairs={{0,4},{4,0},{8,12},{12,8},{16,20},{20,16},{24,28},{28,24},{1,5},{5... | collective-permute-start | bytes 786440 | tf_op jit(solution)/shard_map/ppermute | solution.py:263
  131.8 7.0 %collective-permute-start.41 = (bf16[256,256]{1,0:T(8,128)(2,1)S(1)}, bf16[256,256]{1,0:T(8,128)(2,1)S(1)}, u32[]{:S(2)}, u32[]{:S(2)}) collective-permute-start(bf16[256,256]{1,0:T(8,128)(2,1)S(1)} %pad_maximum_fusion.8), channel_id=1, source_target_pairs={{0,8},{4,12},{8,0},{12,4},{16,24},{20,28},{24,16},{28,20},{1,9},{5... | collective-permute-start | bytes 393224 | tf_op jit(solution)/shard_map/ppermute | solution.py:263
  145.0 7.8 %collective-permute-start.44 = (bf16[576,256]{1,0:T(8,128)(2,1)S(1)}, bf16[576,256]{1,0:T(8,128)(2,1)S(1)}, u32[]{:S(2)}, u32[]{:S(2)}) collective-permute-start(bf16[576,256]{1,0:T(8,128)(2,1)S(1)} %pad_maximum_fusion.3), channel_id=1, source_target_pairs={{0,4},{4,0},{8,12},{12,8},{16,20},{20,16},{24,28},{28,24},{1,5},{5... | collective-permute-start | bytes 884744 | tf_op jit(solution)/shard_map/ppermute | solution.py:263
  (54 other events, 332.7 us)

commit v8 on v7

--- a/solution.py
+++ b/solution.py
@@ -25,13 +25,14 @@
     return lax.dot_general(left, right, dims, preferred_element_type=F32)
 
 
-def run(body, place, operands, outs, scratch=(), megabytes=8, gflop=0.1):
+def run(body, place, operands, outs, scratch=(), megabytes=8, gflop=0.1, fetched=0):
     moved = sum(x.size * x.dtype.itemsize for x in operands)
     return pl.pallas_call(
         body,
         out_shape=[jax.ShapeDtypeStruct(shape, dtype) for shape, dtype in outs],
         in_specs=[pl.BlockSpec(memory_space=pltpu.SMEM)]
-        + [pl.BlockSpec(memory_space=pltpu.VMEM)] * len(operands),
+        + [pl.BlockSpec(memory_space=pltpu.VMEM)] * (len(operands) - fetched)
+        + [pl.BlockSpec(memory_space=pltpu.HBM)] * fetched,
         out_specs=[pl.BlockSpec(memory_space=pltpu.VMEM)] * len(outs),
         scratch_shapes=list(scratch),
         compiler_params=pltpu.CompilerParams(vmem_limit_bytes=megabytes << 20),
@@ -39,8 +40,26 @@
     )(place, *operands)
 
 
+def fetch(sources, targets, semaphores):
+    copies = [
+        pltpu.make_async_copy(source, target, semaphores.at[k])
+        for k, (source, target) in enumerate(zip(sources, targets))
+    ]
+    for copy in copies:
+        copy.start()
+    return copies
+
+
+def fetch_scratch(operands):
+    return [pltpu.VMEM(x.shape, x.dtype) for x in operands] + [pltpu.SemaphoreType.DMA((len(operands),))]
+
+
 def part(index, size, multiple=None):
     return pl.ds(pl.multiple_of(index * size, multiple or size), size)
+
+
+def saved_rows(rows, number):
+    return -(-(FORE[number] + rows + AFT[number]) // 16) * 16
 
 
 def anti_identity(rows):
@@ -49,9 +68,12 @@
     return (down + across == rows - 1).astype(F32).astype(BF16)
 
 
-def input_kernel(place, tokens, hidden, embedding, block_in, padded):
+def input_kernel(place, tokens_hbm, hidden_hbm, embedding_hbm, block_in, padded, tokens, hidden, embedding, semaphores):
+    copies = fetch((tokens_hbm, hidden_hbm, embedding_hbm), (tokens, hidden, embedding), semaphores)
     bases, rows = embedding.shape[0], hidden.shape[0]
     padded[...] = jnp.zeros_like(padded)
+    for copy in copies:
+        copy.wait()
     padded[:bases] = embedding[...].astype(F32)
     base = lax.broadcasted_iota(jnp.int32, (padded.shape[0], rows), 0)
     one_hot = (base == tokens[...]).astype(F32).astype(BF16)
@@ -59,13 +81,12 @@
     block_in[...] = (hidden[...].astype(F32) + shift).astype(BF16)
 
 
-def setup_kernel(place, block_in, cotangent, order, first, second, flipped, choose):
+def setup_kernel(place, block_in, order, first, second, choose):
     odd = place[0] % 2
     far = block_in.shape[0] - EDGE
     first[...] = block_in[pl.ds(pl.multiple_of((1 - odd) * far, 16), EDGE), :]
     second[...] = block_in[pl.ds(pl.multiple_of(odd * far, 16), EDGE), :]
-    flipped[...] = dot(anti_identity(cotangent.shape[0]), cotangent[...]).astype(BF16)
-    me, width = place[1], cotangent.shape[1]
+    me, width = place[1], block_in.shape[1]
     down = lax.broadcasted_iota(jnp.int32, (width, width), 0)
     for j in range(order.shape[1] // width):
         for i in range(order.shape[1] // width):
@@ -76,13 +97,14 @@
 
 
 def project_kernel(channels, place, *refs):
-    mains, (w_in, w_gate, projected, gate_pre) = refs[:channels], refs[channels:]
+    mains, (w_in, w_gate, projected, gate_pre, w_in_on) = refs[:channels], refs[channels:]
     me, width = place[1], mains[0].shape[1]
     for weight, out in ((w_in, projected), (w_gate, gate_pre)):
         total = dot(mains[0][...], weight[part(me, width), :])
         for j in range(1, channels):
             total += dot(mains[j][...], weight[part(me ^ j, width), :])
         out[...] = total
+    w_in_on[...] = w_in[...]
 
 
 def keep_inside(total, place, before, rows):
@@ -91,7 +113,7 @@
 
 
 def forward_kernel(channels, place, edges, edges_core, w_in, projected, gate_pre, conv_w, *outs):
-    level_0, level_1, level_2, level_3, gated = outs
+    levels, level_3, gated, *stages = outs
     me, odd = place[1], place[0] % 2
     rows, width = projected.shape
     left = jnp.zeros((EDGE, width), F32)
@@ -102,23 +124,30 @@
         weight = w_in[part(me ^ j, width), :]
         left += dot(source[pl.ds(pl.multiple_of(base + (1 - odd) * EDGE, 16), EDGE), :], weight)
         right += dot(source[pl.ds(pl.multiple_of(base + odd * EDGE, 16), AFT[0]), :], weight)
-    level_0[:EDGE] = left
-    level_0[EDGE : EDGE + rows] = projected[...]
-    level_0[EDGE + rows :] = right
-    source = level_0
-    for number, (dilation, target) in enumerate(zip(DILATIONS, (level_1, level_2, level_3))):
+    source = stages[0]
+    source[:EDGE] = left
+    source[EDGE : EDGE + rows] = projected[...]
+    source[EDGE + rows :] = right
+    top = 0
+    for number, dilation in enumerate(DILATIONS):
+        target = stages[number + 1]
+        levels[top : top + source.shape[0], :] = source[...].astype(BF16)
+        top += source.shape[0]
         shift = FORE[number] - FORE[number + 1]
-        count = target.shape[0]
+        count = FORE[number + 1] + rows + AFT[number + 1]
         total = jnp.zeros((count, width), F32)
         for tap in range(4):
             begin = shift + (tap - 2) * dilation
             total += conv_w[number, tap : tap + 1, :] * source[begin : begin + count]
         if FORE[number + 1]:
             total = keep_inside(total, place, FORE[number + 1], rows)
-        target[...] = total
+        target[:count] = total
+        if count < target.shape[0]:
+            target[count:] = jnp.zeros((target.shape[0] - count, width), F32)
         source = target
     gate = gate_pre[...]
-    gated[...] = (level_3[...] * (gate / (1.0 + jnp.exp(-gate)))).astype(BF16)
+    level_3[...] = source[...].astype(BF16)
+    gated[...] = (source[...] * (gate / (1.0 + jnp.exp(-gate)))).astype(BF16)
 
 
 def flip_kernel(place, block, flipped):
@@ -127,13 +156,8 @@
 
 def norm_grad_kernel(channels, place, *refs):
     own, mirrored = refs[:channels], refs[channels : 2 * channels]
-    near, near_core, far_mine, far_other, far_core_mine, far_core_other, out, far, far_core = refs[2 * channels :]
-    me, side = place[1], place[0] % 2
-    half = far_mine.shape[0]
-    for whole, mine, other in ((far, far_mine, far_other), (far_core, far_core_mine, far_core_other)):
-        whole[part(side, half), :] = mine[...]
-        whole[part(1 - side, half), :] = other[...]
-    weights = (near, near_core, far, far_core)
+    *weights, out = refs[2 * channels :]
+    me = place[1]
     rows, width = own[0].shape
     for block, cotangents in enumerate((own, mirrored)):
         for i in range(channels):
@@ -174,12 +198,12 @@
                 grad_gated[at, :] += dot(grad_comb, choose[:width, :], LAST_DOT)
             return carry
 
-        lax.fori_loop(0, rows // tile, step, 0)
+        lax.fori_loop(0, rows // tile, step, 0, unroll=True)
     gate = gate_pre[...]
     sigmoid = 1.0 / (1.0 + jnp.exp(-gate))
     total = grad_gated[...]
     upstream[...] = (total * (gate * sigmoid)).astype(BF16)
-    grad_gate_pre[...] = (total * level_3[...] * sigmoid * (1.0 + gate * (1.0 - sigmoid))).astype(BF16)
+    grad_gate_pre[...] = (total * level_3[...].astype(F32) * sigmoid * (1.0 + gate * (1.0 - sigmoid))).astype(BF16)
     odd, far = place[0] % 2, rows - EDGE
     first[...] = upstream[pl.ds(pl.multiple_of((1 - odd) * far, 16), EDGE), :]
     second[...] = upstream[pl.ds(pl.multiple_of(odd * far, 16), EDGE), :]
@@ -216,9 +240,9 @@
     gate_kept[...] = whole_gate[part(side, half), :]
 
 
-def backward_kernel(channels, place, upstream, first, second, level_0, level_1, level_2, conv_w, *refs):
-    mains = refs[:channels]
-    sent, kept, whole, grad_3, grad_2, grad_1 = refs[channels:]
+def backward_kernel(channels, place, upstream, first, second, conv_w, *refs):
+    mains, (saved, sent, kept, whole, grad_3, grad_2, grad_1, levels) = refs[:channels], refs[channels:]
+    levels[...] = saved[...].astype(F32)
     me, odd = place[1], place[0] % 2
     rows, width = upstream.shape
     fore = BACK_FORE[3]
@@ -230,17 +254,17 @@
     half = whole.shape[0] // 2
     for top in (half - SPARE, 2 * half - SPARE):
         whole[top : top + SPARE, :] = jnp.zeros((SPARE, width), F32)
-    levels = (level_0, level_1, level_2)
     grads = (None, grad_1, grad_2, grad_3)
     grad_0 = None
     for number in (2, 1, 0):
-        dilation, source, level = DILATIONS[number], grads[number + 1], levels[number]
+        dilation, source = DILATIONS[number], grads[number + 1]
+        top = sum(saved_rows(rows, below) for below in range(number))
         fore = BACK_FORE[number + 1]
         here = source[fore : fore + rows]
         for tap in range(4):
-            begin = FORE[number] + (tap - 2) * dilation
+            begin = top + FORE[number] + (tap - 2) * dilation
             row = half - SPARE + 4 * number + tap
-            whole[row : row + 1, :] = jnp.sum(here * level[begin : begin + rows], axis=0, keepdims=True)
+            whole[row : row + 1, :] = jnp.sum(here * levels[begin : begin + rows], axis=0, keepdims=True)
         count = BACK_FORE[number] + rows + BACK_AFT[number]
         total = jnp.zeros((count, width), F32)
         for tap in range(4):
@@ -322,54 +346,48 @@
     block = ((rows, width), BF16)
     place = jnp.stack([lax.axis_index("seq"), lax.axis_index("ch"), lax.axis_size("seq")]).astype(jnp.int32)
 
+    cotangent_x = exchange(cotangent, "ch", cross)
+    mirrored_cotangent = mirror(cotangent)
+    inputs = (tokens.reshape(1, rows), hidden, embedding)
     local_input = run(
-        input_kernel,
-        place,
-        (tokens.reshape(1, rows), hidden, embedding),
-        [block],
-        [pltpu.VMEM((16, width), F32)],
+        input_kernel, place, inputs, [block], [pltpu.VMEM((16, width), F32), *fetch_scratch(inputs)], 60, fetched=3
     )[0]
     input_x = exchange(local_input, "ch", cross)
     input_core = exchange(local_input, "ch", 1)
-    first, second, flipped_cotangent, choose = run(
+    first, second, choose = run(
         setup_kernel,
         place,
-        (local_input, cotangent, channel_order.reshape(1, full)),
-        [((EDGE, width), BF16), ((EDGE, width), BF16), block, ((full, full), BF16)],
-    )
-    near = swap_edges(first, second)
-    far = swap_edges(first, second, cross)
-    flipped_cotangent, *near = together(flipped_cotangent, *near)
-    mirrored_cotangent = mirror(flipped_cotangent)
-    w_half = lax.dynamic_slice_in_dim(w_out, seq_bit(1) * (full // 2), full // 2, 0)
-    w_half, early_cotangent, input_x = together(w_half, cotangent, input_x)
-    w_x_mine = exchange(w_half, "ch", cross)
+        (local_input, channel_order.reshape(1, full)),
+        [((EDGE, width), BF16), ((EDGE, width), BF16), ((full, full), BF16)],
+    )
+    first, second, mirrored_cotangent, cotangent_x = together(first, second, mirrored_cotangent, cotangent_x)
+    edges = jnp.concatenate(swap_edges(first, second) + swap_edges(first, second, cross), axis=0)
+    edges_core = exchange(edges, "ch", 1)
+    early_w_out, input_x = together(w_out, input_x)
+    w_out_x = exchange(early_w_out, "ch", cross)
     mains = [local_input, input_core, input_x, exchange(input_x, "ch", 1)]
-    edges = jnp.concatenate(near + far, axis=0)
-    edges_core = exchange(edges, "ch", 1)
-    cotangent_x = exchange(early_cotangent, "ch", cross)
-    w_x_other = exchange(w_x_mine, "seq", 1)
-    late_cotangent, cotangent_x = together(mirrored_cotangent, cotangent_x)
-    mirrored_cotangent_x = exchange(late_cotangent, "ch", cross)
-
-    projected, gate_pre = run(
+    mirrored_cotangent = run(flip_kernel, place, (mirrored_cotangent,), [block], gflop=1.0)[0]
+    mirrored_cotangent, mains[3] = together(mirrored_cotangent, mains[3])
+    mirrored_cotangent, w_out_x = together(mirrored_cotangent, w_out_x)
+    mirrored_cotangent_x = exchange(mirrored_cotangent, "ch", cross)
+
+    projected, gate_pre, w_in_on = run(
         functools.partial(project_kernel, channels),
         place,
         (*mains, w_in, w_gate),
-        [((rows, width), F32)] * 2,
+        [((rows, width), F32)] * 2 + [(w_in.shape, BF16)],
         gflop=6.0,
     )
-    level_0, level_1, level_2, level_3, gated = run(
+    levels, level_3, gated = run(
         functools.partial(forward_kernel, channels),
         place,
-        (edges, edges_core, w_in, projected, gate_pre, conv_w),
-        [((fore + rows + aft, width), F32) for fore, aft in zip(FORE, AFT)] + [block],
+        (edges, edges_core, w_in_on, projected, gate_pre, conv_w),
+        [((sum(saved_rows(rows, number) for number in range(3)), width), BF16), block, block],
+        [pltpu.VMEM((saved_rows(rows, number), width), F32) for number in range(4)],
         gflop=0.4,
     )
-    mirrored, w_x_other = together(mirror(gated), w_x_other)
-    mirrored = run(flip_kernel, place, (mirrored,), [block], gflop=12.0)[0]
-    late_gated, mirrored_cotangent = together(gated, mirrored_cotangent)
-    gated_x = exchange(late_gated, "ch", cross)
+    mirrored = run(flip_kernel, place, (mirror(gated),), [block], gflop=12.0)[0]
+    gated_x = exchange(gated, "ch", cross)
     mirrored, mirrored_cotangent_x, gated_x = together(mirrored, mirrored_cotangent_x, gated_x)
     mirrored_x = exchange(mirrored, "ch", cross)
     gated_all = [gated, exchange(gated, "ch", 1), gated_x, exchange(gated_x, "ch", 1)]
@@ -388,13 +406,10 @@
             *mirrored_cotangent_all,
             w_out,
             exchange(w_out, "ch", 1),
-            w_x_mine,
-            w_x_other,
-            exchange(w_x_mine, "ch", 1),
-            exchange(w_x_other, "ch", 1),
+            w_out_x,
+            exchange(w_out_x, "ch", 1),
         ),
         [((2 * rows, full), BF16)],
-        [pltpu.VMEM((full, width), BF16)] * 2,
         gflop=6.0,
     )[0]
     mirrored_x, grad_norm = together(mirrored_x, grad_norm)
@@ -429,10 +444,11 @@
     in_sent, in_kept = run(
         functools.partial(backward_kernel, channels),
         place,
-        (upstream, first, second, level_0, level_1, level_2, conv_w, *mains),
+        (upstream, first, second, conv_w, *mains, levels),
         [((half, width), BF16), ((half, width), F32)],
         [pltpu.VMEM((2 * half, width), F32)]
-        + [pltpu.VMEM((BACK_FORE[k] + rows + BACK_AFT[k], width), F32) for k in (3, 2, 1)],
+        + [pltpu.VMEM((BACK_FORE[k] + rows + BACK_AFT[k], width), F32) for k in (3, 2, 1)]
+        + [pltpu.VMEM(levels.shape, F32)],
         gflop=0.5,
     )
     output = run(

time: 155 us -> 147 us (0.948)
  starting transfers between devices: 61.6 us -> 53.4 us
  waiting for transfers between devices: 45.4 us -> 51.4 us
  local copies, waits for them, and re-layouts: 18 us -> 12.9 us
    ppermute x38 -> x36, starting transfers between devices: 49.4 us -> 36 us  [exchange(): return lax.ppermute(block, axis, [(i, i ^ distance) for i in range(count)])]
    ppermute x38 -> x36, waiting for transfers between devices: 42.8 us -> 50.7 us  [exchange(): return lax.ppermute(block, axis, [(i, i ^ distance) for i in range(count)])]
    unnamed x67 -> x65, local copies, waits for them, and re-layouts: 16.4 us -> 12.1 us
    ppermute x6, starting transfers between devices: 7.3 us -> 10.9 us  [swap_edges(): received.append(lax.ppermute(block, ('seq', 'ch'), route))]
    ppermute x6, waiting for transfers between devices: 2.64 us -> 0.66 us  [swap_edges(): received.append(lax.ppermute(block, ('seq', 'ch'), route))]
    ppermute x2, starting transfers between devices: 4.85 us -> 6.45 us  [mirror(): lax.ppermute(block, 'seq', [(i, count - 1 - i) for i in range(count)])]
    pallas_call x10 -> x11, Pallas kernels: 23.1 us -> 23.3 us  [run(): pl.pallas_call(body, out_shape=[jax.ShapeDtypeStruct(shape, dtype) for sh...]
  transfers between devices with their start and end apart: 46 -> 44, of which waited for: 20 -> 20; matrix products, arithmetic and copies ran while one was open for 3% -> 2% of each run, Pallas kernels for 10% -> 12%
where the time goes in v8:
time: 147 us
  starting transfers between devices  53.4 us (36%)
  waiting for transfers between devices  51.4 us (35%)
  Pallas kernels  23.3 us (16%)
  local copies, waits for them, and re-layouts  12.9 us (9%)
  other arithmetic  4.74 us (3%)
    ppermute x36, waiting for transfers between devices, exchange(): return lax.ppermute(block, axis, [(i, i ^ distance) for i in range(count)])  50.7 us
    ppermute x36, starting transfers between devices, exchange(): return lax.ppermute(block, axis, [(i, i ^ distance) for i in range(count)])  36 us
    pallas_call x11, Pallas kernels, run(): pl.pallas_call(body, out_shape=[jax.ShapeDtypeStruct(shape, dtype) for sh...  23.3 us
    unnamed x65, local copies, waits for them, and re-layouts  12.1 us
    ppermute x6, starting transfers between devices, swap_edges(): received.append(lax.ppermute(block, ('seq', 'ch'), route))  10.9 us
    ppermute x2, starting transfers between devices, mirror(): lax.ppermute(block, 'seq', [(i, count - 1 - i) for i in range(count)])  6.45 us
  transfers between devices with their start and end apart: 44, of which 20 were waited for; matrix products, arithmetic and copies ran while one was open for 2% of the time, Pallas kernels for 12%

profile of v8, /device:TPU:0, one launch (start us, length us, event | category | flops | bytes accessed | tf_op | source)
XLA Modules:
  0.0 146.8 jit_solution(7481481322782250802)
XLA Ops:
  0.6 6.1 %collective-permute-start = (bf16[512,256]{1,0:T(8,128)(2,1)}, bf16[512,256]{1,0:T(8,128)(2,1)S(1)}, u32[]{:S(2)}, u32[]{:S(2)}) collective-permute-start(bf16[512,256]{1,0:T(8,128)(2,1)} %cotangent.1), channel_id=1, source_target_pairs={{0,28},{4,24},{8,20},{12,16},{16,12},{20,8},{24,4},{28,0},{1,29},{... | collective-permute-start | bytes 786440 | tf_op jit(solution)/shard_map/ppermute | solution.py:296
  8.8 2.6 %shard_map.137.block_in.refs_0_ = bf16[512,256]{1,0:T(8,128)(2,1)} custom-call(s32[3]{0:T(128)} %pad_add_fusion.place, s32[1,512]{1,0:T(1,128)} %bitcast.7, bf16[512,256]{1,0:T(8,128)(2,1)} %hidden_hbm.1, bf16[4,256]{1,0:T(4,128)(2,1)} %embedding_hbm.1), custom_call_target="tpu_custom_call" | custom-call | flops 100000000 | bytes 266240 | tf_op jit(solution)/shard_map/pallas_call | solution.py:30
  16.9 2.9 %collective-permute-start.4 = (bf16[160,256]{1,0:T(8,128)(2,1)S(1)}, bf16[160,256]{1,0:T(8,128)(2,1)S(1)}, u32[]{:S(2)}, u32[]{:S(2)}) collective-permute-start(bf16[160,256]{1,0:T(8,128)(2,1)S(1)} %get-tuple-element.61), channel_id=1, source_target_pairs={{0,6},{4,2},{1,7},{5,3},{2,4},{6,0},{3,5},{7,1},{8,14},{12,10},{9,... | collective-permute-start | bytes 245768 | tf_op jit(solution)/shard_map/ppermute | solution.py:308
  30.2 9.0 %collective-permute-done.12.refs_10_ = bf16[1024,256]{1,0:T(8,128)(2,1)S(1)} collective-permute-done((bf16[1024,256]{1,0:T(8,128)(2,1)S(1)}, bf16[1024,256]{1,0:T(8,128)(2,1)S(1)}, u32[]{:S(2)}, u32[]{:S(2)}) %collective-permute-start.12) | collective-permute-done | bytes 524320 | tf_op jit(solution)/shard_map/ppermute | solution.py:287
  41.8 3.0 %collective-permute-done.14.refs_2_ = bf16[512,256]{1,0:T(8,128)(2,1)S(1)} collective-permute-done((bf16[512,256]{1,0:T(8,128)(2,1)S(1)}, bf16[512,256]{1,0:T(8,128)(2,1)S(1)}, u32[]{:S(2)}, u32[]{:S(2)}) %collective-permute-start.14) | collective-permute-done | bytes 262176 | tf_op jit(solution)/shard_map/ppermute | solution.py:287
  44.8 5.2 %collective-permute-done.13.refs_6_ = bf16[512,256]{1,0:T(8,128)(2,1)S(1)} collective-permute-done((bf16[512,256]{1,0:T(8,128)(2,1)S(1)}, bf16[512,256]{1,0:T(8,128)(2,1)S(1)}, u32[]{:S(2)}, u32[]{:S(2)}) %collective-permute-start.13) | collective-permute-done | bytes 262176 | tf_op jit(solution)/shard_map/ppermute | solution.py:287
  52.9 2.9 %shard_map.143.refs_8_ = bf16[1024,1024]{1,0:T(8,128)(2,1)S(1)} custom-call(s32[3]{0:T(128)S(1)} %copy-done.22, bf16[512,256]{1,0:T(8,128)(2,1)S(1)} %copy-done.12, bf16[512,256]{1,0:T(8,128)(2,1)S(1)} %collective-permute-done.18.refs_1_, bf16[512,256]{1,0:T(8,128)(2,1)S(1)} %copy-done.27, bf16[512,256]{1,0:T(8,128)(2,1)S(1)} %collective-permute-done.19.refs_3_, ...), custom_call_target="tpu_custom_call" | custom-call | flops 6000000000 | bytes 4194304 | tf_op jit(solution)/shard_map/pallas_call | solution.py:30
  55.9 3.5 %collective-permute-done.17.refs_6_ = bf16[512,256]{1,0:T(8,128)(2,1)S(1)} collective-permute-done((bf16[512,256]{1,0:T(8,128)(2,1)S(1)}, bf16[512,256]{1,0:T(8,128)(2,1)S(1)}, u32[]{:S(2)}, u32[]{:S(2)}) %collective-permute-start.17) | collective-permute-done | bytes 262176 | tf_op jit(solution)/shard_map/ppermute | solution.py:287
  60.9 5.8 %shard_map.144 = (bf16[1024,1024]{1,0:T(8,128)(2,1)S(1)}, bf16[512,256]{1,0:T(8,128)(2,1)S(1)}, bf16[512,256]{1,0:T(8,128)(2,1)S(1)}, bf16[160,256]{1,0:T(8,128)(2,1)S(1)}, bf16[160,256]{1,0:T(8,128)(2,1)S(1)}) custom-call(s32[3]{0:T(128)S(1)} %copy-done.23, bf16[512,256]{1,0:T(8,128)(2,1)S(1)} %get-tuple-element.69.refs_0_, ...), custom_call_target="tpu_custom_call" | custom-call | flops 2500000000 | bytes 7081984 | tf_op jit(solution)/shard_map/pallas_call | solution.py:30
  66.7 5.3 %collective-permute-start.25 = (bf16[160,256]{1,0:T(8,128)(2,1)S(1)}, bf16[160,256]{1,0:T(8,128)(2,1)S(1)}, u32[]{:S(2)}, u32[]{:S(2)}) collective-permute-start(bf16[160,256]{1,0:T(8,128)(2,1)S(1)} %get-tuple-element.87), channel_id=1, source_target_pairs={{0,4},{4,0},{1,5},{5,1},{2,6},{6,2},{3,7},{7,3},{8,12},{12,8},{9,1... | collective-permute-start | bytes 245768 | tf_op jit(solution)/shard_map/ppermute | solution.py:308
  78.2 3.3 %collective-permute-start.28 = (bf16[256,256]{1,0:T(8,128)(2,1)}, bf16[256,256]{1,0:T(8,128)(2,1)}, u32[]{:S(2)}, u32[]{:S(2)}) collective-permute-start(bf16[256,256]{1,0:T(8,128)(2,1)} %get-tuple-element.97), channel_id=1, source_target_pairs={{0,8},{4,12},{8,0},{12,4},{16,24},{20,28},{24,16},{28,20},{1,9},{5... | collective-permute-start | bytes 393224 | tf_op jit(solution)/shard_map/ppermute | solution.py:287
  81.5 2.7 %collective-permute-start.27 = (bf16[512,256]{1,0:T(8,128)(2,1)}, bf16[512,256]{1,0:T(8,128)(2,1)S(1)}, u32[]{:S(2)}, u32[]{:S(2)}) collective-permute-start(bf16[512,256]{1,0:T(8,128)(2,1)} %copy-done.28), channel_id=1, source_target_pairs={{0,4},{4,0},{8,12},{12,8},{16,20},{20,16},{24,28},{28,24},{1,5},{5... | collective-permute-start | bytes 786440 | tf_op jit(solution)/shard_map/ppermute | solution.py:287
  89.8 2.5 %shard_map.147 = (bf16[576,256]{1,0:T(8,128)(2,1)S(1)}, f32[576,256]{1,0:T(8,128)S(1)}) custom-call(s32[3]{0:T(128)S(1)} %copy-done.23, bf16[512,256]{1,0:T(8,128)(2,1)S(1)} %copy-done.16, bf16[160,256]{1,0:T(8,128)(2,1)S(1)} %copy-done.18, bf16[160,256]{1,0:T(8,128)(2,1)S(1)} %copy-done.20, f32[3,4,256]{2,1,0:T(4,128)S(1)} %copy-done.21, ...), custom_call_target="tpu_custom_call" | custom-call | flops 500000000 | bytes 2609152 | tf_op jit(solution)/shard_map/pallas_call | solution.py:30
  94.7 2.0 %collective-permute-start.29 = (bf16[576,256]{1,0:T(8,128)(2,1)S(1)}, bf16[576,256]{1,0:T(8,128)(2,1)S(1)}, u32[]{:S(2)}, u32[]{:S(2)}) collective-permute-start(bf16[576,256]{1,0:T(8,128)(2,1)S(1)} %get-tuple-element.98), channel_id=1, source_target_pairs={{0,4},{4,0},{8,12},{12,8},{16,20},{20,16},{24,28},{28,24},{1,5},{5... | collective-permute-start | bytes 884744 | tf_op jit(solution)/shard_map/ppermute | solution.py:287
  96.7 2.6 %collective-permute-done.31 = bf16[128,256]{1,0:T(8,128)(2,1)S(1)} collective-permute-done((bf16[128,256]{1,0:T(8,128)(2,1)S(1)}, bf16[128,256]{1,0:T(8,128)(2,1)S(1)}, u32[]{:S(2)}, u32[]{:S(2)}) %collective-permute-start.31) | collective-permute-done | bytes 65568 | tf_op jit(solution)/shard_map/ppermute | solution.py:287
  99.3 3.0 %collective-permute-done.29 = bf16[576,256]{1,0:T(8,128)(2,1)S(1)} collective-permute-done((bf16[576,256]{1,0:T(8,128)(2,1)S(1)}, bf16[576,256]{1,0:T(8,128)(2,1)S(1)}, u32[]{:S(2)}, u32[]{:S(2)}) %collective-permute-start.29) | collective-permute-done | bytes 294944 | tf_op jit(solution)/shard_map/ppermute | solution.py:287
  112.0 2.9 %collective-permute-start.36 = (bf16[128,256]{1,0:T(8,128)(2,1)S(1)}, bf16[128,256]{1,0:T(8,128)(2,1)S(1)}, u32[]{:S(2)}, u32[]{:S(2)}) collective-permute-start(bf16[128,256]{1,0:T(8,128)(2,1)S(1)} %convert_add_fusion.6), channel_id=1, source_target_pairs={{0,16},{4,20},{8,24},{12,28},{16,0},{20,4},{24,8},{28,12},{1,17},{... | collective-permute-start | bytes 196616 | tf_op jit(solution)/shard_map/ppermute | solution.py:287
  115.1 2.2 %collective-permute-done.36 = bf16[128,256]{1,0:T(8,128)(2,1)S(1)} collective-permute-done((bf16[128,256]{1,0:T(8,128)(2,1)S(1)}, bf16[128,256]{1,0:T(8,128)(2,1)S(1)}, u32[]{:S(2)}, u32[]{:S(2)}) %collective-permute-start.36) | collective-permute-done | bytes 65568 | tf_op jit(solution)/shard_map/ppermute | solution.py:287
  117.3 4.8 %collective-permute-done.35 = bf16[144,256]{1,0:T(8,128)(2,1)S(1)} collective-permute-done((bf16[144,256]{1,0:T(8,128)(2,1)S(1)}, bf16[144,256]{1,0:T(8,128)(2,1)S(1)}, u32[]{:S(2)}, u32[]{:S(2)}) %collective-permute-start.35) | collective-permute-done | bytes 73760 | tf_op jit(solution)/shard_map/ppermute | solution.py:287
  124.0 2.0 %collective-permute-start.39 = (bf16[256,256]{1,0:T(8,128)(2,1)S(1)}, bf16[256,256]{1,0:T(8,128)(2,1)S(1)}, u32[]{:S(2)}, u32[]{:S(2)}) collective-permute-start(bf16[256,256]{1,0:T(8,128)(2,1)S(1)} %pad_maximum_fusion.8), channel_id=1, source_target_pairs={{0,8},{4,12},{8,0},{12,4},{16,24},{20,28},{24,16},{28,20},{1,9},{5... | collective-permute-start | bytes 393224 | tf_op jit(solution)/shard_map/ppermute | solution.py:287
  127.7 2.0 %collective-permute-done.39 = bf16[256,256]{1,0:T(8,128)(2,1)S(1)} collective-permute-done((bf16[256,256]{1,0:T(8,128)(2,1)S(1)}, bf16[256,256]{1,0:T(8,128)(2,1)S(1)}, u32[]{:S(2)}, u32[]{:S(2)}) %collective-permute-start.39) | collective-permute-done | bytes 131104 | tf_op jit(solution)/shard_map/ppermute | solution.py:287
  130.7 3.3 %collective-permute-start.41 = (bf16[288,256]{1,0:T(8,128)(2,1)S(1)}, bf16[288,256]{1,0:T(8,128)(2,1)S(1)}, u32[]{:S(2)}, u32[]{:S(2)}) collective-permute-start(bf16[288,256]{1,0:T(8,128)(2,1)S(1)} %pad_maximum_fusion.6), channel_id=1, source_target_pairs={{0,8},{4,12},{8,0},{12,4},{16,24},{20,28},{24,16},{28,20},{1,9},{5... | collective-permute-start | bytes 442376 | tf_op jit(solution)/shard_map/ppermute | solution.py:287
  138.1 3.9 %collective-permute-done.43 = bf16[512,256]{1,0:T(8,128)(2,1)S(1)} collective-permute-done((bf16[512,256]{1,0:T(8,128)(2,1)S(1)}, bf16[512,256]{1,0:T(8,128)(2,1)S(1)}, u32[]{:S(2)}, u32[]{:S(2)}) %collective-permute-start.43) | collective-permute-done | bytes 262176 | tf_op jit(solution)/shard_map/ppermute | solution.py:287
  142.9 2.3 %collective-permute-done.42 = bf16[576,256]{1,0:T(8,128)(2,1)S(1)} collective-permute-done((bf16[576,256]{1,0:T(8,128)(2,1)S(1)}, bf16[576,256]{1,0:T(8,128)(2,1)S(1)}, u32[]{:S(2)}, u32[]{:S(2)}) %collective-permute-start.42) | collective-permute-done | bytes 294944 | tf_op jit(solution)/shard_map/ppermute | solution.py:287
  (177 shorter events, 59.7 us)
Async XLA Ops:
  0.6 14.7 %collective-permute-start = (bf16[512,256]{1,0:T(8,128)(2,1)}, bf16[512,256]{1,0:T(8,128)(2,1)S(1)}, u32[]{:S(2)}, u32[]{:S(2)}) collective-permute-start(bf16[512,256]{1,0:T(8,128)(2,1)} %cotangent.1), channel_id=1, source_target_pairs={{0,28},{4,24},{8,20},{12,16},{16,12},{20,8},{24,4},{28,0},{1,29},{... | collective-permute-start | bytes 786440 | tf_op jit(solution)/shard_map/ppermute | solution.py:296
  6.7 9.0 %collective-permute-start.1 = (bf16[512,256]{1,0:T(8,128)(2,1)}, bf16[512,256]{1,0:T(8,128)(2,1)S(1)}, u32[]{:S(2)}, u32[]{:S(2)}) collective-permute-start(bf16[512,256]{1,0:T(8,128)(2,1)} %cotangent.1), channel_id=1, source_target_pairs={{0,2},{1,3},{2,0},{3,1},{4,6},{5,7},{6,4},{7,5},{8,10},{9,11},{10,... | collective-permute-start | bytes 786440 | tf_op jit(solution)/shard_map/ppermute | solution.py:287
  11.5 9.0 %collective-permute-start.8 = (bf16[512,256]{1,0:T(8,128)(2,1)}, bf16[512,256]{1,0:T(8,128)(2,1)S(1)}, u32[]{:S(2)}, u32[]{:S(2)}) collective-permute-start(bf16[512,256]{1,0:T(8,128)(2,1)} %shard_map.137.block_in.refs_0_), channel_id=1, source_target_pairs={{0,2},{1,3},{2,0},{3,1},{4,6},{5,7},{6,4},{7,5},{8,10},{9,11},{10,... | collective-permute-start | bytes 786440 | tf_op jit(solution)/shard_map/ppermute | solution.py:287
  12.1 12.8 %collective-permute-start.7 = (bf16[512,256]{1,0:T(8,128)(2,1)}, bf16[512,256]{1,0:T(8,128)(2,1)S(1)}, u32[]{:S(2)}, u32[]{:S(2)}) collective-permute-start(bf16[512,256]{1,0:T(8,128)(2,1)} %shard_map.137.block_in.refs_0_), channel_id=1, source_target_pairs={{0,1},{1,0},{2,3},{3,2},{4,5},{5,4},{6,7},{7,6},{8,9},{9,8},{10,11... | collective-permute-start | bytes 786440 | tf_op jit(solution)/shard_map/ppermute | solution.py:287
  16.9 7.6 %collective-permute-start.4 = (bf16[160,256]{1,0:T(8,128)(2,1)S(1)}, bf16[160,256]{1,0:T(8,128)(2,1)S(1)}, u32[]{:S(2)}, u32[]{:S(2)}) collective-permute-start(bf16[160,256]{1,0:T(8,128)(2,1)S(1)} %get-tuple-element.61), channel_id=1, source_target_pairs={{0,6},{4,2},{1,7},{5,3},{2,4},{6,0},{3,5},{7,1},{8,14},{12,10},{9,... | collective-permute-start | bytes 245768 | tf_op jit(solution)/shard_map/ppermute | solution.py:308
  22.7 16.5 %collective-permute-start.12 = (bf16[1024,256]{1,0:T(8,128)(2,1)S(1)}, bf16[1024,256]{1,0:T(8,128)(2,1)S(1)}, u32[]{:S(2)}, u32[]{:S(2)}) collective-permute-start(bf16[1024,256]{1,0:T(8,128)(2,1)S(1)} %copy-done.10), channel_id=1, source_target_pairs={{0,2},{1,3},{2,0},{3,1},{4,6},{5,7},{6,4},{7,5},{8,10},{9,11},{10,... | collective-permute-start | bytes 1572872 | tf_op jit(solution)/shard_map/ppermute | solution.py:287
  28.3 12.7 %collective-permute-start.11 = (bf16[512,256]{1,0:T(8,128)(2,1)S(1)}, bf16[512,256]{1,0:T(8,128)(2,1)S(1)}, u32[]{:S(2)}, u32[]{:S(2)}) collective-permute-start(bf16[512,256]{1,0:T(8,128)(2,1)S(1)} %get-tuple-element.69.refs_0_), channel_id=1, source_target_pairs={{0,28},{4,24},{8,20},{12,16},{16,12},{20,8},{24,4},{28,0},{1,29},{... | collective-permute-start | bytes 786440 | tf_op jit(solution)/shard_map/ppermute | solution.py:296
  28.6 22.0 %collective-permute-start.22 = (bf16[1024,256]{1,0:T(8,128)(2,1)S(1)}, bf16[1024,256]{1,0:T(8,128)(2,1)S(1)}, u32[]{:S(2)}, u32[]{:S(2)}) collective-permute-start(bf16[1024,256]{1,0:T(8,128)(2,1)S(1)} %copy-done.10), channel_id=1, source_target_pairs={{0,1},{1,0},{2,3},{3,2},{4,5},{5,4},{6,7},{7,6},{8,9},{9,8},{10,11... | collective-permute-start | bytes 1572872 | tf_op jit(solution)/shard_map/ppermute | solution.py:287
  28.7 21.4 %collective-permute-start.18 = (bf16[512,256]{1,0:T(8,128)(2,1)S(1)}, bf16[512,256]{1,0:T(8,128)(2,1)S(1)}, u32[]{:S(2)}, u32[]{:S(2)}) collective-permute-start(bf16[512,256]{1,0:T(8,128)(2,1)S(1)} %copy-done.12), channel_id=1, source_target_pairs={{0,1},{1,0},{2,3},{3,2},{4,5},{5,4},{6,7},{7,6},{8,9},{9,8},{10,11... | collective-permute-start | bytes 786440 | tf_op jit(solution)/shard_map/ppermute | solution.py:287
  29.2 15.7 %collective-permute-start.14 = (bf16[512,256]{1,0:T(8,128)(2,1)S(1)}, bf16[512,256]{1,0:T(8,128)(2,1)S(1)}, u32[]{:S(2)}, u32[]{:S(2)}) collective-permute-start(bf16[512,256]{1,0:T(8,128)(2,1)S(1)} %get-tuple-element.69.refs_0_), channel_id=1, source_target_pairs={{0,2},{1,3},{2,0},{3,1},{4,6},{5,7},{6,4},{7,5},{8,10},{9,11},{10,... | collective-permute-start | bytes 786440 | tf_op jit(solution)/shard_map/ppermute | solution.py:287
  39.2 10.8 %collective-permute-start.13 = (bf16[512,256]{1,0:T(8,128)(2,1)S(1)}, bf16[512,256]{1,0:T(8,128)(2,1)S(1)}, u32[]{:S(2)}, u32[]{:S(2)}) collective-permute-start(bf16[512,256]{1,0:T(8,128)(2,1)S(1)} %shard_map.139.refs_4_.mirrored_cotangent), channel_id=1, source_target_pairs={{0,2},{1,3},{2,0},{3,1},{4,6},{5,7},{6,4},{7,5},{8,10},{9,11},{10,... | collective-permute-start | bytes 786440 | tf_op jit(solution)/shard_map/ppermute | solution.py:287
  41.0 12.0 %collective-permute-start.23 = (bf16[1024,256]{1,0:T(8,128)(2,1)S(1)}, bf16[1024,256]{1,0:T(8,128)(2,1)S(1)}, u32[]{:S(2)}, u32[]{:S(2)}) collective-permute-start(bf16[1024,256]{1,0:T(8,128)(2,1)S(1)} %collective-permute-done.12.refs_10_), channel_id=1, source_target_pairs={{0,1},{1,0},{2,3},{3,2},{4,5},{5,4},{6,7},{7,6},{8,9},{9,8},{10,11... | collective-permute-start | bytes 1572872 | tf_op jit(solution)/shard_map/ppermute | solution.py:287
  50.6 8.7 %collective-permute-start.10 = (bf16[512,256]{1,0:T(8,128)(2,1)S(1)}, bf16[512,256]{1,0:T(8,128)(2,1)S(1)}, u32[]{:S(2)}, u32[]{:S(2)}) collective-permute-start(bf16[512,256]{1,0:T(8,128)(2,1)S(1)} %get-tuple-element.69.refs_0_), channel_id=1, source_target_pairs={{0,1},{1,0},{2,3},{3,2},{4,5},{5,4},{6,7},{7,6},{8,9},{9,8},{10,11... | collective-permute-start | bytes 786440 | tf_op jit(solution)/shard_map/ppermute | solution.py:287
  50.7 8.7 %collective-permute-start.17 = (bf16[512,256]{1,0:T(8,128)(2,1)S(1)}, bf16[512,256]{1,0:T(8,128)(2,1)S(1)}, u32[]{:S(2)}, u32[]{:S(2)}) collective-permute-start(bf16[512,256]{1,0:T(8,128)(2,1)S(1)} %shard_map.142.refs_4_), channel_id=1, source_target_pairs={{0,2},{1,3},{2,0},{3,1},{4,6},{5,7},{6,4},{7,5},{8,10},{9,11},{10,... | collective-permute-start | bytes 786440 | tf_op jit(solution)/shard_map/ppermute | solution.py:287
  52.4 6.9 %collective-permute-start.16 = (bf16[512,256]{1,0:T(8,128)(2,1)S(1)}, bf16[512,256]{1,0:T(8,128)(2,1)S(1)}, u32[]{:S(2)}, u32[]{:S(2)}) collective-permute-start(bf16[512,256]{1,0:T(8,128)(2,1)S(1)} %shard_map.142.refs_4_), channel_id=1, source_target_pairs={{0,1},{1,0},{2,3},{3,2},{4,5},{5,4},{6,7},{7,6},{8,9},{9,8},{10,11... | collective-permute-start | bytes 786440 | tf_op jit(solution)/shard_map/ppermute | solution.py:287
  52.6 6.8 %collective-permute-start.15 = (bf16[512,256]{1,0:T(8,128)(2,1)S(1)}, bf16[512,256]{1,0:T(8,128)(2,1)S(1)}, u32[]{:S(2)}, u32[]{:S(2)}) collective-permute-start(bf16[512,256]{1,0:T(8,128)(2,1)S(1)} %collective-permute-done.14.refs_2_), channel_id=1, source_target_pairs={{0,1},{1,0},{2,3},{3,2},{4,5},{5,4},{6,7},{7,6},{8,9},{9,8},{10,11... | collective-permute-start | bytes 786440 | tf_op jit(solution)/shard_map/ppermute | solution.py:287
  66.7 10.3 %collective-permute-start.25 = (bf16[160,256]{1,0:T(8,128)(2,1)S(1)}, bf16[160,256]{1,0:T(8,128)(2,1)S(1)}, u32[]{:S(2)}, u32[]{:S(2)}) collective-permute-start(bf16[160,256]{1,0:T(8,128)(2,1)S(1)} %get-tuple-element.87), channel_id=1, source_target_pairs={{0,4},{4,0},{1,5},{5,1},{2,6},{6,2},{3,7},{7,3},{8,12},{12,8},{9,1... | collective-permute-start | bytes 245768 | tf_op jit(solution)/shard_map/ppermute | solution.py:308
  78.2 14.0 %collective-permute-start.28 = (bf16[256,256]{1,0:T(8,128)(2,1)}, bf16[256,256]{1,0:T(8,128)(2,1)}, u32[]{:S(2)}, u32[]{:S(2)}) collective-permute-start(bf16[256,256]{1,0:T(8,128)(2,1)} %get-tuple-element.97), channel_id=1, source_target_pairs={{0,8},{4,12},{8,0},{12,4},{16,24},{20,28},{24,16},{28,20},{1,9},{5... | collective-permute-start | bytes 393224 | tf_op jit(solution)/shard_map/ppermute | solution.py:287
  81.5 11.7 %collective-permute-start.27 = (bf16[512,256]{1,0:T(8,128)(2,1)}, bf16[512,256]{1,0:T(8,128)(2,1)S(1)}, u32[]{:S(2)}, u32[]{:S(2)}) collective-permute-start(bf16[512,256]{1,0:T(8,128)(2,1)} %copy-done.28), channel_id=1, source_target_pairs={{0,4},{4,0},{8,12},{12,8},{16,20},{20,16},{24,28},{28,24},{1,5},{5... | collective-permute-start | bytes 786440 | tf_op jit(solution)/shard_map/ppermute | solution.py:287
  94.7 7.6 %collective-permute-start.29 = (bf16[576,256]{1,0:T(8,128)(2,1)S(1)}, bf16[576,256]{1,0:T(8,128)(2,1)S(1)}, u32[]{:S(2)}, u32[]{:S(2)}) collective-permute-start(bf16[576,256]{1,0:T(8,128)(2,1)S(1)} %get-tuple-element.98), channel_id=1, source_target_pairs={{0,4},{4,0},{8,12},{12,8},{16,20},{20,16},{24,28},{28,24},{1,5},{5... | collective-permute-start | bytes 884744 | tf_op jit(solution)/shard_map/ppermute | solution.py:287
  111.5 10.7 %collective-permute-start.37 = (bf16[256,256]{1,0:T(8,128)(2,1)S(1)}, bf16[256,256]{1,0:T(8,128)(2,1)S(1)}, u32[]{:S(2)}, u32[]{:S(2)}) collective-permute-start(bf16[256,256]{1,0:T(8,128)(2,1)S(1)} %pad_maximum_fusion.7), channel_id=1, source_target_pairs={{0,8},{4,12},{8,0},{12,4},{16,24},{20,28},{24,16},{28,20},{1,9},{5... | collective-permute-start | bytes 393224 | tf_op jit(solution)/shard_map/ppermute | solution.py:287
  115.0 7.2 %collective-permute-start.35 = (bf16[144,256]{1,0:T(8,128)(2,1)S(1)}, bf16[144,256]{1,0:T(8,128)(2,1)S(1)}, u32[]{:S(2)}, u32[]{:S(2)}) collective-permute-start(bf16[144,256]{1,0:T(8,128)(2,1)S(1)} %dynamic-slice_convert_fusion.2), channel_id=1, source_target_pairs={{0,16},{4,20},{8,24},{12,28},{16,0},{20,4},{24,8},{28,12},{1,17},{... | collective-permute-start | bytes 221192 | tf_op jit(solution)/shard_map/ppermute | solution.py:287
  122.3 7.4 %collective-permute-start.40 = (bf16[512,256]{1,0:T(8,128)(2,1)S(1)}, bf16[512,256]{1,0:T(8,128)(2,1)S(1)}, u32[]{:S(2)}, u32[]{:S(2)}) collective-permute-start(bf16[512,256]{1,0:T(8,128)(2,1)S(1)} %pad_maximum_fusion.4), channel_id=1, source_target_pairs={{0,4},{4,0},{8,12},{12,8},{16,20},{20,16},{24,28},{28,24},{1,5},{5... | collective-permute-start | bytes 786440 | tf_op jit(solution)/shard_map/ppermute | solution.py:287
  137.1 8.0 %collective-permute-start.42 = (bf16[576,256]{1,0:T(8,128)(2,1)S(1)}, bf16[576,256]{1,0:T(8,128)(2,1)S(1)}, u32[]{:S(2)}, u32[]{:S(2)}) collective-permute-start(bf16[576,256]{1,0:T(8,128)(2,1)S(1)} %pad_maximum_fusion.3), channel_id=1, source_target_pairs={{0,4},{4,0},{8,12},{12,8},{16,20},{20,16},{24,28},{28,24},{1,5},{5... | collective-permute-start | bytes 884744 | tf_op jit(solution)/shard_map/ppermute | solution.py:287
  (51 other events, 371.6 us)

commit v9 on v8

--- a/solution.py
+++ b/solution.py
@@ -68,7 +68,8 @@
     return (down + across == rows - 1).astype(F32).astype(BF16)
 
 
-def input_kernel(place, tokens_hbm, hidden_hbm, embedding_hbm, block_in, padded, tokens, hidden, embedding, semaphores):
+def input_kernel(place, tokens_hbm, hidden_hbm, embedding_hbm, block_in, first, second, *scratch):
+    padded, tokens, hidden, embedding, semaphores = scratch
     copies = fetch((tokens_hbm, hidden_hbm, embedding_hbm), (tokens, hidden, embedding), semaphores)
     bases, rows = embedding.shape[0], hidden.shape[0]
     padded[...] = jnp.zeros_like(padded)
@@ -79,21 +80,9 @@
     one_hot = (base == tokens[...]).astype(F32).astype(BF16)
     shift = dot(one_hot, padded[...].astype(BF16), ROWS_DOT)
     block_in[...] = (hidden[...].astype(F32) + shift).astype(BF16)
-
-
-def setup_kernel(place, block_in, order, first, second, choose):
-    odd = place[0] % 2
-    far = block_in.shape[0] - EDGE
+    odd, far = place[0] % 2, rows - EDGE
     first[...] = block_in[pl.ds(pl.multiple_of((1 - odd) * far, 16), EDGE), :]
     second[...] = block_in[pl.ds(pl.multiple_of(odd * far, 16), EDGE), :]
-    me, width = place[1], block_in.shape[1]
-    down = lax.broadcasted_iota(jnp.int32, (width, width), 0)
-    for j in range(order.shape[1] // width):
-        for i in range(order.shape[1] // width):
-            wanted = order[:, part(me ^ i, width)]
-            choose[j * width : (j + 1) * width, i * width : (i + 1) * width] = (
-                (down + (me ^ j) * width == wanted).astype(F32).astype(BF16)
-            )
 
 
 def project_kernel(channels, place, *refs):
@@ -156,15 +145,27 @@
 
 def norm_grad_kernel(channels, place, *refs):
     own, mirrored = refs[:channels], refs[channels : 2 * channels]
-    *weights, out = refs[2 * channels :]
+    *weights, order, out, flipped, choose, scratch = refs[2 * channels :]
     me = place[1]
     rows, width = own[0].shape
-    for block, cotangents in enumerate((own, mirrored)):
+    turn = anti_identity(rows)
+    flipped[...] = dot(turn, mirrored[0][...]).astype(BF16)
+    for j in range(1, channels):
+        scratch[j] = dot(turn, mirrored[j][...]).astype(BF16)
+    for block in range(2):
         for i in range(channels):
             total = jnp.zeros((rows, width), F32)
             for j in range(channels):
-                total += dot(cotangents[j][...], weights[j][part(i ^ me, width), :], LAST_DOT)
+                cotangent = own[j][...] if block == 0 else scratch[j] if j else flipped[...]
+                total += dot(cotangent, weights[j][part(i ^ me, width), :], LAST_DOT)
             out[block * rows : (block + 1) * rows, i * width : (i + 1) * width] = total.astype(BF16)
+    down = lax.broadcasted_iota(jnp.int32, (width, width), 0)
+    for j in range(channels):
+        for i in range(channels):
+            wanted = order[:, part(me ^ i, width)]
+            choose[j * width : (j + 1) * width, i * width : (i + 1) * width] = (
+                (down + (me ^ j) * width == wanted).astype(F32).astype(BF16)
+            )
 
 
 def combine_kernel(channels, place, *refs):
@@ -178,16 +179,15 @@
     for j in range(channels):
         gains[:, j * width : (j + 1) * width] = gain[:, part(me ^ j, width)]
     for block, (here, there) in enumerate(((own, mirrored), (mirrored, own))):
-
-        def step(k, carry, block=block, here=here, there=there):
-            at = part(k, tile)
-            mine = jnp.concatenate([ref[at, :].astype(F32) for ref in here], axis=1)
+        for k in range(4):
+            at = slice(k * tile, (k + 1) * tile)
+            mine = jnp.concatenate([ref[at, :] for ref in here], axis=1)
             other = jnp.concatenate([ref[at, :] for ref in there], axis=1)
-            combined = mine + dot(other, choose[...])
+            combined = mine.astype(F32) + dot(other, choose[...])
             mean = jnp.sum(combined * combined, axis=1, keepdims=True) * (1.0 / full)
             inv_scale = lax.rsqrt(mean + EPSILON)
             hat = combined * inv_scale
-            at_both = pl.ds(pl.multiple_of(block * rows + k * tile, tile), tile)
+            at_both = slice(block * rows + k * tile, block * rows + (k + 1) * tile)
             normalized[at_both, :] = (hat * gains[...]).astype(BF16)
             scaled = grad_norm[at_both, :].astype(F32) * gains[...]
             row_total = jnp.sum(scaled * hat, axis=1, keepdims=True) * (1.0 / full)
@@ -196,9 +196,6 @@
             else:
                 grad_comb = (inv_scale * (scaled - hat * row_total)).astype(BF16)
                 grad_gated[at, :] += dot(grad_comb, choose[:width, :], LAST_DOT)
-            return carry
-
-        lax.fori_loop(0, rows // tile, step, 0, unroll=True)
     gate = gate_pre[...]
     sigmoid = 1.0 / (1.0 + jnp.exp(-gate))
     total = grad_gated[...]
@@ -282,6 +279,86 @@
     kept[...] = whole[part(odd, half), :]
 
 
+def split(total, bit):
+    half = total.shape[0] // 2
+    low, high = total[:half], total[half:]
+    first = jnp.broadcast_to(bit, low.shape) == 0
+    return jnp.where(first, high, low), jnp.where(first, low, high)
+
+
+def join(mine, other, bit):
+    first = jnp.broadcast_to(bit, mine.shape) == 0
+    return jnp.where(first, mine, other), jnp.where(first, other, mine)
+
+
+def step_kernel(plan, place, *refs):
+    sources, targets = refs[: 2 * len(plan)], list(refs[2 * len(plan) :])
+    for k, (done, after) in enumerate(plan):
+        mine, other = sources[2 * k][...].astype(F32), sources[2 * k + 1][...].astype(F32)
+        if done[0] == "halve":
+            total = mine + other
+        else:
+            low, high = join(mine, other, (place[0] // done[1]) % 2)
+            if after is not None and after[0] == "take":
+                grad, taps = targets.pop(0), targets.pop(0)
+                count = low.shape[0] - SPARE
+                grad[:count] = low[:count].astype(BF16)
+                grad[count:] = high[:count].astype(BF16)
+                taps[...] = low[count : count + taps.shape[0]]
+                continue
+            total = jnp.concatenate([low, high], axis=0)
+        if after is not None and after[0] == "halve":
+            sent, kept = split(total, (place[0] // after[1]) % 2)
+            targets.pop(0)[...] = sent.astype(BF16)
+            targets.pop(0)[...] = kept
+        else:
+            targets.pop(0)[...] = total.astype(BF16)
+
+
+def advance(place, items, taps):
+    width = items[0][2].shape[1]
+    outs, counts = [], []
+    for done, after, mine, _ in items:
+        rows = mine.shape[0] * (1 if done[0] == "halve" else 2)
+        if after is not None and after[0] == "halve":
+            outs += [((rows // 2, width), BF16), ((rows // 2, width), F32)]
+            counts.append(2)
+        elif after is not None and after[0] == "take":
+            outs += [((rows - 2 * SPARE, width), BF16), ((taps, width), F32)]
+            counts.append(2)
+        else:
+            outs.append(((rows, width), BF16))
+            counts.append(1)
+    arrays = [array for item in items for array in item[2:]]
+    plan = [item[:2] for item in items]
+    if all(shape[0] % 8 == 0 or shape[0] == taps for shape, _ in outs) and all(x.shape[0] % 8 == 0 for x in arrays):
+        results = run(functools.partial(step_kernel, plan), place, arrays, outs)
+    else:
+        results = []
+        for done, after, mine, other in items:
+            mine, other = mine.astype(F32), other.astype(F32)
+            if done[0] == "halve":
+                total = mine + other
+            else:
+                total = jnp.concatenate(join(mine, other, seq_bit(done[1])), axis=0)
+            if after is not None and after[0] == "halve":
+                sent, kept = split(total, seq_bit(after[1]))
+                results += [sent.astype(BF16), kept]
+            elif after is not None and after[0] == "take":
+                half = total.shape[0] // 2
+                results += [
+                    jnp.concatenate([total[: half - SPARE], total[half:-SPARE]], axis=0).astype(BF16),
+                    total[half - SPARE : half - SPARE + taps],
+                ]
+            else:
+                results.append(total.astype(BF16))
+    grouped = []
+    for count in counts:
+        grouped.append(results[:count])
+        results = results[count:]
+    return grouped
+
+
 def exchange(block, axis, distance):
     count = lax.axis_size(axis)
     return lax.ppermute(block, axis, [(i, i ^ distance) for i in range(count)])
@@ -317,25 +394,6 @@
     return (lax.axis_index("seq") & distance) // distance
 
 
-def halve(total, distance):
-    half = total.shape[0] // 2
-    bit = seq_bit(distance)
-    sent = lax.dynamic_slice_in_dim(total, (1 - bit) * half, half, 0).astype(BF16)
-    kept = lax.dynamic_slice_in_dim(total, bit * half, half, 0)
-    return kept.astype(F32) + exchange(sent, "seq", distance).astype(F32)
-
-
-def double(total, distance):
-    return jnp.concatenate(both_halves(total, distance), axis=0)
-
-
-def both_halves(total, distance):
-    total = total.astype(BF16)
-    other = exchange(total, "seq", distance)
-    first = seq_bit(distance) == 0
-    return jnp.where(first, total, other), jnp.where(first, other, total)
-
-
 def local(tokens, hidden, embedding, w_in, w_gate, conv_w, channel_order, gain, w_out, cotangent):
     rows, width = hidden.shape
     full = gain.shape[0]
@@ -349,27 +407,26 @@
     cotangent_x = exchange(cotangent, "ch", cross)
     mirrored_cotangent = mirror(cotangent)
     inputs = (tokens.reshape(1, rows), hidden, embedding)
-    local_input = run(
-        input_kernel, place, inputs, [block], [pltpu.VMEM((16, width), F32), *fetch_scratch(inputs)], 60, fetched=3
-    )[0]
+    local_input, first, second = run(
+        input_kernel,
+        place,
+        inputs,
+        [block, ((EDGE, width), BF16), ((EDGE, width), BF16)],
+        [pltpu.VMEM((16, width), F32), *fetch_scratch(inputs)],
+        megabytes=60,
+        fetched=3,
+    )
     input_x = exchange(local_input, "ch", cross)
     input_core = exchange(local_input, "ch", 1)
-    first, second, choose = run(
-        setup_kernel,
-        place,
-        (local_input, channel_order.reshape(1, full)),
-        [((EDGE, width), BF16), ((EDGE, width), BF16), ((full, full), BF16)],
-    )
-    first, second, mirrored_cotangent, cotangent_x = together(first, second, mirrored_cotangent, cotangent_x)
-    edges = jnp.concatenate(swap_edges(first, second) + swap_edges(first, second, cross), axis=0)
+    first, second, cotangent_x = together(first, second, cotangent_x)
+    near = swap_edges(first, second)
+    first, second, mirrored_cotangent = together(first, second, mirrored_cotangent)
+    edges = jnp.concatenate(near + swap_edges(first, second, cross), axis=0)
     edges_core = exchange(edges, "ch", 1)
-    early_w_out, input_x = together(w_out, input_x)
+    mirrored_cotangent_x = exchange(mirrored_cotangent, "ch", cross)
+    early_w_out, mirrored_cotangent_x = together(w_out, mirrored_cotangent_x)
     w_out_x = exchange(early_w_out, "ch", cross)
     mains = [local_input, input_core, input_x, exchange(input_x, "ch", 1)]
-    mirrored_cotangent = run(flip_kernel, place, (mirrored_cotangent,), [block], gflop=1.0)[0]
-    mirrored_cotangent, mains[3] = together(mirrored_cotangent, mains[3])
-    mirrored_cotangent, w_out_x = together(mirrored_cotangent, w_out_x)
-    mirrored_cotangent_x = exchange(mirrored_cotangent, "ch", cross)
 
     projected, gate_pre, w_in_on = run(
         functools.partial(project_kernel, channels),
@@ -386,9 +443,10 @@
         [pltpu.VMEM((saved_rows(rows, number), width), F32) for number in range(4)],
         gflop=0.4,
     )
-    mirrored = run(flip_kernel, place, (mirror(gated),), [block], gflop=12.0)[0]
+    mirrored, w_out_x = together(mirror(gated), w_out_x)
+    mirrored = run(flip_kernel, place, (mirrored,), [block], gflop=12.0)[0]
     gated_x = exchange(gated, "ch", cross)
-    mirrored, mirrored_cotangent_x, gated_x = together(mirrored, mirrored_cotangent_x, gated_x)
+    mirrored, gated_x = together(mirrored, gated_x)
     mirrored_x = exchange(mirrored, "ch", cross)
     gated_all = [gated, exchange(gated, "ch", 1), gated_x, exchange(gated_x, "ch", 1)]
     cotangent_all = [cotangent, exchange(cotangent, "ch", 1), cotangent_x, exchange(cotangent_x, "ch", 1)]
@@ -398,7 +456,7 @@
         mirrored_cotangent_x,
         exchange(mirrored_cotangent_x, "ch", 1),
     ]
-    grad_norm = run(
+    grad_norm, flipped_cotangent, choose = run(
         functools.partial(norm_grad_kernel, channels),
         place,
         (
@@ -408,10 +466,12 @@
             exchange(w_out, "ch", 1),
             w_out_x,
             exchange(w_out_x, "ch", 1),
+            channel_order.reshape(1, full),
         ),
-        [((2 * rows, full), BF16)],
-        gflop=6.0,
-    )[0]
+        [((2 * rows, full), BF16), block, ((full, full), BF16)],
+        [pltpu.VMEM((channels, rows, width), BF16)],
+        gflop=2.1,
+    )
     mirrored_x, grad_norm = together(mirrored_x, grad_norm)
     mirrored_all = [mirrored, exchange(mirrored, "ch", 1), mirrored_x, exchange(mirrored_x, "ch", 1)]
 
@@ -427,7 +487,7 @@
     out_sent, out_kept, gate_sent, gate_kept = run(
         functools.partial(products_kernel, channels),
         place,
-        (normalized, cotangent, mirrored_cotangent, grad_gate_pre, *mains),
+        (normalized, cotangent, flipped_cotangent, grad_gate_pre, *mains),
         [
             ((full // 4, width), BF16),
             ((full // 4, width), F32),
@@ -459,28 +519,29 @@
         gflop=0.3,
     )[0]
 
-    sum_out = out_kept + out_other.astype(F32)
-    sum_gate = gate_kept + gate_other.astype(F32)
-    in_sent, sum_gate, sum_out = together(in_sent, sum_gate, sum_out)
-    sum_in = in_kept + exchange(in_sent, "seq", steps[0]).astype(F32)
-    undo = [(double, distance) for distance in steps[::-1]]
-    rest_gate = [(halve, distance) for distance in steps[1:]] + undo
-    rest_out = [(halve, distance) for distance in steps[2:]] + undo
-    rest_in = [(halve, distance) for distance in steps[1:]] + undo[:-1]
-    for number in range(len(rest_in) + 1):
-        if number:
-            sum_in, sum_gate, sum_out = together(sum_in, sum_gate, sum_out)
-            move, distance = rest_in[number - 1]
-            sum_in = move(sum_in, distance)
-        if number < len(rest_gate):
-            move, distance = rest_gate[number]
-            sum_gate = move(sum_gate, distance)
-        if number < len(rest_out):
-            move, distance = rest_out[number]
-            sum_out = move(sum_out, distance)
-    low, high = both_halves(sum_in, steps[0])
-    grad_in = jnp.concatenate([low[: full // 2], high[: full // 2]], axis=0)
-    grad_conv = low[full // 2 : full // 2 + taps].astype(F32).reshape(conv_w.shape)
+    down = [("halve", distance) for distance in steps]
+    up = [("double", distance) for distance in steps[::-1]]
+    routes = [down + up + [("take",)], down + up + [None], down[1:] + up + [None]]
+    state = [None, (gate_kept, gate_other), (out_kept, out_other)]
+    results = [None, None, None]
+    for turn in range(len(routes[0]) - 1):
+        live = [k for k in range(3) if state[k] is not None]
+        places = [turn - 1 if k == 0 else turn for k in live]
+        items = [(routes[k][at], routes[k][at + 1], *state[k]) for k, at in zip(live, places)]
+        prepared = dict(zip(live, advance(place, items, taps)))
+        if turn == 0:
+            prepared[0] = (in_sent, in_kept)
+        for k, at in zip([0] * (turn == 0) + live, [-1] * (turn == 0) + places):
+            upcoming = routes[k][at + 1]
+            if upcoming is None:
+                results[k], state[k] = prepared[k][0], None
+            else:
+                sent, kept = prepared[k] if len(prepared[k]) == 2 else prepared[k] * 2
+                state[k] = (kept, exchange(sent, "seq", upcoming[1]))
+    last = len(routes[0]) - 2
+    (grad_in, grad_conv), = advance(place, [(routes[0][last], routes[0][last + 1], *state[0])], taps)
+    sum_gate, sum_out = results[1:]
+    grad_conv = grad_conv.reshape(conv_w.shape)
     return output, grad_in, sum_gate, sum_out, grad_conv
 
 

time: 147 us -> 148 us (level)
  local copies, waits for them, and re-layouts: 12.9 us -> 4.35 us
  waiting for transfers between devices: 51.4 us -> 59.5 us
  Pallas kernels: 23.3 us -> 29 us
  other arithmetic: 4.74 us -> 0.59 us
    unnamed x65 -> x23, local copies, waits for them, and re-layouts: 12.1 us -> 3.74 us
    ppermute x2, waiting for transfers between devices: 0.01 us -> 7.64 us  [mirror(): lax.ppermute(block, 'seq', [(i, count - 1 - i) for i in range(count)])]
    pallas_call x11 -> x16, Pallas kernels: 23.3 us -> 29 us  [run(): pl.pallas_call(body, out_shape=[jax.ShapeDtypeStruct(shape, dtype) for sh...]
    concatenate x9 -> x0, other arithmetic: 2.58 us -> none  [the longest x8 1.75 us: double(): return jnp.concatenate(both_halves(total, distance), axis=0)]
    ppermute x36, starting transfers between devices: 36 us -> 34.3 us  [exchange(): return lax.ppermute(block, axis, [(i, i ^ distance) for i in range(count)])]
    ppermute x6, waiting for transfers between devices: 0.66 us -> 2.25 us  [swap_edges(): received.append(lax.ppermute(block, ('seq', 'ch'), route))]
  transfers between devices with their start and end apart: 44 -> 44, of which waited for: 20 -> 19; matrix products, arithmetic and copies ran while one was open for 2% -> 0% of each run, Pallas kernels for 12% -> 11%
where the time goes in v9:
time: 148 us; the launch traced here: 147 us
  waiting for transfers between devices  59.5 us (40%)
  starting transfers between devices  53 us (36%)
  Pallas kernels  29 us (20%)
  local copies, waits for them, and re-layouts  4.35 us (3%)
    ppermute x36, waiting for transfers between devices, exchange(): return lax.ppermute(block, axis, [(i, i ^ distance) for i in range(count)])  49.6 us
    ppermute x36, starting transfers between devices, exchange(): return lax.ppermute(block, axis, [(i, i ^ distance) for i in range(count)])  34.3 us
    pallas_call x16, Pallas kernels, run(): pl.pallas_call(body, out_shape=[jax.ShapeDtypeStruct(shape, dtype) for sh...  29 us
    ppermute x6, starting transfers between devices, swap_edges(): received.append(lax.ppermute(block, ('seq', 'ch'), route))  11 us
    ppermute x2, starting transfers between devices, mirror(): lax.ppermute(block, 'seq', [(i, count - 1 - i) for i in range(count)])  7.69 us
    ppermute x2, waiting for transfers between devices, mirror(): lax.ppermute(block, 'seq', [(i, count - 1 - i) for i in range(count)])  7.64 us
    unnamed x23, local copies, waits for them, and re-layouts  3.74 us
  transfers between devices with their start and end apart: 44, of which 19 were waited for; matrix products, arithmetic and copies ran while one was open for 0% of the time, Pallas kernels for 11%

profile of v9, /device:TPU:0, one launch (start us, length us, event | category | flops | bytes accessed | tf_op | source)
XLA Modules:
  0.0 147.3 jit_solution(15657397568534786143)
XLA Ops:
  0.6 3.0 %collective-permute-start = (bf16[512,256]{1,0:T(8,128)(2,1)}, bf16[512,256]{1,0:T(8,128)(2,1)S(1)}, u32[]{:S(2)}, u32[]{:S(2)}) collective-permute-start(bf16[512,256]{1,0:T(8,128)(2,1)} %cotangent.1), channel_id=1, source_target_pairs={{0,2},{1,3},{2,0},{3,1},{4,6},{5,7},{6,4},{7,5},{8,10},{9,11},{10,... | collective-permute-start | bytes 786440 | tf_op jit(solution)/shard_map/ppermute | solution.py:364
  3.6 4.6 %collective-permute-start.3 = (bf16[512,256]{1,0:T(8,128)(2,1)}, bf16[512,256]{1,0:T(8,128)(2,1)S(1)}, u32[]{:S(2)}, u32[]{:S(2)}) collective-permute-start(bf16[512,256]{1,0:T(8,128)(2,1)} %cotangent.1), channel_id=1, source_target_pairs={{0,28},{4,24},{8,20},{12,16},{16,12},{20,8},{24,4},{28,0},{1,29},{... | collective-permute-start | bytes 786440 | tf_op jit(solution)/shard_map/ppermute | solution.py:373
  8.8 2.7 %shard_map.137 = (bf16[512,256]{1,0:T(8,128)(2,1)}, bf16[160,256]{1,0:T(8,128)(2,1)}, bf16[160,256]{1,0:T(8,128)(2,1)}) custom-call(s32[3]{0:T(128)} %pad_add_fusion.place, s32[1,512]{1,0:T(1,128)} %bitcast.7, bf16[512,256]{1,0:T(8,128)(2,1)} %hidden_hbm.1, bf16[4,256]{1,0:T(4,128)(2,1)} %embedding_hbm.1), custom_call_target="tpu_custom_call" | custom-call | flops 100000000 | bytes 266240 | tf_op jit(solution)/shard_map/pallas_call | solution.py:30
  14.6 3.9 %collective-permute-start.4 = (bf16[160,256]{1,0:T(8,128)(2,1)}, bf16[160,256]{1,0:T(8,128)(2,1)S(1)}, u32[]{:S(2)}, u32[]{:S(2)}) collective-permute-start(bf16[160,256]{1,0:T(8,128)(2,1)} %get-tuple-element.73), channel_id=1, source_target_pairs={{0,6},{4,2},{1,7},{5,3},{2,4},{6,0},{3,5},{7,1},{8,14},{12,10},{9,... | collective-permute-start | bytes 245768 | tf_op jit(solution)/shard_map/ppermute | solution.py:385
  21.8 7.5 %collective-permute-done.12.refs_6_ = bf16[512,256]{1,0:T(8,128)(2,1)S(1)} collective-permute-done((bf16[512,256]{1,0:T(8,128)(2,1)S(1)}, bf16[512,256]{1,0:T(8,128)(2,1)S(1)}, u32[]{:S(2)}, u32[]{:S(2)}) %collective-permute-start.12) | collective-permute-done | bytes 262176 | tf_op jit(solution)/shard_map/ppermute | solution.py:364
  37.7 3.1 %collective-permute-start.11 = (bf16[512,256]{1,0:T(8,128)(2,1)S(1)}, bf16[512,256]{1,0:T(8,128)(2,1)S(1)}, u32[]{:S(2)}, u32[]{:S(2)}) collective-permute-start(bf16[512,256]{1,0:T(8,128)(2,1)S(1)} %get-tuple-element.79.refs_0_), channel_id=1, source_target_pairs={{0,28},{4,24},{8,20},{12,16},{16,12},{20,8},{24,4},{28,0},{1,29},{... | collective-permute-start | bytes 786440 | tf_op jit(solution)/shard_map/ppermute | solution.py:373
  41.7 6.3 %collective-permute-done.11.block = bf16[512,256]{1,0:T(8,128)(2,1)S(1)} collective-permute-done((bf16[512,256]{1,0:T(8,128)(2,1)S(1)}, bf16[512,256]{1,0:T(8,128)(2,1)S(1)}, u32[]{:S(2)}, u32[]{:S(2)}) %collective-permute-start.11) | collective-permute-done | bytes 262176 | tf_op jit(solution)/shard_map/ppermute | solution.py:373
  51.8 3.7 %shard_map.141 = (bf16[1024,1024]{1,0:T(8,128)(2,1)S(1)}, bf16[512,256]{1,0:T(8,128)(2,1)S(1)}, bf16[1024,1024]{1,0:T(8,128)(2,1)S(1)}) custom-call(s32[3]{0:T(128)S(1)} %copy-done.4, bf16[512,256]{1,0:T(8,128)(2,1)S(1)} %copy-done.3, bf16[512,256]{1,0:T(8,128)(2,1)S(1)} %collective-permute-done.18.refs_1_, ...), custom_call_target="tpu_custom_call" | custom-call | flops 2100000000 | bytes 4198400 | tf_op jit(solution)/shard_map/pallas_call | solution.py:30
  55.5 3.7 %collective-permute-done.17.refs_6_ = bf16[512,256]{1,0:T(8,128)(2,1)S(1)} collective-permute-done((bf16[512,256]{1,0:T(8,128)(2,1)S(1)}, bf16[512,256]{1,0:T(8,128)(2,1)S(1)}, u32[]{:S(2)}, u32[]{:S(2)}) %collective-permute-start.17) | collective-permute-done | bytes 262176 | tf_op jit(solution)/shard_map/ppermute | solution.py:364
  60.8 5.8 %shard_map.142 = (bf16[1024,1024]{1,0:T(8,128)(2,1)S(1)}, bf16[512,256]{1,0:T(8,128)(2,1)S(1)}, bf16[512,256]{1,0:T(8,128)(2,1)S(1)}, bf16[160,256]{1,0:T(8,128)(2,1)S(1)}, bf16[160,256]{1,0:T(8,128)(2,1)S(1)}) custom-call(s32[3]{0:T(128)S(1)} %copy-done.4, bf16[512,256]{1,0:T(8,128)(2,1)S(1)} %get-tuple-element.79.refs_0_, ...), custom_call_target="tpu_custom_call" | custom-call | flops 2500000000 | bytes 7081984 | tf_op jit(solution)/shard_map/pallas_call | solution.py:30
  66.6 4.5 %collective-permute-start.25 = (bf16[160,256]{1,0:T(8,128)(2,1)S(1)}, bf16[160,256]{1,0:T(8,128)(2,1)S(1)}, u32[]{:S(2)}, u32[]{:S(2)}) collective-permute-start(bf16[160,256]{1,0:T(8,128)(2,1)S(1)} %get-tuple-element.99), channel_id=1, source_target_pairs={{0,4},{4,0},{1,5},{5,1},{2,6},{6,2},{3,7},{7,3},{8,12},{12,8},{9,1... | collective-permute-start | bytes 245768 | tf_op jit(solution)/shard_map/ppermute | solution.py:385
  73.8 4.5 %collective-permute-start.28 = (bf16[512,256]{1,0:T(8,128)(2,1)S(1)}, bf16[512,256]{1,0:T(8,128)(2,1)S(1)}, u32[]{:S(2)}, u32[]{:S(2)}) collective-permute-start(bf16[512,256]{1,0:T(8,128)(2,1)S(1)} %get-tuple-element.107), channel_id=1, source_target_pairs={{0,4},{4,0},{8,12},{12,8},{16,20},{20,16},{24,28},{28,24},{1,5},{5... | collective-permute-start | bytes 786440 | tf_op jit(solution)/shard_map/ppermute | solution.py:364
  80.9 2.9 %collective-permute-start.29 = (bf16[256,256]{1,0:T(8,128)(2,1)S(1)}, bf16[256,256]{1,0:T(8,128)(2,1)S(1)}, u32[]{:S(2)}, u32[]{:S(2)}) collective-permute-start(bf16[256,256]{1,0:T(8,128)(2,1)S(1)} %get-tuple-element.109), channel_id=1, source_target_pairs={{0,8},{4,12},{8,0},{12,4},{16,24},{20,28},{24,16},{28,20},{1,9},{5... | collective-permute-start | bytes 393224 | tf_op jit(solution)/shard_map/ppermute | solution.py:364
  83.8 2.9 %collective-permute-done.29.refs_3_ = bf16[256,256]{1,0:T(8,128)(2,1)S(1)} collective-permute-done((bf16[256,256]{1,0:T(8,128)(2,1)S(1)}, bf16[256,256]{1,0:T(8,128)(2,1)S(1)}, u32[]{:S(2)}, u32[]{:S(2)}) %collective-permute-start.29) | collective-permute-done | bytes 131104 | tf_op jit(solution)/shard_map/ppermute | solution.py:364
  91.7 3.0 %collective-permute-done.31.refs_5_ = bf16[128,256]{1,0:T(8,128)(2,1)S(1)} collective-permute-done((bf16[128,256]{1,0:T(8,128)(2,1)S(1)}, bf16[128,256]{1,0:T(8,128)(2,1)S(1)}, u32[]{:S(2)}, u32[]{:S(2)}) %collective-permute-start.31) | collective-permute-done | bytes 65568 | tf_op jit(solution)/shard_map/ppermute | solution.py:364
  95.3 3.0 %collective-permute-start.32 = (bf16[288,256]{1,0:T(8,128)(2,1)S(1)}, bf16[288,256]{1,0:T(8,128)(2,1)S(1)}, u32[]{:S(2)}, u32[]{:S(2)}) collective-permute-start(bf16[288,256]{1,0:T(8,128)(2,1)S(1)} %get-tuple-element.115), channel_id=1, source_target_pairs={{0,8},{4,12},{8,0},{12,4},{16,24},{20,28},{24,16},{28,20},{1,9},{5... | collective-permute-start | bytes 442376 | tf_op jit(solution)/shard_map/ppermute | solution.py:364
  101.2 2.5 %collective-permute-done.33.refs_3_ = bf16[128,256]{1,0:T(8,128)(2,1)S(1)} collective-permute-done((bf16[128,256]{1,0:T(8,128)(2,1)S(1)}, bf16[128,256]{1,0:T(8,128)(2,1)S(1)}, u32[]{:S(2)}, u32[]{:S(2)}) %collective-permute-start.33) | collective-permute-done | bytes 65568 | tf_op jit(solution)/shard_map/ppermute | solution.py:364
  103.7 3.6 %collective-permute-done.34.refs_5_ = bf16[128,256]{1,0:T(8,128)(2,1)S(1)} collective-permute-done((bf16[128,256]{1,0:T(8,128)(2,1)S(1)}, bf16[128,256]{1,0:T(8,128)(2,1)S(1)}, u32[]{:S(2)}, u32[]{:S(2)}) %collective-permute-start.34) | collective-permute-done | bytes 65568 | tf_op jit(solution)/shard_map/ppermute | solution.py:364
  111.1 6.1 %collective-permute-done.36.refs_3_ = bf16[128,256]{1,0:T(8,128)(2,1)S(1)} collective-permute-done((bf16[128,256]{1,0:T(8,128)(2,1)S(1)}, bf16[128,256]{1,0:T(8,128)(2,1)S(1)}, u32[]{:S(2)}, u32[]{:S(2)}) %collective-permute-start.36) | collective-permute-done | bytes 65568 | tf_op jit(solution)/shard_map/ppermute | solution.py:364
  119.3 2.6 %collective-permute-start.38 = (bf16[144,256]{1,0:T(8,128)(2,1)S(1)}, bf16[144,256]{1,0:T(8,128)(2,1)S(1)}, u32[]{:S(2)}, u32[]{:S(2)}) collective-permute-start(bf16[144,256]{1,0:T(8,128)(2,1)S(1)} %get-tuple-element.123.refs_0_), channel_id=1, source_target_pairs={{0,16},{4,20},{8,24},{12,28},{16,0},{20,4},{24,8},{28,12},{1,17},{... | collective-permute-start | bytes 221192 | tf_op jit(solution)/shard_map/ppermute | solution.py:364
  121.9 2.8 %collective-permute-done.38.refs_1_ = bf16[144,256]{1,0:T(8,128)(2,1)S(1)} collective-permute-done((bf16[144,256]{1,0:T(8,128)(2,1)S(1)}, bf16[144,256]{1,0:T(8,128)(2,1)S(1)}, u32[]{:S(2)}, u32[]{:S(2)}) %collective-permute-start.38) | collective-permute-done | bytes 73760 | tf_op jit(solution)/shard_map/ppermute | solution.py:364
  129.3 5.1 %collective-permute-done.41.refs_1_ = bf16[288,256]{1,0:T(8,128)(2,1)S(1)} collective-permute-done((bf16[288,256]{1,0:T(8,128)(2,1)S(1)}, bf16[288,256]{1,0:T(8,128)(2,1)S(1)}, u32[]{:S(2)}, u32[]{:S(2)}) %collective-permute-start.41) | collective-permute-done | bytes 147488 | tf_op jit(solution)/shard_map/ppermute | solution.py:364
  134.5 2.6 %collective-permute-done.42.refs_3_ = bf16[512,256]{1,0:T(8,128)(2,1)S(1)} collective-permute-done((bf16[512,256]{1,0:T(8,128)(2,1)S(1)}, bf16[512,256]{1,0:T(8,128)(2,1)S(1)}, u32[]{:S(2)}, u32[]{:S(2)}) %collective-permute-start.42) | collective-permute-done | bytes 262176 | tf_op jit(solution)/shard_map/ppermute | solution.py:364
  140.5 4.7 %collective-permute-done.43.refs_1_ = bf16[576,256]{1,0:T(8,128)(2,1)S(1)} collective-permute-done((bf16[576,256]{1,0:T(8,128)(2,1)S(1)}, bf16[576,256]{1,0:T(8,128)(2,1)S(1)}, u32[]{:S(2)}, u32[]{:S(2)}) %collective-permute-start.43) | collective-permute-done | bytes 294944 | tf_op jit(solution)/shard_map/ppermute | solution.py:364
  (106 shorter events, 51.3 us)
Async XLA Ops:
  0.6 11.5 %collective-permute-start = (bf16[512,256]{1,0:T(8,128)(2,1)}, bf16[512,256]{1,0:T(8,128)(2,1)S(1)}, u32[]{:S(2)}, u32[]{:S(2)}) collective-permute-start(bf16[512,256]{1,0:T(8,128)(2,1)} %cotangent.1), channel_id=1, source_target_pairs={{0,2},{1,3},{2,0},{3,1},{4,6},{5,7},{6,4},{7,5},{8,10},{9,11},{10,... | collective-permute-start | bytes 786440 | tf_op jit(solution)/shard_map/ppermute | solution.py:364
  3.6 11.0 %collective-permute-start.3 = (bf16[512,256]{1,0:T(8,128)(2,1)}, bf16[512,256]{1,0:T(8,128)(2,1)S(1)}, u32[]{:S(2)}, u32[]{:S(2)}) collective-permute-start(bf16[512,256]{1,0:T(8,128)(2,1)} %cotangent.1), channel_id=1, source_target_pairs={{0,28},{4,24},{8,20},{12,16},{16,12},{20,8},{24,4},{28,0},{1,29},{... | collective-permute-start | bytes 786440 | tf_op jit(solution)/shard_map/ppermute | solution.py:373
  11.5 7.8 %collective-permute-start.8 = (bf16[512,256]{1,0:T(8,128)(2,1)}, bf16[512,256]{1,0:T(8,128)(2,1)S(1)}, u32[]{:S(2)}, u32[]{:S(2)}) collective-permute-start(bf16[512,256]{1,0:T(8,128)(2,1)} %get-tuple-element.75.refs_0_.block_in), channel_id=1, source_target_pairs={{0,2},{1,3},{2,0},{3,1},{4,6},{5,7},{6,4},{7,5},{8,10},{9,11},{10,... | collective-permute-start | bytes 786440 | tf_op jit(solution)/shard_map/ppermute | solution.py:364
  12.6 18.2 %collective-permute-start.7 = (bf16[512,256]{1,0:T(8,128)(2,1)}, bf16[512,256]{1,0:T(8,128)(2,1)S(1)}, u32[]{:S(2)}, u32[]{:S(2)}) collective-permute-start(bf16[512,256]{1,0:T(8,128)(2,1)} %get-tuple-element.75.refs_0_.block_in), channel_id=1, source_target_pairs={{0,1},{1,0},{2,3},{3,2},{4,5},{5,4},{6,7},{7,6},{8,9},{9,8},{10,11... | collective-permute-start | bytes 786440 | tf_op jit(solution)/shard_map/ppermute | solution.py:364
  19.3 10.0 %collective-permute-start.12 = (bf16[512,256]{1,0:T(8,128)(2,1)S(1)}, bf16[512,256]{1,0:T(8,128)(2,1)S(1)}, u32[]{:S(2)}, u32[]{:S(2)}) collective-permute-start(bf16[512,256]{1,0:T(8,128)(2,1)S(1)} %collective-permute-done.3.refs_4_), channel_id=1, source_target_pairs={{0,2},{1,3},{2,0},{3,1},{4,6},{5,7},{6,4},{7,5},{8,10},{9,11},{10,... | collective-permute-start | bytes 786440 | tf_op jit(solution)/shard_map/ppermute | solution.py:364
  19.8 11.0 %collective-permute-start.9 = (bf16[512,256]{1,0:T(8,128)(2,1)S(1)}, bf16[512,256]{1,0:T(8,128)(2,1)S(1)}, u32[]{:S(2)}, u32[]{:S(2)}) collective-permute-start(bf16[512,256]{1,0:T(8,128)(2,1)S(1)} %collective-permute-done.8.refs_2_), channel_id=1, source_target_pairs={{0,1},{1,0},{2,3},{3,2},{4,5},{5,4},{6,7},{7,6},{8,9},{9,8},{10,11... | collective-permute-start | bytes 786440 | tf_op jit(solution)/shard_map/ppermute | solution.py:364
  21.7 14.0 %collective-permute-start.6 = (bf16[640,256]{1,0:T(8,128)(2,1)S(1)}, bf16[640,256]{1,0:T(8,128)(2,1)S(1)}, u32[]{:S(2)}, u32[]{:S(2)}) collective-permute-start(bf16[640,256]{1,0:T(8,128)(2,1)S(1)} %constant_dynamic-update-slice_fusion.edges), channel_id=1, source_target_pairs={{0,1},{1,0},{2,3},{3,2},{4,5},{5,4},{6,7},{7,6},{8,9},{9,8},{10,11... | collective-permute-start | bytes 983048 | tf_op jit(solution)/shard_map/ppermute | solution.py:364
  29.3 18.7 %collective-permute-start.13 = (bf16[1024,256]{1,0:T(8,128)(2,1)}, bf16[1024,256]{1,0:T(8,128)(2,1)S(1)}, u32[]{:S(2)}, u32[]{:S(2)}) collective-permute-start(bf16[1024,256]{1,0:T(8,128)(2,1)} %w_out.1), channel_id=1, source_target_pairs={{0,2},{1,3},{2,0},{3,1},{4,6},{5,7},{6,4},{7,5},{8,10},{9,11},{10,... | collective-permute-start | bytes 1572872 | tf_op jit(solution)/shard_map/ppermute | solution.py:364
  37.7 10.2 %collective-permute-start.11 = (bf16[512,256]{1,0:T(8,128)(2,1)S(1)}, bf16[512,256]{1,0:T(8,128)(2,1)S(1)}, u32[]{:S(2)}, u32[]{:S(2)}) collective-permute-start(bf16[512,256]{1,0:T(8,128)(2,1)S(1)} %get-tuple-element.79.refs_0_), channel_id=1, source_target_pairs={{0,28},{4,24},{8,20},{12,16},{16,12},{20,8},{24,4},{28,0},{1,29},{... | collective-permute-start | bytes 786440 | tf_op jit(solution)/shard_map/ppermute | solution.py:373
  40.9 8.7 %collective-permute-start.14 = (bf16[512,256]{1,0:T(8,128)(2,1)S(1)}, bf16[512,256]{1,0:T(8,128)(2,1)S(1)}, u32[]{:S(2)}, u32[]{:S(2)}) collective-permute-start(bf16[512,256]{1,0:T(8,128)(2,1)S(1)} %get-tuple-element.79.refs_0_), channel_id=1, source_target_pairs={{0,2},{1,3},{2,0},{3,1},{4,6},{5,7},{6,4},{7,5},{8,10},{9,11},{10,... | collective-permute-start | bytes 786440 | tf_op jit(solution)/shard_map/ppermute | solution.py:364
  41.4 9.9 %collective-permute-start.22 = (bf16[1024,256]{1,0:T(8,128)(2,1)S(1)}, bf16[1024,256]{1,0:T(8,128)(2,1)S(1)}, u32[]{:S(2)}, u32[]{:S(2)}) collective-permute-start(bf16[1024,256]{1,0:T(8,128)(2,1)S(1)} %copy-done.2), channel_id=1, source_target_pairs={{0,1},{1,0},{2,3},{3,2},{4,5},{5,4},{6,7},{7,6},{8,9},{9,8},{10,11... | collective-permute-start | bytes 1572872 | tf_op jit(solution)/shard_map/ppermute | solution.py:364
  50.4 8.8 %collective-permute-start.17 = (bf16[512,256]{1,0:T(8,128)(2,1)S(1)}, bf16[512,256]{1,0:T(8,128)(2,1)S(1)}, u32[]{:S(2)}, u32[]{:S(2)}) collective-permute-start(bf16[512,256]{1,0:T(8,128)(2,1)S(1)} %shard_map.140.refs_4_), channel_id=1, source_target_pairs={{0,2},{1,3},{2,0},{3,1},{4,6},{5,7},{6,4},{7,5},{8,10},{9,11},{10,... | collective-permute-start | bytes 786440 | tf_op jit(solution)/shard_map/ppermute | solution.py:364
  51.1 8.2 %collective-permute-start.10 = (bf16[512,256]{1,0:T(8,128)(2,1)S(1)}, bf16[512,256]{1,0:T(8,128)(2,1)S(1)}, u32[]{:S(2)}, u32[]{:S(2)}) collective-permute-start(bf16[512,256]{1,0:T(8,128)(2,1)S(1)} %get-tuple-element.79.refs_0_), channel_id=1, source_target_pairs={{0,1},{1,0},{2,3},{3,2},{4,5},{5,4},{6,7},{7,6},{8,9},{9,8},{10,11... | collective-permute-start | bytes 786440 | tf_op jit(solution)/shard_map/ppermute | solution.py:364
  51.3 7.9 %collective-permute-start.16 = (bf16[512,256]{1,0:T(8,128)(2,1)S(1)}, bf16[512,256]{1,0:T(8,128)(2,1)S(1)}, u32[]{:S(2)}, u32[]{:S(2)}) collective-permute-start(bf16[512,256]{1,0:T(8,128)(2,1)S(1)} %shard_map.140.refs_4_), channel_id=1, source_target_pairs={{0,1},{1,0},{2,3},{3,2},{4,5},{5,4},{6,7},{7,6},{8,9},{9,8},{10,11... | collective-permute-start | bytes 786440 | tf_op jit(solution)/shard_map/ppermute | solution.py:364
  51.6 7.6 %collective-permute-start.15 = (bf16[512,256]{1,0:T(8,128)(2,1)S(1)}, bf16[512,256]{1,0:T(8,128)(2,1)S(1)}, u32[]{:S(2)}, u32[]{:S(2)}) collective-permute-start(bf16[512,256]{1,0:T(8,128)(2,1)S(1)} %collective-permute-done.14.refs_2_), channel_id=1, source_target_pairs={{0,1},{1,0},{2,3},{3,2},{4,5},{5,4},{6,7},{7,6},{8,9},{9,8},{10,11... | collective-permute-start | bytes 786440 | tf_op jit(solution)/shard_map/ppermute | solution.py:364
  73.8 12.9 %collective-permute-start.28 = (bf16[512,256]{1,0:T(8,128)(2,1)S(1)}, bf16[512,256]{1,0:T(8,128)(2,1)S(1)}, u32[]{:S(2)}, u32[]{:S(2)}) collective-permute-start(bf16[512,256]{1,0:T(8,128)(2,1)S(1)} %get-tuple-element.107), channel_id=1, source_target_pairs={{0,4},{4,0},{8,12},{12,8},{16,20},{20,16},{24,28},{28,24},{1,5},{5... | collective-permute-start | bytes 786440 | tf_op jit(solution)/shard_map/ppermute | solution.py:364
  80.8 10.8 %collective-permute-start.27 = (bf16[576,256]{1,0:T(8,128)(2,1)S(1)}, bf16[576,256]{1,0:T(8,128)(2,1)S(1)}, u32[]{:S(2)}, u32[]{:S(2)}) collective-permute-start(bf16[576,256]{1,0:T(8,128)(2,1)S(1)} %get-tuple-element.105), channel_id=1, source_target_pairs={{0,4},{4,0},{8,12},{12,8},{16,20},{20,16},{24,28},{28,24},{1,5},{5... | collective-permute-start | bytes 884744 | tf_op jit(solution)/shard_map/ppermute | solution.py:364
  95.3 12.1 %collective-permute-start.32 = (bf16[288,256]{1,0:T(8,128)(2,1)S(1)}, bf16[288,256]{1,0:T(8,128)(2,1)S(1)}, u32[]{:S(2)}, u32[]{:S(2)}) collective-permute-start(bf16[288,256]{1,0:T(8,128)(2,1)S(1)} %get-tuple-element.115), channel_id=1, source_target_pairs={{0,8},{4,12},{8,0},{12,4},{16,24},{20,28},{24,16},{28,20},{1,9},{5... | collective-permute-start | bytes 442376 | tf_op jit(solution)/shard_map/ppermute | solution.py:364
  99.8 7.6 %collective-permute-start.34 = (bf16[128,256]{1,0:T(8,128)(2,1)S(1)}, bf16[128,256]{1,0:T(8,128)(2,1)S(1)}, u32[]{:S(2)}, u32[]{:S(2)}) collective-permute-start(bf16[128,256]{1,0:T(8,128)(2,1)S(1)} %get-tuple-element.118.refs_4_), channel_id=1, source_target_pairs={{0,16},{4,20},{8,24},{12,28},{16,0},{20,4},{24,8},{28,12},{1,17},{... | collective-permute-start | bytes 196616 | tf_op jit(solution)/shard_map/ppermute | solution.py:364
  108.0 9.2 %collective-permute-start.37 = (bf16[256,256]{1,0:T(8,128)(2,1)S(1)}, bf16[256,256]{1,0:T(8,128)(2,1)S(1)}, u32[]{:S(2)}, u32[]{:S(2)}) collective-permute-start(bf16[256,256]{1,0:T(8,128)(2,1)S(1)} %get-tuple-element.122.refs_4_), channel_id=1, source_target_pairs={{0,8},{4,12},{8,0},{12,4},{16,24},{20,28},{24,16},{28,20},{1,9},{5... | collective-permute-start | bytes 393224 | tf_op jit(solution)/shard_map/ppermute | solution.py:364
  108.1 9.1 %collective-permute-start.35 = (bf16[144,256]{1,0:T(8,128)(2,1)S(1)}, bf16[144,256]{1,0:T(8,128)(2,1)S(1)}, u32[]{:S(2)}, u32[]{:S(2)}) collective-permute-start(bf16[144,256]{1,0:T(8,128)(2,1)S(1)} %get-tuple-element.120), channel_id=1, source_target_pairs={{0,16},{4,20},{8,24},{12,28},{16,0},{20,4},{24,8},{28,12},{1,17},{... | collective-permute-start | bytes 221192 | tf_op jit(solution)/shard_map/ppermute | solution.py:364
  108.9 8.3 %collective-permute-start.36 = (bf16[128,256]{1,0:T(8,128)(2,1)S(1)}, bf16[128,256]{1,0:T(8,128)(2,1)S(1)}, u32[]{:S(2)}, u32[]{:S(2)}) collective-permute-start(bf16[128,256]{1,0:T(8,128)(2,1)S(1)} %get-tuple-element.121.refs_2_), channel_id=1, source_target_pairs={{0,16},{4,20},{8,24},{12,28},{16,0},{20,4},{24,8},{28,12},{1,17},{... | collective-permute-start | bytes 196616 | tf_op jit(solution)/shard_map/ppermute | solution.py:364
  117.9 9.1 %collective-permute-start.40 = (bf16[512,256]{1,0:T(8,128)(2,1)S(1)}, bf16[512,256]{1,0:T(8,128)(2,1)S(1)}, u32[]{:S(2)}, u32[]{:S(2)}) collective-permute-start(bf16[512,256]{1,0:T(8,128)(2,1)S(1)} %get-tuple-element.125.refs_4_), channel_id=1, source_target_pairs={{0,4},{4,0},{8,12},{12,8},{16,20},{20,16},{24,28},{28,24},{1,5},{5... | collective-permute-start | bytes 786440 | tf_op jit(solution)/shard_map/ppermute | solution.py:364
  128.5 8.6 %collective-permute-start.42 = (bf16[512,256]{1,0:T(8,128)(2,1)S(1)}, bf16[512,256]{1,0:T(8,128)(2,1)S(1)}, u32[]{:S(2)}, u32[]{:S(2)}) collective-permute-start(bf16[512,256]{1,0:T(8,128)(2,1)S(1)} %get-tuple-element.127.refs_2_), channel_id=1, source_target_pairs={{0,4},{4,0},{8,12},{12,8},{16,20},{20,16},{24,28},{28,24},{1,5},{5... | collective-permute-start | bytes 786440 | tf_op jit(solution)/shard_map/ppermute | solution.py:364
  (30 other events, 164.1 us)

commit v10 on v9

--- a/solution.py
+++ b/solution.py
@@ -420,9 +420,9 @@
     input_core = exchange(local_input, "ch", 1)
     first, second, cotangent_x = together(first, second, cotangent_x)
     near = swap_edges(first, second)
-    first, second, mirrored_cotangent = together(first, second, mirrored_cotangent)
-    edges = jnp.concatenate(near + swap_edges(first, second, cross), axis=0)
-    edges_core = exchange(edges, "ch", 1)
+    far = swap_edges(first, second, cross)
+    mirrored_cotangent, *far = together(mirrored_cotangent, *far)
+    edges = jnp.concatenate(near + far, axis=0)
     mirrored_cotangent_x = exchange(mirrored_cotangent, "ch", cross)
     early_w_out, mirrored_cotangent_x = together(w_out, mirrored_cotangent_x)
     w_out_x = exchange(early_w_out, "ch", cross)
@@ -435,6 +435,8 @@
         [((rows, width), F32)] * 2 + [(w_in.shape, BF16)],
         gflop=6.0,
     )
+    edges, projected, gate_pre = together(edges, projected, gate_pre)
+    edges_core = exchange(edges, "ch", 1)
     levels, level_3, gated = run(
         functools.partial(forward_kernel, channels),
         place,
@@ -522,25 +524,20 @@
     down = [("halve", distance) for distance in steps]
     up = [("double", distance) for distance in steps[::-1]]
     routes = [down + up + [("take",)], down + up + [None], down[1:] + up + [None]]
-    state = [None, (gate_kept, gate_other), (out_kept, out_other)]
-    results = [None, None, None]
-    for turn in range(len(routes[0]) - 1):
-        live = [k for k in range(3) if state[k] is not None]
-        places = [turn - 1 if k == 0 else turn for k in live]
-        items = [(routes[k][at], routes[k][at + 1], *state[k]) for k, at in zip(live, places)]
-        prepared = dict(zip(live, advance(place, items, taps)))
-        if turn == 0:
-            prepared[0] = (in_sent, in_kept)
-        for k, at in zip([0] * (turn == 0) + live, [-1] * (turn == 0) + places):
-            upcoming = routes[k][at + 1]
-            if upcoming is None:
-                results[k], state[k] = prepared[k][0], None
-            else:
-                sent, kept = prepared[k] if len(prepared[k]) == 2 else prepared[k] * 2
-                state[k] = (kept, exchange(sent, "seq", upcoming[1]))
-    last = len(routes[0]) - 2
-    (grad_in, grad_conv), = advance(place, [(routes[0][last], routes[0][last + 1], *state[0])], taps)
-    sum_gate, sum_out = results[1:]
+    in_sent, gate_other, out_other = together(in_sent, gate_other, out_other)
+    results = []
+    for route, sent, kept, other in zip(
+        routes, (in_sent, None, None), (in_kept, gate_kept, out_kept), (None, gate_other, out_other)
+    ):
+        if other is None:
+            other = exchange(sent, "seq", route[0][1])
+        for done, upcoming in zip(route, route[1:]):
+            prepared = advance(place, [(done, upcoming, kept, other)], taps)[0]
+            if upcoming is not None and upcoming[0] != "take":
+                sent, kept = prepared if len(prepared) == 2 else prepared * 2
+                other = exchange(sent, "seq", upcoming[1])
+        results.append(prepared)
+    (grad_in, grad_conv), (sum_gate,), (sum_out,) = results
     grad_conv = grad_conv.reshape(conv_w.shape)
     return output, grad_in, sum_gate, sum_out, grad_conv
 

time: 148 us -> 143 us (0.966)
  waiting for transfers between devices: 59.5 us -> 43.1 us
  starting transfers between devices: 53 us -> 59.4 us
  Pallas kernels: 29 us -> 34.6 us
    ppermute x36, waiting for transfers between devices: 49.6 us -> 31.9 us  [exchange(): return lax.ppermute(block, axis, [(i, i ^ distance) for i in range(count)])]
    pallas_call x16 -> x26, Pallas kernels: 29 us -> 34.6 us  [run(): pl.pallas_call(body, out_shape=[jax.ShapeDtypeStruct(shape, dtype) for sh...]
    ppermute x2, starting transfers between devices: 7.69 us -> 10.4 us  [mirror(): lax.ppermute(block, 'seq', [(i, count - 1 - i) for i in range(count)])]
    ppermute x36, starting transfers between devices: 34.3 us -> 37 us  [exchange(): return lax.ppermute(block, axis, [(i, i ^ distance) for i in range(count)])]
    unnamed x23 -> x20, local copies, waits for them, and re-layouts: 3.74 us -> 3.76 us
  transfers between devices with their start and end apart: 44 -> 44, of which waited for: 19 -> 19; matrix products, arithmetic and copies ran while one was open for 0% -> 0% of each run, Pallas kernels for 11% -> 19%
where the time goes in v10:
time: 143 us
  starting transfers between devices  59.4 us (42%)
  waiting for transfers between devices  43.1 us (30%)
  Pallas kernels  34.6 us (24%)
  local copies, waits for them, and re-layouts  4.37 us (3%)
    ppermute x36, starting transfers between devices, exchange(): return lax.ppermute(block, axis, [(i, i ^ distance) for i in range(count)])  37 us
    pallas_call x26, Pallas kernels, run(): pl.pallas_call(body, out_shape=[jax.ShapeDtypeStruct(shape, dtype) for sh...  34.6 us
    ppermute x36, waiting for transfers between devices, exchange(): return lax.ppermute(block, axis, [(i, i ^ distance) for i in range(count)])  31.9 us
    ppermute x6, starting transfers between devices, swap_edges(): received.append(lax.ppermute(block, ('seq', 'ch'), route))  12 us
    ppermute x2, starting transfers between devices, mirror(): lax.ppermute(block, 'seq', [(i, count - 1 - i) for i in range(count)])  10.4 us
    ppermute x2, waiting for transfers between devices, mirror(): lax.ppermute(block, 'seq', [(i, count - 1 - i) for i in range(count)])  8.38 us
    unnamed x20, local copies, waits for them, and re-layouts  3.76 us
  transfers between devices with their start and end apart: 44, of which 19 were waited for; matrix products, arithmetic and copies ran while one was open for 0% of the time, Pallas kernels for 19%

profile of v10, /device:TPU:0, one launch (start us, length us, event | category | flops | bytes accessed | tf_op | source)
XLA Modules:
  0.0 143.1 jit_solution(17281188932082935419)
XLA Ops:
  0.6 3.0 %collective-permute-start = (bf16[512,256]{1,0:T(8,128)(2,1)}, bf16[512,256]{1,0:T(8,128)(2,1)S(1)}, u32[]{:S(2)}, u32[]{:S(2)}) collective-permute-start(bf16[512,256]{1,0:T(8,128)(2,1)} %cotangent.1), channel_id=1, source_target_pairs={{0,2},{1,3},{2,0},{3,1},{4,6},{5,7},{6,4},{7,5},{8,10},{9,11},{10,... | collective-permute-start | bytes 786440 | tf_op jit(solution)/shard_map/ppermute | solution.py:364
  4.2 2.7 %shard_map.137 = (bf16[512,256]{1,0:T(8,128)(2,1)}, bf16[160,256]{1,0:T(8,128)(2,1)}, bf16[160,256]{1,0:T(8,128)(2,1)}) custom-call(s32[3]{0:T(128)} %pad_add_fusion.place, s32[1,512]{1,0:T(1,128)} %bitcast.7, bf16[512,256]{1,0:T(8,128)(2,1)} %hidden_hbm.1, bf16[4,256]{1,0:T(4,128)(2,1)} %embedding_hbm.1), custom_call_target="tpu_custom_call" | custom-call | flops 100000000 | bytes 266240 | tf_op jit(solution)/shard_map/pallas_call | solution.py:30
  7.0 5.1 %collective-permute-start.3 = (bf16[512,256]{1,0:T(8,128)(2,1)}, bf16[512,256]{1,0:T(8,128)(2,1)S(1)}, u32[]{:S(2)}, u32[]{:S(2)}) collective-permute-start(bf16[512,256]{1,0:T(8,128)(2,1)} %cotangent.1), channel_id=1, source_target_pairs={{0,28},{4,24},{8,20},{12,16},{16,12},{20,8},{24,4},{28,0},{1,29},{... | collective-permute-start | bytes 786440 | tf_op jit(solution)/shard_map/ppermute | solution.py:373
  14.0 2.5 %collective-permute-done.7.refs_2_ = bf16[512,256]{1,0:T(8,128)(2,1)S(1)} collective-permute-done((bf16[512,256]{1,0:T(8,128)(2,1)}, bf16[512,256]{1,0:T(8,128)(2,1)S(1)}, u32[]{:S(2)}, u32[]{:S(2)}) %collective-permute-start.7) | collective-permute-done | bytes 262176 | tf_op jit(solution)/shard_map/ppermute | solution.py:364
  17.2 2.4 %collective-permute-done.3.refs_4_ = bf16[512,256]{1,0:T(8,128)(2,1)S(1)} collective-permute-done((bf16[512,256]{1,0:T(8,128)(2,1)}, bf16[512,256]{1,0:T(8,128)(2,1)S(1)}, u32[]{:S(2)}, u32[]{:S(2)}) %collective-permute-start.3) | collective-permute-done | bytes 262176 | tf_op jit(solution)/shard_map/ppermute | solution.py:373
  19.6 3.3 %collective-permute-start.1 = (bf16[160,256]{1,0:T(8,128)(2,1)}, bf16[160,256]{1,0:T(8,128)(2,1)S(1)}, u32[]{:S(2)}, u32[]{:S(2)}) collective-permute-start(bf16[160,256]{1,0:T(8,128)(2,1)} %get-tuple-element.66), channel_id=1, source_target_pairs={{0,4},{4,0},{1,5},{5,1},{2,6},{6,2},{3,7},{7,3},{8,12},{12,8},{9,1... | collective-permute-start | bytes 245768 | tf_op jit(solution)/shard_map/ppermute | solution.py:385
  24.1 2.5 %collective-permute-done.1 = bf16[160,256]{1,0:T(8,128)(2,1)S(1)} collective-permute-done((bf16[160,256]{1,0:T(8,128)(2,1)}, bf16[160,256]{1,0:T(8,128)(2,1)S(1)}, u32[]{:S(2)}, u32[]{:S(2)}) %collective-permute-start.1) | collective-permute-done | bytes 81952 | tf_op jit(solution)/shard_map/ppermute | solution.py:385
  35.4 5.3 %collective-permute-start.11 = (bf16[512,256]{1,0:T(8,128)(2,1)S(1)}, bf16[512,256]{1,0:T(8,128)(2,1)S(1)}, u32[]{:S(2)}, u32[]{:S(2)}) collective-permute-start(bf16[512,256]{1,0:T(8,128)(2,1)S(1)} %get-tuple-element.77.refs_0_), channel_id=1, source_target_pairs={{0,28},{4,24},{8,20},{12,16},{16,12},{20,8},{24,4},{28,0},{1,29},{... | collective-permute-start | bytes 786440 | tf_op jit(solution)/shard_map/ppermute | solution.py:373
  41.4 6.0 %collective-permute-done.11.block = bf16[512,256]{1,0:T(8,128)(2,1)S(1)} collective-permute-done((bf16[512,256]{1,0:T(8,128)(2,1)S(1)}, bf16[512,256]{1,0:T(8,128)(2,1)S(1)}, u32[]{:S(2)}, u32[]{:S(2)}) %collective-permute-start.11) | collective-permute-done | bytes 262176 | tf_op jit(solution)/shard_map/ppermute | solution.py:373
  48.0 3.7 %collective-permute-done.14.refs_2_ = bf16[512,256]{1,0:T(8,128)(2,1)S(1)} collective-permute-done((bf16[512,256]{1,0:T(8,128)(2,1)S(1)}, bf16[512,256]{1,0:T(8,128)(2,1)S(1)}, u32[]{:S(2)}, u32[]{:S(2)}) %collective-permute-start.14) | collective-permute-done | bytes 262176 | tf_op jit(solution)/shard_map/ppermute | solution.py:364
  54.3 3.7 %shard_map.141 = (bf16[1024,1024]{1,0:T(8,128)(2,1)S(1)}, bf16[512,256]{1,0:T(8,128)(2,1)S(1)}, bf16[1024,1024]{1,0:T(8,128)(2,1)S(1)}) custom-call(s32[3]{0:T(128)S(1)} %copy-done.4, bf16[512,256]{1,0:T(8,128)(2,1)S(1)} %copy-done.3, bf16[512,256]{1,0:T(8,128)(2,1)S(1)} %collective-permute-done.18.refs_1_, ...), custom_call_target="tpu_custom_call" | custom-call | flops 2100000000 | bytes 4198400 | tf_op jit(solution)/shard_map/pallas_call | solution.py:30
  58.0 3.4 %collective-permute-done.17.refs_6_ = bf16[512,256]{1,0:T(8,128)(2,1)S(1)} collective-permute-done((bf16[512,256]{1,0:T(8,128)(2,1)S(1)}, bf16[512,256]{1,0:T(8,128)(2,1)S(1)}, u32[]{:S(2)}, u32[]{:S(2)}) %collective-permute-start.17) | collective-permute-done | bytes 262176 | tf_op jit(solution)/shard_map/ppermute | solution.py:364
  62.9 5.8 %shard_map.142 = (bf16[1024,1024]{1,0:T(8,128)(2,1)S(1)}, bf16[512,256]{1,0:T(8,128)(2,1)S(1)}, bf16[512,256]{1,0:T(8,128)(2,1)S(1)}, bf16[160,256]{1,0:T(8,128)(2,1)S(1)}, bf16[160,256]{1,0:T(8,128)(2,1)S(1)}) custom-call(s32[3]{0:T(128)S(1)} %copy-done.4, bf16[512,256]{1,0:T(8,128)(2,1)S(1)} %get-tuple-element.77.refs_0_, ...), custom_call_target="tpu_custom_call" | custom-call | flops 2500000000 | bytes 7081984 | tf_op jit(solution)/shard_map/pallas_call | solution.py:30
  68.7 4.7 %collective-permute-start.25 = (bf16[160,256]{1,0:T(8,128)(2,1)S(1)}, bf16[160,256]{1,0:T(8,128)(2,1)S(1)}, u32[]{:S(2)}, u32[]{:S(2)}) collective-permute-start(bf16[160,256]{1,0:T(8,128)(2,1)S(1)} %get-tuple-element.97), channel_id=1, source_target_pairs={{0,4},{4,0},{1,5},{5,1},{2,6},{6,2},{3,7},{7,3},{8,12},{12,8},{9,1... | collective-permute-start | bytes 245768 | tf_op jit(solution)/shard_map/ppermute | solution.py:385
  76.1 5.7 %collective-permute-start.27 = (bf16[512,256]{1,0:T(8,128)(2,1)S(1)}, bf16[512,256]{1,0:T(8,128)(2,1)S(1)}, u32[]{:S(2)}, u32[]{:S(2)}) collective-permute-start(bf16[512,256]{1,0:T(8,128)(2,1)S(1)} %get-tuple-element.104), channel_id=1, source_target_pairs={{0,4},{4,0},{8,12},{12,8},{16,20},{20,16},{24,28},{28,24},{1,5},{5... | collective-permute-start | bytes 786440 | tf_op jit(solution)/shard_map/ppermute | solution.py:364
  84.1 2.5 %shard_map.145 = (bf16[576,256]{1,0:T(8,128)(2,1)S(1)}, f32[576,256]{1,0:T(8,128)S(1)}) custom-call(s32[3]{0:T(128)S(1)} %copy-done.4, bf16[512,256]{1,0:T(8,128)(2,1)S(1)} %get-tuple-element.92.upstream, bf16[160,256]{1,0:T(8,128)(2,1)S(1)} %collective-permute-done.25.first, bf16[160,256]{1,0:T(8,128)(2,1)S(1)} %collective-permute-done.26.second, ...), custom_call_target="tpu_custom_call" | custom-call | flops 500000000 | bytes 2609152 | tf_op jit(solution)/shard_map/pallas_call | solution.py:30
  89.4 5.8 %collective-permute-done.29.refs_1_ = bf16[576,256]{1,0:T(8,128)(2,1)S(1)} collective-permute-done((bf16[576,256]{1,0:T(8,128)(2,1)S(1)}, bf16[576,256]{1,0:T(8,128)(2,1)S(1)}, u32[]{:S(2)}, u32[]{:S(2)}) %collective-permute-start.29) | collective-permute-done | bytes 294944 | tf_op jit(solution)/shard_map/ppermute | solution.py:364
  98.7 2.4 %collective-permute-done.30.refs_1_ = bf16[288,256]{1,0:T(8,128)(2,1)S(1)} collective-permute-done((bf16[288,256]{1,0:T(8,128)(2,1)S(1)}, bf16[288,256]{1,0:T(8,128)(2,1)S(1)}, u32[]{:S(2)}, u32[]{:S(2)}) %collective-permute-start.30) | collective-permute-done | bytes 147488 | tf_op jit(solution)/shard_map/ppermute | solution.py:364
  101.7 2.9 %collective-permute-start.31 = (bf16[144,256]{1,0:T(8,128)(2,1)S(1)}, bf16[144,256]{1,0:T(8,128)(2,1)S(1)}, u32[]{:S(2)}, u32[]{:S(2)}) collective-permute-start(bf16[144,256]{1,0:T(8,128)(2,1)S(1)} %get-tuple-element.110), channel_id=1, source_target_pairs={{0,16},{4,20},{8,24},{12,28},{16,0},{20,4},{24,8},{28,12},{1,17},{... | collective-permute-start | bytes 221192 | tf_op jit(solution)/shard_map/ppermute | solution.py:364
  105.9 3.0 %collective-permute-start.36 = (bf16[128,256]{1,0:T(8,128)(2,1)S(1)}, bf16[128,256]{1,0:T(8,128)(2,1)S(1)}, u32[]{:S(2)}, u32[]{:S(2)}) collective-permute-start(bf16[128,256]{1,0:T(8,128)(2,1)S(1)} %get-tuple-element.117), channel_id=1, source_target_pairs={{0,16},{4,20},{8,24},{12,28},{16,0},{20,4},{24,8},{28,12},{1,17},{... | collective-permute-start | bytes 196616 | tf_op jit(solution)/shard_map/ppermute | solution.py:364
  111.1 2.7 %collective-permute-done.40.refs_1_ = bf16[128,256]{1,0:T(8,128)(2,1)S(1)} collective-permute-done((bf16[128,256]{1,0:T(8,128)(2,1)S(1)}, bf16[128,256]{1,0:T(8,128)(2,1)S(1)}, u32[]{:S(2)}, u32[]{:S(2)}) %collective-permute-start.40) | collective-permute-done | bytes 65568 | tf_op jit(solution)/shard_map/ppermute | solution.py:364
  115.8 2.2 %collective-permute-start.37 = (bf16[128,256]{1,0:T(8,128)(2,1)S(1)}, bf16[128,256]{1,0:T(8,128)(2,1)S(1)}, u32[]{:S(2)}, u32[]{:S(2)}) collective-permute-start(bf16[128,256]{1,0:T(8,128)(2,1)S(1)} %shard_map.154.refs_0_), channel_id=1, source_target_pairs={{0,16},{4,20},{8,24},{12,28},{16,0},{20,4},{24,8},{28,12},{1,17},{... | collective-permute-start | bytes 196616 | tf_op jit(solution)/shard_map/ppermute | solution.py:364
  121.9 2.2 %collective-permute-start.38 = (bf16[256,256]{1,0:T(8,128)(2,1)S(1)}, bf16[256,256]{1,0:T(8,128)(2,1)S(1)}, u32[]{:S(2)}, u32[]{:S(2)}) collective-permute-start(bf16[256,256]{1,0:T(8,128)(2,1)S(1)} %shard_map.155.refs_0_), channel_id=1, source_target_pairs={{0,8},{4,12},{8,0},{12,4},{16,24},{20,28},{24,16},{28,20},{1,9},{5... | collective-permute-start | bytes 393224 | tf_op jit(solution)/shard_map/ppermute | solution.py:364
  131.4 5.3 %collective-permute-done.43.refs_1_ = bf16[512,256]{1,0:T(8,128)(2,1)S(1)} collective-permute-done((bf16[512,256]{1,0:T(8,128)(2,1)S(1)}, bf16[512,256]{1,0:T(8,128)(2,1)S(1)}, u32[]{:S(2)}, u32[]{:S(2)}) %collective-permute-start.43) | collective-permute-done | bytes 262176 | tf_op jit(solution)/shard_map/ppermute | solution.py:364
  (113 shorter events, 53.3 us)
Async XLA Ops:
  0.6 11.5 %collective-permute-start = (bf16[512,256]{1,0:T(8,128)(2,1)}, bf16[512,256]{1,0:T(8,128)(2,1)S(1)}, u32[]{:S(2)}, u32[]{:S(2)}) collective-permute-start(bf16[512,256]{1,0:T(8,128)(2,1)} %cotangent.1), channel_id=1, source_target_pairs={{0,2},{1,3},{2,0},{3,1},{4,6},{5,7},{6,4},{7,5},{8,10},{9,11},{10,... | collective-permute-start | bytes 786440 | tf_op jit(solution)/shard_map/ppermute | solution.py:364
  6.9 9.6 %collective-permute-start.7 = (bf16[512,256]{1,0:T(8,128)(2,1)}, bf16[512,256]{1,0:T(8,128)(2,1)S(1)}, u32[]{:S(2)}, u32[]{:S(2)}) collective-permute-start(bf16[512,256]{1,0:T(8,128)(2,1)} %get-tuple-element.70.refs_0_.block_in), channel_id=1, source_target_pairs={{0,2},{1,3},{2,0},{3,1},{4,6},{5,7},{6,4},{7,5},{8,10},{9,11},{10,... | collective-permute-start | bytes 786440 | tf_op jit(solution)/shard_map/ppermute | solution.py:364
  7.0 12.5 %collective-permute-start.3 = (bf16[512,256]{1,0:T(8,128)(2,1)}, bf16[512,256]{1,0:T(8,128)(2,1)S(1)}, u32[]{:S(2)}, u32[]{:S(2)}) collective-permute-start(bf16[512,256]{1,0:T(8,128)(2,1)} %cotangent.1), channel_id=1, source_target_pairs={{0,28},{4,24},{8,20},{12,16},{16,12},{20,8},{24,4},{28,0},{1,29},{... | collective-permute-start | bytes 786440 | tf_op jit(solution)/shard_map/ppermute | solution.py:373
  12.1 10.8 %collective-permute-start.4 = (bf16[160,256]{1,0:T(8,128)(2,1)}, bf16[160,256]{1,0:T(8,128)(2,1)S(1)}, u32[]{:S(2)}, u32[]{:S(2)}) collective-permute-start(bf16[160,256]{1,0:T(8,128)(2,1)} %get-tuple-element.66), channel_id=1, source_target_pairs={{0,6},{4,2},{1,7},{5,3},{2,4},{6,0},{3,5},{7,1},{8,14},{12,10},{9,... | collective-permute-start | bytes 245768 | tf_op jit(solution)/shard_map/ppermute | solution.py:385
  14.0 12.7 %collective-permute-start.6 = (bf16[512,256]{1,0:T(8,128)(2,1)}, bf16[512,256]{1,0:T(8,128)(2,1)S(1)}, u32[]{:S(2)}, u32[]{:S(2)}) collective-permute-start(bf16[512,256]{1,0:T(8,128)(2,1)} %get-tuple-element.70.refs_0_.block_in), channel_id=1, source_target_pairs={{0,1},{1,0},{2,3},{3,2},{4,5},{5,4},{6,7},{7,6},{8,9},{9,8},{10,11... | collective-permute-start | bytes 786440 | tf_op jit(solution)/shard_map/ppermute | solution.py:364
  16.5 10.2 %collective-permute-start.8 = (bf16[512,256]{1,0:T(8,128)(2,1)S(1)}, bf16[512,256]{1,0:T(8,128)(2,1)S(1)}, u32[]{:S(2)}, u32[]{:S(2)}) collective-permute-start(bf16[512,256]{1,0:T(8,128)(2,1)S(1)} %collective-permute-done.7.refs_2_), channel_id=1, source_target_pairs={{0,1},{1,0},{2,3},{3,2},{4,5},{5,4},{6,7},{7,6},{8,9},{9,8},{10,11... | collective-permute-start | bytes 786440 | tf_op jit(solution)/shard_map/ppermute | solution.py:364
  23.5 8.2 %collective-permute-start.12 = (bf16[512,256]{1,0:T(8,128)(2,1)S(1)}, bf16[512,256]{1,0:T(8,128)(2,1)S(1)}, u32[]{:S(2)}, u32[]{:S(2)}) collective-permute-start(bf16[512,256]{1,0:T(8,128)(2,1)S(1)} %collective-permute-done.3.refs_4_), channel_id=1, source_target_pairs={{0,2},{1,3},{2,0},{3,1},{4,6},{5,7},{6,4},{7,5},{8,10},{9,11},{10,... | collective-permute-start | bytes 786440 | tf_op jit(solution)/shard_map/ppermute | solution.py:364
  31.8 15.6 %collective-permute-start.13 = (bf16[1024,256]{1,0:T(8,128)(2,1)S(1)}, bf16[1024,256]{1,0:T(8,128)(2,1)S(1)}, u32[]{:S(2)}, u32[]{:S(2)}) collective-permute-start(bf16[1024,256]{1,0:T(8,128)(2,1)S(1)} %copy-done.2), channel_id=1, source_target_pairs={{0,2},{1,3},{2,0},{3,1},{4,6},{5,7},{6,4},{7,5},{8,10},{9,11},{10,... | collective-permute-start | bytes 1572872 | tf_op jit(solution)/shard_map/ppermute | solution.py:364
  35.4 12.0 %collective-permute-start.11 = (bf16[512,256]{1,0:T(8,128)(2,1)S(1)}, bf16[512,256]{1,0:T(8,128)(2,1)S(1)}, u32[]{:S(2)}, u32[]{:S(2)}) collective-permute-start(bf16[512,256]{1,0:T(8,128)(2,1)S(1)} %get-tuple-element.77.refs_0_), channel_id=1, source_target_pairs={{0,28},{4,24},{8,20},{12,16},{16,12},{20,8},{24,4},{28,0},{1,29},{... | collective-permute-start | bytes 786440 | tf_op jit(solution)/shard_map/ppermute | solution.py:373
  40.7 11.0 %collective-permute-start.14 = (bf16[512,256]{1,0:T(8,128)(2,1)S(1)}, bf16[512,256]{1,0:T(8,128)(2,1)S(1)}, u32[]{:S(2)}, u32[]{:S(2)}) collective-permute-start(bf16[512,256]{1,0:T(8,128)(2,1)S(1)} %get-tuple-element.77.refs_0_), channel_id=1, source_target_pairs={{0,2},{1,3},{2,0},{3,1},{4,6},{5,7},{6,4},{7,5},{8,10},{9,11},{10,... | collective-permute-start | bytes 786440 | tf_op jit(solution)/shard_map/ppermute | solution.py:364
  41.2 12.3 %collective-permute-start.22 = (bf16[1024,256]{1,0:T(8,128)(2,1)S(1)}, bf16[1024,256]{1,0:T(8,128)(2,1)S(1)}, u32[]{:S(2)}, u32[]{:S(2)}) collective-permute-start(bf16[1024,256]{1,0:T(8,128)(2,1)S(1)} %copy-done.2), channel_id=1, source_target_pairs={{0,1},{1,0},{2,3},{3,2},{4,5},{5,4},{6,7},{7,6},{8,9},{9,8},{10,11... | collective-permute-start | bytes 1572872 | tf_op jit(solution)/shard_map/ppermute | solution.py:364
  52.6 8.8 %collective-permute-start.17 = (bf16[512,256]{1,0:T(8,128)(2,1)S(1)}, bf16[512,256]{1,0:T(8,128)(2,1)S(1)}, u32[]{:S(2)}, u32[]{:S(2)}) collective-permute-start(bf16[512,256]{1,0:T(8,128)(2,1)S(1)} %shard_map.140.refs_4_), channel_id=1, source_target_pairs={{0,2},{1,3},{2,0},{3,1},{4,6},{5,7},{6,4},{7,5},{8,10},{9,11},{10,... | collective-permute-start | bytes 786440 | tf_op jit(solution)/shard_map/ppermute | solution.py:364
  53.6 7.8 %collective-permute-start.10 = (bf16[512,256]{1,0:T(8,128)(2,1)S(1)}, bf16[512,256]{1,0:T(8,128)(2,1)S(1)}, u32[]{:S(2)}, u32[]{:S(2)}) collective-permute-start(bf16[512,256]{1,0:T(8,128)(2,1)S(1)} %get-tuple-element.77.refs_0_), channel_id=1, source_target_pairs={{0,1},{1,0},{2,3},{3,2},{4,5},{5,4},{6,7},{7,6},{8,9},{9,8},{10,11... | collective-permute-start | bytes 786440 | tf_op jit(solution)/shard_map/ppermute | solution.py:364
  53.8 7.6 %collective-permute-start.16 = (bf16[512,256]{1,0:T(8,128)(2,1)S(1)}, bf16[512,256]{1,0:T(8,128)(2,1)S(1)}, u32[]{:S(2)}, u32[]{:S(2)}) collective-permute-start(bf16[512,256]{1,0:T(8,128)(2,1)S(1)} %shard_map.140.refs_4_), channel_id=1, source_target_pairs={{0,1},{1,0},{2,3},{3,2},{4,5},{5,4},{6,7},{7,6},{8,9},{9,8},{10,11... | collective-permute-start | bytes 786440 | tf_op jit(solution)/shard_map/ppermute | solution.py:364
  54.1 7.3 %collective-permute-start.15 = (bf16[512,256]{1,0:T(8,128)(2,1)S(1)}, bf16[512,256]{1,0:T(8,128)(2,1)S(1)}, u32[]{:S(2)}, u32[]{:S(2)}) collective-permute-start(bf16[512,256]{1,0:T(8,128)(2,1)S(1)} %collective-permute-done.14.refs_2_), channel_id=1, source_target_pairs={{0,1},{1,0},{2,3},{3,2},{4,5},{5,4},{6,7},{7,6},{8,9},{9,8},{10,11... | collective-permute-start | bytes 786440 | tf_op jit(solution)/shard_map/ppermute | solution.py:364
  68.7 7.5 %collective-permute-start.25 = (bf16[160,256]{1,0:T(8,128)(2,1)S(1)}, bf16[160,256]{1,0:T(8,128)(2,1)S(1)}, u32[]{:S(2)}, u32[]{:S(2)}) collective-permute-start(bf16[160,256]{1,0:T(8,128)(2,1)S(1)} %get-tuple-element.97), channel_id=1, source_target_pairs={{0,4},{4,0},{1,5},{5,1},{2,6},{6,2},{3,7},{7,3},{8,12},{12,8},{9,1... | collective-permute-start | bytes 245768 | tf_op jit(solution)/shard_map/ppermute | solution.py:385
  76.1 11.5 %collective-permute-start.27 = (bf16[512,256]{1,0:T(8,128)(2,1)S(1)}, bf16[512,256]{1,0:T(8,128)(2,1)S(1)}, u32[]{:S(2)}, u32[]{:S(2)}) collective-permute-start(bf16[512,256]{1,0:T(8,128)(2,1)S(1)} %get-tuple-element.104), channel_id=1, source_target_pairs={{0,4},{4,0},{8,12},{12,8},{16,20},{20,16},{24,28},{28,24},{1,5},{5... | collective-permute-start | bytes 786440 | tf_op jit(solution)/shard_map/ppermute | solution.py:364
  87.7 7.6 %collective-permute-start.29 = (bf16[576,256]{1,0:T(8,128)(2,1)S(1)}, bf16[576,256]{1,0:T(8,128)(2,1)S(1)}, u32[]{:S(2)}, u32[]{:S(2)}) collective-permute-start(bf16[576,256]{1,0:T(8,128)(2,1)S(1)} %get-tuple-element.106), channel_id=1, source_target_pairs={{0,4},{4,0},{8,12},{12,8},{16,20},{20,16},{24,28},{28,24},{1,5},{5... | collective-permute-start | bytes 884744 | tf_op jit(solution)/shard_map/ppermute | solution.py:364
  105.2 8.6 %collective-permute-start.40 = (bf16[128,256]{1,0:T(8,128)(2,1)S(1)}, bf16[128,256]{1,0:T(8,128)(2,1)S(1)}, u32[]{:S(2)}, u32[]{:S(2)}) collective-permute-start(bf16[128,256]{1,0:T(8,128)(2,1)S(1)} %get-tuple-element.121), channel_id=1, source_target_pairs={{0,16},{4,20},{8,24},{12,28},{16,0},{20,4},{24,8},{28,12},{1,17},{... | collective-permute-start | bytes 196616 | tf_op jit(solution)/shard_map/ppermute | solution.py:364
  105.9 9.3 %collective-permute-start.36 = (bf16[128,256]{1,0:T(8,128)(2,1)S(1)}, bf16[128,256]{1,0:T(8,128)(2,1)S(1)}, u32[]{:S(2)}, u32[]{:S(2)}) collective-permute-start(bf16[128,256]{1,0:T(8,128)(2,1)S(1)} %get-tuple-element.117), channel_id=1, source_target_pairs={{0,16},{4,20},{8,24},{12,28},{16,0},{20,4},{24,8},{28,12},{1,17},{... | collective-permute-start | bytes 196616 | tf_op jit(solution)/shard_map/ppermute | solution.py:364
  109.5 8.5 %collective-permute-start.32 = (bf16[144,256]{1,0:T(8,128)(2,1)S(1)}, bf16[144,256]{1,0:T(8,128)(2,1)S(1)}, u32[]{:S(2)}, u32[]{:S(2)}) collective-permute-start(bf16[144,256]{1,0:T(8,128)(2,1)S(1)} %shard_map.148.refs_0_), channel_id=1, source_target_pairs={{0,16},{4,20},{8,24},{12,28},{16,0},{20,4},{24,8},{28,12},{1,17},{... | collective-permute-start | bytes 221192 | tf_op jit(solution)/shard_map/ppermute | solution.py:364
  125.3 15.7 %collective-permute-start.34 = (bf16[576,256]{1,0:T(8,128)(2,1)S(1)}, bf16[576,256]{1,0:T(8,128)(2,1)S(1)}, u32[]{:S(2)}, u32[]{:S(2)}) collective-permute-start(bf16[576,256]{1,0:T(8,128)(2,1)S(1)} %shard_map.150.refs_0_), channel_id=1, source_target_pairs={{0,4},{4,0},{8,12},{12,8},{16,20},{20,16},{24,28},{28,24},{1,5},{5... | collective-permute-start | bytes 884744 | tf_op jit(solution)/shard_map/ppermute | solution.py:364
  127.0 9.8 %collective-permute-start.43 = (bf16[512,256]{1,0:T(8,128)(2,1)S(1)}, bf16[512,256]{1,0:T(8,128)(2,1)S(1)}, u32[]{:S(2)}, u32[]{:S(2)}) collective-permute-start(bf16[512,256]{1,0:T(8,128)(2,1)S(1)} %shard_map.161.refs_0_), channel_id=1, source_target_pairs={{0,4},{4,0},{8,12},{12,8},{16,20},{20,16},{24,28},{28,24},{1,5},{5... | collective-permute-start | bytes 786440 | tf_op jit(solution)/shard_map/ppermute | solution.py:364
  128.7 10.8 %collective-permute-start.39 = (bf16[512,256]{1,0:T(8,128)(2,1)S(1)}, bf16[512,256]{1,0:T(8,128)(2,1)S(1)}, u32[]{:S(2)}, u32[]{:S(2)}) collective-permute-start(bf16[512,256]{1,0:T(8,128)(2,1)S(1)} %shard_map.156.refs_0_), channel_id=1, source_target_pairs={{0,4},{4,0},{8,12},{12,8},{16,20},{20,16},{24,28},{28,24},{1,5},{5... | collective-permute-start | bytes 786440 | tf_op jit(solution)/shard_map/ppermute | solution.py:364
  (30 other events, 168.7 us)

commit v11 on v10

--- a/solution.py
+++ b/solution.py
@@ -85,26 +85,25 @@
     second[...] = block_in[pl.ds(pl.multiple_of(odd * far, 16), EDGE), :]
 
 
-def project_kernel(channels, place, *refs):
-    mains, (w_in, w_gate, projected, gate_pre, w_in_on) = refs[:channels], refs[channels:]
-    me, width = place[1], mains[0].shape[1]
-    for weight, out in ((w_in, projected), (w_gate, gate_pre)):
-        total = dot(mains[0][...], weight[part(me, width), :])
-        for j in range(1, channels):
-            total += dot(mains[j][...], weight[part(me ^ j, width), :])
-        out[...] = total
-    w_in_on[...] = w_in[...]
-
-
 def keep_inside(total, place, before, rows):
     position = lax.broadcasted_iota(jnp.int32, total.shape, 0) + (place[0] * rows - before)
     return jnp.where((position >= 0) & (position < place[2] * rows), total, 0.0)
 
 
-def forward_kernel(channels, place, edges, edges_core, w_in, projected, gate_pre, conv_w, *outs):
-    levels, level_3, gated, *stages = outs
+def forward_kernel(channels, place, *refs):
+    count = channels + 5
+    gate_pre, levels, level_3, gated, *held = refs[count:]
+    copies = fetch(refs[:count], held[:count], held[count])
+    w_in, w_gate, conv_w, edges, edges_core, *mains = held[:count]
+    stages = held[count + 1 :]
     me, odd = place[1], place[0] % 2
-    rows, width = projected.shape
+    rows, width = mains[0].shape
+    for copy in copies:
+        copy.wait()
+    projected, gate = (
+        sum(dot(mains[j][...], weight[part(me ^ j, width), :]) for j in range(channels)) for weight in (w_in, w_gate)
+    )
+    gate_pre[...] = gate
     left = jnp.zeros((EDGE, width), F32)
     right = jnp.zeros((AFT[0], width), F32)
     for j in range(channels):
@@ -115,7 +114,7 @@
         right += dot(source[pl.ds(pl.multiple_of(base + odd * EDGE, 16), AFT[0]), :], weight)
     source = stages[0]
     source[:EDGE] = left
-    source[EDGE : EDGE + rows] = projected[...]
+    source[EDGE : EDGE + rows] = projected
     source[EDGE + rows :] = right
     top = 0
     for number, dilation in enumerate(DILATIONS):
@@ -134,7 +133,6 @@
         if count < target.shape[0]:
             target[count:] = jnp.zeros((target.shape[0] - count, width), F32)
         source = target
-    gate = gate_pre[...]
     level_3[...] = source[...].astype(BF16)
     gated[...] = (source[...] * (gate / (1.0 + jnp.exp(-gate)))).astype(BF16)
 
@@ -418,32 +416,25 @@
     )
     input_x = exchange(local_input, "ch", cross)
     input_core = exchange(local_input, "ch", 1)
-    first, second, cotangent_x = together(first, second, cotangent_x)
     near = swap_edges(first, second)
     far = swap_edges(first, second, cross)
-    mirrored_cotangent, *far = together(mirrored_cotangent, *far)
+    input_x, cotangent_x, *near = together(input_x, cotangent_x, *near)
     edges = jnp.concatenate(near + far, axis=0)
     mirrored_cotangent_x = exchange(mirrored_cotangent, "ch", cross)
     early_w_out, mirrored_cotangent_x = together(w_out, mirrored_cotangent_x)
     w_out_x = exchange(early_w_out, "ch", cross)
     mains = [local_input, input_core, input_x, exchange(input_x, "ch", 1)]
 
-    projected, gate_pre, w_in_on = run(
-        functools.partial(project_kernel, channels),
-        place,
-        (*mains, w_in, w_gate),
-        [((rows, width), F32)] * 2 + [(w_in.shape, BF16)],
-        gflop=6.0,
-    )
-    edges, projected, gate_pre = together(edges, projected, gate_pre)
-    edges_core = exchange(edges, "ch", 1)
-    levels, level_3, gated = run(
+    operands = (w_in, w_gate, conv_w, edges, exchange(edges, "ch", 1), *mains)
+    gate_pre, levels, level_3, gated = run(
         functools.partial(forward_kernel, channels),
         place,
-        (edges, edges_core, w_in_on, projected, gate_pre, conv_w),
-        [((sum(saved_rows(rows, number) for number in range(3)), width), BF16), block, block],
-        [pltpu.VMEM((saved_rows(rows, number), width), F32) for number in range(4)],
-        gflop=0.4,
+        operands,
+        [((rows, width), F32), ((sum(saved_rows(rows, number) for number in range(3)), width), BF16), block, block],
+        fetch_scratch(operands) + [pltpu.VMEM((saved_rows(rows, number), width), F32) for number in range(4)],
+        megabytes=60,
+        gflop=1.0,
+        fetched=len(operands),
     )
     mirrored, w_out_x = together(mirror(gated), w_out_x)
     mirrored = run(flip_kernel, place, (mirrored,), [block], gflop=12.0)[0]
@@ -524,19 +515,39 @@
     down = [("halve", distance) for distance in steps]
     up = [("double", distance) for distance in steps[::-1]]
     routes = [down + up + [("take",)], down + up + [None], down[1:] + up + [None]]
-    in_sent, gate_other, out_other = together(in_sent, gate_other, out_other)
-    results = []
-    for route, sent, kept, other in zip(
-        routes, (in_sent, None, None), (in_kept, gate_kept, out_kept), (None, gate_other, out_other)
-    ):
-        if other is None:
-            other = exchange(sent, "seq", route[0][1])
-        for done, upcoming in zip(route, route[1:]):
-            prepared = advance(place, [(done, upcoming, kept, other)], taps)[0]
-            if upcoming is not None and upcoming[0] != "take":
-                sent, kept = prepared if len(prepared) == 2 else prepared * 2
-                other = exchange(sent, "seq", upcoming[1])
-        results.append(prepared)
+    sends = [(in_sent, in_kept), (None, gate_kept, gate_other), (None, out_kept, out_other)]
+    results = [None, None, None]
+
+    def move_on(k, at):
+        if results[k] is not None:
+            return
+        done, upcoming = routes[k][at], routes[k][at + 1]
+        prepared = advance(place, [(done, upcoming, *sends[k][1:])], taps)[0]
+        if upcoming is None or upcoming[0] == "take":
+            results[k] = prepared
+        else:
+            sends[k] = tuple(prepared) if len(prepared) == 2 else (prepared[0], prepared[0])
+
+    def send(k, at):
+        if results[k] is None:
+            sent, kept = sends[k]
+            sends[k] = (sent, kept, exchange(sent, "seq", routes[k][at][1]))
+
+    for at in range(len(routes[0]) - 1):
+        open_sums = [k for k in range(3) if results[k] is None]
+        ending = [k for k in open_sums if k and routes[k][at + 1] is None]
+        for k in open_sums:
+            if k and k not in ending:
+                move_on(k, at)
+        tied = together(*[sends[k][2 if k in ending else 0] for k in open_sums])
+        for k, array in zip(open_sums, tied):
+            sends[k] = (*sends[k][:2], array) if k in ending else (array, *sends[k][1:])
+        for k in ending:
+            move_on(k, at)
+        for k in (2, 1):
+            send(k, at + 1)
+        send(0, at)
+        move_on(0, at)
     (grad_in, grad_conv), (sum_gate,), (sum_out,) = results
     grad_conv = grad_conv.reshape(conv_w.shape)
     return output, grad_in, sum_gate, sum_out, grad_conv

time: 143 us -> 146 us (1.021)
  waiting for transfers between devices: 43.1 us -> 50.5 us
  starting transfers between devices: 59.4 us -> 54.2 us
  Pallas kernels: 34.6 us -> 36.8 us
  local copies, waits for them, and re-layouts: 4.37 us -> 2.2 us
    ppermute x6, waiting for transfers between devices: 2.85 us -> 10.9 us  [swap_edges(): received.append(lax.ppermute(block, ('seq', 'ch'), route))]
    ppermute x6, starting transfers between devices: 12 us -> 6.32 us  [swap_edges(): received.append(lax.ppermute(block, ('seq', 'ch'), route))]
    ppermute x36, starting transfers between devices: 37 us -> 41.3 us  [exchange(): return lax.ppermute(block, axis, [(i, i ^ distance) for i in range(count)])]
    ppermute x2, starting transfers between devices: 10.4 us -> 6.56 us  [mirror(): lax.ppermute(block, 'seq', [(i, count - 1 - i) for i in range(count)])]
    pallas_call x26 -> x25, Pallas kernels: 34.6 us -> 36.8 us  [run(): pl.pallas_call(body, out_shape=[jax.ShapeDtypeStruct(shape, dtype) for sh...]
    unnamed x20 -> x41, local copies, waits for them, and re-layouts: 3.76 us -> 1.58 us
  transfers between devices with their start and end apart: 44 -> 44, of which waited for: 19 -> 18; matrix products, arithmetic and copies ran while one was open for 0% -> 0% of each run, Pallas kernels for 19% -> 17%
where the time goes in v11:
time: 146 us; the launch traced here: 145 us
  starting transfers between devices  54.2 us (37%)
  waiting for transfers between devices  50.5 us (35%)
  Pallas kernels  36.8 us (25%)
  local copies, waits for them, and re-layouts  2.2 us (2%)
    ppermute x36, starting transfers between devices, exchange(): return lax.ppermute(block, axis, [(i, i ^ distance) for i in range(count)])  41.3 us
    pallas_call x25, Pallas kernels, run(): pl.pallas_call(body, out_shape=[jax.ShapeDtypeStruct(shape, dtype) for sh...  36.8 us
    ppermute x36, waiting for transfers between devices, exchange(): return lax.ppermute(block, axis, [(i, i ^ distance) for i in range(count)])  32 us
    ppermute x6, waiting for transfers between devices, swap_edges(): received.append(lax.ppermute(block, ('seq', 'ch'), route))  10.9 us
    ppermute x2, waiting for transfers between devices, mirror(): lax.ppermute(block, 'seq', [(i, count - 1 - i) for i in range(count)])  7.61 us
    ppermute x2, starting transfers between devices, mirror(): lax.ppermute(block, 'seq', [(i, count - 1 - i) for i in range(count)])  6.56 us
    ppermute x6, starting transfers between devices, swap_edges(): received.append(lax.ppermute(block, ('seq', 'ch'), route))  6.32 us
  transfers between devices with their start and end apart: 44, of which 18 were waited for; matrix products, arithmetic and copies ran while one was open for 0% of the time, Pallas kernels for 17%

profile of v11, /device:TPU:0, one launch (start us, length us, event | category | flops | bytes accessed | tf_op | source)
XLA Modules:
  0.0 145.5 jit_solution(13911348313257250071)
XLA Ops:
  1.2 2.7 %shard_map.137 = (bf16[512,256]{1,0:T(8,128)(2,1)}, bf16[160,256]{1,0:T(8,128)(2,1)}, bf16[160,256]{1,0:T(8,128)(2,1)}) custom-call(s32[3]{0:T(128)} %pad_add_fusion.place, s32[1,512]{1,0:T(1,128)} %bitcast.7, bf16[512,256]{1,0:T(8,128)(2,1)} %hidden_hbm.1, bf16[4,256]{1,0:T(4,128)(2,1)} %embedding_hbm.1), custom_call_target="tpu_custom_call" | custom-call | flops 100000000 | bytes 266240 | tf_op jit(solution)/shard_map/pallas_call | solution.py:30
  3.9 3.0 %collective-permute-start = (bf16[512,256]{1,0:T(8,128)(2,1)}, bf16[512,256]{1,0:T(8,128)(2,1)S(1)}, u32[]{:S(2)}, u32[]{:S(2)}) collective-permute-start(bf16[512,256]{1,0:T(8,128)(2,1)} %get-tuple-element.71.refs_5_.block_in.refs_0_), channel_id=1, source_target_pairs={{0,2},{1,3},{2,0},{3,1},{4,6},{5,7},{6,4},{7,5},{8,10},{9,11},{10,... | collective-permute-start | bytes 786440 | tf_op jit(solution)/shard_map/ppermute | solution.py:362
  7.0 5.0 %collective-permute-start.11 = (bf16[512,256]{1,0:T(8,128)(2,1)}, bf16[512,256]{1,0:T(8,128)(2,1)S(1)}, u32[]{:S(2)}, u32[]{:S(2)}) collective-permute-start(bf16[512,256]{1,0:T(8,128)(2,1)} %cotangent.1), channel_id=1, source_target_pairs={{0,28},{4,24},{8,20},{12,16},{16,12},{20,8},{24,4},{28,0},{1,29},{... | collective-permute-start | bytes 786440 | tf_op jit(solution)/shard_map/ppermute | solution.py:371
  13.2 7.4 %collective-permute-done.2 = bf16[160,256]{1,0:T(8,128)(2,1)S(1)} collective-permute-done((bf16[160,256]{1,0:T(8,128)(2,1)}, bf16[160,256]{1,0:T(8,128)(2,1)S(1)}, u32[]{:S(2)}, u32[]{:S(2)}) %collective-permute-start.2) | collective-permute-done | bytes 81952 | tf_op jit(solution)/shard_map/ppermute | solution.py:383
  20.6 3.3 %collective-permute-start.4 = (bf16[160,256]{1,0:T(8,128)(2,1)}, bf16[160,256]{1,0:T(8,128)(2,1)S(1)}, u32[]{:S(2)}, u32[]{:S(2)}) collective-permute-start(bf16[160,256]{1,0:T(8,128)(2,1)} %get-tuple-element.72), channel_id=1, source_target_pairs={{0,6},{4,2},{1,7},{5,3},{2,4},{6,0},{3,5},{7,1},{8,14},{12,10},{9,... | collective-permute-start | bytes 245768 | tf_op jit(solution)/shard_map/ppermute | solution.py:383
  25.3 1.8 %collective-permute-done.4 = bf16[160,256]{1,0:T(8,128)(2,1)S(1)} collective-permute-done((bf16[160,256]{1,0:T(8,128)(2,1)}, bf16[160,256]{1,0:T(8,128)(2,1)S(1)}, u32[]{:S(2)}, u32[]{:S(2)}) %collective-permute-start.4) | collective-permute-done | bytes 81952 | tf_op jit(solution)/shard_map/ppermute | solution.py:383
  27.8 6.7 %collective-permute-done.12.refs_6_ = bf16[512,256]{1,0:T(8,128)(2,1)S(1)} collective-permute-done((bf16[512,256]{1,0:T(8,128)(2,1)S(1)}, bf16[512,256]{1,0:T(8,128)(2,1)S(1)}, u32[]{:S(2)}, u32[]{:S(2)}) %collective-permute-start.12) | collective-permute-done | bytes 262176 | tf_op jit(solution)/shard_map/ppermute | solution.py:362
  37.4 5.3 %shard_map.138 = (f32[512,256]{1,0:T(8,128)}, bf16[2192,256]{1,0:T(8,128)(2,1)}, bf16[512,256]{1,0:T(8,128)(2,1)}, bf16[512,256]{1,0:T(8,128)(2,1)}) custom-call(s32[3]{0:T(128)} %pad_add_fusion.place, bf16[1024,256]{1,0:T(8,128)(2,1)} %refs_0_.2, bf16[1024,256]{1,0:T(8,128)(2,1)} %refs_1_.1, f32[3,4,256]{2,1,0:T(4,128)} %conv_w.1, ...), custom_call_target="tpu_custom_call" | custom-call | flops 1000000000 | bytes 2764800 | tf_op jit(solution)/shard_map/pallas_call | solution.py:30
  45.3 7.6 %collective-permute-done.10.block = bf16[512,256]{1,0:T(8,128)(2,1)S(1)} collective-permute-done((bf16[512,256]{1,0:T(8,128)(2,1)}, bf16[512,256]{1,0:T(8,128)(2,1)S(1)}, u32[]{:S(2)}, u32[]{:S(2)}) %collective-permute-start.10) | collective-permute-done | bytes 262176 | tf_op jit(solution)/shard_map/ppermute | solution.py:371
  56.4 3.7 %shard_map.140 = (bf16[1024,1024]{1,0:T(8,128)(2,1)S(1)}, bf16[512,256]{1,0:T(8,128)(2,1)S(1)}, bf16[1024,1024]{1,0:T(8,128)(2,1)S(1)}) custom-call(s32[3]{0:T(128)S(1)} %copy-done.10, bf16[512,256]{1,0:T(8,128)(2,1)S(1)} %copy-done.9, bf16[512,256]{1,0:T(8,128)(2,1)S(1)} %collective-permute-done.18.refs_1_, ...), custom_call_target="tpu_custom_call" | custom-call | flops 2100000000 | bytes 4198400 | tf_op jit(solution)/shard_map/pallas_call | solution.py:30
  60.1 3.1 %collective-permute-done.17.refs_6_ = bf16[512,256]{1,0:T(8,128)(2,1)S(1)} collective-permute-done((bf16[512,256]{1,0:T(8,128)(2,1)S(1)}, bf16[512,256]{1,0:T(8,128)(2,1)S(1)}, u32[]{:S(2)}, u32[]{:S(2)}) %collective-permute-start.17) | collective-permute-done | bytes 262176 | tf_op jit(solution)/shard_map/ppermute | solution.py:362
  64.8 5.8 %shard_map.141 = (bf16[1024,1024]{1,0:T(8,128)(2,1)S(1)}, bf16[512,256]{1,0:T(8,128)(2,1)S(1)}, bf16[512,256]{1,0:T(8,128)(2,1)S(1)}, bf16[160,256]{1,0:T(8,128)(2,1)S(1)}, bf16[160,256]{1,0:T(8,128)(2,1)S(1)}) custom-call(s32[3]{0:T(128)S(1)} %copy-done.10, bf16[512,256]{1,0:T(8,128)(2,1)S(1)} %copy-done.12, ...), custom_call_target="tpu_custom_call" | custom-call | flops 2500000000 | bytes 7081984 | tf_op jit(solution)/shard_map/pallas_call | solution.py:30
  75.2 7.1 %collective-permute-start.27 = (bf16[512,256]{1,0:T(8,128)(2,1)S(1)}, bf16[512,256]{1,0:T(8,128)(2,1)S(1)}, u32[]{:S(2)}, u32[]{:S(2)}) collective-permute-start(bf16[512,256]{1,0:T(8,128)(2,1)S(1)} %get-tuple-element.105), channel_id=1, source_target_pairs={{0,4},{4,0},{8,12},{12,8},{16,20},{20,16},{24,28},{28,24},{1,5},{5... | collective-permute-start | bytes 786440 | tf_op jit(solution)/shard_map/ppermute | solution.py:362
  82.3 2.6 %collective-permute-start.28 = (bf16[256,256]{1,0:T(8,128)(2,1)S(1)}, bf16[256,256]{1,0:T(8,128)(2,1)S(1)}, u32[]{:S(2)}, u32[]{:S(2)}) collective-permute-start(bf16[256,256]{1,0:T(8,128)(2,1)S(1)} %get-tuple-element.108), channel_id=1, source_target_pairs={{0,8},{4,12},{8,0},{12,4},{16,24},{20,28},{24,16},{28,20},{1,9},{5... | collective-permute-start | bytes 393224 | tf_op jit(solution)/shard_map/ppermute | solution.py:362
  84.9 2.5 %shard_map.144 = (bf16[576,256]{1,0:T(8,128)(2,1)S(1)}, f32[576,256]{1,0:T(8,128)S(1)}) custom-call(s32[3]{0:T(128)S(1)} %copy-done.10, bf16[512,256]{1,0:T(8,128)(2,1)S(1)} %get-tuple-element.92.upstream, bf16[160,256]{1,0:T(8,128)(2,1)S(1)} %collective-permute-done.25.first, bf16[160,256]{1,0:T(8,128)(2,1)S(1)} %collective-permute-done.26.second, ...), custom_call_target="tpu_custom_call" | custom-call | flops 500000000 | bytes 2609152 | tf_op jit(solution)/shard_map/pallas_call | solution.py:30
  90.5 2.0 %collective-permute-start.30 = (bf16[256,256]{1,0:T(8,128)(2,1)S(1)}, bf16[256,256]{1,0:T(8,128)(2,1)S(1)}, u32[]{:S(2)}, u32[]{:S(2)}) collective-permute-start(bf16[256,256]{1,0:T(8,128)(2,1)S(1)} %get-tuple-element.114), channel_id=1, source_target_pairs={{0,8},{4,12},{8,0},{12,4},{16,24},{20,28},{24,16},{28,20},{1,9},{5... | collective-permute-start | bytes 393224 | tf_op jit(solution)/shard_map/ppermute | solution.py:362
  94.0 3.7 %collective-permute-done.31.refs_1_ = bf16[128,256]{1,0:T(8,128)(2,1)S(1)} collective-permute-done((bf16[128,256]{1,0:T(8,128)(2,1)S(1)}, bf16[128,256]{1,0:T(8,128)(2,1)S(1)}, u32[]{:S(2)}, u32[]{:S(2)}) %collective-permute-start.31) | collective-permute-done | bytes 65568 | tf_op jit(solution)/shard_map/ppermute | solution.py:362
  99.5 2.1 %collective-permute-start.32 = (bf16[288,256]{1,0:T(8,128)(2,1)S(1)}, bf16[288,256]{1,0:T(8,128)(2,1)S(1)}, u32[]{:S(2)}, u32[]{:S(2)}) collective-permute-start(bf16[288,256]{1,0:T(8,128)(2,1)S(1)} %get-tuple-element.118), channel_id=1, source_target_pairs={{0,8},{4,12},{8,0},{12,4},{16,24},{20,28},{24,16},{28,20},{1,9},{5... | collective-permute-start | bytes 442376 | tf_op jit(solution)/shard_map/ppermute | solution.py:362
  104.5 2.7 %collective-permute-done.34.refs_1_ = bf16[128,256]{1,0:T(8,128)(2,1)S(1)} collective-permute-done((bf16[128,256]{1,0:T(8,128)(2,1)S(1)}, bf16[128,256]{1,0:T(8,128)(2,1)S(1)}, u32[]{:S(2)}, u32[]{:S(2)}) %collective-permute-start.34) | collective-permute-done | bytes 65568 | tf_op jit(solution)/shard_map/ppermute | solution.py:362
  113.0 2.3 %collective-permute-done.36.refs_1_ = bf16[128,256]{1,0:T(8,128)(2,1)S(1)} collective-permute-done((bf16[128,256]{1,0:T(8,128)(2,1)S(1)}, bf16[128,256]{1,0:T(8,128)(2,1)S(1)}, u32[]{:S(2)}, u32[]{:S(2)}) %collective-permute-start.36) | collective-permute-done | bytes 65568 | tf_op jit(solution)/shard_map/ppermute | solution.py:362
  118.8 2.4 %collective-permute-start.40 = (bf16[512,256]{1,0:T(8,128)(2,1)S(1)}, bf16[512,256]{1,0:T(8,128)(2,1)S(1)}, u32[]{:S(2)}, u32[]{:S(2)}) collective-permute-start(bf16[512,256]{1,0:T(8,128)(2,1)S(1)} %shard_map.155.refs_0_), channel_id=1, source_target_pairs={{0,4},{4,0},{8,12},{12,8},{16,20},{20,16},{24,28},{28,24},{1,5},{5... | collective-permute-start | bytes 786440 | tf_op jit(solution)/shard_map/ppermute | solution.py:362
  121.2 2.5 %collective-permute-start.38 = (bf16[144,256]{1,0:T(8,128)(2,1)S(1)}, bf16[144,256]{1,0:T(8,128)(2,1)S(1)}, u32[]{:S(2)}, u32[]{:S(2)}) collective-permute-start(bf16[144,256]{1,0:T(8,128)(2,1)S(1)} %shard_map.153.refs_0_), channel_id=1, source_target_pairs={{0,16},{4,20},{8,24},{12,28},{16,0},{20,4},{24,8},{28,12},{1,17},{... | collective-permute-start | bytes 221192 | tf_op jit(solution)/shard_map/ppermute | solution.py:362
  123.7 2.8 %collective-permute-done.38.refs_1_ = bf16[144,256]{1,0:T(8,128)(2,1)S(1)} collective-permute-done((bf16[144,256]{1,0:T(8,128)(2,1)S(1)}, bf16[144,256]{1,0:T(8,128)(2,1)S(1)}, u32[]{:S(2)}, u32[]{:S(2)}) %collective-permute-start.38) | collective-permute-done | bytes 73760 | tf_op jit(solution)/shard_map/ppermute | solution.py:362
  131.2 3.6 %collective-permute-done.41.refs_1_ = bf16[288,256]{1,0:T(8,128)(2,1)S(1)} collective-permute-done((bf16[288,256]{1,0:T(8,128)(2,1)S(1)}, bf16[288,256]{1,0:T(8,128)(2,1)S(1)}, u32[]{:S(2)}, u32[]{:S(2)}) %collective-permute-start.41) | collective-permute-done | bytes 147488 | tf_op jit(solution)/shard_map/ppermute | solution.py:362
  (133 shorter events, 52.5 us)
Async XLA Ops:
  3.9 20.7 %collective-permute-start = (bf16[512,256]{1,0:T(8,128)(2,1)}, bf16[512,256]{1,0:T(8,128)(2,1)S(1)}, u32[]{:S(2)}, u32[]{:S(2)}) collective-permute-start(bf16[512,256]{1,0:T(8,128)(2,1)} %get-tuple-element.71.refs_5_.block_in.refs_0_), channel_id=1, source_target_pairs={{0,2},{1,3},{2,0},{3,1},{4,6},{5,7},{6,4},{7,5},{8,10},{9,11},{10,... | collective-permute-start | bytes 786440 | tf_op jit(solution)/shard_map/ppermute | solution.py:362
  6.9 17.7 %collective-permute-start.1 = (bf16[512,256]{1,0:T(8,128)(2,1)}, bf16[512,256]{1,0:T(8,128)(2,1)S(1)}, u32[]{:S(2)}, u32[]{:S(2)}) collective-permute-start(bf16[512,256]{1,0:T(8,128)(2,1)} %cotangent.1), channel_id=1, source_target_pairs={{0,2},{1,3},{2,0},{3,1},{4,6},{5,7},{6,4},{7,5},{8,10},{9,11},{10,... | collective-permute-start | bytes 786440 | tf_op jit(solution)/shard_map/ppermute | solution.py:362
  7.0 17.7 %collective-permute-start.11 = (bf16[512,256]{1,0:T(8,128)(2,1)}, bf16[512,256]{1,0:T(8,128)(2,1)S(1)}, u32[]{:S(2)}, u32[]{:S(2)}) collective-permute-start(bf16[512,256]{1,0:T(8,128)(2,1)} %cotangent.1), channel_id=1, source_target_pairs={{0,28},{4,24},{8,20},{12,16},{16,12},{20,8},{24,4},{28,0},{1,29},{... | collective-permute-start | bytes 786440 | tf_op jit(solution)/shard_map/ppermute | solution.py:371
  12.0 8.6 %collective-permute-start.2 = (bf16[160,256]{1,0:T(8,128)(2,1)}, bf16[160,256]{1,0:T(8,128)(2,1)S(1)}, u32[]{:S(2)}, u32[]{:S(2)}) collective-permute-start(bf16[160,256]{1,0:T(8,128)(2,1)} %get-tuple-element.72), channel_id=1, source_target_pairs={{0,4},{4,0},{1,5},{5,1},{2,6},{6,2},{3,7},{7,3},{8,12},{12,8},{9,1... | collective-permute-start | bytes 245768 | tf_op jit(solution)/shard_map/ppermute | solution.py:383
  12.5 11.4 %collective-permute-start.3 = (bf16[160,256]{1,0:T(8,128)(2,1)}, bf16[160,256]{1,0:T(8,128)(2,1)S(1)}, u32[]{:S(2)}, u32[]{:S(2)}) collective-permute-start(bf16[160,256]{1,0:T(8,128)(2,1)} %get-tuple-element.73), channel_id=1, source_target_pairs={{4,8},{8,4},{5,9},{9,5},{6,10},{10,6},{7,11},{11,7},{12,16},{16,12... | collective-permute-start | bytes 245768 | tf_op jit(solution)/shard_map/ppermute | solution.py:383
  24.7 9.8 %collective-permute-start.12 = (bf16[512,256]{1,0:T(8,128)(2,1)S(1)}, bf16[512,256]{1,0:T(8,128)(2,1)S(1)}, u32[]{:S(2)}, u32[]{:S(2)}) collective-permute-start(bf16[512,256]{1,0:T(8,128)(2,1)S(1)} %collective-permute-done.11.refs_4_), channel_id=1, source_target_pairs={{0,2},{1,3},{2,0},{3,1},{4,6},{5,7},{6,4},{7,5},{8,10},{9,11},{10,... | collective-permute-start | bytes 786440 | tf_op jit(solution)/shard_map/ppermute | solution.py:362
  27.1 8.8 %collective-permute-start.6 = (bf16[640,256]{1,0:T(8,128)(2,1)S(1)}, bf16[640,256]{1,0:T(8,128)(2,1)S(1)}, u32[]{:S(2)}, u32[]{:S(2)}) collective-permute-start(bf16[640,256]{1,0:T(8,128)(2,1)S(1)} %constant_dynamic-update-slice_fusion.refs_3_), channel_id=1, source_target_pairs={{0,1},{1,0},{2,3},{3,2},{4,5},{5,4},{6,7},{7,6},{8,9},{9,8},{10,11... | collective-permute-start | bytes 983048 | tf_op jit(solution)/shard_map/ppermute | solution.py:362
  27.2 8.7 %collective-permute-start.7 = (bf16[512,256]{1,0:T(8,128)(2,1)}, bf16[512,256]{1,0:T(8,128)(2,1)S(1)}, u32[]{:S(2)}, u32[]{:S(2)}) collective-permute-start(bf16[512,256]{1,0:T(8,128)(2,1)} %get-tuple-element.71.refs_5_.block_in.refs_0_), channel_id=1, source_target_pairs={{0,1},{1,0},{2,3},{3,2},{4,5},{5,4},{6,7},{7,6},{8,9},{9,8},{10,11... | collective-permute-start | bytes 786440 | tf_op jit(solution)/shard_map/ppermute | solution.py:362
  27.7 8.2 %collective-permute-start.8 = (bf16[512,256]{1,0:T(8,128)(2,1)S(1)}, bf16[512,256]{1,0:T(8,128)(2,1)S(1)}, u32[]{:S(2)}, u32[]{:S(2)}) collective-permute-start(bf16[512,256]{1,0:T(8,128)(2,1)S(1)} %collective-permute-done.refs_7_.refs_2_), channel_id=1, source_target_pairs={{0,1},{1,0},{2,3},{3,2},{4,5},{5,4},{6,7},{7,6},{8,9},{9,8},{10,11... | collective-permute-start | bytes 786440 | tf_op jit(solution)/shard_map/ppermute | solution.py:362
  34.5 18.5 %collective-permute-start.13 = (bf16[1024,256]{1,0:T(8,128)(2,1)}, bf16[1024,256]{1,0:T(8,128)(2,1)S(1)}, u32[]{:S(2)}, u32[]{:S(2)}) collective-permute-start(bf16[1024,256]{1,0:T(8,128)(2,1)} %w_out.1), channel_id=1, source_target_pairs={{0,2},{1,3},{2,0},{3,1},{4,6},{5,7},{6,4},{7,5},{8,10},{9,11},{10,... | collective-permute-start | bytes 1572872 | tf_op jit(solution)/shard_map/ppermute | solution.py:362
  42.8 10.2 %collective-permute-start.10 = (bf16[512,256]{1,0:T(8,128)(2,1)}, bf16[512,256]{1,0:T(8,128)(2,1)S(1)}, u32[]{:S(2)}, u32[]{:S(2)}) collective-permute-start(bf16[512,256]{1,0:T(8,128)(2,1)} %get-tuple-element.77.refs_0_), channel_id=1, source_target_pairs={{0,28},{4,24},{8,20},{12,16},{16,12},{20,8},{24,4},{28,0},{1,29},{... | collective-permute-start | bytes 786440 | tf_op jit(solution)/shard_map/ppermute | solution.py:371
  44.3 9.1 %collective-permute-start.18 = (bf16[512,256]{1,0:T(8,128)(2,1)S(1)}, bf16[512,256]{1,0:T(8,128)(2,1)S(1)}, u32[]{:S(2)}, u32[]{:S(2)}) collective-permute-start(bf16[512,256]{1,0:T(8,128)(2,1)S(1)} %copy-done.9), channel_id=1, source_target_pairs={{0,1},{1,0},{2,3},{3,2},{4,5},{5,4},{6,7},{7,6},{8,9},{9,8},{10,11... | collective-permute-start | bytes 786440 | tf_op jit(solution)/shard_map/ppermute | solution.py:362
  44.3 9.2 %collective-permute-start.14 = (bf16[512,256]{1,0:T(8,128)(2,1)}, bf16[512,256]{1,0:T(8,128)(2,1)S(1)}, u32[]{:S(2)}, u32[]{:S(2)}) collective-permute-start(bf16[512,256]{1,0:T(8,128)(2,1)} %get-tuple-element.77.refs_0_), channel_id=1, source_target_pairs={{0,2},{1,3},{2,0},{3,1},{4,6},{5,7},{6,4},{7,5},{8,10},{9,11},{10,... | collective-permute-start | bytes 786440 | tf_op jit(solution)/shard_map/ppermute | solution.py:362
  45.1 10.8 %collective-permute-start.22 = (bf16[1024,256]{1,0:T(8,128)(2,1)S(1)}, bf16[1024,256]{1,0:T(8,128)(2,1)S(1)}, u32[]{:S(2)}, u32[]{:S(2)}) collective-permute-start(bf16[1024,256]{1,0:T(8,128)(2,1)S(1)} %copy-done.8), channel_id=1, source_target_pairs={{0,1},{1,0},{2,3},{3,2},{4,5},{5,4},{6,7},{7,6},{8,9},{9,8},{10,11... | collective-permute-start | bytes 1572872 | tf_op jit(solution)/shard_map/ppermute | solution.py:362
  54.8 8.3 %collective-permute-start.17 = (bf16[512,256]{1,0:T(8,128)(2,1)S(1)}, bf16[512,256]{1,0:T(8,128)(2,1)S(1)}, u32[]{:S(2)}, u32[]{:S(2)}) collective-permute-start(bf16[512,256]{1,0:T(8,128)(2,1)S(1)} %shard_map.139.refs_4_), channel_id=1, source_target_pairs={{0,2},{1,3},{2,0},{3,1},{4,6},{5,7},{6,4},{7,5},{8,10},{9,11},{10,... | collective-permute-start | bytes 786440 | tf_op jit(solution)/shard_map/ppermute | solution.py:362
  55.6 7.5 %collective-permute-start.9 = (bf16[512,256]{1,0:T(8,128)(2,1)S(1)}, bf16[512,256]{1,0:T(8,128)(2,1)S(1)}, u32[]{:S(2)}, u32[]{:S(2)}) collective-permute-start(bf16[512,256]{1,0:T(8,128)(2,1)S(1)} %copy-done.12), channel_id=1, source_target_pairs={{0,1},{1,0},{2,3},{3,2},{4,5},{5,4},{6,7},{7,6},{8,9},{9,8},{10,11... | collective-permute-start | bytes 786440 | tf_op jit(solution)/shard_map/ppermute | solution.py:362
  55.9 7.3 %collective-permute-start.16 = (bf16[512,256]{1,0:T(8,128)(2,1)S(1)}, bf16[512,256]{1,0:T(8,128)(2,1)S(1)}, u32[]{:S(2)}, u32[]{:S(2)}) collective-permute-start(bf16[512,256]{1,0:T(8,128)(2,1)S(1)} %shard_map.139.refs_4_), channel_id=1, source_target_pairs={{0,1},{1,0},{2,3},{3,2},{4,5},{5,4},{6,7},{7,6},{8,9},{9,8},{10,11... | collective-permute-start | bytes 786440 | tf_op jit(solution)/shard_map/ppermute | solution.py:362
  75.2 13.3 %collective-permute-start.27 = (bf16[512,256]{1,0:T(8,128)(2,1)S(1)}, bf16[512,256]{1,0:T(8,128)(2,1)S(1)}, u32[]{:S(2)}, u32[]{:S(2)}) collective-permute-start(bf16[512,256]{1,0:T(8,128)(2,1)S(1)} %get-tuple-element.105), channel_id=1, source_target_pairs={{0,4},{4,0},{8,12},{12,8},{16,20},{20,16},{24,28},{28,24},{1,5},{5... | collective-permute-start | bytes 786440 | tf_op jit(solution)/shard_map/ppermute | solution.py:362
  89.1 9.8 %collective-permute-start.29 = (bf16[576,256]{1,0:T(8,128)(2,1)S(1)}, bf16[576,256]{1,0:T(8,128)(2,1)S(1)}, u32[]{:S(2)}, u32[]{:S(2)}) collective-permute-start(bf16[576,256]{1,0:T(8,128)(2,1)S(1)} %get-tuple-element.110), channel_id=1, source_target_pairs={{0,4},{4,0},{8,12},{12,8},{16,20},{20,16},{24,28},{28,24},{1,5},{5... | collective-permute-start | bytes 884744 | tf_op jit(solution)/shard_map/ppermute | solution.py:362
  90.5 7.7 %collective-permute-start.30 = (bf16[256,256]{1,0:T(8,128)(2,1)S(1)}, bf16[256,256]{1,0:T(8,128)(2,1)S(1)}, u32[]{:S(2)}, u32[]{:S(2)}) collective-permute-start(bf16[256,256]{1,0:T(8,128)(2,1)S(1)} %get-tuple-element.114), channel_id=1, source_target_pairs={{0,8},{4,12},{8,0},{12,4},{16,24},{20,28},{24,16},{28,20},{1,9},{5... | collective-permute-start | bytes 393224 | tf_op jit(solution)/shard_map/ppermute | solution.py:362
  99.5 9.8 %collective-permute-start.32 = (bf16[288,256]{1,0:T(8,128)(2,1)S(1)}, bf16[288,256]{1,0:T(8,128)(2,1)S(1)}, u32[]{:S(2)}, u32[]{:S(2)}) collective-permute-start(bf16[288,256]{1,0:T(8,128)(2,1)S(1)} %get-tuple-element.118), channel_id=1, source_target_pairs={{0,8},{4,12},{8,0},{12,4},{16,24},{20,28},{24,16},{28,20},{1,9},{5... | collective-permute-start | bytes 442376 | tf_op jit(solution)/shard_map/ppermute | solution.py:362
  109.9 8.2 %collective-permute-start.37 = (bf16[256,256]{1,0:T(8,128)(2,1)S(1)}, bf16[256,256]{1,0:T(8,128)(2,1)S(1)}, u32[]{:S(2)}, u32[]{:S(2)}) collective-permute-start(bf16[256,256]{1,0:T(8,128)(2,1)S(1)} %shard_map.152.refs_0_), channel_id=1, source_target_pairs={{0,8},{4,12},{8,0},{12,4},{16,24},{20,28},{24,16},{28,20},{1,9},{5... | collective-permute-start | bytes 393224 | tf_op jit(solution)/shard_map/ppermute | solution.py:362
  118.8 9.4 %collective-permute-start.40 = (bf16[512,256]{1,0:T(8,128)(2,1)S(1)}, bf16[512,256]{1,0:T(8,128)(2,1)S(1)}, u32[]{:S(2)}, u32[]{:S(2)}) collective-permute-start(bf16[512,256]{1,0:T(8,128)(2,1)S(1)} %shard_map.155.refs_0_), channel_id=1, source_target_pairs={{0,4},{4,0},{8,12},{12,8},{16,20},{20,16},{24,28},{28,24},{1,5},{5... | collective-permute-start | bytes 786440 | tf_op jit(solution)/shard_map/ppermute | solution.py:362
  128.2 8.5 %collective-permute-start.42 = (bf16[512,256]{1,0:T(8,128)(2,1)S(1)}, bf16[512,256]{1,0:T(8,128)(2,1)S(1)}, u32[]{:S(2)}, u32[]{:S(2)}) collective-permute-start(bf16[512,256]{1,0:T(8,128)(2,1)S(1)} %shard_map.157.refs_0_), channel_id=1, source_target_pairs={{0,4},{4,0},{8,12},{12,8},{16,20},{20,16},{24,28},{28,24},{1,5},{5... | collective-permute-start | bytes 786440 | tf_op jit(solution)/shard_map/ppermute | solution.py:362
  (39 other events, 293.9 us)

commit v12 on v10

--- a/solution.py
+++ b/solution.py
@@ -83,6 +83,17 @@
     odd, far = place[0] % 2, rows - EDGE
     first[...] = block_in[pl.ds(pl.multiple_of((1 - odd) * far, 16), EDGE), :]
     second[...] = block_in[pl.ds(pl.multiple_of(odd * far, 16), EDGE), :]
+
+
+def setup_kernel(width, place, order, choose):
+    me, full = place[1], order.shape[1]
+    down = lax.broadcasted_iota(jnp.int32, (width, width), 0)
+    for j in range(full // width):
+        for i in range(full // width):
+            wanted = order[:, part(me ^ i, width)]
+            choose[j * width : (j + 1) * width, i * width : (i + 1) * width] = (
+                (down + (me ^ j) * width == wanted).astype(F32).astype(BF16)
+            )
 
 
 def project_kernel(channels, place, *refs):
@@ -145,27 +156,15 @@
 
 def norm_grad_kernel(channels, place, *refs):
     own, mirrored = refs[:channels], refs[channels : 2 * channels]
-    *weights, order, out, flipped, choose, scratch = refs[2 * channels :]
+    *weights, out = refs[2 * channels :]
     me = place[1]
     rows, width = own[0].shape
-    turn = anti_identity(rows)
-    flipped[...] = dot(turn, mirrored[0][...]).astype(BF16)
-    for j in range(1, channels):
-        scratch[j] = dot(turn, mirrored[j][...]).astype(BF16)
-    for block in range(2):
+    for block, cotangents in enumerate((own, mirrored)):
         for i in range(channels):
             total = jnp.zeros((rows, width), F32)
             for j in range(channels):
-                cotangent = own[j][...] if block == 0 else scratch[j] if j else flipped[...]
-                total += dot(cotangent, weights[j][part(i ^ me, width), :], LAST_DOT)
+                total += dot(cotangents[j][...], weights[j][part(i ^ me, width), :], LAST_DOT)
             out[block * rows : (block + 1) * rows, i * width : (i + 1) * width] = total.astype(BF16)
-    down = lax.broadcasted_iota(jnp.int32, (width, width), 0)
-    for j in range(channels):
-        for i in range(channels):
-            wanted = order[:, part(me ^ i, width)]
-            choose[j * width : (j + 1) * width, i * width : (i + 1) * width] = (
-                (down + (me ^ j) * width == wanted).astype(F32).astype(BF16)
-            )
 
 
 def combine_kernel(channels, place, *refs):
@@ -218,7 +217,7 @@
 def products_kernel(channels, place, normalized, cotangent, mirrored_cotangent, grad_gate_pre, *refs):
     mains = refs[:channels]
     out_sent, out_kept, gate_sent, gate_kept, whole_out, whole_gate = refs[channels:]
-    me, side = place[1], place[0] % 2
+    me, side = place[1], (place[0] // 2) % 2
     rows, width = cotangent.shape
     for j in range(channels // 2):
         block = (side * (channels // 2) + j) ^ me
@@ -227,14 +226,14 @@
             normalized[:rows, columns], cotangent[...], ROWS_DOT
         ) + dot(normalized[rows:, columns], mirrored_cotangent[...], ROWS_DOT)
     half = whole_out.shape[0] // 2
-    bit = (place[0] // 2) % 2
+    bit = place[0] % 2
     out_sent[...] = whole_out[part(1 - bit, half), :].astype(BF16)
     out_kept[...] = whole_out[part(bit, half), :]
     for j in range(channels):
         whole_gate[part(me ^ j, width), :] = dot(mains[j][...], grad_gate_pre[...], ROWS_DOT)
     half = whole_gate.shape[0] // 2
-    gate_sent[...] = whole_gate[part(1 - side, half), :].astype(BF16)
-    gate_kept[...] = whole_gate[part(side, half), :]
+    gate_sent[...] = whole_gate[part(1 - bit, half), :].astype(BF16)
+    gate_kept[...] = whole_gate[part(bit, half), :]
 
 
 def backward_kernel(channels, place, upstream, first, second, conv_w, *refs):
@@ -418,14 +417,22 @@
     )
     input_x = exchange(local_input, "ch", cross)
     input_core = exchange(local_input, "ch", 1)
+    choose = run(
+        functools.partial(setup_kernel, width),
+        place,
+        (channel_order.reshape(1, full),),
+        [((full, full), BF16)],
+        gflop=2.0,
+    )[0]
     first, second, cotangent_x = together(first, second, cotangent_x)
     near = swap_edges(first, second)
+    first, second, mirrored_cotangent = together(first, second, mirrored_cotangent)
     far = swap_edges(first, second, cross)
-    mirrored_cotangent, *far = together(mirrored_cotangent, *far)
     edges = jnp.concatenate(near + far, axis=0)
-    mirrored_cotangent_x = exchange(mirrored_cotangent, "ch", cross)
-    early_w_out, mirrored_cotangent_x = together(w_out, mirrored_cotangent_x)
+    early_w_out, input_x = together(w_out, input_x)
     w_out_x = exchange(early_w_out, "ch", cross)
+    mirrored_cotangent = run(flip_kernel, place, (mirrored_cotangent,), [block], gflop=1.0)[0]
+    mirrored_cotangent, input_core, choose = together(mirrored_cotangent, input_core, choose)
     mains = [local_input, input_core, input_x, exchange(input_x, "ch", 1)]
 
     projected, gate_pre, w_in_on = run(
@@ -435,7 +442,6 @@
         [((rows, width), F32)] * 2 + [(w_in.shape, BF16)],
         gflop=6.0,
     )
-    edges, projected, gate_pre = together(edges, projected, gate_pre)
     edges_core = exchange(edges, "ch", 1)
     levels, level_3, gated = run(
         functools.partial(forward_kernel, channels),
@@ -445,10 +451,11 @@
         [pltpu.VMEM((saved_rows(rows, number), width), F32) for number in range(4)],
         gflop=0.4,
     )
-    mirrored, w_out_x = together(mirror(gated), w_out_x)
-    mirrored = run(flip_kernel, place, (mirrored,), [block], gflop=12.0)[0]
+    mirrored = run(flip_kernel, place, (mirror(gated),), [block], gflop=12.0)[0]
     gated_x = exchange(gated, "ch", cross)
-    mirrored, gated_x = together(mirrored, gated_x)
+    mirrored_cotangent, w_out_x = together(mirrored_cotangent, w_out_x)
+    mirrored_cotangent_x = exchange(mirrored_cotangent, "ch", cross)
+    mirrored, gated_x, mirrored_cotangent_x = together(mirrored, gated_x, mirrored_cotangent_x)
     mirrored_x = exchange(mirrored, "ch", cross)
     gated_all = [gated, exchange(gated, "ch", 1), gated_x, exchange(gated_x, "ch", 1)]
     cotangent_all = [cotangent, exchange(cotangent, "ch", 1), cotangent_x, exchange(cotangent_x, "ch", 1)]
@@ -458,7 +465,7 @@
         mirrored_cotangent_x,
         exchange(mirrored_cotangent_x, "ch", 1),
     ]
-    grad_norm, flipped_cotangent, choose = run(
+    grad_norm = run(
         functools.partial(norm_grad_kernel, channels),
         place,
         (
@@ -468,12 +475,10 @@
             exchange(w_out, "ch", 1),
             w_out_x,
             exchange(w_out_x, "ch", 1),
-            channel_order.reshape(1, full),
         ),
-        [((2 * rows, full), BF16), block, ((full, full), BF16)],
-        [pltpu.VMEM((channels, rows, width), BF16)],
+        [((2 * rows, full), BF16)],
         gflop=2.1,
-    )
+    )[0]
     mirrored_x, grad_norm = together(mirrored_x, grad_norm)
     mirrored_all = [mirrored, exchange(mirrored, "ch", 1), mirrored_x, exchange(mirrored_x, "ch", 1)]
 
@@ -489,7 +494,7 @@
     out_sent, out_kept, gate_sent, gate_kept = run(
         functools.partial(products_kernel, channels),
         place,
-        (normalized, cotangent, flipped_cotangent, grad_gate_pre, *mains),
+        (normalized, cotangent, mirrored_cotangent, grad_gate_pre, *mains),
         [
             ((full // 4, width), BF16),
             ((full // 4, width), F32),
@@ -500,7 +505,7 @@
         gflop=0.8,
     )
     out_sent, gate_sent, first, second = together(out_sent, gate_sent, first, second)
-    out_other = exchange(out_sent, "seq", steps[1])
+    out_other = exchange(out_sent, "seq", steps[0])
     gate_other = exchange(gate_sent, "seq", steps[0])
     half = full // 2 + SPARE
     in_sent, in_kept = run(
@@ -523,7 +528,8 @@
 
     down = [("halve", distance) for distance in steps]
     up = [("double", distance) for distance in steps[::-1]]
-    routes = [down + up + [("take",)], down + up + [None], down[1:] + up + [None]]
+    out_down, out_up = down[:1] + down[2:], up[:-2] + up[-1:] + up[-2:-1]
+    routes = [down + up + [("take",)], down + up + [None], out_down + out_up + [None]]
     in_sent, gate_other, out_other = together(in_sent, gate_other, out_other)
     results = []
     for route, sent, kept, other in zip(

time: 143 us -> 139 us (0.972)
  starting transfers between devices: 59.4 us -> 49.2 us
  waiting for transfers between devices: 43.1 us -> 50.8 us
  local copies, waits for them, and re-layouts: 4.37 us -> 2.03 us
    ppermute x36, waiting for transfers between devices: 31.9 us -> 50.4 us  [exchange(): return lax.ppermute(block, axis, [(i, i ^ distance) for i in range(count)])]
    ppermute x2, waiting for transfers between devices: 8.38 us -> 0.01 us  [mirror(): lax.ppermute(block, 'seq', [(i, count - 1 - i) for i in range(count)])]
    ppermute x36, starting transfers between devices: 37 us -> 31 us  [exchange(): return lax.ppermute(block, axis, [(i, i ^ distance) for i in range(count)])]
    ppermute x2, starting transfers between devices: 10.4 us -> 7.85 us  [mirror(): lax.ppermute(block, 'seq', [(i, count - 1 - i) for i in range(count)])]
    ppermute x6, waiting for transfers between devices: 2.85 us -> 0.46 us  [swap_edges(): received.append(lax.ppermute(block, ('seq', 'ch'), route))]
    unnamed x20 -> x27, local copies, waits for them, and re-layouts: 3.76 us -> 1.41 us
    ppermute x6, starting transfers between devices: 12 us -> 10.3 us  [swap_edges(): received.append(lax.ppermute(block, ('seq', 'ch'), route))]
    pallas_call x26 -> x28, Pallas kernels: 34.6 us -> 35.6 us  [run(): pl.pallas_call(body, out_shape=[jax.ShapeDtypeStruct(shape, dtype) for sh...]
  transfers between devices with their start and end apart: 44 -> 44, of which waited for: 19 -> 18; matrix products, arithmetic and copies ran while one was open for 0% -> 0% of each run, Pallas kernels for 19% -> 20%
where the time goes in v12:
time: 139 us
  waiting for transfers between devices  50.8 us (37%)
  starting transfers between devices  49.2 us (35%)
  Pallas kernels  35.6 us (26%)
  local copies, waits for them, and re-layouts  2.03 us (1%)
    ppermute x36, waiting for transfers between devices, exchange(): return lax.ppermute(block, axis, [(i, i ^ distance) for i in range(count)])  50.4 us
    pallas_call x28, Pallas kernels, run(): pl.pallas_call(body, out_shape=[jax.ShapeDtypeStruct(shape, dtype) for sh...  35.6 us
    ppermute x36, starting transfers between devices, exchange(): return lax.ppermute(block, axis, [(i, i ^ distance) for i in range(count)])  31 us
    ppermute x6, starting transfers between devices, swap_edges(): received.append(lax.ppermute(block, ('seq', 'ch'), route))  10.3 us
    ppermute x2, starting transfers between devices, mirror(): lax.ppermute(block, 'seq', [(i, count - 1 - i) for i in range(count)])  7.85 us
  transfers between devices with their start and end apart: 44, of which 18 were waited for; matrix products, arithmetic and copies ran while one was open for 0% of the time, Pallas kernels for 20%

profile of v12, /device:TPU:0, one launch (start us, length us, event | category | flops | bytes accessed | tf_op | source)
XLA Modules:
  0.0 139.2 jit_solution(4175537881358122887)
XLA Ops:
  0.6 6.1 %collective-permute-start.3 = (bf16[512,256]{1,0:T(8,128)(2,1)}, bf16[512,256]{1,0:T(8,128)(2,1)S(1)}, u32[]{:S(2)}, u32[]{:S(2)}) collective-permute-start(bf16[512,256]{1,0:T(8,128)(2,1)} %cotangent.1), channel_id=1, source_target_pairs={{0,28},{4,24},{8,20},{12,16},{16,12},{20,8},{24,4},{28,0},{1,29},{... | collective-permute-start | bytes 786440 | tf_op jit(solution)/shard_map/ppermute | solution.py:372
  8.8 2.7 %shard_map.137 = (bf16[512,256]{1,0:T(8,128)(2,1)}, bf16[160,256]{1,0:T(8,128)(2,1)}, bf16[160,256]{1,0:T(8,128)(2,1)}) custom-call(s32[3]{0:T(128)} %pad_add_fusion.place, s32[1,512]{1,0:T(1,128)} %bitcast.7, bf16[512,256]{1,0:T(8,128)(2,1)} %hidden_hbm.1, bf16[4,256]{1,0:T(4,128)(2,1)} %embedding_hbm.1), custom_call_target="tpu_custom_call" | custom-call | flops 100000000 | bytes 266240 | tf_op jit(solution)/shard_map/pallas_call | solution.py:30
  16.9 4.3 %collective-permute-start.4 = (bf16[160,256]{1,0:T(8,128)(2,1)S(1)}, bf16[160,256]{1,0:T(8,128)(2,1)S(1)}, u32[]{:S(2)}, u32[]{:S(2)}) collective-permute-start(bf16[160,256]{1,0:T(8,128)(2,1)S(1)} %copy-done.11), channel_id=1, source_target_pairs={{0,6},{4,2},{1,7},{5,3},{2,4},{6,0},{3,5},{7,1},{8,14},{12,10},{9,... | collective-permute-start | bytes 245768 | tf_op jit(solution)/shard_map/ppermute | solution.py:384
  25.6 2.0 %shard_map.141 = (bf16[2192,256]{1,0:T(8,128)(2,1)S(1)}, bf16[512,256]{1,0:T(8,128)(2,1)S(1)}, bf16[512,256]{1,0:T(8,128)(2,1)S(1)}) custom-call(s32[3]{0:T(128)S(1)} %copy-done.4, bf16[640,256]{1,0:T(8,128)(2,1)S(1)} %constant_dynamic-update-slice_fusion.edges, bf16[640,256]{1,0:T(8,128)(2,1)S(1)} %collective-permute-done.6.edges_core, ...), custom_call_target="tpu_custom_call" | custom-call | flops 400000000 | bytes 2240512 | tf_op jit(solution)/shard_map/pallas_call | solution.py:30
  31.0 7.4 %collective-permute-done.13.refs_10_ = bf16[1024,256]{1,0:T(8,128)(2,1)S(1)} collective-permute-done((bf16[1024,256]{1,0:T(8,128)(2,1)S(1)}, bf16[1024,256]{1,0:T(8,128)(2,1)S(1)}, u32[]{:S(2)}, u32[]{:S(2)}) %collective-permute-start.13) | collective-permute-done | bytes 524320 | tf_op jit(solution)/shard_map/ppermute | solution.py:363
  38.5 5.1 %collective-permute-done.12.refs_2_ = bf16[512,256]{1,0:T(8,128)(2,1)S(1)} collective-permute-done((bf16[512,256]{1,0:T(8,128)(2,1)S(1)}, bf16[512,256]{1,0:T(8,128)(2,1)S(1)}, u32[]{:S(2)}, u32[]{:S(2)}) %collective-permute-start.12) | collective-permute-done | bytes 262176 | tf_op jit(solution)/shard_map/ppermute | solution.py:363
  45.5 6.0 %collective-permute-done.14.refs_6_ = bf16[512,256]{1,0:T(8,128)(2,1)S(1)} collective-permute-done((bf16[512,256]{1,0:T(8,128)(2,1)S(1)}, bf16[512,256]{1,0:T(8,128)(2,1)S(1)}, u32[]{:S(2)}, u32[]{:S(2)}) %collective-permute-start.14) | collective-permute-done | bytes 262176 | tf_op jit(solution)/shard_map/ppermute | solution.py:363
  53.8 2.9 %shard_map.143.refs_8_ = bf16[1024,1024]{1,0:T(8,128)(2,1)S(1)} custom-call(s32[3]{0:T(128)S(1)} %copy-done.4, bf16[512,256]{1,0:T(8,128)(2,1)S(1)} %copy-done.2, bf16[512,256]{1,0:T(8,128)(2,1)S(1)} %collective-permute-done.18.refs_1_, bf16[512,256]{1,0:T(8,128)(2,1)S(1)} %collective-permute-done.refs_2_, ...), custom_call_target="tpu_custom_call" | custom-call | flops 2100000000 | bytes 4194304 | tf_op jit(solution)/shard_map/pallas_call | solution.py:30
  56.7 3.5 %collective-permute-done.17.refs_6_ = bf16[512,256]{1,0:T(8,128)(2,1)S(1)} collective-permute-done((bf16[512,256]{1,0:T(8,128)(2,1)S(1)}, bf16[512,256]{1,0:T(8,128)(2,1)S(1)}, u32[]{:S(2)}, u32[]{:S(2)}) %collective-permute-start.17) | collective-permute-done | bytes 262176 | tf_op jit(solution)/shard_map/ppermute | solution.py:363
  61.8 5.7 %shard_map.144 = (bf16[1024,1024]{1,0:T(8,128)(2,1)S(1)}, bf16[512,256]{1,0:T(8,128)(2,1)S(1)}, bf16[512,256]{1,0:T(8,128)(2,1)S(1)}, bf16[160,256]{1,0:T(8,128)(2,1)S(1)}, bf16[160,256]{1,0:T(8,128)(2,1)S(1)}) custom-call(s32[3]{0:T(128)S(1)} %copy-done.4, bf16[512,256]{1,0:T(8,128)(2,1)S(1)} %get-tuple-element.75.refs_0_, ...), custom_call_target="tpu_custom_call" | custom-call | flops 2500000000 | bytes 7081984 | tf_op jit(solution)/shard_map/pallas_call | solution.py:30
  67.5 3.4 %collective-permute-start.25 = (bf16[160,256]{1,0:T(8,128)(2,1)S(1)}, bf16[160,256]{1,0:T(8,128)(2,1)S(1)}, u32[]{:S(2)}, u32[]{:S(2)}) collective-permute-start(bf16[160,256]{1,0:T(8,128)(2,1)S(1)} %get-tuple-element.93), channel_id=1, source_target_pairs={{0,4},{4,0},{1,5},{5,1},{2,6},{6,2},{3,7},{7,3},{8,12},{12,8},{9,1... | collective-permute-start | bytes 245768 | tf_op jit(solution)/shard_map/ppermute | solution.py:384
  73.6 4.5 %collective-permute-start.27 = (bf16[512,256]{1,0:T(8,128)(2,1)S(1)}, bf16[512,256]{1,0:T(8,128)(2,1)S(1)}, u32[]{:S(2)}, u32[]{:S(2)}) collective-permute-start(bf16[512,256]{1,0:T(8,128)(2,1)S(1)} %get-tuple-element.100), channel_id=1, source_target_pairs={{0,4},{4,0},{8,12},{12,8},{16,20},{20,16},{24,28},{28,24},{1,5},{5... | collective-permute-start | bytes 786440 | tf_op jit(solution)/shard_map/ppermute | solution.py:363
  78.2 2.5 %shard_map.147 = (bf16[576,256]{1,0:T(8,128)(2,1)S(1)}, f32[576,256]{1,0:T(8,128)S(1)}) custom-call(s32[3]{0:T(128)S(1)} %copy-done.4, bf16[512,256]{1,0:T(8,128)(2,1)S(1)} %get-tuple-element.89.upstream, bf16[160,256]{1,0:T(8,128)(2,1)S(1)} %collective-permute-done.25.first, bf16[160,256]{1,0:T(8,128)(2,1)S(1)} %collective-permute-done.26.second, ...), custom_call_target="tpu_custom_call" | custom-call | flops 500000000 | bytes 2609152 | tf_op jit(solution)/shard_map/pallas_call | solution.py:30
  80.7 6.1 %collective-permute-done.28.refs_1_ = bf16[256,256]{1,0:T(8,128)(2,1)S(1)} collective-permute-done((bf16[256,256]{1,0:T(8,128)(2,1)S(1)}, bf16[256,256]{1,0:T(8,128)(2,1)S(1)}, u32[]{:S(2)}, u32[]{:S(2)}) %collective-permute-start.28) | collective-permute-done | bytes 131104 | tf_op jit(solution)/shard_map/ppermute | solution.py:363
  88.5 5.8 %collective-permute-done.29.refs_1_ = bf16[576,256]{1,0:T(8,128)(2,1)S(1)} collective-permute-done((bf16[576,256]{1,0:T(8,128)(2,1)S(1)}, bf16[576,256]{1,0:T(8,128)(2,1)S(1)}, u32[]{:S(2)}, u32[]{:S(2)}) %collective-permute-start.29) | collective-permute-done | bytes 294944 | tf_op jit(solution)/shard_map/ppermute | solution.py:363
  95.0 2.0 %collective-permute-start.30 = (bf16[288,256]{1,0:T(8,128)(2,1)S(1)}, bf16[288,256]{1,0:T(8,128)(2,1)S(1)}, u32[]{:S(2)}, u32[]{:S(2)}) collective-permute-start(bf16[288,256]{1,0:T(8,128)(2,1)S(1)} %get-tuple-element.104), channel_id=1, source_target_pairs={{0,8},{4,12},{8,0},{12,4},{16,24},{20,28},{24,16},{28,20},{1,9},{5... | collective-permute-start | bytes 442376 | tf_op jit(solution)/shard_map/ppermute | solution.py:363
  97.7 2.6 %collective-permute-done.30.refs_1_ = bf16[288,256]{1,0:T(8,128)(2,1)S(1)} collective-permute-done((bf16[288,256]{1,0:T(8,128)(2,1)S(1)}, bf16[288,256]{1,0:T(8,128)(2,1)S(1)}, u32[]{:S(2)}, u32[]{:S(2)}) %collective-permute-start.30) | collective-permute-done | bytes 147488 | tf_op jit(solution)/shard_map/ppermute | solution.py:363
  101.0 2.9 %collective-permute-start.31 = (bf16[144,256]{1,0:T(8,128)(2,1)S(1)}, bf16[144,256]{1,0:T(8,128)(2,1)S(1)}, u32[]{:S(2)}, u32[]{:S(2)}) collective-permute-start(bf16[144,256]{1,0:T(8,128)(2,1)S(1)} %get-tuple-element.106), channel_id=1, source_target_pairs={{0,16},{4,20},{8,24},{12,28},{16,0},{20,4},{24,8},{28,12},{1,17},{... | collective-permute-start | bytes 221192 | tf_op jit(solution)/shard_map/ppermute | solution.py:363
  105.2 2.9 %collective-permute-start.36 = (bf16[128,256]{1,0:T(8,128)(2,1)S(1)}, bf16[128,256]{1,0:T(8,128)(2,1)S(1)}, u32[]{:S(2)}, u32[]{:S(2)}) collective-permute-start(bf16[128,256]{1,0:T(8,128)(2,1)S(1)} %get-tuple-element.113), channel_id=1, source_target_pairs={{0,16},{4,20},{8,24},{12,28},{16,0},{20,4},{24,8},{28,12},{1,17},{... | collective-permute-start | bytes 196616 | tf_op jit(solution)/shard_map/ppermute | solution.py:363
  108.1 2.7 %collective-permute-done.31.refs_1_ = bf16[144,256]{1,0:T(8,128)(2,1)S(1)} collective-permute-done((bf16[144,256]{1,0:T(8,128)(2,1)S(1)}, bf16[144,256]{1,0:T(8,128)(2,1)S(1)}, u32[]{:S(2)}, u32[]{:S(2)}) %collective-permute-start.31) | collective-permute-done | bytes 73760 | tf_op jit(solution)/shard_map/ppermute | solution.py:363
  111.5 2.2 %collective-permute-done.40.refs_1_ = bf16[128,256]{1,0:T(8,128)(2,1)S(1)} collective-permute-done((bf16[128,256]{1,0:T(8,128)(2,1)S(1)}, bf16[128,256]{1,0:T(8,128)(2,1)S(1)}, u32[]{:S(2)}, u32[]{:S(2)}) %collective-permute-start.40) | collective-permute-done | bytes 65568 | tf_op jit(solution)/shard_map/ppermute | solution.py:363
  115.6 2.2 %collective-permute-start.37 = (bf16[128,256]{1,0:T(8,128)(2,1)S(1)}, bf16[128,256]{1,0:T(8,128)(2,1)S(1)}, u32[]{:S(2)}, u32[]{:S(2)}) collective-permute-start(bf16[128,256]{1,0:T(8,128)(2,1)S(1)} %shard_map.156.refs_0_), channel_id=1, source_target_pairs={{0,16},{4,20},{8,24},{12,28},{16,0},{20,4},{24,8},{28,12},{1,17},{... | collective-permute-start | bytes 196616 | tf_op jit(solution)/shard_map/ppermute | solution.py:363
  128.5 2.1 %collective-permute-start.39 = (bf16[512,256]{1,0:T(8,128)(2,1)S(1)}, bf16[512,256]{1,0:T(8,128)(2,1)S(1)}, u32[]{:S(2)}, u32[]{:S(2)}) collective-permute-start(bf16[512,256]{1,0:T(8,128)(2,1)S(1)} %shard_map.158.refs_0_), channel_id=1, source_target_pairs={{0,4},{4,0},{8,12},{12,8},{16,20},{20,16},{24,28},{28,24},{1,5},{5... | collective-permute-start | bytes 786440 | tf_op jit(solution)/shard_map/ppermute | solution.py:363
  132.3 2.0 %collective-permute-done.43.refs_1_ = bf16[512,256]{1,0:T(8,128)(2,1)S(1)} collective-permute-done((bf16[512,256]{1,0:T(8,128)(2,1)S(1)}, bf16[512,256]{1,0:T(8,128)(2,1)S(1)}, u32[]{:S(2)}, u32[]{:S(2)}) %collective-permute-start.43) | collective-permute-done | bytes 262176 | tf_op jit(solution)/shard_map/ppermute | solution.py:363
  (122 shorter events, 48.6 us)
Async XLA Ops:
  0.6 16.3 %collective-permute-start.3 = (bf16[512,256]{1,0:T(8,128)(2,1)}, bf16[512,256]{1,0:T(8,128)(2,1)S(1)}, u32[]{:S(2)}, u32[]{:S(2)}) collective-permute-start(bf16[512,256]{1,0:T(8,128)(2,1)} %cotangent.1), channel_id=1, source_target_pairs={{0,28},{4,24},{8,20},{12,16},{16,12},{20,8},{24,4},{28,0},{1,29},{... | collective-permute-start | bytes 786440 | tf_op jit(solution)/shard_map/ppermute | solution.py:372
  6.7 8.9 %collective-permute-start = (bf16[512,256]{1,0:T(8,128)(2,1)}, bf16[512,256]{1,0:T(8,128)(2,1)S(1)}, u32[]{:S(2)}, u32[]{:S(2)}) collective-permute-start(bf16[512,256]{1,0:T(8,128)(2,1)} %cotangent.1), channel_id=1, source_target_pairs={{0,2},{1,3},{2,0},{3,1},{4,6},{5,7},{6,4},{7,5},{8,10},{9,11},{10,... | collective-permute-start | bytes 786440 | tf_op jit(solution)/shard_map/ppermute | solution.py:363
  11.5 9.7 %collective-permute-start.8 = (bf16[512,256]{1,0:T(8,128)(2,1)}, bf16[512,256]{1,0:T(8,128)(2,1)S(1)}, u32[]{:S(2)}, u32[]{:S(2)}) collective-permute-start(bf16[512,256]{1,0:T(8,128)(2,1)} %get-tuple-element.68.refs_0_.block_in), channel_id=1, source_target_pairs={{0,2},{1,3},{2,0},{3,1},{4,6},{5,7},{6,4},{7,5},{8,10},{9,11},{10,... | collective-permute-start | bytes 786440 | tf_op jit(solution)/shard_map/ppermute | solution.py:363
  12.1 10.6 %collective-permute-start.7 = (bf16[512,256]{1,0:T(8,128)(2,1)}, bf16[512,256]{1,0:T(8,128)(2,1)S(1)}, u32[]{:S(2)}, u32[]{:S(2)}) collective-permute-start(bf16[512,256]{1,0:T(8,128)(2,1)} %get-tuple-element.68.refs_0_.block_in), channel_id=1, source_target_pairs={{0,1},{1,0},{2,3},{3,2},{4,5},{5,4},{6,7},{7,6},{8,9},{9,8},{10,11... | collective-permute-start | bytes 786440 | tf_op jit(solution)/shard_map/ppermute | solution.py:363
  15.7 7.1 %collective-permute-start.1 = (bf16[160,256]{1,0:T(8,128)(2,1)S(1)}, bf16[160,256]{1,0:T(8,128)(2,1)S(1)}, u32[]{:S(2)}, u32[]{:S(2)}) collective-permute-start(bf16[160,256]{1,0:T(8,128)(2,1)S(1)} %copy-done.11), channel_id=1, source_target_pairs={{0,4},{4,0},{1,5},{5,1},{2,6},{6,2},{3,7},{7,3},{8,12},{12,8},{9,1... | collective-permute-start | bytes 245768 | tf_op jit(solution)/shard_map/ppermute | solution.py:384
  16.2 7.2 %collective-permute-start.2 = (bf16[160,256]{1,0:T(8,128)(2,1)S(1)}, bf16[160,256]{1,0:T(8,128)(2,1)S(1)}, u32[]{:S(2)}, u32[]{:S(2)}) collective-permute-start(bf16[160,256]{1,0:T(8,128)(2,1)S(1)} %copy-done.10), channel_id=1, source_target_pairs={{4,8},{8,4},{5,9},{9,5},{6,10},{10,6},{7,11},{11,7},{12,16},{16,12... | collective-permute-start | bytes 245768 | tf_op jit(solution)/shard_map/ppermute | solution.py:384
  22.8 15.7 %collective-permute-start.13 = (bf16[1024,256]{1,0:T(8,128)(2,1)S(1)}, bf16[1024,256]{1,0:T(8,128)(2,1)S(1)}, u32[]{:S(2)}, u32[]{:S(2)}) collective-permute-start(bf16[1024,256]{1,0:T(8,128)(2,1)S(1)} %copy-done.1), channel_id=1, source_target_pairs={{0,2},{1,3},{2,0},{3,1},{4,6},{5,7},{6,4},{7,5},{8,10},{9,11},{10,... | collective-permute-start | bytes 1572872 | tf_op jit(solution)/shard_map/ppermute | solution.py:363
  27.6 16.0 %collective-permute-start.12 = (bf16[512,256]{1,0:T(8,128)(2,1)S(1)}, bf16[512,256]{1,0:T(8,128)(2,1)S(1)}, u32[]{:S(2)}, u32[]{:S(2)}) collective-permute-start(bf16[512,256]{1,0:T(8,128)(2,1)S(1)} %get-tuple-element.75.refs_0_), channel_id=1, source_target_pairs={{0,2},{1,3},{2,0},{3,1},{4,6},{5,7},{6,4},{7,5},{8,10},{9,11},{10,... | collective-permute-start | bytes 786440 | tf_op jit(solution)/shard_map/ppermute | solution.py:363
  28.7 15.9 %collective-permute-start.11 = (bf16[512,256]{1,0:T(8,128)(2,1)S(1)}, bf16[512,256]{1,0:T(8,128)(2,1)S(1)}, u32[]{:S(2)}, u32[]{:S(2)}) collective-permute-start(bf16[512,256]{1,0:T(8,128)(2,1)S(1)} %get-tuple-element.75.refs_0_), channel_id=1, source_target_pairs={{0,28},{4,24},{8,20},{12,16},{16,12},{20,8},{24,4},{28,0},{1,29},{... | collective-permute-start | bytes 786440 | tf_op jit(solution)/shard_map/ppermute | solution.py:372
  30.5 21.0 %collective-permute-start.18 = (bf16[512,256]{1,0:T(8,128)(2,1)S(1)}, bf16[512,256]{1,0:T(8,128)(2,1)S(1)}, u32[]{:S(2)}, u32[]{:S(2)}) collective-permute-start(bf16[512,256]{1,0:T(8,128)(2,1)S(1)} %copy-done.2), channel_id=1, source_target_pairs={{0,1},{1,0},{2,3},{3,2},{4,5},{5,4},{6,7},{7,6},{8,9},{9,8},{10,11... | collective-permute-start | bytes 786440 | tf_op jit(solution)/shard_map/ppermute | solution.py:363
  30.5 22.7 %collective-permute-start.22 = (bf16[1024,256]{1,0:T(8,128)(2,1)S(1)}, bf16[1024,256]{1,0:T(8,128)(2,1)S(1)}, u32[]{:S(2)}, u32[]{:S(2)}) collective-permute-start(bf16[1024,256]{1,0:T(8,128)(2,1)S(1)} %copy-done.1), channel_id=1, source_target_pairs={{0,1},{1,0},{2,3},{3,2},{4,5},{5,4},{6,7},{7,6},{8,9},{9,8},{10,11... | collective-permute-start | bytes 1572872 | tf_op jit(solution)/shard_map/ppermute | solution.py:363
  38.5 13.5 %collective-permute-start.19 = (bf16[512,256]{1,0:T(8,128)(2,1)S(1)}, bf16[512,256]{1,0:T(8,128)(2,1)S(1)}, u32[]{:S(2)}, u32[]{:S(2)}) collective-permute-start(bf16[512,256]{1,0:T(8,128)(2,1)S(1)} %collective-permute-done.refs_2_), channel_id=1, source_target_pairs={{0,1},{1,0},{2,3},{3,2},{4,5},{5,4},{6,7},{7,6},{8,9},{9,8},{10,11... | collective-permute-start | bytes 786440 | tf_op jit(solution)/shard_map/ppermute | solution.py:363
  43.6 7.8 %collective-permute-start.14 = (bf16[512,256]{1,0:T(8,128)(2,1)S(1)}, bf16[512,256]{1,0:T(8,128)(2,1)S(1)}, u32[]{:S(2)}, u32[]{:S(2)}) collective-permute-start(bf16[512,256]{1,0:T(8,128)(2,1)S(1)} %shard_map.138.refs_4_.mirrored_cotangent), channel_id=1, source_target_pairs={{0,2},{1,3},{2,0},{3,1},{4,6},{5,7},{6,4},{7,5},{8,10},{9,11},{10,... | collective-permute-start | bytes 786440 | tf_op jit(solution)/shard_map/ppermute | solution.py:363
  44.6 9.1 %collective-permute-start.23 = (bf16[1024,256]{1,0:T(8,128)(2,1)S(1)}, bf16[1024,256]{1,0:T(8,128)(2,1)S(1)}, u32[]{:S(2)}, u32[]{:S(2)}) collective-permute-start(bf16[1024,256]{1,0:T(8,128)(2,1)S(1)} %collective-permute-done.13.refs_10_), channel_id=1, source_target_pairs={{0,1},{1,0},{2,3},{3,2},{4,5},{5,4},{6,7},{7,6},{8,9},{9,8},{10,11... | collective-permute-start | bytes 1572872 | tf_op jit(solution)/shard_map/ppermute | solution.py:363
  52.0 8.3 %collective-permute-start.17 = (bf16[512,256]{1,0:T(8,128)(2,1)S(1)}, bf16[512,256]{1,0:T(8,128)(2,1)S(1)}, u32[]{:S(2)}, u32[]{:S(2)}) collective-permute-start(bf16[512,256]{1,0:T(8,128)(2,1)S(1)} %shard_map.142.refs_4_), channel_id=1, source_target_pairs={{0,2},{1,3},{2,0},{3,1},{4,6},{5,7},{6,4},{7,5},{8,10},{9,11},{10,... | collective-permute-start | bytes 786440 | tf_op jit(solution)/shard_map/ppermute | solution.py:363
  53.2 7.1 %collective-permute-start.16 = (bf16[512,256]{1,0:T(8,128)(2,1)S(1)}, bf16[512,256]{1,0:T(8,128)(2,1)S(1)}, u32[]{:S(2)}, u32[]{:S(2)}) collective-permute-start(bf16[512,256]{1,0:T(8,128)(2,1)S(1)} %shard_map.142.refs_4_), channel_id=1, source_target_pairs={{0,1},{1,0},{2,3},{3,2},{4,5},{5,4},{6,7},{7,6},{8,9},{9,8},{10,11... | collective-permute-start | bytes 786440 | tf_op jit(solution)/shard_map/ppermute | solution.py:363
  73.6 13.1 %collective-permute-start.27 = (bf16[512,256]{1,0:T(8,128)(2,1)S(1)}, bf16[512,256]{1,0:T(8,128)(2,1)S(1)}, u32[]{:S(2)}, u32[]{:S(2)}) collective-permute-start(bf16[512,256]{1,0:T(8,128)(2,1)S(1)} %get-tuple-element.100), channel_id=1, source_target_pairs={{0,4},{4,0},{8,12},{12,8},{16,20},{20,16},{24,28},{28,24},{1,5},{5... | collective-permute-start | bytes 786440 | tf_op jit(solution)/shard_map/ppermute | solution.py:363
  78.1 8.6 %collective-permute-start.28 = (bf16[256,256]{1,0:T(8,128)(2,1)S(1)}, bf16[256,256]{1,0:T(8,128)(2,1)S(1)}, u32[]{:S(2)}, u32[]{:S(2)}) collective-permute-start(bf16[256,256]{1,0:T(8,128)(2,1)S(1)} %get-tuple-element.101), channel_id=1, source_target_pairs={{0,4},{4,0},{8,12},{12,8},{16,20},{20,16},{24,28},{28,24},{1,5},{5... | collective-permute-start | bytes 393224 | tf_op jit(solution)/shard_map/ppermute | solution.py:363
  86.7 7.6 %collective-permute-start.29 = (bf16[576,256]{1,0:T(8,128)(2,1)S(1)}, bf16[576,256]{1,0:T(8,128)(2,1)S(1)}, u32[]{:S(2)}, u32[]{:S(2)}) collective-permute-start(bf16[576,256]{1,0:T(8,128)(2,1)S(1)} %get-tuple-element.102), channel_id=1, source_target_pairs={{0,4},{4,0},{8,12},{12,8},{16,20},{20,16},{24,28},{28,24},{1,5},{5... | collective-permute-start | bytes 884744 | tf_op jit(solution)/shard_map/ppermute | solution.py:363
  101.0 9.9 %collective-permute-start.31 = (bf16[144,256]{1,0:T(8,128)(2,1)S(1)}, bf16[144,256]{1,0:T(8,128)(2,1)S(1)}, u32[]{:S(2)}, u32[]{:S(2)}) collective-permute-start(bf16[144,256]{1,0:T(8,128)(2,1)S(1)} %get-tuple-element.106), channel_id=1, source_target_pairs={{0,16},{4,20},{8,24},{12,28},{16,0},{20,4},{24,8},{28,12},{1,17},{... | collective-permute-start | bytes 221192 | tf_op jit(solution)/shard_map/ppermute | solution.py:363
  104.5 9.2 %collective-permute-start.40 = (bf16[128,256]{1,0:T(8,128)(2,1)S(1)}, bf16[128,256]{1,0:T(8,128)(2,1)S(1)}, u32[]{:S(2)}, u32[]{:S(2)}) collective-permute-start(bf16[128,256]{1,0:T(8,128)(2,1)S(1)} %get-tuple-element.117), channel_id=1, source_target_pairs={{0,16},{4,20},{8,24},{12,28},{16,0},{20,4},{24,8},{28,12},{1,17},{... | collective-permute-start | bytes 196616 | tf_op jit(solution)/shard_map/ppermute | solution.py:363
  105.2 9.8 %collective-permute-start.36 = (bf16[128,256]{1,0:T(8,128)(2,1)S(1)}, bf16[128,256]{1,0:T(8,128)(2,1)S(1)}, u32[]{:S(2)}, u32[]{:S(2)}) collective-permute-start(bf16[128,256]{1,0:T(8,128)(2,1)S(1)} %get-tuple-element.113), channel_id=1, source_target_pairs={{0,16},{4,20},{8,24},{12,28},{16,0},{20,4},{24,8},{28,12},{1,17},{... | collective-permute-start | bytes 196616 | tf_op jit(solution)/shard_map/ppermute | solution.py:363
  125.2 12.0 %collective-permute-start.34 = (bf16[576,256]{1,0:T(8,128)(2,1)S(1)}, bf16[576,256]{1,0:T(8,128)(2,1)S(1)}, u32[]{:S(2)}, u32[]{:S(2)}) collective-permute-start(bf16[576,256]{1,0:T(8,128)(2,1)S(1)} %shard_map.152.refs_0_), channel_id=1, source_target_pairs={{0,4},{4,0},{8,12},{12,8},{16,20},{20,16},{24,28},{28,24},{1,5},{5... | collective-permute-start | bytes 884744 | tf_op jit(solution)/shard_map/ppermute | solution.py:363
  128.5 7.2 %collective-permute-start.39 = (bf16[512,256]{1,0:T(8,128)(2,1)S(1)}, bf16[512,256]{1,0:T(8,128)(2,1)S(1)}, u32[]{:S(2)}, u32[]{:S(2)}) collective-permute-start(bf16[512,256]{1,0:T(8,128)(2,1)S(1)} %shard_map.158.refs_0_), channel_id=1, source_target_pairs={{0,4},{4,0},{8,12},{12,8},{16,20},{20,16},{24,28},{28,24},{1,5},{5... | collective-permute-start | bytes 786440 | tf_op jit(solution)/shard_map/ppermute | solution.py:363
  (32 other events, 168.9 us)

commit v13 on v12

--- a/solution.py
+++ b/solution.py
@@ -232,8 +232,8 @@
     for j in range(channels):
         whole_gate[part(me ^ j, width), :] = dot(mains[j][...], grad_gate_pre[...], ROWS_DOT)
     half = whole_gate.shape[0] // 2
-    gate_sent[...] = whole_gate[part(1 - bit, half), :].astype(BF16)
-    gate_kept[...] = whole_gate[part(bit, half), :]
+    gate_sent[...] = whole_gate[part(1 - side, half), :].astype(BF16)
+    gate_kept[...] = whole_gate[part(side, half), :]
 
 
 def backward_kernel(channels, place, upstream, first, second, conv_w, *refs):
@@ -303,7 +303,9 @@
                 count = low.shape[0] - SPARE
                 grad[:count] = low[:count].astype(BF16)
                 grad[count:] = high[:count].astype(BF16)
-                taps[...] = low[count : count + taps.shape[0]]
+                for number in range(taps.shape[0]):
+                    start = count + number * taps.shape[1]
+                    taps[number] = low[start : start + taps.shape[1]]
                 continue
             total = jnp.concatenate([low, high], axis=0)
         if after is not None and after[0] == "halve":
@@ -323,14 +325,14 @@
             outs += [((rows // 2, width), BF16), ((rows // 2, width), F32)]
             counts.append(2)
         elif after is not None and after[0] == "take":
-            outs += [((rows - 2 * SPARE, width), BF16), ((taps, width), F32)]
+            outs += [((rows - 2 * SPARE, width), BF16), ((*taps, width), F32)]
             counts.append(2)
         else:
             outs.append(((rows, width), BF16))
             counts.append(1)
     arrays = [array for item in items for array in item[2:]]
     plan = [item[:2] for item in items]
-    if all(shape[0] % 8 == 0 or shape[0] == taps for shape, _ in outs) and all(x.shape[0] % 8 == 0 for x in arrays):
+    if all(shape[0] % 8 == 0 or len(shape) == 3 for shape, _ in outs) and all(x.shape[0] % 8 == 0 for x in arrays):
         results = run(functools.partial(step_kernel, plan), place, arrays, outs)
     else:
         results = []
@@ -347,7 +349,7 @@
                 half = total.shape[0] // 2
                 results += [
                     jnp.concatenate([total[: half - SPARE], total[half:-SPARE]], axis=0).astype(BF16),
-                    total[half - SPARE : half - SPARE + taps],
+                    total[half - SPARE : half - SPARE + taps[0] * taps[1]].reshape(*taps, width),
                 ]
             else:
                 results.append(total.astype(BF16))
@@ -398,7 +400,6 @@
     full = gain.shape[0]
     channels = full // width
     cross = channels // 2
-    taps = conv_w.shape[0] * conv_w.shape[1]
     steps = distances("seq")
     block = ((rows, width), BF16)
     place = jnp.stack([lax.axis_index("seq"), lax.axis_index("ch"), lax.axis_size("seq")]).astype(jnp.int32)
@@ -424,12 +425,11 @@
         [((full, full), BF16)],
         gflop=2.0,
     )[0]
-    first, second, cotangent_x = together(first, second, cotangent_x)
+    first, second, early_w_out, cotangent_x = together(first, second, w_out, cotangent_x)
     near = swap_edges(first, second)
     first, second, mirrored_cotangent = together(first, second, mirrored_cotangent)
     far = swap_edges(first, second, cross)
     edges = jnp.concatenate(near + far, axis=0)
-    early_w_out, input_x = together(w_out, input_x)
     w_out_x = exchange(early_w_out, "ch", cross)
     mirrored_cotangent = run(flip_kernel, place, (mirrored_cotangent,), [block], gflop=1.0)[0]
     mirrored_cotangent, input_core, choose = together(mirrored_cotangent, input_core, choose)
@@ -451,11 +451,12 @@
         [pltpu.VMEM((saved_rows(rows, number), width), F32) for number in range(4)],
         gflop=0.4,
     )
-    mirrored = run(flip_kernel, place, (mirror(gated),), [block], gflop=12.0)[0]
-    gated_x = exchange(gated, "ch", cross)
     mirrored_cotangent, w_out_x = together(mirrored_cotangent, w_out_x)
     mirrored_cotangent_x = exchange(mirrored_cotangent, "ch", cross)
-    mirrored, gated_x, mirrored_cotangent_x = together(mirrored, gated_x, mirrored_cotangent_x)
+    mirrored, mirrored_cotangent_x = together(mirror(gated), mirrored_cotangent_x)
+    mirrored = run(flip_kernel, place, (mirrored,), [block], gflop=12.0)[0]
+    gated_x = exchange(gated, "ch", cross)
+    mirrored, gated_x = together(mirrored, gated_x)
     mirrored_x = exchange(mirrored, "ch", cross)
     gated_all = [gated, exchange(gated, "ch", 1), gated_x, exchange(gated_x, "ch", 1)]
     cotangent_all = [cotangent, exchange(cotangent, "ch", 1), cotangent_x, exchange(cotangent_x, "ch", 1)]
@@ -506,7 +507,7 @@
     )
     out_sent, gate_sent, first, second = together(out_sent, gate_sent, first, second)
     out_other = exchange(out_sent, "seq", steps[0])
-    gate_other = exchange(gate_sent, "seq", steps[0])
+    gate_other = exchange(gate_sent, "seq", steps[1])
     half = full // 2 + SPARE
     in_sent, in_kept = run(
         functools.partial(backward_kernel, channels),
@@ -529,22 +530,26 @@
     down = [("halve", distance) for distance in steps]
     up = [("double", distance) for distance in steps[::-1]]
     out_down, out_up = down[:1] + down[2:], up[:-2] + up[-1:] + up[-2:-1]
-    routes = [down + up + [("take",)], down + up + [None], out_down + out_up + [None]]
-    in_sent, gate_other, out_other = together(in_sent, gate_other, out_other)
+    gate_down, gate_up = down[1:] + down[:1], up[-1:] + up[:-1]
+    routes = [down + up + [("take",)], gate_down + gate_up + [None], out_down + out_up + [None]]
+    in_sent, out_other = together(in_sent, out_other)
     results = []
     for route, sent, kept, other in zip(
         routes, (in_sent, None, None), (in_kept, gate_kept, out_kept), (None, gate_other, out_other)
     ):
         if other is None:
             other = exchange(sent, "seq", route[0][1])
-        for done, upcoming in zip(route, route[1:]):
-            prepared = advance(place, [(done, upcoming, kept, other)], taps)[0]
+        elif len(results) == 1:
+            other = gate_other
+        for number, (done, upcoming) in enumerate(zip(route, route[1:])):
+            prepared = advance(place, [(done, upcoming, kept, other)], conv_w.shape[:2])[0]
             if upcoming is not None and upcoming[0] != "take":
                 sent, kept = prepared if len(prepared) == 2 else prepared * 2
+                if not results and number == 0:
+                    sent, gate_other = together(sent, gate_other)
                 other = exchange(sent, "seq", upcoming[1])
         results.append(prepared)
     (grad_in, grad_conv), (sum_gate,), (sum_out,) = results
-    grad_conv = grad_conv.reshape(conv_w.shape)
     return output, grad_in, sum_gate, sum_out, grad_conv
 
 

time: 139 us -> 136 us (0.978)
  waiting for transfers between devices: 50.8 us -> 37.1 us
  starting transfers between devices: 49.2 us -> 59.6 us
    ppermute x36, waiting for transfers between devices: 50.4 us -> 34.1 us  [exchange(): return lax.ppermute(block, axis, [(i, i ^ distance) for i in range(count)])]
    ppermute x36, starting transfers between devices: 31 us -> 42.5 us  [exchange(): return lax.ppermute(block, axis, [(i, i ^ distance) for i in range(count)])]
    ppermute x6, waiting for transfers between devices: 0.46 us -> 2.11 us  [swap_edges(): received.append(lax.ppermute(block, ('seq', 'ch'), route))]
  transfers between devices with their start and end apart: 44 -> 44, of which waited for: 18 -> 21; matrix products, arithmetic and copies ran while one was open for 0% -> 0% of each run, Pallas kernels for 20% -> 21%
where the time goes in v13:
time: 136 us; the launch traced here: 135 us
  starting transfers between devices  59.6 us (44%)
  waiting for transfers between devices  37.1 us (27%)
  Pallas kernels  35.6 us (26%)
  local copies, waits for them, and re-layouts  1.42 us (1%)
    ppermute x36, starting transfers between devices, exchange(): return lax.ppermute(block, axis, [(i, i ^ distance) for i in range(count)])  42.5 us
    pallas_call x28, Pallas kernels, run(): pl.pallas_call(body, out_shape=[jax.ShapeDtypeStruct(shape, dtype) for sh...  35.6 us
    ppermute x36, waiting for transfers between devices, exchange(): return lax.ppermute(block, axis, [(i, i ^ distance) for i in range(count)])  34.1 us
    ppermute x6, starting transfers between devices, swap_edges(): received.append(lax.ppermute(block, ('seq', 'ch'), route))  9.11 us
    ppermute x2, starting transfers between devices, mirror(): lax.ppermute(block, 'seq', [(i, count - 1 - i) for i in range(count)])  7.96 us
  transfers between devices with their start and end apart: 44, of which 21 were waited for; matrix products, arithmetic and copies ran while one was open for 0% of the time, Pallas kernels for 21%

profile of v13, /device:TPU:0, one launch (start us, length us, event | category | flops | bytes accessed | tf_op | source)
XLA Modules:
  0.0 135.3 jit_solution(3638040567375582951)
XLA Ops:
  0.6 6.1 %collective-permute-start.3 = (bf16[512,256]{1,0:T(8,128)(2,1)}, bf16[512,256]{1,0:T(8,128)(2,1)S(1)}, u32[]{:S(2)}, u32[]{:S(2)}) collective-permute-start(bf16[512,256]{1,0:T(8,128)(2,1)} %cotangent.1), channel_id=1, source_target_pairs={{0,28},{4,24},{8,20},{12,16},{16,12},{20,8},{24,4},{28,0},{1,29},{... | collective-permute-start | bytes 786440 | tf_op jit(solution)/shard_map/ppermute | solution.py:374
  8.8 2.7 %shard_map.137 = (bf16[512,256]{1,0:T(8,128)(2,1)}, bf16[160,256]{1,0:T(8,128)(2,1)}, bf16[160,256]{1,0:T(8,128)(2,1)}) custom-call(s32[3]{0:T(128)} %pad_add_fusion.place, s32[1,512]{1,0:T(1,128)} %bitcast.7, bf16[512,256]{1,0:T(8,128)(2,1)} %hidden_hbm.1, bf16[4,256]{1,0:T(4,128)(2,1)} %embedding_hbm.1), custom_call_target="tpu_custom_call" | custom-call | flops 100000000 | bytes 266240 | tf_op jit(solution)/shard_map/pallas_call | solution.py:30
  16.9 4.3 %collective-permute-start.4 = (bf16[160,256]{1,0:T(8,128)(2,1)S(1)}, bf16[160,256]{1,0:T(8,128)(2,1)S(1)}, u32[]{:S(2)}, u32[]{:S(2)}) collective-permute-start(bf16[160,256]{1,0:T(8,128)(2,1)S(1)} %copy-done.11), channel_id=1, source_target_pairs={{0,6},{4,2},{1,7},{5,3},{2,4},{6,0},{3,5},{7,1},{8,14},{12,10},{9,... | collective-permute-start | bytes 245768 | tf_op jit(solution)/shard_map/ppermute | solution.py:386
  26.4 2.0 %shard_map.141 = (bf16[2192,256]{1,0:T(8,128)(2,1)S(1)}, bf16[512,256]{1,0:T(8,128)(2,1)S(1)}, bf16[512,256]{1,0:T(8,128)(2,1)S(1)}) custom-call(s32[3]{0:T(128)S(1)} %copy-done.4, bf16[640,256]{1,0:T(8,128)(2,1)S(1)} %constant_dynamic-update-slice_fusion.edges, bf16[640,256]{1,0:T(8,128)(2,1)S(1)} %collective-permute-done.6.edges_core, ...), custom_call_target="tpu_custom_call" | custom-call | flops 400000000 | bytes 2240512 | tf_op jit(solution)/shard_map/pallas_call | solution.py:30
  28.4 1.9 %collective-permute-start.11 = (bf16[512,256]{1,0:T(8,128)(2,1)S(1)}, bf16[512,256]{1,0:T(8,128)(2,1)S(1)}, u32[]{:S(2)}, u32[]{:S(2)}) collective-permute-start(bf16[512,256]{1,0:T(8,128)(2,1)S(1)} %get-tuple-element.75.refs_0_), channel_id=1, source_target_pairs={{0,28},{4,24},{8,20},{12,16},{16,12},{20,8},{24,4},{28,0},{1,29},{... | collective-permute-start | bytes 786440 | tf_op jit(solution)/shard_map/ppermute | solution.py:374
  30.3 6.3 %collective-permute-done.12.refs_10_ = bf16[1024,256]{1,0:T(8,128)(2,1)S(1)} collective-permute-done((bf16[1024,256]{1,0:T(8,128)(2,1)S(1)}, bf16[1024,256]{1,0:T(8,128)(2,1)S(1)}, u32[]{:S(2)}, u32[]{:S(2)}) %collective-permute-start.12) | collective-permute-done | bytes 524320 | tf_op jit(solution)/shard_map/ppermute | solution.py:365
  39.7 5.5 %collective-permute-done.13.refs_6_ = bf16[512,256]{1,0:T(8,128)(2,1)S(1)} collective-permute-done((bf16[512,256]{1,0:T(8,128)(2,1)S(1)}, bf16[512,256]{1,0:T(8,128)(2,1)S(1)}, u32[]{:S(2)}, u32[]{:S(2)}) %collective-permute-start.13) | collective-permute-done | bytes 262176 | tf_op jit(solution)/shard_map/ppermute | solution.py:365
  45.8 3.0 %collective-permute-done.14.refs_2_ = bf16[512,256]{1,0:T(8,128)(2,1)S(1)} collective-permute-done((bf16[512,256]{1,0:T(8,128)(2,1)S(1)}, bf16[512,256]{1,0:T(8,128)(2,1)S(1)}, u32[]{:S(2)}, u32[]{:S(2)}) %collective-permute-start.14) | collective-permute-done | bytes 262176 | tf_op jit(solution)/shard_map/ppermute | solution.py:365
  52.2 2.9 %shard_map.143.refs_8_ = bf16[1024,1024]{1,0:T(8,128)(2,1)S(1)} custom-call(s32[3]{0:T(128)S(1)} %copy-done.4, bf16[512,256]{1,0:T(8,128)(2,1)S(1)} %copy-done.2, bf16[512,256]{1,0:T(8,128)(2,1)S(1)} %collective-permute-done.18.refs_1_, bf16[512,256]{1,0:T(8,128)(2,1)S(1)} %collective-permute-done.refs_2_, ...), custom_call_target="tpu_custom_call" | custom-call | flops 2100000000 | bytes 4194304 | tf_op jit(solution)/shard_map/pallas_call | solution.py:30
  55.2 3.3 %collective-permute-done.17.refs_6_ = bf16[512,256]{1,0:T(8,128)(2,1)S(1)} collective-permute-done((bf16[512,256]{1,0:T(8,128)(2,1)S(1)}, bf16[512,256]{1,0:T(8,128)(2,1)S(1)}, u32[]{:S(2)}, u32[]{:S(2)}) %collective-permute-start.17) | collective-permute-done | bytes 262176 | tf_op jit(solution)/shard_map/ppermute | solution.py:365
  60.0 5.7 %shard_map.144 = (bf16[1024,1024]{1,0:T(8,128)(2,1)S(1)}, bf16[512,256]{1,0:T(8,128)(2,1)S(1)}, bf16[512,256]{1,0:T(8,128)(2,1)S(1)}, bf16[160,256]{1,0:T(8,128)(2,1)S(1)}, bf16[160,256]{1,0:T(8,128)(2,1)S(1)}) custom-call(s32[3]{0:T(128)S(1)} %copy-done.4, bf16[512,256]{1,0:T(8,128)(2,1)S(1)} %get-tuple-element.75.refs_0_, ...), custom_call_target="tpu_custom_call" | custom-call | flops 2500000000 | bytes 7081984 | tf_op jit(solution)/shard_map/pallas_call | solution.py:30
  65.7 2.1 %collective-permute-start.25 = (bf16[160,256]{1,0:T(8,128)(2,1)S(1)}, bf16[160,256]{1,0:T(8,128)(2,1)S(1)}, u32[]{:S(2)}, u32[]{:S(2)}) collective-permute-start(bf16[160,256]{1,0:T(8,128)(2,1)S(1)} %get-tuple-element.94), channel_id=1, source_target_pairs={{0,4},{4,0},{1,5},{5,1},{2,6},{6,2},{3,7},{7,3},{8,12},{12,8},{9,1... | collective-permute-start | bytes 245768 | tf_op jit(solution)/shard_map/ppermute | solution.py:386
  70.6 5.0 %collective-permute-start.27 = (bf16[256,256]{1,0:T(8,128)(2,1)S(1)}, bf16[256,256]{1,0:T(8,128)(2,1)S(1)}, u32[]{:S(2)}, u32[]{:S(2)}) collective-permute-start(bf16[256,256]{1,0:T(8,128)(2,1)S(1)} %get-tuple-element.101), channel_id=1, source_target_pairs={{0,4},{4,0},{8,12},{12,8},{16,20},{20,16},{24,28},{28,24},{1,5},{5... | collective-permute-start | bytes 393224 | tf_op jit(solution)/shard_map/ppermute | solution.py:365
  75.6 2.5 %shard_map.147 = (bf16[576,256]{1,0:T(8,128)(2,1)S(1)}, f32[576,256]{1,0:T(8,128)S(1)}) custom-call(s32[3]{0:T(128)S(1)} %copy-done.4, bf16[512,256]{1,0:T(8,128)(2,1)S(1)} %get-tuple-element.90.upstream, bf16[160,256]{1,0:T(8,128)(2,1)S(1)} %collective-permute-done.25.first, bf16[160,256]{1,0:T(8,128)(2,1)S(1)} %collective-permute-done.26.second, ...), custom_call_target="tpu_custom_call" | custom-call | flops 500000000 | bytes 2609152 | tf_op jit(solution)/shard_map/pallas_call | solution.py:30
  78.6 2.0 %collective-permute-start.28 = (bf16[576,256]{1,0:T(8,128)(2,1)S(1)}, bf16[576,256]{1,0:T(8,128)(2,1)S(1)}, u32[]{:S(2)}, u32[]{:S(2)}) collective-permute-start(bf16[576,256]{1,0:T(8,128)(2,1)S(1)} %get-tuple-element.102), channel_id=1, source_target_pairs={{0,4},{4,0},{8,12},{12,8},{16,20},{20,16},{24,28},{28,24},{1,5},{5... | collective-permute-start | bytes 884744 | tf_op jit(solution)/shard_map/ppermute | solution.py:365
  80.6 1.9 %collective-permute-start.29 = (bf16[512,256]{1,0:T(8,128)(2,1)S(1)}, bf16[512,256]{1,0:T(8,128)(2,1)S(1)}, u32[]{:S(2)}, u32[]{:S(2)}) collective-permute-start(bf16[512,256]{1,0:T(8,128)(2,1)S(1)} %get-tuple-element.105), channel_id=1, source_target_pairs={{0,8},{4,12},{8,0},{12,4},{16,24},{20,28},{24,16},{28,20},{1,9},{5... | collective-permute-start | bytes 786440 | tf_op jit(solution)/shard_map/ppermute | solution.py:365
  82.5 3.6 %collective-permute-done.28.refs_1_ = bf16[576,256]{1,0:T(8,128)(2,1)S(1)} collective-permute-done((bf16[576,256]{1,0:T(8,128)(2,1)S(1)}, bf16[576,256]{1,0:T(8,128)(2,1)S(1)}, u32[]{:S(2)}, u32[]{:S(2)}) %collective-permute-start.28) | collective-permute-done | bytes 294944 | tf_op jit(solution)/shard_map/ppermute | solution.py:365
  86.9 2.5 %collective-permute-start.30 = (bf16[288,256]{1,0:T(8,128)(2,1)S(1)}, bf16[288,256]{1,0:T(8,128)(2,1)S(1)}, u32[]{:S(2)}, u32[]{:S(2)}) collective-permute-start(bf16[288,256]{1,0:T(8,128)(2,1)S(1)} %get-tuple-element.106), channel_id=1, source_target_pairs={{0,8},{4,12},{8,0},{12,4},{16,24},{20,28},{24,16},{28,20},{1,9},{5... | collective-permute-start | bytes 442376 | tf_op jit(solution)/shard_map/ppermute | solution.py:365
  93.3 4.6 %collective-permute-start.31 = (bf16[144,256]{1,0:T(8,128)(2,1)S(1)}, bf16[144,256]{1,0:T(8,128)(2,1)S(1)}, u32[]{:S(2)}, u32[]{:S(2)}) collective-permute-start(bf16[144,256]{1,0:T(8,128)(2,1)S(1)} %get-tuple-element.108), channel_id=1, source_target_pairs={{0,16},{4,20},{8,24},{12,28},{16,0},{20,4},{24,8},{28,12},{1,17},{... | collective-permute-start | bytes 221192 | tf_op jit(solution)/shard_map/ppermute | solution.py:365
  99.3 3.7 %collective-permute-start.36 = (bf16[128,256]{1,0:T(8,128)(2,1)S(1)}, bf16[128,256]{1,0:T(8,128)(2,1)S(1)}, u32[]{:S(2)}, u32[]{:S(2)}) collective-permute-start(bf16[128,256]{1,0:T(8,128)(2,1)S(1)} %get-tuple-element.115), channel_id=1, source_target_pairs={{0,4},{4,0},{8,12},{12,8},{16,20},{20,16},{24,28},{28,24},{1,5},{5... | collective-permute-start | bytes 196616 | tf_op jit(solution)/shard_map/ppermute | solution.py:365
  107.8 3.1 %collective-permute-start.37 = (bf16[128,256]{1,0:T(8,128)(2,1)S(1)}, bf16[128,256]{1,0:T(8,128)(2,1)S(1)}, u32[]{:S(2)}, u32[]{:S(2)}) collective-permute-start(bf16[128,256]{1,0:T(8,128)(2,1)S(1)} %shard_map.156.refs_0_), channel_id=1, source_target_pairs={{0,4},{4,0},{8,12},{12,8},{16,20},{20,16},{24,28},{28,24},{1,5},{5... | collective-permute-start | bytes 196616 | tf_op jit(solution)/shard_map/ppermute | solution.py:365
  114.5 2.2 %collective-permute-start.42 = (bf16[256,256]{1,0:T(8,128)(2,1)S(1)}, bf16[256,256]{1,0:T(8,128)(2,1)S(1)}, u32[]{:S(2)}, u32[]{:S(2)}) collective-permute-start(bf16[256,256]{1,0:T(8,128)(2,1)S(1)} %shard_map.162.refs_0_), channel_id=1, source_target_pairs={{0,4},{4,0},{8,12},{12,8},{16,20},{20,16},{24,28},{28,24},{1,5},{5... | collective-permute-start | bytes 393224 | tf_op jit(solution)/shard_map/ppermute | solution.py:365
  119.0 3.5 %collective-permute-start.34 = (bf16[576,256]{1,0:T(8,128)(2,1)S(1)}, bf16[576,256]{1,0:T(8,128)(2,1)S(1)}, u32[]{:S(2)}, u32[]{:S(2)}) collective-permute-start(bf16[576,256]{1,0:T(8,128)(2,1)S(1)} %shard_map.152.refs_0_), channel_id=1, source_target_pairs={{0,4},{4,0},{8,12},{12,8},{16,20},{20,16},{24,28},{28,24},{1,5},{5... | collective-permute-start | bytes 884744 | tf_op jit(solution)/shard_map/ppermute | solution.py:365
  127.6 2.0 %collective-permute-done.43.refs_1_ = bf16[512,256]{1,0:T(8,128)(2,1)S(1)} collective-permute-done((bf16[512,256]{1,0:T(8,128)(2,1)S(1)}, bf16[512,256]{1,0:T(8,128)(2,1)S(1)}, u32[]{:S(2)}, u32[]{:S(2)}) %collective-permute-start.43) | collective-permute-done | bytes 262176 | tf_op jit(solution)/shard_map/ppermute | solution.py:365
  (121 shorter events, 51.7 us)
Async XLA Ops:
  0.6 16.3 %collective-permute-start.3 = (bf16[512,256]{1,0:T(8,128)(2,1)}, bf16[512,256]{1,0:T(8,128)(2,1)S(1)}, u32[]{:S(2)}, u32[]{:S(2)}) collective-permute-start(bf16[512,256]{1,0:T(8,128)(2,1)} %cotangent.1), channel_id=1, source_target_pairs={{0,28},{4,24},{8,20},{12,16},{16,12},{20,8},{24,4},{28,0},{1,29},{... | collective-permute-start | bytes 786440 | tf_op jit(solution)/shard_map/ppermute | solution.py:374
  6.7 8.9 %collective-permute-start = (bf16[512,256]{1,0:T(8,128)(2,1)}, bf16[512,256]{1,0:T(8,128)(2,1)S(1)}, u32[]{:S(2)}, u32[]{:S(2)}) collective-permute-start(bf16[512,256]{1,0:T(8,128)(2,1)} %cotangent.1), channel_id=1, source_target_pairs={{0,2},{1,3},{2,0},{3,1},{4,6},{5,7},{6,4},{7,5},{8,10},{9,11},{10,... | collective-permute-start | bytes 786440 | tf_op jit(solution)/shard_map/ppermute | solution.py:365
  11.5 11.2 %collective-permute-start.8 = (bf16[512,256]{1,0:T(8,128)(2,1)}, bf16[512,256]{1,0:T(8,128)(2,1)S(1)}, u32[]{:S(2)}, u32[]{:S(2)}) collective-permute-start(bf16[512,256]{1,0:T(8,128)(2,1)} %get-tuple-element.69.refs_0_.block_in), channel_id=1, source_target_pairs={{0,2},{1,3},{2,0},{3,1},{4,6},{5,7},{6,4},{7,5},{8,10},{9,11},{10,... | collective-permute-start | bytes 786440 | tf_op jit(solution)/shard_map/ppermute | solution.py:365
  12.1 9.9 %collective-permute-start.7 = (bf16[512,256]{1,0:T(8,128)(2,1)}, bf16[512,256]{1,0:T(8,128)(2,1)S(1)}, u32[]{:S(2)}, u32[]{:S(2)}) collective-permute-start(bf16[512,256]{1,0:T(8,128)(2,1)} %get-tuple-element.69.refs_0_.block_in), channel_id=1, source_target_pairs={{0,1},{1,0},{2,3},{3,2},{4,5},{5,4},{6,7},{7,6},{8,9},{9,8},{10,11... | collective-permute-start | bytes 786440 | tf_op jit(solution)/shard_map/ppermute | solution.py:365
  16.9 7.8 %collective-permute-start.4 = (bf16[160,256]{1,0:T(8,128)(2,1)S(1)}, bf16[160,256]{1,0:T(8,128)(2,1)S(1)}, u32[]{:S(2)}, u32[]{:S(2)}) collective-permute-start(bf16[160,256]{1,0:T(8,128)(2,1)S(1)} %copy-done.11), channel_id=1, source_target_pairs={{0,6},{4,2},{1,7},{5,3},{2,4},{6,0},{3,5},{7,1},{8,14},{12,10},{9,... | collective-permute-start | bytes 245768 | tf_op jit(solution)/shard_map/ppermute | solution.py:386
  22.7 13.9 %collective-permute-start.12 = (bf16[1024,256]{1,0:T(8,128)(2,1)S(1)}, bf16[1024,256]{1,0:T(8,128)(2,1)S(1)}, u32[]{:S(2)}, u32[]{:S(2)}) collective-permute-start(bf16[1024,256]{1,0:T(8,128)(2,1)S(1)} %copy-done.1), channel_id=1, source_target_pairs={{0,2},{1,3},{2,0},{3,1},{4,6},{5,7},{6,4},{7,5},{8,10},{9,11},{10,... | collective-permute-start | bytes 1572872 | tf_op jit(solution)/shard_map/ppermute | solution.py:365
  28.4 11.3 %collective-permute-start.11 = (bf16[512,256]{1,0:T(8,128)(2,1)S(1)}, bf16[512,256]{1,0:T(8,128)(2,1)S(1)}, u32[]{:S(2)}, u32[]{:S(2)}) collective-permute-start(bf16[512,256]{1,0:T(8,128)(2,1)S(1)} %get-tuple-element.75.refs_0_), channel_id=1, source_target_pairs={{0,28},{4,24},{8,20},{12,16},{16,12},{20,8},{24,4},{28,0},{1,29},{... | collective-permute-start | bytes 786440 | tf_op jit(solution)/shard_map/ppermute | solution.py:374
  36.6 8.6 %collective-permute-start.13 = (bf16[512,256]{1,0:T(8,128)(2,1)S(1)}, bf16[512,256]{1,0:T(8,128)(2,1)S(1)}, u32[]{:S(2)}, u32[]{:S(2)}) collective-permute-start(bf16[512,256]{1,0:T(8,128)(2,1)S(1)} %shard_map.138.refs_4_.mirrored_cotangent), channel_id=1, source_target_pairs={{0,2},{1,3},{2,0},{3,1},{4,6},{5,7},{6,4},{7,5},{8,10},{9,11},{10,... | collective-permute-start | bytes 786440 | tf_op jit(solution)/shard_map/ppermute | solution.py:365
  38.0 7.2 %collective-permute-start.18 = (bf16[512,256]{1,0:T(8,128)(2,1)S(1)}, bf16[512,256]{1,0:T(8,128)(2,1)S(1)}, u32[]{:S(2)}, u32[]{:S(2)}) collective-permute-start(bf16[512,256]{1,0:T(8,128)(2,1)S(1)} %copy-done.2), channel_id=1, source_target_pairs={{0,1},{1,0},{2,3},{3,2},{4,5},{5,4},{6,7},{7,6},{8,9},{9,8},{10,11... | collective-permute-start | bytes 786440 | tf_op jit(solution)/shard_map/ppermute | solution.py:365
  38.0 10.8 %collective-permute-start.14 = (bf16[512,256]{1,0:T(8,128)(2,1)S(1)}, bf16[512,256]{1,0:T(8,128)(2,1)S(1)}, u32[]{:S(2)}, u32[]{:S(2)}) collective-permute-start(bf16[512,256]{1,0:T(8,128)(2,1)S(1)} %get-tuple-element.75.refs_0_), channel_id=1, source_target_pairs={{0,2},{1,3},{2,0},{3,1},{4,6},{5,7},{6,4},{7,5},{8,10},{9,11},{10,... | collective-permute-start | bytes 786440 | tf_op jit(solution)/shard_map/ppermute | solution.py:365
  38.7 12.8 %collective-permute-start.22 = (bf16[1024,256]{1,0:T(8,128)(2,1)S(1)}, bf16[1024,256]{1,0:T(8,128)(2,1)S(1)}, u32[]{:S(2)}, u32[]{:S(2)}) collective-permute-start(bf16[1024,256]{1,0:T(8,128)(2,1)S(1)} %copy-done.1), channel_id=1, source_target_pairs={{0,1},{1,0},{2,3},{3,2},{4,5},{5,4},{6,7},{7,6},{8,9},{9,8},{10,11... | collective-permute-start | bytes 1572872 | tf_op jit(solution)/shard_map/ppermute | solution.py:365
  39.7 10.0 %collective-permute-start.19 = (bf16[512,256]{1,0:T(8,128)(2,1)S(1)}, bf16[512,256]{1,0:T(8,128)(2,1)S(1)}, u32[]{:S(2)}, u32[]{:S(2)}) collective-permute-start(bf16[512,256]{1,0:T(8,128)(2,1)S(1)} %collective-permute-done.refs_2_), channel_id=1, source_target_pairs={{0,1},{1,0},{2,3},{3,2},{4,5},{5,4},{6,7},{7,6},{8,9},{9,8},{10,11... | collective-permute-start | bytes 786440 | tf_op jit(solution)/shard_map/ppermute | solution.py:365
  49.7 8.8 %collective-permute-start.17 = (bf16[512,256]{1,0:T(8,128)(2,1)S(1)}, bf16[512,256]{1,0:T(8,128)(2,1)S(1)}, u32[]{:S(2)}, u32[]{:S(2)}) collective-permute-start(bf16[512,256]{1,0:T(8,128)(2,1)S(1)} %shard_map.142.refs_4_), channel_id=1, source_target_pairs={{0,2},{1,3},{2,0},{3,1},{4,6},{5,7},{6,4},{7,5},{8,10},{9,11},{10,... | collective-permute-start | bytes 786440 | tf_op jit(solution)/shard_map/ppermute | solution.py:365
  70.6 8.0 %collective-permute-start.27 = (bf16[256,256]{1,0:T(8,128)(2,1)S(1)}, bf16[256,256]{1,0:T(8,128)(2,1)S(1)}, u32[]{:S(2)}, u32[]{:S(2)}) collective-permute-start(bf16[256,256]{1,0:T(8,128)(2,1)S(1)} %get-tuple-element.101), channel_id=1, source_target_pairs={{0,4},{4,0},{8,12},{12,8},{16,20},{20,16},{24,28},{28,24},{1,5},{5... | collective-permute-start | bytes 393224 | tf_op jit(solution)/shard_map/ppermute | solution.py:365
  78.6 7.5 %collective-permute-start.28 = (bf16[576,256]{1,0:T(8,128)(2,1)S(1)}, bf16[576,256]{1,0:T(8,128)(2,1)S(1)}, u32[]{:S(2)}, u32[]{:S(2)}) collective-permute-start(bf16[576,256]{1,0:T(8,128)(2,1)S(1)} %get-tuple-element.102), channel_id=1, source_target_pairs={{0,4},{4,0},{8,12},{12,8},{16,20},{20,16},{24,28},{28,24},{1,5},{5... | collective-permute-start | bytes 884744 | tf_op jit(solution)/shard_map/ppermute | solution.py:365
  90.0 8.7 %collective-permute-start.35 = (bf16[256,256]{1,0:T(8,128)(2,1)S(1)}, bf16[256,256]{1,0:T(8,128)(2,1)S(1)}, u32[]{:S(2)}, u32[]{:S(2)}) collective-permute-start(bf16[256,256]{1,0:T(8,128)(2,1)S(1)} %get-tuple-element.113), channel_id=1, source_target_pairs={{0,16},{4,20},{8,24},{12,28},{16,0},{20,4},{24,8},{28,12},{1,17},{... | collective-permute-start | bytes 393224 | tf_op jit(solution)/shard_map/ppermute | solution.py:365
  93.3 9.8 %collective-permute-start.31 = (bf16[144,256]{1,0:T(8,128)(2,1)S(1)}, bf16[144,256]{1,0:T(8,128)(2,1)S(1)}, u32[]{:S(2)}, u32[]{:S(2)}) collective-permute-start(bf16[144,256]{1,0:T(8,128)(2,1)S(1)} %get-tuple-element.108), channel_id=1, source_target_pairs={{0,16},{4,20},{8,24},{12,28},{16,0},{20,4},{24,8},{28,12},{1,17},{... | collective-permute-start | bytes 221192 | tf_op jit(solution)/shard_map/ppermute | solution.py:365
  99.3 7.9 %collective-permute-start.36 = (bf16[128,256]{1,0:T(8,128)(2,1)S(1)}, bf16[128,256]{1,0:T(8,128)(2,1)S(1)}, u32[]{:S(2)}, u32[]{:S(2)}) collective-permute-start(bf16[128,256]{1,0:T(8,128)(2,1)S(1)} %get-tuple-element.115), channel_id=1, source_target_pairs={{0,4},{4,0},{8,12},{12,8},{16,20},{20,16},{24,28},{28,24},{1,5},{5... | collective-permute-start | bytes 196616 | tf_op jit(solution)/shard_map/ppermute | solution.py:365
  103.6 7.3 %collective-permute-start.32 = (bf16[144,256]{1,0:T(8,128)(2,1)S(1)}, bf16[144,256]{1,0:T(8,128)(2,1)S(1)}, u32[]{:S(2)}, u32[]{:S(2)}) collective-permute-start(bf16[144,256]{1,0:T(8,128)(2,1)S(1)} %shard_map.150.refs_0_), channel_id=1, source_target_pairs={{0,16},{4,20},{8,24},{12,28},{16,0},{20,4},{24,8},{28,12},{1,17},{... | collective-permute-start | bytes 221192 | tf_op jit(solution)/shard_map/ppermute | solution.py:365
  106.0 8.0 %collective-permute-start.41 = (bf16[128,256]{1,0:T(8,128)(2,1)S(1)}, bf16[128,256]{1,0:T(8,128)(2,1)S(1)}, u32[]{:S(2)}, u32[]{:S(2)}) collective-permute-start(bf16[128,256]{1,0:T(8,128)(2,1)S(1)} %shard_map.161.refs_0_), channel_id=1, source_target_pairs={{0,16},{4,20},{8,24},{12,28},{16,0},{20,4},{24,8},{28,12},{1,17},{... | collective-permute-start | bytes 196616 | tf_op jit(solution)/shard_map/ppermute | solution.py:365
  107.8 9.0 %collective-permute-start.37 = (bf16[128,256]{1,0:T(8,128)(2,1)S(1)}, bf16[128,256]{1,0:T(8,128)(2,1)S(1)}, u32[]{:S(2)}, u32[]{:S(2)}) collective-permute-start(bf16[128,256]{1,0:T(8,128)(2,1)S(1)} %shard_map.156.refs_0_), channel_id=1, source_target_pairs={{0,4},{4,0},{8,12},{12,8},{16,20},{20,16},{24,28},{28,24},{1,5},{5... | collective-permute-start | bytes 196616 | tf_op jit(solution)/shard_map/ppermute | solution.py:365
  114.5 7.9 %collective-permute-start.42 = (bf16[256,256]{1,0:T(8,128)(2,1)S(1)}, bf16[256,256]{1,0:T(8,128)(2,1)S(1)}, u32[]{:S(2)}, u32[]{:S(2)}) collective-permute-start(bf16[256,256]{1,0:T(8,128)(2,1)S(1)} %shard_map.162.refs_0_), channel_id=1, source_target_pairs={{0,4},{4,0},{8,12},{12,8},{16,20},{20,16},{24,28},{28,24},{1,5},{5... | collective-permute-start | bytes 393224 | tf_op jit(solution)/shard_map/ppermute | solution.py:365
  117.4 7.3 %collective-permute-start.38 = (bf16[256,256]{1,0:T(8,128)(2,1)S(1)}, bf16[256,256]{1,0:T(8,128)(2,1)S(1)}, u32[]{:S(2)}, u32[]{:S(2)}) collective-permute-start(bf16[256,256]{1,0:T(8,128)(2,1)S(1)} %shard_map.157.refs_0_), channel_id=1, source_target_pairs={{0,16},{4,20},{8,24},{12,28},{16,0},{20,4},{24,8},{28,12},{1,17},{... | collective-permute-start | bytes 393224 | tf_op jit(solution)/shard_map/ppermute | solution.py:365
  119.0 14.8 %collective-permute-start.34 = (bf16[576,256]{1,0:T(8,128)(2,1)S(1)}, bf16[576,256]{1,0:T(8,128)(2,1)S(1)}, u32[]{:S(2)}, u32[]{:S(2)}) collective-permute-start(bf16[576,256]{1,0:T(8,128)(2,1)S(1)} %shard_map.152.refs_0_), channel_id=1, source_target_pairs={{0,4},{4,0},{8,12},{12,8},{16,20},{20,16},{24,28},{28,24},{1,5},{5... | collective-permute-start | bytes 884744 | tf_op jit(solution)/shard_map/ppermute | solution.py:365
  (32 other events, 180.9 us)

commit v14 on v13

--- a/solution.py
+++ b/solution.py
@@ -293,27 +293,29 @@
 def step_kernel(plan, place, *refs):
     sources, targets = refs[: 2 * len(plan)], list(refs[2 * len(plan) :])
     for k, (done, after) in enumerate(plan):
-        mine, other = sources[2 * k][...].astype(F32), sources[2 * k + 1][...].astype(F32)
-        if done[0] == "halve":
-            total = mine + other
+        mine, other = sources[2 * k : 2 * k + 2]
+        rows = mine.shape[0]
+        if done[0] == "double":
+            bit = (place[0] // done[1]) % 2
+            target = targets.pop(0)
+            count = rows - SPARE if after is not None and after[0] == "take" else rows
+            target[part(bit, count, 16), :] = mine[:count]
+            target[part(1 - bit, count, 16), :] = other[:count]
+            if count < rows:
+                taps = targets.pop(0)
+                first = mine[count:].astype(F32), other[count:].astype(F32)
+                low, _ = join(*first, bit)
+                for number in range(taps.shape[0]):
+                    taps[number] = low[number * taps.shape[1] : (number + 1) * taps.shape[1]]
+        elif after is not None and after[0] == "halve":
+            half = rows // 2
+            bit = (place[0] // after[1]) % 2
+            for way in (1 - bit, bit):
+                at = part(way, half, 16)
+                target = targets.pop(0)
+                target[...] = (mine[at, :] + other[at, :].astype(F32)).astype(target.dtype)
         else:
-            low, high = join(mine, other, (place[0] // done[1]) % 2)
-            if after is not None and after[0] == "take":
-                grad, taps = targets.pop(0), targets.pop(0)
-                count = low.shape[0] - SPARE
-                grad[:count] = low[:count].astype(BF16)
-                grad[count:] = high[:count].astype(BF16)
-                for number in range(taps.shape[0]):
-                    start = count + number * taps.shape[1]
-                    taps[number] = low[start : start + taps.shape[1]]
-                continue
-            total = jnp.concatenate([low, high], axis=0)
-        if after is not None and after[0] == "halve":
-            sent, kept = split(total, (place[0] // after[1]) % 2)
-            targets.pop(0)[...] = sent.astype(BF16)
-            targets.pop(0)[...] = kept
-        else:
-            targets.pop(0)[...] = total.astype(BF16)
+            targets.pop(0)[...] = (mine[...] + other[...].astype(F32)).astype(BF16)
 
 
 def advance(place, items, taps):
@@ -332,7 +334,16 @@
             counts.append(1)
     arrays = [array for item in items for array in item[2:]]
     plan = [item[:2] for item in items]
-    if all(shape[0] % 8 == 0 or len(shape) == 3 for shape, _ in outs) and all(x.shape[0] % 8 == 0 for x in arrays):
+    fits = True
+    for done, after, mine, _ in items:
+        rows = mine.shape[0]
+        if done[0] == "double":
+            fits &= rows % 16 == 0
+        elif after is not None and after[0] == "halve":
+            fits &= rows % 32 == 0
+        else:
+            fits &= rows % 8 == 0
+    if fits:
         results = run(functools.partial(step_kernel, plan), place, arrays, outs)
     else:
         results = []
@@ -374,16 +385,14 @@
     return lax.ppermute(block, "seq", [(i, count - 1 - i) for i in range(count)])
 
 
-def swap_edges(first, second, far=0):
-    count, channels = lax.axis_size("seq"), lax.axis_size("ch")
+def swap_edges(first, second):
+    count = lax.axis_size("seq")
     received = []
     for turn, block in enumerate((first, second)):
         route = []
         for low in range(turn, count - 1, 2):
-            for c in range(channels):
-                route.append((low * channels + c, (low + 1) * channels + (c ^ far)))
-                route.append(((low + 1) * channels + c, low * channels + (c ^ far)))
-        received.append(lax.ppermute(block, ("seq", "ch"), route))
+            route += [(low, low + 1), (low + 1, low)]
+        received.append(lax.ppermute(block, "seq", route))
     return received
 
 
@@ -425,11 +434,12 @@
         [((full, full), BF16)],
         gflop=2.0,
     )[0]
-    first, second, early_w_out, cotangent_x = together(first, second, w_out, cotangent_x)
+    first, second, cotangent_x = together(first, second, cotangent_x)
     near = swap_edges(first, second)
-    first, second, mirrored_cotangent = together(first, second, mirrored_cotangent)
-    far = swap_edges(first, second, cross)
-    edges = jnp.concatenate(near + far, axis=0)
+    near = jnp.concatenate(near, axis=0)
+    far = exchange(near, "ch", cross)
+    early_w_out, far = together(w_out, far)
+    edges = jnp.concatenate([near, far], axis=0)
     w_out_x = exchange(early_w_out, "ch", cross)
     mirrored_cotangent = run(flip_kernel, place, (mirrored_cotangent,), [block], gflop=1.0)[0]
     mirrored_cotangent, input_core, choose = together(mirrored_cotangent, input_core, choose)
@@ -453,10 +463,9 @@
     )
     mirrored_cotangent, w_out_x = together(mirrored_cotangent, w_out_x)
     mirrored_cotangent_x = exchange(mirrored_cotangent, "ch", cross)
-    mirrored, mirrored_cotangent_x = together(mirror(gated), mirrored_cotangent_x)
+    gated_x = exchange(gated, "ch", cross)
+    mirrored, mirrored_cotangent_x, gated_x = together(mirror(gated), mirrored_cotangent_x, gated_x)
     mirrored = run(flip_kernel, place, (mirrored,), [block], gflop=12.0)[0]
-    gated_x = exchange(gated, "ch", cross)
-    mirrored, gated_x = together(mirrored, gated_x)
     mirrored_x = exchange(mirrored, "ch", cross)
     gated_all = [gated, exchange(gated, "ch", 1), gated_x, exchange(gated_x, "ch", 1)]
     cotangent_all = [cotangent, exchange(cotangent, "ch", 1), cotangent_x, exchange(cotangent_x, "ch", 1)]

time: 136 us -> 136 us (level)
  waiting for transfers between devices: 37.1 us -> 51.5 us
  starting transfers between devices: 59.6 us -> 46.1 us
    ppermute x36 -> x37, waiting for transfers between devices: 34.1 us -> 51.2 us  [exchange(): return lax.ppermute(block, axis, [(i, i ^ distance) for i in range(count)])]
    ppermute x36 -> x37, starting transfers between devices: 42.5 us -> 33.9 us  [exchange(): return lax.ppermute(block, axis, [(i, i ^ distance) for i in range(count)])]
    ppermute x6 -> x4, starting transfers between devices: 9.11 us -> 5.77 us  [swap_edges(): received.append(lax.ppermute(block, 'seq', route))]
    ppermute x6 -> x4, waiting for transfers between devices: 2.11 us -> 0.35 us  [swap_edges(): received.append(lax.ppermute(block, 'seq', route))]
    ppermute x2, starting transfers between devices: 7.96 us -> 6.43 us  [mirror(): lax.ppermute(block, 'seq', [(i, count - 1 - i) for i in range(count)])]
  transfers between devices with their start and end apart: 44 -> 43, of which waited for: 21 -> 21; matrix products, arithmetic and copies ran while one was open for 0% -> 0% of each run, Pallas kernels for 21% -> 21%
where the time goes in v14:
time: 136 us
  waiting for transfers between devices  51.5 us (38%)
  starting transfers between devices  46.1 us (34%)
  Pallas kernels  35.1 us (26%)
  local copies, waits for them, and re-layouts  1.42 us (1%)
    ppermute x37, waiting for transfers between devices, exchange(): return lax.ppermute(block, axis, [(i, i ^ distance) for i in range(count)])  51.2 us
    pallas_call x28, Pallas kernels, run(): pl.pallas_call(body, out_shape=[jax.ShapeDtypeStruct(shape, dtype) for sh...  35.1 us
    ppermute x37, starting transfers between devices, exchange(): return lax.ppermute(block, axis, [(i, i ^ distance) for i in range(count)])  33.9 us
    ppermute x2, starting transfers between devices, mirror(): lax.ppermute(block, 'seq', [(i, count - 1 - i) for i in range(count)])  6.43 us
    ppermute x4, starting transfers between devices, swap_edges(): received.append(lax.ppermute(block, 'seq', route))  5.77 us
  transfers between devices with their start and end apart: 43, of which 21 were waited for; matrix products, arithmetic and copies ran while one was open for 0% of the time, Pallas kernels for 21%

profile of v14, /device:TPU:0, one launch (start us, length us, event | category | flops | bytes accessed | tf_op | source)
XLA Modules:
  0.0 135.7 jit_solution(3872688016529131798)
XLA Ops:
  0.6 6.1 %collective-permute-start.5 = (bf16[512,256]{1,0:T(8,128)(2,1)}, bf16[512,256]{1,0:T(8,128)(2,1)S(1)}, u32[]{:S(2)}, u32[]{:S(2)}) collective-permute-start(bf16[512,256]{1,0:T(8,128)(2,1)} %cotangent.1), channel_id=1, source_target_pairs={{0,28},{4,24},{8,20},{12,16},{16,12},{20,8},{24,4},{28,0},{1,29},{... | collective-permute-start | bytes 786440 | tf_op jit(solution)/shard_map/ppermute | solution.py:385
  8.8 2.7 %shard_map.137 = (bf16[512,256]{1,0:T(8,128)(2,1)}, bf16[160,256]{1,0:T(8,128)(2,1)}, bf16[160,256]{1,0:T(8,128)(2,1)}) custom-call(s32[3]{0:T(128)} %pad_add_fusion.place, s32[1,512]{1,0:T(1,128)} %bitcast.7, bf16[512,256]{1,0:T(8,128)(2,1)} %hidden_hbm.1, bf16[4,256]{1,0:T(4,128)(2,1)} %embedding_hbm.1), custom_call_target="tpu_custom_call" | custom-call | flops 100000000 | bytes 266240 | tf_op jit(solution)/shard_map/pallas_call | solution.py:30
  17.8 2.5 %collective-permute-done.7.refs_2_ = bf16[512,256]{1,0:T(8,128)(2,1)S(1)} collective-permute-done((bf16[512,256]{1,0:T(8,128)(2,1)}, bf16[512,256]{1,0:T(8,128)(2,1)S(1)}, u32[]{:S(2)}, u32[]{:S(2)}) %collective-permute-start.7) | collective-permute-done | bytes 262176 | tf_op jit(solution)/shard_map/ppermute | solution.py:376
  20.3 1.9 %collective-permute-start.3 = (bf16[320,256]{1,0:T(8,128)(2,1)S(1)}, bf16[320,256]{1,0:T(8,128)(2,1)S(1)}, u32[]{:S(2)}, u32[]{:S(2)}) collective-permute-start(bf16[320,256]{1,0:T(8,128)(2,1)S(1)} %pad_maximum_fusion), channel_id=1, source_target_pairs={{0,2},{1,3},{2,0},{3,1},{4,6},{5,7},{6,4},{7,5},{8,10},{9,11},{10,... | collective-permute-start | bytes 491528 | tf_op jit(solution)/shard_map/ppermute | solution.py:376
  22.3 4.7 %collective-permute-done.3 = bf16[320,256]{1,0:T(8,128)(2,1)S(1)} collective-permute-done((bf16[320,256]{1,0:T(8,128)(2,1)S(1)}, bf16[320,256]{1,0:T(8,128)(2,1)S(1)}, u32[]{:S(2)}, u32[]{:S(2)}) %collective-permute-start.3) | collective-permute-done | bytes 163872 | tf_op jit(solution)/shard_map/ppermute | solution.py:376
  30.0 2.0 %shard_map.141 = (bf16[2192,256]{1,0:T(8,128)(2,1)S(1)}, bf16[512,256]{1,0:T(8,128)(2,1)S(1)}, bf16[512,256]{1,0:T(8,128)(2,1)S(1)}) custom-call(s32[3]{0:T(128)S(1)} %copy-done.4, bf16[640,256]{1,0:T(8,128)(2,1)S(1)} %constant_dynamic-update-slice_fusion.edges, bf16[640,256]{1,0:T(8,128)(2,1)S(1)} %collective-permute-done.4.edges_core, ...), custom_call_target="tpu_custom_call" | custom-call | flops 400000000 | bytes 2240512 | tf_op jit(solution)/shard_map/pallas_call | solution.py:30
  33.0 9.0 %collective-permute-done.11.refs_10_ = bf16[1024,256]{1,0:T(8,128)(2,1)S(1)} collective-permute-done((bf16[1024,256]{1,0:T(8,128)(2,1)S(1)}, bf16[1024,256]{1,0:T(8,128)(2,1)S(1)}, u32[]{:S(2)}, u32[]{:S(2)}) %collective-permute-start.11) | collective-permute-done | bytes 524320 | tf_op jit(solution)/shard_map/ppermute | solution.py:376
  43.9 3.6 %collective-permute-done.13.refs_2_ = bf16[512,256]{1,0:T(8,128)(2,1)S(1)} collective-permute-done((bf16[512,256]{1,0:T(8,128)(2,1)S(1)}, bf16[512,256]{1,0:T(8,128)(2,1)S(1)}, u32[]{:S(2)}, u32[]{:S(2)}) %collective-permute-start.13) | collective-permute-done | bytes 262176 | tf_op jit(solution)/shard_map/ppermute | solution.py:376
  48.0 4.6 %collective-permute-done.12.refs_6_ = bf16[512,256]{1,0:T(8,128)(2,1)S(1)} collective-permute-done((bf16[512,256]{1,0:T(8,128)(2,1)S(1)}, bf16[512,256]{1,0:T(8,128)(2,1)S(1)}, u32[]{:S(2)}, u32[]{:S(2)}) %collective-permute-start.12) | collective-permute-done | bytes 262176 | tf_op jit(solution)/shard_map/ppermute | solution.py:376
  56.2 2.9 %shard_map.143.refs_8_ = bf16[1024,1024]{1,0:T(8,128)(2,1)S(1)} custom-call(s32[3]{0:T(128)S(1)} %copy-done.4, bf16[512,256]{1,0:T(8,128)(2,1)S(1)} %copy-done.2, bf16[512,256]{1,0:T(8,128)(2,1)S(1)} %collective-permute-done.17.refs_1_, bf16[512,256]{1,0:T(8,128)(2,1)S(1)} %collective-permute-done.refs_2_, ...), custom_call_target="tpu_custom_call" | custom-call | flops 2100000000 | bytes 4194304 | tf_op jit(solution)/shard_map/pallas_call | solution.py:30
  59.1 3.2 %collective-permute-done.16.refs_6_ = bf16[512,256]{1,0:T(8,128)(2,1)S(1)} collective-permute-done((bf16[512,256]{1,0:T(8,128)(2,1)S(1)}, bf16[512,256]{1,0:T(8,128)(2,1)S(1)}, u32[]{:S(2)}, u32[]{:S(2)}) %collective-permute-start.16) | collective-permute-done | bytes 262176 | tf_op jit(solution)/shard_map/ppermute | solution.py:376
  63.9 5.7 %shard_map.144 = (bf16[1024,1024]{1,0:T(8,128)(2,1)S(1)}, bf16[512,256]{1,0:T(8,128)(2,1)S(1)}, bf16[512,256]{1,0:T(8,128)(2,1)S(1)}, bf16[160,256]{1,0:T(8,128)(2,1)S(1)}, bf16[160,256]{1,0:T(8,128)(2,1)S(1)}) custom-call(s32[3]{0:T(128)S(1)} %copy-done.4, bf16[512,256]{1,0:T(8,128)(2,1)S(1)} %get-tuple-element.70.refs_0_, ...), custom_call_target="tpu_custom_call" | custom-call | flops 2500000000 | bytes 7081984 | tf_op jit(solution)/shard_map/pallas_call | solution.py:30
  69.6 3.7 %collective-permute-start.24 = (bf16[160,256]{1,0:T(8,128)(2,1)S(1)}, bf16[160,256]{1,0:T(8,128)(2,1)S(1)}, u32[]{:S(2)}, u32[]{:S(2)}) collective-permute-start(bf16[160,256]{1,0:T(8,128)(2,1)S(1)} %get-tuple-element.88), channel_id=1, source_target_pairs={{0,4},{4,0},{8,12},{12,8},{16,20},{20,16},{24,28},{28,24},{1,5},{5... | collective-permute-start | bytes 245768 | tf_op jit(solution)/shard_map/ppermute | solution.py:395
  76.0 4.5 %collective-permute-start.26 = (bf16[256,256]{1,0:T(8,128)(2,1)S(1)}, bf16[256,256]{1,0:T(8,128)(2,1)S(1)}, u32[]{:S(2)}, u32[]{:S(2)}) collective-permute-start(bf16[256,256]{1,0:T(8,128)(2,1)S(1)} %get-tuple-element.95), channel_id=1, source_target_pairs={{0,4},{4,0},{8,12},{12,8},{16,20},{20,16},{24,28},{28,24},{1,5},{5... | collective-permute-start | bytes 393224 | tf_op jit(solution)/shard_map/ppermute | solution.py:376
  80.6 2.5 %shard_map.147 = (bf16[576,256]{1,0:T(8,128)(2,1)S(1)}, f32[576,256]{1,0:T(8,128)S(1)}) custom-call(s32[3]{0:T(128)S(1)} %copy-done.4, bf16[512,256]{1,0:T(8,128)(2,1)S(1)} %get-tuple-element.84.upstream, bf16[160,256]{1,0:T(8,128)(2,1)S(1)} %collective-permute-done.24.first, bf16[160,256]{1,0:T(8,128)(2,1)S(1)} %collective-permute-done.25.second, ...), custom_call_target="tpu_custom_call" | custom-call | flops 500000000 | bytes 2609152 | tf_op jit(solution)/shard_map/pallas_call | solution.py:30
  83.5 2.0 %collective-permute-start.27 = (bf16[576,256]{1,0:T(8,128)(2,1)S(1)}, bf16[576,256]{1,0:T(8,128)(2,1)S(1)}, u32[]{:S(2)}, u32[]{:S(2)}) collective-permute-start(bf16[576,256]{1,0:T(8,128)(2,1)S(1)} %get-tuple-element.96), channel_id=1, source_target_pairs={{0,4},{4,0},{8,12},{12,8},{16,20},{20,16},{24,28},{28,24},{1,5},{5... | collective-permute-start | bytes 884744 | tf_op jit(solution)/shard_map/ppermute | solution.py:376
  86.1 5.0 %collective-permute-done.27.refs_1_ = bf16[576,256]{1,0:T(8,128)(2,1)S(1)} collective-permute-done((bf16[576,256]{1,0:T(8,128)(2,1)S(1)}, bf16[576,256]{1,0:T(8,128)(2,1)S(1)}, u32[]{:S(2)}, u32[]{:S(2)}) %collective-permute-start.27) | collective-permute-done | bytes 294944 | tf_op jit(solution)/shard_map/ppermute | solution.py:376
  93.3 3.9 %collective-permute-done.29.refs_1_ = bf16[288,256]{1,0:T(8,128)(2,1)S(1)} collective-permute-done((bf16[288,256]{1,0:T(8,128)(2,1)S(1)}, bf16[288,256]{1,0:T(8,128)(2,1)S(1)}, u32[]{:S(2)}, u32[]{:S(2)}) %collective-permute-start.29) | collective-permute-done | bytes 147488 | tf_op jit(solution)/shard_map/ppermute | solution.py:376
  97.8 1.6 %collective-permute-start.30 = (bf16[144,256]{1,0:T(8,128)(2,1)S(1)}, bf16[144,256]{1,0:T(8,128)(2,1)S(1)}, u32[]{:S(2)}, u32[]{:S(2)}) collective-permute-start(bf16[144,256]{1,0:T(8,128)(2,1)S(1)} %get-tuple-element.102), channel_id=1, source_target_pairs={{0,16},{4,20},{8,24},{12,28},{16,0},{20,4},{24,8},{28,12},{1,17},{... | collective-permute-start | bytes 221192 | tf_op jit(solution)/shard_map/ppermute | solution.py:376
  101.4 4.8 %collective-permute-done.34.refs_1_ = bf16[256,256]{1,0:T(8,128)(2,1)S(1)} collective-permute-done((bf16[256,256]{1,0:T(8,128)(2,1)S(1)}, bf16[256,256]{1,0:T(8,128)(2,1)S(1)}, u32[]{:S(2)}, u32[]{:S(2)}) %collective-permute-start.34) | collective-permute-done | bytes 131104 | tf_op jit(solution)/shard_map/ppermute | solution.py:376
  109.2 2.8 %collective-permute-start.40 = (bf16[128,256]{1,0:T(8,128)(2,1)S(1)}, bf16[128,256]{1,0:T(8,128)(2,1)S(1)}, u32[]{:S(2)}, u32[]{:S(2)}) collective-permute-start(bf16[128,256]{1,0:T(8,128)(2,1)S(1)} %shard_map.161.refs_0_), channel_id=1, source_target_pairs={{0,16},{4,20},{8,24},{12,28},{16,0},{20,4},{24,8},{28,12},{1,17},{... | collective-permute-start | bytes 196616 | tf_op jit(solution)/shard_map/ppermute | solution.py:376
  117.4 2.1 %collective-permute-start.37 = (bf16[256,256]{1,0:T(8,128)(2,1)S(1)}, bf16[256,256]{1,0:T(8,128)(2,1)S(1)}, u32[]{:S(2)}, u32[]{:S(2)}) collective-permute-start(bf16[256,256]{1,0:T(8,128)(2,1)S(1)} %shard_map.157.refs_0_), channel_id=1, source_target_pairs={{0,16},{4,20},{8,24},{12,28},{16,0},{20,4},{24,8},{28,12},{1,17},{... | collective-permute-start | bytes 393224 | tf_op jit(solution)/shard_map/ppermute | solution.py:376
  124.5 2.4 %collective-permute-start.38 = (bf16[512,256]{1,0:T(8,128)(2,1)S(1)}, bf16[512,256]{1,0:T(8,128)(2,1)S(1)}, u32[]{:S(2)}, u32[]{:S(2)}) collective-permute-start(bf16[512,256]{1,0:T(8,128)(2,1)S(1)} %shard_map.158.refs_0_), channel_id=1, source_target_pairs={{0,8},{4,12},{8,0},{12,4},{16,24},{20,28},{24,16},{28,20},{1,9},{5... | collective-permute-start | bytes 786440 | tf_op jit(solution)/shard_map/ppermute | solution.py:376
  126.9 1.7 %shard_map.145 = bf16[512,256]{1,0:T(8,128)(2,1)} custom-call(s32[3]{0:T(128)S(1)} %copy-done.4, bf16[1024,1024]{1,0:T(8,128)(2,1)S(1)} %get-tuple-element.83.normalized, bf16[1024,256]{1,0:T(8,128)(2,1)S(1)} %copy-done.1, bf16[512,256]{1,0:T(8,128)(2,1)S(1)} %copy-done), custom_call_target="tpu_custom_call" | custom-call | flops 300000000 | bytes 2883584 | tf_op jit(solution)/shard_map/pallas_call | solution.py:30
  (119 shorter events, 48.6 us)
Async XLA Ops:
  0.6 16.3 %collective-permute-start.5 = (bf16[512,256]{1,0:T(8,128)(2,1)}, bf16[512,256]{1,0:T(8,128)(2,1)S(1)}, u32[]{:S(2)}, u32[]{:S(2)}) collective-permute-start(bf16[512,256]{1,0:T(8,128)(2,1)} %cotangent.1), channel_id=1, source_target_pairs={{0,28},{4,24},{8,20},{12,16},{16,12},{20,8},{24,4},{28,0},{1,29},{... | collective-permute-start | bytes 786440 | tf_op jit(solution)/shard_map/ppermute | solution.py:385
  6.7 8.9 %collective-permute-start = (bf16[512,256]{1,0:T(8,128)(2,1)}, bf16[512,256]{1,0:T(8,128)(2,1)S(1)}, u32[]{:S(2)}, u32[]{:S(2)}) collective-permute-start(bf16[512,256]{1,0:T(8,128)(2,1)} %cotangent.1), channel_id=1, source_target_pairs={{0,2},{1,3},{2,0},{3,1},{4,6},{5,7},{6,4},{7,5},{8,10},{9,11},{10,... | collective-permute-start | bytes 786440 | tf_op jit(solution)/shard_map/ppermute | solution.py:376
  11.5 8.8 %collective-permute-start.7 = (bf16[512,256]{1,0:T(8,128)(2,1)}, bf16[512,256]{1,0:T(8,128)(2,1)S(1)}, u32[]{:S(2)}, u32[]{:S(2)}) collective-permute-start(bf16[512,256]{1,0:T(8,128)(2,1)} %get-tuple-element.65.refs_0_.block_in), channel_id=1, source_target_pairs={{0,2},{1,3},{2,0},{3,1},{4,6},{5,7},{6,4},{7,5},{8,10},{9,11},{10,... | collective-permute-start | bytes 786440 | tf_op jit(solution)/shard_map/ppermute | solution.py:376
  20.3 8.4 %collective-permute-start.8 = (bf16[512,256]{1,0:T(8,128)(2,1)S(1)}, bf16[512,256]{1,0:T(8,128)(2,1)S(1)}, u32[]{:S(2)}, u32[]{:S(2)}) collective-permute-start(bf16[512,256]{1,0:T(8,128)(2,1)S(1)} %collective-permute-done.7.refs_2_), channel_id=1, source_target_pairs={{0,1},{1,0},{2,3},{3,2},{4,5},{5,4},{6,7},{7,6},{8,9},{9,8},{10,11... | collective-permute-start | bytes 786440 | tf_op jit(solution)/shard_map/ppermute | solution.py:376
  27.1 14.8 %collective-permute-start.11 = (bf16[1024,256]{1,0:T(8,128)(2,1)S(1)}, bf16[1024,256]{1,0:T(8,128)(2,1)S(1)}, u32[]{:S(2)}, u32[]{:S(2)}) collective-permute-start(bf16[1024,256]{1,0:T(8,128)(2,1)S(1)} %copy-done.1), channel_id=1, source_target_pairs={{0,2},{1,3},{2,0},{3,1},{4,6},{5,7},{6,4},{7,5},{8,10},{9,11},{10,... | collective-permute-start | bytes 1572872 | tf_op jit(solution)/shard_map/ppermute | solution.py:376
  32.0 15.5 %collective-permute-start.13 = (bf16[512,256]{1,0:T(8,128)(2,1)S(1)}, bf16[512,256]{1,0:T(8,128)(2,1)S(1)}, u32[]{:S(2)}, u32[]{:S(2)}) collective-permute-start(bf16[512,256]{1,0:T(8,128)(2,1)S(1)} %get-tuple-element.70.refs_0_), channel_id=1, source_target_pairs={{0,2},{1,3},{2,0},{3,1},{4,6},{5,7},{6,4},{7,5},{8,10},{9,11},{10,... | collective-permute-start | bytes 786440 | tf_op jit(solution)/shard_map/ppermute | solution.py:376
  32.6 14.9 %collective-permute-start.10 = (bf16[512,256]{1,0:T(8,128)(2,1)S(1)}, bf16[512,256]{1,0:T(8,128)(2,1)S(1)}, u32[]{:S(2)}, u32[]{:S(2)}) collective-permute-start(bf16[512,256]{1,0:T(8,128)(2,1)S(1)} %get-tuple-element.70.refs_0_), channel_id=1, source_target_pairs={{0,28},{4,24},{8,20},{12,16},{16,12},{20,8},{24,4},{28,0},{1,29},{... | collective-permute-start | bytes 786440 | tf_op jit(solution)/shard_map/ppermute | solution.py:385
  41.9 10.8 %collective-permute-start.12 = (bf16[512,256]{1,0:T(8,128)(2,1)S(1)}, bf16[512,256]{1,0:T(8,128)(2,1)S(1)}, u32[]{:S(2)}, u32[]{:S(2)}) collective-permute-start(bf16[512,256]{1,0:T(8,128)(2,1)S(1)} %shard_map.138.refs_4_.mirrored_cotangent), channel_id=1, source_target_pairs={{0,2},{1,3},{2,0},{3,1},{4,6},{5,7},{6,4},{7,5},{8,10},{9,11},{10,... | collective-permute-start | bytes 786440 | tf_op jit(solution)/shard_map/ppermute | solution.py:376
  43.4 9.3 %collective-permute-start.17 = (bf16[512,256]{1,0:T(8,128)(2,1)S(1)}, bf16[512,256]{1,0:T(8,128)(2,1)S(1)}, u32[]{:S(2)}, u32[]{:S(2)}) collective-permute-start(bf16[512,256]{1,0:T(8,128)(2,1)S(1)} %copy-done.2), channel_id=1, source_target_pairs={{0,1},{1,0},{2,3},{3,2},{4,5},{5,4},{6,7},{7,6},{8,9},{9,8},{10,11... | collective-permute-start | bytes 786440 | tf_op jit(solution)/shard_map/ppermute | solution.py:376
  43.4 12.2 %collective-permute-start.21 = (bf16[1024,256]{1,0:T(8,128)(2,1)S(1)}, bf16[1024,256]{1,0:T(8,128)(2,1)S(1)}, u32[]{:S(2)}, u32[]{:S(2)}) collective-permute-start(bf16[1024,256]{1,0:T(8,128)(2,1)S(1)} %copy-done.1), channel_id=1, source_target_pairs={{0,1},{1,0},{2,3},{3,2},{4,5},{5,4},{6,7},{7,6},{8,9},{9,8},{10,11... | collective-permute-start | bytes 1572872 | tf_op jit(solution)/shard_map/ppermute | solution.py:376
  47.5 8.1 %collective-permute-start.19 = (bf16[512,256]{1,0:T(8,128)(2,1)S(1)}, bf16[512,256]{1,0:T(8,128)(2,1)S(1)}, u32[]{:S(2)}, u32[]{:S(2)}) collective-permute-start(bf16[512,256]{1,0:T(8,128)(2,1)S(1)} %shard_map.138.refs_4_.mirrored_cotangent), channel_id=1, source_target_pairs={{0,1},{1,0},{2,3},{3,2},{4,5},{5,4},{6,7},{7,6},{8,9},{9,8},{10,11... | collective-permute-start | bytes 786440 | tf_op jit(solution)/shard_map/ppermute | solution.py:376
  54.1 8.3 %collective-permute-start.16 = (bf16[512,256]{1,0:T(8,128)(2,1)S(1)}, bf16[512,256]{1,0:T(8,128)(2,1)S(1)}, u32[]{:S(2)}, u32[]{:S(2)}) collective-permute-start(bf16[512,256]{1,0:T(8,128)(2,1)S(1)} %shard_map.142.refs_4_), channel_id=1, source_target_pairs={{0,2},{1,3},{2,0},{3,1},{4,6},{5,7},{6,4},{7,5},{8,10},{9,11},{10,... | collective-permute-start | bytes 786440 | tf_op jit(solution)/shard_map/ppermute | solution.py:376
  55.6 6.7 %collective-permute-start.9 = (bf16[512,256]{1,0:T(8,128)(2,1)S(1)}, bf16[512,256]{1,0:T(8,128)(2,1)S(1)}, u32[]{:S(2)}, u32[]{:S(2)}) collective-permute-start(bf16[512,256]{1,0:T(8,128)(2,1)S(1)} %get-tuple-element.70.refs_0_), channel_id=1, source_target_pairs={{0,1},{1,0},{2,3},{3,2},{4,5},{5,4},{6,7},{7,6},{8,9},{9,8},{10,11... | collective-permute-start | bytes 786440 | tf_op jit(solution)/shard_map/ppermute | solution.py:376
  55.6 6.7 %collective-permute-start.15 = (bf16[512,256]{1,0:T(8,128)(2,1)S(1)}, bf16[512,256]{1,0:T(8,128)(2,1)S(1)}, u32[]{:S(2)}, u32[]{:S(2)}) collective-permute-start(bf16[512,256]{1,0:T(8,128)(2,1)S(1)} %shard_map.142.refs_4_), channel_id=1, source_target_pairs={{0,1},{1,0},{2,3},{3,2},{4,5},{5,4},{6,7},{7,6},{8,9},{9,8},{10,11... | collective-permute-start | bytes 786440 | tf_op jit(solution)/shard_map/ppermute | solution.py:376
  76.0 7.5 %collective-permute-start.26 = (bf16[256,256]{1,0:T(8,128)(2,1)S(1)}, bf16[256,256]{1,0:T(8,128)(2,1)S(1)}, u32[]{:S(2)}, u32[]{:S(2)}) collective-permute-start(bf16[256,256]{1,0:T(8,128)(2,1)S(1)} %get-tuple-element.95), channel_id=1, source_target_pairs={{0,4},{4,0},{8,12},{12,8},{16,20},{20,16},{24,28},{28,24},{1,5},{5... | collective-permute-start | bytes 393224 | tf_op jit(solution)/shard_map/ppermute | solution.py:376
  83.5 7.5 %collective-permute-start.27 = (bf16[576,256]{1,0:T(8,128)(2,1)S(1)}, bf16[576,256]{1,0:T(8,128)(2,1)S(1)}, u32[]{:S(2)}, u32[]{:S(2)}) collective-permute-start(bf16[576,256]{1,0:T(8,128)(2,1)S(1)} %get-tuple-element.96), channel_id=1, source_target_pairs={{0,4},{4,0},{8,12},{12,8},{16,20},{20,16},{24,28},{28,24},{1,5},{5... | collective-permute-start | bytes 884744 | tf_op jit(solution)/shard_map/ppermute | solution.py:376
  93.1 13.1 %collective-permute-start.34 = (bf16[256,256]{1,0:T(8,128)(2,1)S(1)}, bf16[256,256]{1,0:T(8,128)(2,1)S(1)}, u32[]{:S(2)}, u32[]{:S(2)}) collective-permute-start(bf16[256,256]{1,0:T(8,128)(2,1)S(1)} %get-tuple-element.107), channel_id=1, source_target_pairs={{0,16},{4,20},{8,24},{12,28},{16,0},{20,4},{24,8},{28,12},{1,17},{... | collective-permute-start | bytes 393224 | tf_op jit(solution)/shard_map/ppermute | solution.py:376
  97.8 10.0 %collective-permute-start.30 = (bf16[144,256]{1,0:T(8,128)(2,1)S(1)}, bf16[144,256]{1,0:T(8,128)(2,1)S(1)}, u32[]{:S(2)}, u32[]{:S(2)}) collective-permute-start(bf16[144,256]{1,0:T(8,128)(2,1)S(1)} %get-tuple-element.102), channel_id=1, source_target_pairs={{0,16},{4,20},{8,24},{12,28},{16,0},{20,4},{24,8},{28,12},{1,17},{... | collective-permute-start | bytes 221192 | tf_op jit(solution)/shard_map/ppermute | solution.py:376
  99.9 8.7 %collective-permute-start.39 = (bf16[128,256]{1,0:T(8,128)(2,1)S(1)}, bf16[128,256]{1,0:T(8,128)(2,1)S(1)}, u32[]{:S(2)}, u32[]{:S(2)}) collective-permute-start(bf16[128,256]{1,0:T(8,128)(2,1)S(1)} %get-tuple-element.113), channel_id=1, source_target_pairs={{0,16},{4,20},{8,24},{12,28},{16,0},{20,4},{24,8},{28,12},{1,17},{... | collective-permute-start | bytes 196616 | tf_op jit(solution)/shard_map/ppermute | solution.py:376
  114.3 6.8 %collective-permute-start.32 = (bf16[288,256]{1,0:T(8,128)(2,1)S(1)}, bf16[288,256]{1,0:T(8,128)(2,1)S(1)}, u32[]{:S(2)}, u32[]{:S(2)}) collective-permute-start(bf16[288,256]{1,0:T(8,128)(2,1)S(1)} %shard_map.151.refs_0_), channel_id=1, source_target_pairs={{0,8},{4,12},{8,0},{12,4},{16,24},{20,28},{24,16},{28,20},{1,9},{5... | collective-permute-start | bytes 442376 | tf_op jit(solution)/shard_map/ppermute | solution.py:376
  115.0 7.5 %collective-permute-start.41 = (bf16[256,256]{1,0:T(8,128)(2,1)S(1)}, bf16[256,256]{1,0:T(8,128)(2,1)S(1)}, u32[]{:S(2)}, u32[]{:S(2)}) collective-permute-start(bf16[256,256]{1,0:T(8,128)(2,1)S(1)} %shard_map.162.refs_0_), channel_id=1, source_target_pairs={{0,4},{4,0},{8,12},{12,8},{16,20},{20,16},{24,28},{28,24},{1,5},{5... | collective-permute-start | bytes 393224 | tf_op jit(solution)/shard_map/ppermute | solution.py:376
  121.7 12.6 %collective-permute-start.33 = (bf16[576,256]{1,0:T(8,128)(2,1)S(1)}, bf16[576,256]{1,0:T(8,128)(2,1)S(1)}, u32[]{:S(2)}, u32[]{:S(2)}) collective-permute-start(bf16[576,256]{1,0:T(8,128)(2,1)S(1)} %shard_map.152.refs_0_), channel_id=1, source_target_pairs={{0,4},{4,0},{8,12},{12,8},{16,20},{20,16},{24,28},{28,24},{1,5},{5... | collective-permute-start | bytes 884744 | tf_op jit(solution)/shard_map/ppermute | solution.py:376
  123.1 7.0 %collective-permute-start.42 = (bf16[512,256]{1,0:T(8,128)(2,1)S(1)}, bf16[512,256]{1,0:T(8,128)(2,1)S(1)}, u32[]{:S(2)}, u32[]{:S(2)}) collective-permute-start(bf16[512,256]{1,0:T(8,128)(2,1)S(1)} %shard_map.163.refs_0_), channel_id=1, source_target_pairs={{0,8},{4,12},{8,0},{12,4},{16,24},{20,28},{24,16},{28,20},{1,9},{5... | collective-permute-start | bytes 786440 | tf_op jit(solution)/shard_map/ppermute | solution.py:376
  124.5 8.5 %collective-permute-start.38 = (bf16[512,256]{1,0:T(8,128)(2,1)S(1)}, bf16[512,256]{1,0:T(8,128)(2,1)S(1)}, u32[]{:S(2)}, u32[]{:S(2)}) collective-permute-start(bf16[512,256]{1,0:T(8,128)(2,1)S(1)} %shard_map.158.refs_0_), channel_id=1, source_target_pairs={{0,8},{4,12},{8,0},{12,4},{16,24},{20,28},{24,16},{28,20},{1,9},{5... | collective-permute-start | bytes 786440 | tf_op jit(solution)/shard_map/ppermute | solution.py:376
  (31 other events, 188.8 us)

commit v15 on v14

--- a/solution.py
+++ b/solution.py
@@ -68,12 +68,14 @@
     return (down + across == rows - 1).astype(F32).astype(BF16)
 
 
-def input_kernel(place, tokens_hbm, hidden_hbm, embedding_hbm, block_in, first, second, *scratch):
-    padded, tokens, hidden, embedding, semaphores = scratch
-    copies = fetch((tokens_hbm, hidden_hbm, embedding_hbm), (tokens, hidden, embedding), semaphores)
+def input_kernel(place, tokens_hbm, hidden_hbm, embedding_hbm, w_out_hbm, block_in, first, second, w_half, *scratch):
+    padded, tokens, hidden, embedding, w_out, semaphores = scratch
+    copies = fetch(
+        (tokens_hbm, hidden_hbm, embedding_hbm, w_out_hbm), (tokens, hidden, embedding, w_out), semaphores
+    )
     bases, rows = embedding.shape[0], hidden.shape[0]
     padded[...] = jnp.zeros_like(padded)
-    for copy in copies:
+    for copy in copies[:3]:
         copy.wait()
     padded[:bases] = embedding[...].astype(F32)
     base = lax.broadcasted_iota(jnp.int32, (padded.shape[0], rows), 0)
@@ -83,6 +85,8 @@
     odd, far = place[0] % 2, rows - EDGE
     first[...] = block_in[pl.ds(pl.multiple_of((1 - odd) * far, 16), EDGE), :]
     second[...] = block_in[pl.ds(pl.multiple_of(odd * far, 16), EDGE), :]
+    copies[3].wait()
+    w_half[...] = w_out[part(odd, w_half.shape[0]), :]
 
 
 def setup_kernel(width, place, order, choose):
@@ -156,8 +160,12 @@
 
 def norm_grad_kernel(channels, place, *refs):
     own, mirrored = refs[:channels], refs[channels : 2 * channels]
-    *weights, out = refs[2 * channels :]
-    me = place[1]
+    near, near_core, mine, other, mine_core, other_core, out, far, far_core = refs[2 * channels :]
+    me, side, half = place[1], place[0] % 2, mine.shape[0]
+    for whole, first, second in ((far, mine, other), (far_core, mine_core, other_core)):
+        whole[part(side, half), :] = first[...]
+        whole[part(1 - side, half), :] = second[...]
+    weights = (near, near_core, far, far_core)
     rows, width = own[0].shape
     for block, cotangents in enumerate((own, mirrored)):
         for i in range(channels):
@@ -415,15 +423,15 @@
 
     cotangent_x = exchange(cotangent, "ch", cross)
     mirrored_cotangent = mirror(cotangent)
-    inputs = (tokens.reshape(1, rows), hidden, embedding)
-    local_input, first, second = run(
+    inputs = (tokens.reshape(1, rows), hidden, embedding, w_out)
+    local_input, first, second, w_half = run(
         input_kernel,
         place,
         inputs,
-        [block, ((EDGE, width), BF16), ((EDGE, width), BF16)],
+        [block, ((EDGE, width), BF16), ((EDGE, width), BF16), ((full // 2, width), BF16)],
         [pltpu.VMEM((16, width), F32), *fetch_scratch(inputs)],
         megabytes=60,
-        fetched=3,
+        fetched=4,
     )
     input_x = exchange(local_input, "ch", cross)
     input_core = exchange(local_input, "ch", 1)
@@ -436,11 +444,13 @@
     )[0]
     first, second, cotangent_x = together(first, second, cotangent_x)
     near = swap_edges(first, second)
+    mirrored_cotangent, *near = together(mirrored_cotangent, *near)
     near = jnp.concatenate(near, axis=0)
     far = exchange(near, "ch", cross)
-    early_w_out, far = together(w_out, far)
+    w_half, far = together(w_half, far)
+    w_x_mine = exchange(w_half, "ch", cross)
+    w_x_other = exchange(w_x_mine, "seq", 1)
     edges = jnp.concatenate([near, far], axis=0)
-    w_out_x = exchange(early_w_out, "ch", cross)
     mirrored_cotangent = run(flip_kernel, place, (mirrored_cotangent,), [block], gflop=1.0)[0]
     mirrored_cotangent, input_core, choose = together(mirrored_cotangent, input_core, choose)
     mains = [local_input, input_core, input_x, exchange(input_x, "ch", 1)]
@@ -461,7 +471,6 @@
         [pltpu.VMEM((saved_rows(rows, number), width), F32) for number in range(4)],
         gflop=0.4,
     )
-    mirrored_cotangent, w_out_x = together(mirrored_cotangent, w_out_x)
     mirrored_cotangent_x = exchange(mirrored_cotangent, "ch", cross)
     gated_x = exchange(gated, "ch", cross)
     mirrored, mirrored_cotangent_x, gated_x = together(mirror(gated), mirrored_cotangent_x, gated_x)
@@ -483,10 +492,13 @@
             *mirrored_cotangent_all,
             w_out,
             exchange(w_out, "ch", 1),
-            w_out_x,
-            exchange(w_out_x, "ch", 1),
+            w_x_mine,
+            w_x_other,
+            exchange(w_x_mine, "ch", 1),
+            exchange(w_x_other, "ch", 1),
         ),
         [((2 * rows, full), BF16)],
+        [pltpu.VMEM((full, width), BF16)] * 2,
         gflop=2.1,
     )[0]
     mirrored_x, grad_norm = together(mirrored_x, grad_norm)

time: 136 us -> 135 us (level)
  waiting for transfers between devices: 51.5 us -> 49.8 us
    ppermute x37 -> x39, starting transfers between devices: 33.9 us -> 36.8 us  [exchange(): return lax.ppermute(block, axis, [(i, i ^ distance) for i in range(count)])]
    ppermute x37 -> x39, waiting for transfers between devices: 51.2 us -> 49.1 us  [exchange(): return lax.ppermute(block, axis, [(i, i ^ distance) for i in range(count)])]
  transfers between devices with their start and end apart: 43 -> 45, of which waited for: 21 -> 23; matrix products, arithmetic and copies ran while one was open for 0% -> 0% of each run, Pallas kernels for 21% -> 21%
where the time goes in v15:
time: 135 us
  waiting for transfers between devices  49.8 us (37%)
  starting transfers between devices  47.3 us (35%)
  Pallas kernels  35.2 us (26%)
    ppermute x39, waiting for transfers between devices, exchange(): return lax.ppermute(block, axis, [(i, i ^ distance) for i in range(count)])  49.1 us
    ppermute x39, starting transfers between devices, exchange(): return lax.ppermute(block, axis, [(i, i ^ distance) for i in range(count)])  36.8 us
    pallas_call x28, Pallas kernels, run(): pl.pallas_call(body, out_shape=[jax.ShapeDtypeStruct(shape, dtype) for sh...  35.2 us
    ppermute x2, starting transfers between devices, mirror(): lax.ppermute(block, 'seq', [(i, count - 1 - i) for i in range(count)])  5.98 us
    ppermute x4, starting transfers between devices, swap_edges(): received.append(lax.ppermute(block, 'seq', route))  4.46 us
  transfers between devices with their start and end apart: 45, of which 23 were waited for; matrix products, arithmetic and copies ran while one was open for 0% of the time, Pallas kernels for 21%

profile of v15, /device:TPU:0, one launch (start us, length us, event | category | flops | bytes accessed | tf_op | source)
XLA Modules:
  0.0 135.2 jit_solution(15766749424861892445)
XLA Ops:
  0.6 3.0 %collective-permute-start.1 = (bf16[512,256]{1,0:T(8,128)(2,1)}, bf16[512,256]{1,0:T(8,128)(2,1)S(1)}, u32[]{:S(2)}, u32[]{:S(2)}) collective-permute-start(bf16[512,256]{1,0:T(8,128)(2,1)} %cotangent.1), channel_id=1, source_target_pairs={{0,2},{1,3},{2,0},{3,1},{4,6},{5,7},{6,4},{7,5},{8,10},{9,11},{10,... | collective-permute-start | bytes 786440 | tf_op jit(solution)/shard_map/ppermute | solution.py:384
  3.6 4.6 %collective-permute-start = (bf16[512,256]{1,0:T(8,128)(2,1)}, bf16[512,256]{1,0:T(8,128)(2,1)S(1)}, u32[]{:S(2)}, u32[]{:S(2)}) collective-permute-start(bf16[512,256]{1,0:T(8,128)(2,1)} %cotangent.1), channel_id=1, source_target_pairs={{0,28},{4,24},{8,20},{12,16},{16,12},{20,8},{24,4},{28,0},{1,29},{... | collective-permute-start | bytes 786440 | tf_op jit(solution)/shard_map/ppermute | solution.py:393
  8.8 2.8 %shard_map.137 = (bf16[512,256]{1,0:T(8,128)(2,1)}, bf16[160,256]{1,0:T(8,128)(2,1)}, bf16[160,256]{1,0:T(8,128)(2,1)}, bf16[512,256]{1,0:T(8,128)(2,1)}) custom-call(s32[3]{0:T(128)} %pad_add_fusion.place, s32[1,512]{1,0:T(1,128)} %bitcast.7, bf16[512,256]{1,0:T(8,128)(2,1)} %hidden_hbm.1, bf16[4,256]{1,0:T(4,128)(2,1)} %embedding_hbm.1, ...), custom_call_target="tpu_custom_call" | custom-call | flops 100000000 | bytes 790528 | tf_op jit(solution)/shard_map/pallas_call | solution.py:30
  15.9 3.5 %collective-permute-done.7.refs_2_ = bf16[512,256]{1,0:T(8,128)(2,1)S(1)} collective-permute-done((bf16[512,256]{1,0:T(8,128)(2,1)}, bf16[512,256]{1,0:T(8,128)(2,1)S(1)}, u32[]{:S(2)}, u32[]{:S(2)}) %collective-permute-start.7) | collective-permute-done | bytes 262176 | tf_op jit(solution)/shard_map/ppermute | solution.py:384
  22.4 4.0 %collective-permute-done.4 = bf16[320,256]{1,0:T(8,128)(2,1)S(1)} collective-permute-done((bf16[320,256]{1,0:T(8,128)(2,1)S(1)}, bf16[320,256]{1,0:T(8,128)(2,1)S(1)}, u32[]{:S(2)}, u32[]{:S(2)}) %collective-permute-start.4) | collective-permute-done | bytes 163872 | tf_op jit(solution)/shard_map/ppermute | solution.py:384
  33.7 4.0 %collective-permute-done.21.refs_10_ = bf16[512,256]{1,0:T(8,128)(2,1)S(1)} collective-permute-done((bf16[512,256]{1,0:T(8,128)(2,1)S(1)}, bf16[512,256]{1,0:T(8,128)(2,1)S(1)}, u32[]{:S(2)}, u32[]{:S(2)}) %collective-permute-start.21) | collective-permute-done | bytes 262176 | tf_op jit(solution)/shard_map/ppermute | solution.py:384
  37.7 2.3 %collective-permute-start.22 = (bf16[512,256]{1,0:T(8,128)(2,1)S(1)}, bf16[512,256]{1,0:T(8,128)(2,1)S(1)}, u32[]{:S(2)}, u32[]{:S(2)}) collective-permute-start(bf16[512,256]{1,0:T(8,128)(2,1)S(1)} %collective-permute-done.21.refs_10_), channel_id=1, source_target_pairs={{0,4},{4,0},{8,12},{12,8},{16,20},{20,16},{24,28},{28,24},{1,5},{5... | collective-permute-start | bytes 786440 | tf_op jit(solution)/shard_map/ppermute | solution.py:384
  40.0 2.9 %collective-permute-done.12.refs_2_ = bf16[512,256]{1,0:T(8,128)(2,1)S(1)} collective-permute-done((bf16[512,256]{1,0:T(8,128)(2,1)S(1)}, bf16[512,256]{1,0:T(8,128)(2,1)S(1)}, u32[]{:S(2)}, u32[]{:S(2)}) %collective-permute-start.12) | collective-permute-done | bytes 262176 | tf_op jit(solution)/shard_map/ppermute | solution.py:384
  43.7 5.0 %collective-permute-done.22.refs_11_ = bf16[512,256]{1,0:T(8,128)(2,1)S(1)} collective-permute-done((bf16[512,256]{1,0:T(8,128)(2,1)S(1)}, bf16[512,256]{1,0:T(8,128)(2,1)S(1)}, u32[]{:S(2)}, u32[]{:S(2)}) %collective-permute-start.22) | collective-permute-done | bytes 262176 | tf_op jit(solution)/shard_map/ppermute | solution.py:384
  52.4 2.9 %shard_map.143.refs_8_ = bf16[1024,1024]{1,0:T(8,128)(2,1)S(1)} custom-call(s32[3]{0:T(128)S(1)} %copy-done.4, bf16[512,256]{1,0:T(8,128)(2,1)S(1)} %copy-done.2, bf16[512,256]{1,0:T(8,128)(2,1)S(1)} %collective-permute-done.16.refs_1_, bf16[512,256]{1,0:T(8,128)(2,1)S(1)} %collective-permute-done.1.refs_2_, ...), custom_call_target="tpu_custom_call" | custom-call | flops 2100000000 | bytes 4194304 | tf_op jit(solution)/shard_map/pallas_call | solution.py:30
  55.3 3.1 %collective-permute-done.15.refs_6_ = bf16[512,256]{1,0:T(8,128)(2,1)S(1)} collective-permute-done((bf16[512,256]{1,0:T(8,128)(2,1)S(1)}, bf16[512,256]{1,0:T(8,128)(2,1)S(1)}, u32[]{:S(2)}, u32[]{:S(2)}) %collective-permute-start.15) | collective-permute-done | bytes 262176 | tf_op jit(solution)/shard_map/ppermute | solution.py:384
  60.0 5.7 %shard_map.144 = (bf16[1024,1024]{1,0:T(8,128)(2,1)S(1)}, bf16[512,256]{1,0:T(8,128)(2,1)S(1)}, bf16[512,256]{1,0:T(8,128)(2,1)S(1)}, bf16[160,256]{1,0:T(8,128)(2,1)S(1)}, bf16[160,256]{1,0:T(8,128)(2,1)S(1)}) custom-call(s32[3]{0:T(128)S(1)} %copy-done.4, bf16[512,256]{1,0:T(8,128)(2,1)S(1)} %get-tuple-element.76.refs_0_, ...), custom_call_target="tpu_custom_call" | custom-call | flops 2500000000 | bytes 7081984 | tf_op jit(solution)/shard_map/pallas_call | solution.py:30
  65.7 2.5 %collective-permute-start.26 = (bf16[160,256]{1,0:T(8,128)(2,1)S(1)}, bf16[160,256]{1,0:T(8,128)(2,1)S(1)}, u32[]{:S(2)}, u32[]{:S(2)}) collective-permute-start(bf16[160,256]{1,0:T(8,128)(2,1)S(1)} %get-tuple-element.92), channel_id=1, source_target_pairs={{0,4},{4,0},{8,12},{12,8},{16,20},{20,16},{24,28},{28,24},{1,5},{5... | collective-permute-start | bytes 245768 | tf_op jit(solution)/shard_map/ppermute | solution.py:403
  70.9 5.5 %collective-permute-start.28 = (bf16[256,256]{1,0:T(8,128)(2,1)S(1)}, bf16[256,256]{1,0:T(8,128)(2,1)S(1)}, u32[]{:S(2)}, u32[]{:S(2)}) collective-permute-start(bf16[256,256]{1,0:T(8,128)(2,1)S(1)} %get-tuple-element.99), channel_id=1, source_target_pairs={{0,4},{4,0},{8,12},{12,8},{16,20},{20,16},{24,28},{28,24},{1,5},{5... | collective-permute-start | bytes 393224 | tf_op jit(solution)/shard_map/ppermute | solution.py:384
  76.4 2.5 %shard_map.147 = (bf16[576,256]{1,0:T(8,128)(2,1)S(1)}, f32[576,256]{1,0:T(8,128)S(1)}) custom-call(s32[3]{0:T(128)S(1)} %copy-done.4, bf16[512,256]{1,0:T(8,128)(2,1)S(1)} %get-tuple-element.88.upstream, bf16[160,256]{1,0:T(8,128)(2,1)S(1)} %collective-permute-done.26.first, bf16[160,256]{1,0:T(8,128)(2,1)S(1)} %collective-permute-done.27.second, ...), custom_call_target="tpu_custom_call" | custom-call | flops 500000000 | bytes 2609152 | tf_op jit(solution)/shard_map/pallas_call | solution.py:30
  81.4 3.1 %collective-permute-start.30 = (bf16[512,256]{1,0:T(8,128)(2,1)S(1)}, bf16[512,256]{1,0:T(8,128)(2,1)S(1)}, u32[]{:S(2)}, u32[]{:S(2)}) collective-permute-start(bf16[512,256]{1,0:T(8,128)(2,1)S(1)} %get-tuple-element.103), channel_id=1, source_target_pairs={{0,8},{4,12},{8,0},{12,4},{16,24},{20,28},{24,16},{28,20},{1,9},{5... | collective-permute-start | bytes 786440 | tf_op jit(solution)/shard_map/ppermute | solution.py:384
  84.5 2.4 %collective-permute-done.29.refs_1_ = bf16[576,256]{1,0:T(8,128)(2,1)S(1)} collective-permute-done((bf16[576,256]{1,0:T(8,128)(2,1)S(1)}, bf16[576,256]{1,0:T(8,128)(2,1)S(1)}, u32[]{:S(2)}, u32[]{:S(2)}) %collective-permute-start.29) | collective-permute-done | bytes 294944 | tf_op jit(solution)/shard_map/ppermute | solution.py:384
  89.5 2.3 %collective-permute-start.31 = (bf16[288,256]{1,0:T(8,128)(2,1)S(1)}, bf16[288,256]{1,0:T(8,128)(2,1)S(1)}, u32[]{:S(2)}, u32[]{:S(2)}) collective-permute-start(bf16[288,256]{1,0:T(8,128)(2,1)S(1)} %get-tuple-element.104), channel_id=1, source_target_pairs={{0,8},{4,12},{8,0},{12,4},{16,24},{20,28},{24,16},{28,20},{1,9},{5... | collective-permute-start | bytes 442376 | tf_op jit(solution)/shard_map/ppermute | solution.py:384
  92.4 3.9 %collective-permute-done.31.refs_1_ = bf16[288,256]{1,0:T(8,128)(2,1)S(1)} collective-permute-done((bf16[288,256]{1,0:T(8,128)(2,1)S(1)}, bf16[288,256]{1,0:T(8,128)(2,1)S(1)}, u32[]{:S(2)}, u32[]{:S(2)}) %collective-permute-start.31) | collective-permute-done | bytes 147488 | tf_op jit(solution)/shard_map/ppermute | solution.py:384
  97.8 2.7 %collective-permute-start.41 = (bf16[128,256]{1,0:T(8,128)(2,1)S(1)}, bf16[128,256]{1,0:T(8,128)(2,1)S(1)}, u32[]{:S(2)}, u32[]{:S(2)}) collective-permute-start(bf16[128,256]{1,0:T(8,128)(2,1)S(1)} %get-tuple-element.117), channel_id=1, source_target_pairs={{0,16},{4,20},{8,24},{12,28},{16,0},{20,4},{24,8},{28,12},{1,17},{... | collective-permute-start | bytes 196616 | tf_op jit(solution)/shard_map/ppermute | solution.py:384
  103.2 3.1 %collective-permute-done.32.refs_1_ = bf16[144,256]{1,0:T(8,128)(2,1)S(1)} collective-permute-done((bf16[144,256]{1,0:T(8,128)(2,1)S(1)}, bf16[144,256]{1,0:T(8,128)(2,1)S(1)}, u32[]{:S(2)}, u32[]{:S(2)}) %collective-permute-start.32) | collective-permute-done | bytes 73760 | tf_op jit(solution)/shard_map/ppermute | solution.py:384
  107.5 2.9 %collective-permute-start.42 = (bf16[128,256]{1,0:T(8,128)(2,1)S(1)}, bf16[128,256]{1,0:T(8,128)(2,1)S(1)}, u32[]{:S(2)}, u32[]{:S(2)}) collective-permute-start(bf16[128,256]{1,0:T(8,128)(2,1)S(1)} %shard_map.161.refs_0_), channel_id=1, source_target_pairs={{0,16},{4,20},{8,24},{12,28},{16,0},{20,4},{24,8},{28,12},{1,17},{... | collective-permute-start | bytes 196616 | tf_op jit(solution)/shard_map/ppermute | solution.py:384
  111.1 3.7 %collective-permute-done.33.refs_1_ = bf16[144,256]{1,0:T(8,128)(2,1)S(1)} collective-permute-done((bf16[144,256]{1,0:T(8,128)(2,1)S(1)}, bf16[144,256]{1,0:T(8,128)(2,1)S(1)}, u32[]{:S(2)}, u32[]{:S(2)}) %collective-permute-start.33) | collective-permute-done | bytes 73760 | tf_op jit(solution)/shard_map/ppermute | solution.py:384
  117.5 2.7 %collective-permute-start.39 = (bf16[256,256]{1,0:T(8,128)(2,1)S(1)}, bf16[256,256]{1,0:T(8,128)(2,1)S(1)}, u32[]{:S(2)}, u32[]{:S(2)}) collective-permute-start(bf16[256,256]{1,0:T(8,128)(2,1)S(1)} %shard_map.157.refs_0_), channel_id=1, source_target_pairs={{0,16},{4,20},{8,24},{12,28},{16,0},{20,4},{24,8},{28,12},{1,17},{... | collective-permute-start | bytes 393224 | tf_op jit(solution)/shard_map/ppermute | solution.py:384
  (121 shorter events, 53.1 us)
Async XLA Ops:
  0.6 11.5 %collective-permute-start.1 = (bf16[512,256]{1,0:T(8,128)(2,1)}, bf16[512,256]{1,0:T(8,128)(2,1)S(1)}, u32[]{:S(2)}, u32[]{:S(2)}) collective-permute-start(bf16[512,256]{1,0:T(8,128)(2,1)} %cotangent.1), channel_id=1, source_target_pairs={{0,2},{1,3},{2,0},{3,1},{4,6},{5,7},{6,4},{7,5},{8,10},{9,11},{10,... | collective-permute-start | bytes 786440 | tf_op jit(solution)/shard_map/ppermute | solution.py:384
  3.6 11.9 %collective-permute-start = (bf16[512,256]{1,0:T(8,128)(2,1)}, bf16[512,256]{1,0:T(8,128)(2,1)S(1)}, u32[]{:S(2)}, u32[]{:S(2)}) collective-permute-start(bf16[512,256]{1,0:T(8,128)(2,1)} %cotangent.1), channel_id=1, source_target_pairs={{0,28},{4,24},{8,20},{12,16},{16,12},{20,8},{24,4},{28,0},{1,29},{... | collective-permute-start | bytes 786440 | tf_op jit(solution)/shard_map/ppermute | solution.py:393
  11.6 7.8 %collective-permute-start.7 = (bf16[512,256]{1,0:T(8,128)(2,1)}, bf16[512,256]{1,0:T(8,128)(2,1)S(1)}, u32[]{:S(2)}, u32[]{:S(2)}) collective-permute-start(bf16[512,256]{1,0:T(8,128)(2,1)} %get-tuple-element.70.refs_0_.block_in), channel_id=1, source_target_pairs={{0,2},{1,3},{2,0},{3,1},{4,6},{5,7},{6,4},{7,5},{8,10},{9,11},{10,... | collective-permute-start | bytes 786440 | tf_op jit(solution)/shard_map/ppermute | solution.py:384
  12.2 36.6 %collective-permute-start.20 = (bf16[1024,256]{1,0:T(8,128)(2,1)}, bf16[1024,256]{1,0:T(8,128)(2,1)S(1)}, u32[]{:S(2)}, u32[]{:S(2)}) collective-permute-start(bf16[1024,256]{1,0:T(8,128)(2,1)} %w_out.1), channel_id=1, source_target_pairs={{0,1},{1,0},{2,3},{3,2},{4,5},{5,4},{6,7},{7,6},{8,9},{9,8},{10,11... | collective-permute-start | bytes 1572872 | tf_op jit(solution)/shard_map/ppermute | solution.py:384
  19.3 7.7 %collective-permute-start.8 = (bf16[512,256]{1,0:T(8,128)(2,1)S(1)}, bf16[512,256]{1,0:T(8,128)(2,1)S(1)}, u32[]{:S(2)}, u32[]{:S(2)}) collective-permute-start(bf16[512,256]{1,0:T(8,128)(2,1)S(1)} %collective-permute-done.7.refs_2_), channel_id=1, source_target_pairs={{0,1},{1,0},{2,3},{3,2},{4,5},{5,4},{6,7},{7,6},{8,9},{9,8},{10,11... | collective-permute-start | bytes 786440 | tf_op jit(solution)/shard_map/ppermute | solution.py:384
  20.8 12.8 %collective-permute-start.11 = (bf16[512,256]{1,0:T(8,128)(2,1)S(1)}, bf16[512,256]{1,0:T(8,128)(2,1)S(1)}, u32[]{:S(2)}, u32[]{:S(2)}) collective-permute-start(bf16[512,256]{1,0:T(8,128)(2,1)S(1)} %shard_map.138.refs_4_.mirrored_cotangent), channel_id=1, source_target_pairs={{0,2},{1,3},{2,0},{3,1},{4,6},{5,7},{6,4},{7,5},{8,10},{9,11},{10,... | collective-permute-start | bytes 786440 | tf_op jit(solution)/shard_map/ppermute | solution.py:384
  26.4 11.2 %collective-permute-start.21 = (bf16[512,256]{1,0:T(8,128)(2,1)S(1)}, bf16[512,256]{1,0:T(8,128)(2,1)S(1)}, u32[]{:S(2)}, u32[]{:S(2)}) collective-permute-start(bf16[512,256]{1,0:T(8,128)(2,1)S(1)} %copy-done.10), channel_id=1, source_target_pairs={{0,2},{1,3},{2,0},{3,1},{4,6},{5,7},{6,4},{7,5},{8,10},{9,11},{10,... | collective-permute-start | bytes 786440 | tf_op jit(solution)/shard_map/ppermute | solution.py:384
  30.7 12.2 %collective-permute-start.12 = (bf16[512,256]{1,0:T(8,128)(2,1)S(1)}, bf16[512,256]{1,0:T(8,128)(2,1)S(1)}, u32[]{:S(2)}, u32[]{:S(2)}) collective-permute-start(bf16[512,256]{1,0:T(8,128)(2,1)S(1)} %get-tuple-element.76.refs_0_), channel_id=1, source_target_pairs={{0,2},{1,3},{2,0},{3,1},{4,6},{5,7},{6,4},{7,5},{8,10},{9,11},{10,... | collective-permute-start | bytes 786440 | tf_op jit(solution)/shard_map/ppermute | solution.py:384
  32.2 11.0 %collective-permute-start.10 = (bf16[512,256]{1,0:T(8,128)(2,1)S(1)}, bf16[512,256]{1,0:T(8,128)(2,1)S(1)}, u32[]{:S(2)}, u32[]{:S(2)}) collective-permute-start(bf16[512,256]{1,0:T(8,128)(2,1)S(1)} %get-tuple-element.76.refs_0_), channel_id=1, source_target_pairs={{0,28},{4,24},{8,20},{12,16},{16,12},{20,8},{24,4},{28,0},{1,29},{... | collective-permute-start | bytes 786440 | tf_op jit(solution)/shard_map/ppermute | solution.py:393
  33.7 9.7 %collective-permute-start.16 = (bf16[512,256]{1,0:T(8,128)(2,1)S(1)}, bf16[512,256]{1,0:T(8,128)(2,1)S(1)}, u32[]{:S(2)}, u32[]{:S(2)}) collective-permute-start(bf16[512,256]{1,0:T(8,128)(2,1)S(1)} %copy-done.2), channel_id=1, source_target_pairs={{0,1},{1,0},{2,3},{3,2},{4,5},{5,4},{6,7},{7,6},{8,9},{9,8},{10,11... | collective-permute-start | bytes 786440 | tf_op jit(solution)/shard_map/ppermute | solution.py:384
  37.7 11.1 %collective-permute-start.22 = (bf16[512,256]{1,0:T(8,128)(2,1)S(1)}, bf16[512,256]{1,0:T(8,128)(2,1)S(1)}, u32[]{:S(2)}, u32[]{:S(2)}) collective-permute-start(bf16[512,256]{1,0:T(8,128)(2,1)S(1)} %collective-permute-done.21.refs_10_), channel_id=1, source_target_pairs={{0,4},{4,0},{8,12},{12,8},{16,20},{20,16},{24,28},{28,24},{1,5},{5... | collective-permute-start | bytes 786440 | tf_op jit(solution)/shard_map/ppermute | solution.py:384
  43.2 8.6 %collective-permute-start.18 = (bf16[512,256]{1,0:T(8,128)(2,1)S(1)}, bf16[512,256]{1,0:T(8,128)(2,1)S(1)}, u32[]{:S(2)}, u32[]{:S(2)}) collective-permute-start(bf16[512,256]{1,0:T(8,128)(2,1)S(1)} %shard_map.138.refs_4_.mirrored_cotangent), channel_id=1, source_target_pairs={{0,1},{1,0},{2,3},{3,2},{4,5},{5,4},{6,7},{7,6},{8,9},{9,8},{10,11... | collective-permute-start | bytes 786440 | tf_op jit(solution)/shard_map/ppermute | solution.py:384
  43.4 8.4 %collective-permute-start.23 = (bf16[512,256]{1,0:T(8,128)(2,1)S(1)}, bf16[512,256]{1,0:T(8,128)(2,1)S(1)}, u32[]{:S(2)}, u32[]{:S(2)}) collective-permute-start(bf16[512,256]{1,0:T(8,128)(2,1)S(1)} %collective-permute-done.21.refs_10_), channel_id=1, source_target_pairs={{0,1},{1,0},{2,3},{3,2},{4,5},{5,4},{6,7},{7,6},{8,9},{9,8},{10,11... | collective-permute-start | bytes 786440 | tf_op jit(solution)/shard_map/ppermute | solution.py:384
  50.1 8.3 %collective-permute-start.15 = (bf16[512,256]{1,0:T(8,128)(2,1)S(1)}, bf16[512,256]{1,0:T(8,128)(2,1)S(1)}, u32[]{:S(2)}, u32[]{:S(2)}) collective-permute-start(bf16[512,256]{1,0:T(8,128)(2,1)S(1)} %shard_map.142.refs_4_), channel_id=1, source_target_pairs={{0,2},{1,3},{2,0},{3,1},{4,6},{5,7},{6,4},{7,5},{8,10},{9,11},{10,... | collective-permute-start | bytes 786440 | tf_op jit(solution)/shard_map/ppermute | solution.py:384
  70.9 8.4 %collective-permute-start.28 = (bf16[256,256]{1,0:T(8,128)(2,1)S(1)}, bf16[256,256]{1,0:T(8,128)(2,1)S(1)}, u32[]{:S(2)}, u32[]{:S(2)}) collective-permute-start(bf16[256,256]{1,0:T(8,128)(2,1)S(1)} %get-tuple-element.99), channel_id=1, source_target_pairs={{0,4},{4,0},{8,12},{12,8},{16,20},{20,16},{24,28},{28,24},{1,5},{5... | collective-permute-start | bytes 393224 | tf_op jit(solution)/shard_map/ppermute | solution.py:384
  79.4 7.5 %collective-permute-start.29 = (bf16[576,256]{1,0:T(8,128)(2,1)S(1)}, bf16[576,256]{1,0:T(8,128)(2,1)S(1)}, u32[]{:S(2)}, u32[]{:S(2)}) collective-permute-start(bf16[576,256]{1,0:T(8,128)(2,1)S(1)} %get-tuple-element.100), channel_id=1, source_target_pairs={{0,4},{4,0},{8,12},{12,8},{16,20},{20,16},{24,28},{28,24},{1,5},{5... | collective-permute-start | bytes 884744 | tf_op jit(solution)/shard_map/ppermute | solution.py:384
  81.4 8.1 %collective-permute-start.30 = (bf16[512,256]{1,0:T(8,128)(2,1)S(1)}, bf16[512,256]{1,0:T(8,128)(2,1)S(1)}, u32[]{:S(2)}, u32[]{:S(2)}) collective-permute-start(bf16[512,256]{1,0:T(8,128)(2,1)S(1)} %get-tuple-element.103), channel_id=1, source_target_pairs={{0,8},{4,12},{8,0},{12,4},{16,24},{20,28},{24,16},{28,20},{1,9},{5... | collective-permute-start | bytes 786440 | tf_op jit(solution)/shard_map/ppermute | solution.py:384
  92.4 10.1 %collective-permute-start.36 = (bf16[256,256]{1,0:T(8,128)(2,1)S(1)}, bf16[256,256]{1,0:T(8,128)(2,1)S(1)}, u32[]{:S(2)}, u32[]{:S(2)}) collective-permute-start(bf16[256,256]{1,0:T(8,128)(2,1)S(1)} %get-tuple-element.111), channel_id=1, source_target_pairs={{0,16},{4,20},{8,24},{12,28},{16,0},{20,4},{24,8},{28,12},{1,17},{... | collective-permute-start | bytes 393224 | tf_op jit(solution)/shard_map/ppermute | solution.py:384
  96.9 9.3 %collective-permute-start.32 = (bf16[144,256]{1,0:T(8,128)(2,1)S(1)}, bf16[144,256]{1,0:T(8,128)(2,1)S(1)}, u32[]{:S(2)}, u32[]{:S(2)}) collective-permute-start(bf16[144,256]{1,0:T(8,128)(2,1)S(1)} %get-tuple-element.106), channel_id=1, source_target_pairs={{0,16},{4,20},{8,24},{12,28},{16,0},{20,4},{24,8},{28,12},{1,17},{... | collective-permute-start | bytes 221192 | tf_op jit(solution)/shard_map/ppermute | solution.py:384
  97.8 9.1 %collective-permute-start.41 = (bf16[128,256]{1,0:T(8,128)(2,1)S(1)}, bf16[128,256]{1,0:T(8,128)(2,1)S(1)}, u32[]{:S(2)}, u32[]{:S(2)}) collective-permute-start(bf16[128,256]{1,0:T(8,128)(2,1)S(1)} %get-tuple-element.117), channel_id=1, source_target_pairs={{0,16},{4,20},{8,24},{12,28},{16,0},{20,4},{24,8},{28,12},{1,17},{... | collective-permute-start | bytes 196616 | tf_op jit(solution)/shard_map/ppermute | solution.py:384
  106.8 8.0 %collective-permute-start.33 = (bf16[144,256]{1,0:T(8,128)(2,1)S(1)}, bf16[144,256]{1,0:T(8,128)(2,1)S(1)}, u32[]{:S(2)}, u32[]{:S(2)}) collective-permute-start(bf16[144,256]{1,0:T(8,128)(2,1)S(1)} %shard_map.150.refs_0_), channel_id=1, source_target_pairs={{0,16},{4,20},{8,24},{12,28},{16,0},{20,4},{24,8},{28,12},{1,17},{... | collective-permute-start | bytes 221192 | tf_op jit(solution)/shard_map/ppermute | solution.py:384
  107.5 8.7 %collective-permute-start.42 = (bf16[128,256]{1,0:T(8,128)(2,1)S(1)}, bf16[128,256]{1,0:T(8,128)(2,1)S(1)}, u32[]{:S(2)}, u32[]{:S(2)}) collective-permute-start(bf16[128,256]{1,0:T(8,128)(2,1)S(1)} %shard_map.161.refs_0_), channel_id=1, source_target_pairs={{0,16},{4,20},{8,24},{12,28},{16,0},{20,4},{24,8},{28,12},{1,17},{... | collective-permute-start | bytes 196616 | tf_op jit(solution)/shard_map/ppermute | solution.py:384
  117.5 7.4 %collective-permute-start.39 = (bf16[256,256]{1,0:T(8,128)(2,1)S(1)}, bf16[256,256]{1,0:T(8,128)(2,1)S(1)}, u32[]{:S(2)}, u32[]{:S(2)}) collective-permute-start(bf16[256,256]{1,0:T(8,128)(2,1)S(1)} %shard_map.157.refs_0_), channel_id=1, source_target_pairs={{0,16},{4,20},{8,24},{12,28},{16,0},{20,4},{24,8},{28,12},{1,17},{... | collective-permute-start | bytes 393224 | tf_op jit(solution)/shard_map/ppermute | solution.py:384
  122.6 11.3 %collective-permute-start.35 = (bf16[576,256]{1,0:T(8,128)(2,1)S(1)}, bf16[576,256]{1,0:T(8,128)(2,1)S(1)}, u32[]{:S(2)}, u32[]{:S(2)}) collective-permute-start(bf16[576,256]{1,0:T(8,128)(2,1)S(1)} %shard_map.152.refs_0_), channel_id=1, source_target_pairs={{0,4},{4,0},{8,12},{12,8},{16,20},{20,16},{24,28},{28,24},{1,5},{5... | collective-permute-start | bytes 884744 | tf_op jit(solution)/shard_map/ppermute | solution.py:384
  (32 other events, 188.4 us)

commit v16 on v15

--- a/solution.py
+++ b/solution.py
@@ -224,7 +224,7 @@
 
 def products_kernel(channels, place, normalized, cotangent, mirrored_cotangent, grad_gate_pre, *refs):
     mains = refs[:channels]
-    out_sent, out_kept, gate_sent, gate_kept, whole_out, whole_gate = refs[channels:]
+    whole_out, gate_sent, gate_kept, whole_gate = refs[channels:]
     me, side = place[1], (place[0] // 2) % 2
     rows, width = cotangent.shape
     for j in range(channels // 2):
@@ -233,10 +233,6 @@
         whole_out[j * width : (j + 1) * width, :] = dot(
             normalized[:rows, columns], cotangent[...], ROWS_DOT
         ) + dot(normalized[rows:, columns], mirrored_cotangent[...], ROWS_DOT)
-    half = whole_out.shape[0] // 2
-    bit = place[0] % 2
-    out_sent[...] = whole_out[part(1 - bit, half), :].astype(BF16)
-    out_kept[...] = whole_out[part(bit, half), :]
     for j in range(channels):
         whole_gate[part(me ^ j, width), :] = dot(mains[j][...], grad_gate_pre[...], ROWS_DOT)
     half = whole_gate.shape[0] // 2
@@ -298,12 +294,25 @@
     return jnp.where(first, mine, other), jnp.where(first, other, mine)
 
 
+def pair_kernel(place, gate_kept, gate_other, out, sent, kept):
+    gate = gate_kept[...] + gate_other[...].astype(F32)
+    first = jnp.broadcast_to(place[0] % 2, gate.shape) == 0
+    sent[...] = jnp.where(first, out[...], gate).astype(BF16)
+    kept[...] = jnp.where(first, gate, out[...])
+
+
 def step_kernel(plan, place, *refs):
     sources, targets = refs[: 2 * len(plan)], list(refs[2 * len(plan) :])
     for k, (done, after) in enumerate(plan):
         mine, other = sources[2 * k : 2 * k + 2]
         rows = mine.shape[0]
-        if done[0] == "double":
+        if after is not None and after[0] == "pair":
+            bit, half = (place[0] // done[1]) % 2, rows // 2
+            for number in range(2):
+                target = targets.pop(0)
+                target[part(bit, half, 16), :] = mine[number * half : (number + 1) * half]
+                target[part(1 - bit, half, 16), :] = other[number * half : (number + 1) * half]
+        elif done[0] == "double":
             bit = (place[0] // done[1]) % 2
             target = targets.pop(0)
             count = rows - SPARE if after is not None and after[0] == "take" else rows
@@ -336,6 +345,9 @@
             counts.append(2)
         elif after is not None and after[0] == "take":
             outs += [((rows - 2 * SPARE, width), BF16), ((*taps, width), F32)]
+            counts.append(2)
+        elif after is not None and after[0] == "pair":
+            outs += [((rows // 2, width), BF16)] * 2
             counts.append(2)
         else:
             outs.append(((rows, width), BF16))
@@ -513,21 +525,19 @@
         gflop=2.5,
     )
     first, second = swap_edges(first, second)
-    out_sent, out_kept, gate_sent, gate_kept = run(
+    out_half, gate_sent, gate_kept = run(
         functools.partial(products_kernel, channels),
         place,
         (normalized, cotangent, mirrored_cotangent, grad_gate_pre, *mains),
         [
-            ((full // 4, width), BF16),
-            ((full // 4, width), F32),
+            ((full // 2, width), F32),
             ((full // 2, width), BF16),
             ((full // 2, width), F32),
         ],
-        [pltpu.VMEM((full // 2, width), F32), pltpu.VMEM((full, width), F32)],
+        [pltpu.VMEM((full, width), F32)],
         gflop=0.8,
     )
-    out_sent, gate_sent, first, second = together(out_sent, gate_sent, first, second)
-    out_other = exchange(out_sent, "seq", steps[0])
+    gate_sent, first, second = together(gate_sent, first, second)
     gate_other = exchange(gate_sent, "seq", steps[1])
     half = full // 2 + SPARE
     in_sent, in_kept = run(
@@ -550,27 +560,32 @@
 
     down = [("halve", distance) for distance in steps]
     up = [("double", distance) for distance in steps[::-1]]
-    out_down, out_up = down[:1] + down[2:], up[:-2] + up[-1:] + up[-2:-1]
-    gate_down, gate_up = down[1:] + down[:1], up[-1:] + up[:-1]
-    routes = [down + up + [("take",)], gate_down + gate_up + [None], out_down + out_up + [None]]
-    in_sent, out_other = together(in_sent, out_other)
-    results = []
-    for route, sent, kept, other in zip(
-        routes, (in_sent, None, None), (in_kept, gate_kept, out_kept), (None, gate_other, out_other)
-    ):
-        if other is None:
-            other = exchange(sent, "seq", route[0][1])
-        elif len(results) == 1:
-            other = gate_other
-        for number, (done, upcoming) in enumerate(zip(route, route[1:])):
+    both_steps = steps[:1] + steps[2:]
+    both_route = [("halve", distance) for distance in both_steps]
+    both_route += [("double", distance) for distance in [*both_steps[::-1], steps[1]]] + [("pair",)]
+    gate_other, in_kept = together(gate_other, in_kept)
+    half_shape = (full // 2, width)
+    both_sent, both_kept = run(
+        pair_kernel, place, (gate_kept, gate_other, out_half), [(half_shape, BF16), (half_shape, F32)]
+    )
+    in_route = down + up + [("take",)]
+    sums = [[in_route, in_sent, in_kept, None], [both_route, both_sent, both_kept, None]]
+    results = [None, None]
+    for number in range(len(in_route) - 1):
+        for k, (route, sent, kept, _) in enumerate(sums):
+            if results[k] is not None:
+                continue
+            done, upcoming = route[number : number + 2]
+            other = exchange(sent, "seq", done[1])
             prepared = advance(place, [(done, upcoming, kept, other)], conv_w.shape[:2])[0]
-            if upcoming is not None and upcoming[0] != "take":
+            if upcoming[0] in ("halve", "double"):
                 sent, kept = prepared if len(prepared) == 2 else prepared * 2
-                if not results and number == 0:
-                    sent, gate_other = together(sent, gate_other)
-                other = exchange(sent, "seq", upcoming[1])
-        results.append(prepared)
-    (grad_in, grad_conv), (sum_gate,), (sum_out,) = results
+                sums[k] = [route, sent, kept, other]
+            else:
+                results[k] = prepared
+        if number < 3 and results[1] is None:
+            sums[0][1], sums[1][1] = together(sums[0][1], sums[1][1])
+    (grad_in, grad_conv), (sum_gate, sum_out) = results
     return output, grad_in, sum_gate, sum_out, grad_conv
 
 

time: 135 us -> 145 us (1.074)
  waiting for transfers between devices: 49.8 us -> 65.9 us
  Pallas kernels: 35.2 us -> 31.7 us
  starting transfers between devices: 47.3 us -> 44.2 us
    ppermute x39 -> x34, waiting for transfers between devices: 49.1 us -> 65 us  [exchange(): return lax.ppermute(block, axis, [(i, i ^ distance) for i in range(count)])]
    pallas_call x28 -> x23, Pallas kernels: 35.2 us -> 31.7 us  [run(): pl.pallas_call(body, out_shape=[jax.ShapeDtypeStruct(shape, dtype) for sh...]
    ppermute x39 -> x34, starting transfers between devices: 36.8 us -> 33.9 us  [exchange(): return lax.ppermute(block, axis, [(i, i ^ distance) for i in range(count)])]
  transfers between devices with their start and end apart: 45 -> 40, of which waited for: 23 -> 18; matrix products, arithmetic and copies ran while one was open for 0% -> 0% of each run, Pallas kernels for 21% -> 16%
where the time goes in v16:
time: 145 us
  waiting for transfers between devices  65.9 us (45%)
  starting transfers between devices  44.2 us (30%)
  Pallas kernels  31.7 us (22%)
    ppermute x34, waiting for transfers between devices, exchange(): return lax.ppermute(block, axis, [(i, i ^ distance) for i in range(count)])  65 us
    ppermute x34, starting transfers between devices, exchange(): return lax.ppermute(block, axis, [(i, i ^ distance) for i in range(count)])  33.9 us
    pallas_call x23, Pallas kernels, run(): pl.pallas_call(body, out_shape=[jax.ShapeDtypeStruct(shape, dtype) for sh...  31.7 us
    ppermute x2, starting transfers between devices, mirror(): lax.ppermute(block, 'seq', [(i, count - 1 - i) for i in range(count)])  5.87 us
    ppermute x4, starting transfers between devices, swap_edges(): received.append(lax.ppermute(block, 'seq', route))  4.48 us
  transfers between devices with their start and end apart: 40, of which 18 were waited for; matrix products, arithmetic and copies ran while one was open for 0% of the time, Pallas kernels for 16%

profile of v16, /device:TPU:0, one launch (start us, length us, event | category | flops | bytes accessed | tf_op | source)
XLA Modules:
  0.0 144.9 jit_solution(4140170400220000559)
XLA Ops:
  0.6 3.0 %collective-permute-start.1 = (bf16[512,256]{1,0:T(8,128)(2,1)}, bf16[512,256]{1,0:T(8,128)(2,1)S(1)}, u32[]{:S(2)}, u32[]{:S(2)}) collective-permute-start(bf16[512,256]{1,0:T(8,128)(2,1)} %cotangent.1), channel_id=1, source_target_pairs={{0,2},{1,3},{2,0},{3,1},{4,6},{5,7},{6,4},{7,5},{8,10},{9,11},{10,... | collective-permute-start | bytes 786440 | tf_op jit(solution)/shard_map/ppermute | solution.py:396
  3.6 4.6 %collective-permute-start = (bf16[512,256]{1,0:T(8,128)(2,1)}, bf16[512,256]{1,0:T(8,128)(2,1)S(1)}, u32[]{:S(2)}, u32[]{:S(2)}) collective-permute-start(bf16[512,256]{1,0:T(8,128)(2,1)} %cotangent.1), channel_id=1, source_target_pairs={{0,28},{4,24},{8,20},{12,16},{16,12},{20,8},{24,4},{28,0},{1,29},{... | collective-permute-start | bytes 786440 | tf_op jit(solution)/shard_map/ppermute | solution.py:405
  8.9 2.8 %shard_map.137 = (bf16[512,256]{1,0:T(8,128)(2,1)}, bf16[160,256]{1,0:T(8,128)(2,1)}, bf16[160,256]{1,0:T(8,128)(2,1)}, bf16[512,256]{1,0:T(8,128)(2,1)}) custom-call(s32[3]{0:T(128)} %pad_add_fusion.place, s32[1,512]{1,0:T(1,128)} %bitcast.7, bf16[512,256]{1,0:T(8,128)(2,1)} %hidden_hbm.1, bf16[4,256]{1,0:T(4,128)(2,1)} %embedding_hbm.1, ...), custom_call_target="tpu_custom_call" | custom-call | flops 100000000 | bytes 790528 | tf_op jit(solution)/shard_map/pallas_call | solution.py:30
  16.1 3.4 %collective-permute-done.7.refs_2_ = bf16[512,256]{1,0:T(8,128)(2,1)S(1)} collective-permute-done((bf16[512,256]{1,0:T(8,128)(2,1)}, bf16[512,256]{1,0:T(8,128)(2,1)S(1)}, u32[]{:S(2)}, u32[]{:S(2)}) %collective-permute-start.7) | collective-permute-done | bytes 262176 | tf_op jit(solution)/shard_map/ppermute | solution.py:396
  22.5 4.0 %collective-permute-done.4 = bf16[320,256]{1,0:T(8,128)(2,1)S(1)} collective-permute-done((bf16[320,256]{1,0:T(8,128)(2,1)S(1)}, bf16[320,256]{1,0:T(8,128)(2,1)S(1)}, u32[]{:S(2)}, u32[]{:S(2)}) %collective-permute-start.4) | collective-permute-done | bytes 163872 | tf_op jit(solution)/shard_map/ppermute | solution.py:396
  33.7 4.1 %collective-permute-done.21.refs_10_ = bf16[512,256]{1,0:T(8,128)(2,1)S(1)} collective-permute-done((bf16[512,256]{1,0:T(8,128)(2,1)S(1)}, bf16[512,256]{1,0:T(8,128)(2,1)S(1)}, u32[]{:S(2)}, u32[]{:S(2)}) %collective-permute-start.21) | collective-permute-done | bytes 262176 | tf_op jit(solution)/shard_map/ppermute | solution.py:396
  37.8 2.3 %collective-permute-start.22 = (bf16[512,256]{1,0:T(8,128)(2,1)S(1)}, bf16[512,256]{1,0:T(8,128)(2,1)S(1)}, u32[]{:S(2)}, u32[]{:S(2)}) collective-permute-start(bf16[512,256]{1,0:T(8,128)(2,1)S(1)} %collective-permute-done.21.refs_10_), channel_id=1, source_target_pairs={{0,4},{4,0},{8,12},{12,8},{16,20},{20,16},{24,28},{28,24},{1,5},{5... | collective-permute-start | bytes 786440 | tf_op jit(solution)/shard_map/ppermute | solution.py:396
  40.1 2.9 %collective-permute-done.12.refs_2_ = bf16[512,256]{1,0:T(8,128)(2,1)S(1)} collective-permute-done((bf16[512,256]{1,0:T(8,128)(2,1)S(1)}, bf16[512,256]{1,0:T(8,128)(2,1)S(1)}, u32[]{:S(2)}, u32[]{:S(2)}) %collective-permute-start.12) | collective-permute-done | bytes 262176 | tf_op jit(solution)/shard_map/ppermute | solution.py:396
  43.8 5.0 %collective-permute-done.22.refs_11_ = bf16[512,256]{1,0:T(8,128)(2,1)S(1)} collective-permute-done((bf16[512,256]{1,0:T(8,128)(2,1)S(1)}, bf16[512,256]{1,0:T(8,128)(2,1)S(1)}, u32[]{:S(2)}, u32[]{:S(2)}) %collective-permute-start.22) | collective-permute-done | bytes 262176 | tf_op jit(solution)/shard_map/ppermute | solution.py:396
  52.5 2.9 %shard_map.143.refs_8_ = bf16[1024,1024]{1,0:T(8,128)(2,1)S(1)} custom-call(s32[3]{0:T(128)S(1)} %copy-done.4, bf16[512,256]{1,0:T(8,128)(2,1)S(1)} %copy-done.2, bf16[512,256]{1,0:T(8,128)(2,1)S(1)} %collective-permute-done.16.refs_1_, bf16[512,256]{1,0:T(8,128)(2,1)S(1)} %collective-permute-done.1.refs_2_, ...), custom_call_target="tpu_custom_call" | custom-call | flops 2100000000 | bytes 4194304 | tf_op jit(solution)/shard_map/pallas_call | solution.py:30
  55.4 3.1 %collective-permute-done.15.refs_6_ = bf16[512,256]{1,0:T(8,128)(2,1)S(1)} collective-permute-done((bf16[512,256]{1,0:T(8,128)(2,1)S(1)}, bf16[512,256]{1,0:T(8,128)(2,1)S(1)}, u32[]{:S(2)}, u32[]{:S(2)}) %collective-permute-start.15) | collective-permute-done | bytes 262176 | tf_op jit(solution)/shard_map/ppermute | solution.py:396
  60.0 5.8 %shard_map.144 = (bf16[1024,1024]{1,0:T(8,128)(2,1)S(1)}, bf16[512,256]{1,0:T(8,128)(2,1)S(1)}, bf16[512,256]{1,0:T(8,128)(2,1)S(1)}, bf16[160,256]{1,0:T(8,128)(2,1)S(1)}, bf16[160,256]{1,0:T(8,128)(2,1)S(1)}) custom-call(s32[3]{0:T(128)S(1)} %copy-done.4, bf16[512,256]{1,0:T(8,128)(2,1)S(1)} %get-tuple-element.78.refs_0_, ...), custom_call_target="tpu_custom_call" | custom-call | flops 2500000000 | bytes 7081984 | tf_op jit(solution)/shard_map/pallas_call | solution.py:30
  65.8 2.5 %collective-permute-start.26 = (bf16[160,256]{1,0:T(8,128)(2,1)S(1)}, bf16[160,256]{1,0:T(8,128)(2,1)S(1)}, u32[]{:S(2)}, u32[]{:S(2)}) collective-permute-start(bf16[160,256]{1,0:T(8,128)(2,1)S(1)} %get-tuple-element.92), channel_id=1, source_target_pairs={{0,4},{4,0},{8,12},{12,8},{16,20},{20,16},{24,28},{28,24},{1,5},{5... | collective-permute-start | bytes 245768 | tf_op jit(solution)/shard_map/ppermute | solution.py:415
  71.0 6.9 %collective-permute-start.28 = (bf16[512,256]{1,0:T(8,128)(2,1)S(1)}, bf16[512,256]{1,0:T(8,128)(2,1)S(1)}, u32[]{:S(2)}, u32[]{:S(2)}) collective-permute-start(bf16[512,256]{1,0:T(8,128)(2,1)S(1)} %get-tuple-element.94), channel_id=1, source_target_pairs={{0,8},{4,12},{8,0},{12,4},{16,24},{20,28},{24,16},{28,20},{1,9},{5... | collective-permute-start | bytes 786440 | tf_op jit(solution)/shard_map/ppermute | solution.py:396
  77.9 2.5 %shard_map.147 = (bf16[576,256]{1,0:T(8,128)(2,1)S(1)}, f32[576,256]{1,0:T(8,128)S(1)}) custom-call(s32[3]{0:T(128)S(1)} %copy-done.4, bf16[512,256]{1,0:T(8,128)(2,1)S(1)} %get-tuple-element.95.upstream, bf16[160,256]{1,0:T(8,128)(2,1)S(1)} %collective-permute-done.26.first, bf16[160,256]{1,0:T(8,128)(2,1)S(1)} %collective-permute-done.27.second, ...), custom_call_target="tpu_custom_call" | custom-call | flops 500000000 | bytes 2609152 | tf_op jit(solution)/shard_map/pallas_call | solution.py:30
  85.8 4.6 %collective-permute-done.29.refs_1_ = bf16[576,256]{1,0:T(8,128)(2,1)S(1)} collective-permute-done((bf16[576,256]{1,0:T(8,128)(2,1)S(1)}, bf16[576,256]{1,0:T(8,128)(2,1)S(1)}, u32[]{:S(2)}, u32[]{:S(2)}) %collective-permute-start.29) | collective-permute-done | bytes 294944 | tf_op jit(solution)/shard_map/ppermute | solution.py:396
  91.1 3.0 %collective-permute-done.30.refs_1_ = bf16[512,256]{1,0:T(8,128)(2,1)S(1)} collective-permute-done((bf16[512,256]{1,0:T(8,128)(2,1)S(1)}, bf16[512,256]{1,0:T(8,128)(2,1)S(1)}, u32[]{:S(2)}, u32[]{:S(2)}) %collective-permute-start.30) | collective-permute-done | bytes 262176 | tf_op jit(solution)/shard_map/ppermute | solution.py:396
  95.0 2.2 %collective-permute-start.32 = (bf16[256,256]{1,0:T(8,128)(2,1)S(1)}, bf16[256,256]{1,0:T(8,128)(2,1)S(1)}, u32[]{:S(2)}, u32[]{:S(2)}) collective-permute-start(bf16[256,256]{1,0:T(8,128)(2,1)S(1)} %get-tuple-element.114), channel_id=1, source_target_pairs={{0,16},{4,20},{8,24},{12,28},{16,0},{20,4},{24,8},{28,12},{1,17},{... | collective-permute-start | bytes 393224 | tf_op jit(solution)/shard_map/ppermute | solution.py:396
  97.2 5.3 %collective-permute-done.32.refs_1_ = bf16[256,256]{1,0:T(8,128)(2,1)S(1)} collective-permute-done((bf16[256,256]{1,0:T(8,128)(2,1)S(1)}, bf16[256,256]{1,0:T(8,128)(2,1)S(1)}, u32[]{:S(2)}, u32[]{:S(2)}) %collective-permute-start.32) | collective-permute-done | bytes 131104 | tf_op jit(solution)/shard_map/ppermute | solution.py:396
  104.5 2.2 %collective-permute-start.33 = (bf16[144,256]{1,0:T(8,128)(2,1)S(1)}, bf16[144,256]{1,0:T(8,128)(2,1)S(1)}, u32[]{:S(2)}, u32[]{:S(2)}) collective-permute-start(bf16[144,256]{1,0:T(8,128)(2,1)S(1)} %get-tuple-element.115), channel_id=1, source_target_pairs={{0,16},{4,20},{8,24},{12,28},{16,0},{20,4},{24,8},{28,12},{1,17},{... | collective-permute-start | bytes 221192 | tf_op jit(solution)/shard_map/ppermute | solution.py:396
  106.7 6.0 %collective-permute-done.33.refs_1_ = bf16[144,256]{1,0:T(8,128)(2,1)S(1)} collective-permute-done((bf16[144,256]{1,0:T(8,128)(2,1)S(1)}, bf16[144,256]{1,0:T(8,128)(2,1)S(1)}, u32[]{:S(2)}, u32[]{:S(2)}) %collective-permute-start.33) | collective-permute-done | bytes 73760 | tf_op jit(solution)/shard_map/ppermute | solution.py:396
  114.9 5.4 %collective-permute-done.38.refs_1_ = bf16[512,256]{1,0:T(8,128)(2,1)S(1)} collective-permute-done((bf16[512,256]{1,0:T(8,128)(2,1)S(1)}, bf16[512,256]{1,0:T(8,128)(2,1)S(1)}, u32[]{:S(2)}, u32[]{:S(2)}) %collective-permute-start.38) | collective-permute-done | bytes 262176 | tf_op jit(solution)/shard_map/ppermute | solution.py:396
  123.6 10.9 %collective-permute-done.36.refs_1_ = bf16[288,256]{1,0:T(8,128)(2,1)S(1)} collective-permute-done((bf16[288,256]{1,0:T(8,128)(2,1)S(1)}, bf16[288,256]{1,0:T(8,128)(2,1)S(1)}, u32[]{:S(2)}, u32[]{:S(2)}) %collective-permute-start.36) | collective-permute-done | bytes 147488 | tf_op jit(solution)/shard_map/ppermute | solution.py:396
  137.8 4.2 %collective-permute-done.37.refs_1_ = bf16[576,256]{1,0:T(8,128)(2,1)S(1)} collective-permute-done((bf16[576,256]{1,0:T(8,128)(2,1)S(1)}, bf16[576,256]{1,0:T(8,128)(2,1)S(1)}, u32[]{:S(2)}, u32[]{:S(2)}) %collective-permute-start.37) | collective-permute-done | bytes 294944 | tf_op jit(solution)/shard_map/ppermute | solution.py:396
  (106 shorter events, 44.3 us)
Async XLA Ops:
  0.6 11.6 %collective-permute-start.1 = (bf16[512,256]{1,0:T(8,128)(2,1)}, bf16[512,256]{1,0:T(8,128)(2,1)S(1)}, u32[]{:S(2)}, u32[]{:S(2)}) collective-permute-start(bf16[512,256]{1,0:T(8,128)(2,1)} %cotangent.1), channel_id=1, source_target_pairs={{0,2},{1,3},{2,0},{3,1},{4,6},{5,7},{6,4},{7,5},{8,10},{9,11},{10,... | collective-permute-start | bytes 786440 | tf_op jit(solution)/shard_map/ppermute | solution.py:396
  3.6 12.1 %collective-permute-start = (bf16[512,256]{1,0:T(8,128)(2,1)}, bf16[512,256]{1,0:T(8,128)(2,1)S(1)}, u32[]{:S(2)}, u32[]{:S(2)}) collective-permute-start(bf16[512,256]{1,0:T(8,128)(2,1)} %cotangent.1), channel_id=1, source_target_pairs={{0,28},{4,24},{8,20},{12,16},{16,12},{20,8},{24,4},{28,0},{1,29},{... | collective-permute-start | bytes 786440 | tf_op jit(solution)/shard_map/ppermute | solution.py:405
  11.7 7.8 %collective-permute-start.7 = (bf16[512,256]{1,0:T(8,128)(2,1)}, bf16[512,256]{1,0:T(8,128)(2,1)S(1)}, u32[]{:S(2)}, u32[]{:S(2)}) collective-permute-start(bf16[512,256]{1,0:T(8,128)(2,1)} %get-tuple-element.72.refs_0_.block_in), channel_id=1, source_target_pairs={{0,2},{1,3},{2,0},{3,1},{4,6},{5,7},{6,4},{7,5},{8,10},{9,11},{10,... | collective-permute-start | bytes 786440 | tf_op jit(solution)/shard_map/ppermute | solution.py:396
  12.3 36.6 %collective-permute-start.20 = (bf16[1024,256]{1,0:T(8,128)(2,1)}, bf16[1024,256]{1,0:T(8,128)(2,1)S(1)}, u32[]{:S(2)}, u32[]{:S(2)}) collective-permute-start(bf16[1024,256]{1,0:T(8,128)(2,1)} %w_out.1), channel_id=1, source_target_pairs={{0,1},{1,0},{2,3},{3,2},{4,5},{5,4},{6,7},{7,6},{8,9},{9,8},{10,11... | collective-permute-start | bytes 1572872 | tf_op jit(solution)/shard_map/ppermute | solution.py:396
  19.4 7.7 %collective-permute-start.8 = (bf16[512,256]{1,0:T(8,128)(2,1)S(1)}, bf16[512,256]{1,0:T(8,128)(2,1)S(1)}, u32[]{:S(2)}, u32[]{:S(2)}) collective-permute-start(bf16[512,256]{1,0:T(8,128)(2,1)S(1)} %collective-permute-done.7.refs_2_), channel_id=1, source_target_pairs={{0,1},{1,0},{2,3},{3,2},{4,5},{5,4},{6,7},{7,6},{8,9},{9,8},{10,11... | collective-permute-start | bytes 786440 | tf_op jit(solution)/shard_map/ppermute | solution.py:396
  21.0 12.7 %collective-permute-start.11 = (bf16[512,256]{1,0:T(8,128)(2,1)S(1)}, bf16[512,256]{1,0:T(8,128)(2,1)S(1)}, u32[]{:S(2)}, u32[]{:S(2)}) collective-permute-start(bf16[512,256]{1,0:T(8,128)(2,1)S(1)} %shard_map.138.refs_4_.mirrored_cotangent), channel_id=1, source_target_pairs={{0,2},{1,3},{2,0},{3,1},{4,6},{5,7},{6,4},{7,5},{8,10},{9,11},{10,... | collective-permute-start | bytes 786440 | tf_op jit(solution)/shard_map/ppermute | solution.py:396
  26.5 11.2 %collective-permute-start.21 = (bf16[512,256]{1,0:T(8,128)(2,1)S(1)}, bf16[512,256]{1,0:T(8,128)(2,1)S(1)}, u32[]{:S(2)}, u32[]{:S(2)}) collective-permute-start(bf16[512,256]{1,0:T(8,128)(2,1)S(1)} %copy-done.10), channel_id=1, source_target_pairs={{0,2},{1,3},{2,0},{3,1},{4,6},{5,7},{6,4},{7,5},{8,10},{9,11},{10,... | collective-permute-start | bytes 786440 | tf_op jit(solution)/shard_map/ppermute | solution.py:396
  30.8 12.2 %collective-permute-start.12 = (bf16[512,256]{1,0:T(8,128)(2,1)S(1)}, bf16[512,256]{1,0:T(8,128)(2,1)S(1)}, u32[]{:S(2)}, u32[]{:S(2)}) collective-permute-start(bf16[512,256]{1,0:T(8,128)(2,1)S(1)} %get-tuple-element.78.refs_0_), channel_id=1, source_target_pairs={{0,2},{1,3},{2,0},{3,1},{4,6},{5,7},{6,4},{7,5},{8,10},{9,11},{10,... | collective-permute-start | bytes 786440 | tf_op jit(solution)/shard_map/ppermute | solution.py:396
  32.3 11.0 %collective-permute-start.10 = (bf16[512,256]{1,0:T(8,128)(2,1)S(1)}, bf16[512,256]{1,0:T(8,128)(2,1)S(1)}, u32[]{:S(2)}, u32[]{:S(2)}) collective-permute-start(bf16[512,256]{1,0:T(8,128)(2,1)S(1)} %get-tuple-element.78.refs_0_), channel_id=1, source_target_pairs={{0,28},{4,24},{8,20},{12,16},{16,12},{20,8},{24,4},{28,0},{1,29},{... | collective-permute-start | bytes 786440 | tf_op jit(solution)/shard_map/ppermute | solution.py:405
  33.7 9.8 %collective-permute-start.16 = (bf16[512,256]{1,0:T(8,128)(2,1)S(1)}, bf16[512,256]{1,0:T(8,128)(2,1)S(1)}, u32[]{:S(2)}, u32[]{:S(2)}) collective-permute-start(bf16[512,256]{1,0:T(8,128)(2,1)S(1)} %copy-done.2), channel_id=1, source_target_pairs={{0,1},{1,0},{2,3},{3,2},{4,5},{5,4},{6,7},{7,6},{8,9},{9,8},{10,11... | collective-permute-start | bytes 786440 | tf_op jit(solution)/shard_map/ppermute | solution.py:396
  37.8 11.1 %collective-permute-start.22 = (bf16[512,256]{1,0:T(8,128)(2,1)S(1)}, bf16[512,256]{1,0:T(8,128)(2,1)S(1)}, u32[]{:S(2)}, u32[]{:S(2)}) collective-permute-start(bf16[512,256]{1,0:T(8,128)(2,1)S(1)} %collective-permute-done.21.refs_10_), channel_id=1, source_target_pairs={{0,4},{4,0},{8,12},{12,8},{16,20},{20,16},{24,28},{28,24},{1,5},{5... | collective-permute-start | bytes 786440 | tf_op jit(solution)/shard_map/ppermute | solution.py:396
  43.0 7.2 %collective-permute-start.17 = (bf16[512,256]{1,0:T(8,128)(2,1)S(1)}, bf16[512,256]{1,0:T(8,128)(2,1)S(1)}, u32[]{:S(2)}, u32[]{:S(2)}) collective-permute-start(bf16[512,256]{1,0:T(8,128)(2,1)S(1)} %collective-permute-done.1.refs_2_), channel_id=1, source_target_pairs={{0,1},{1,0},{2,3},{3,2},{4,5},{5,4},{6,7},{7,6},{8,9},{9,8},{10,11... | collective-permute-start | bytes 786440 | tf_op jit(solution)/shard_map/ppermute | solution.py:396
  43.3 8.6 %collective-permute-start.18 = (bf16[512,256]{1,0:T(8,128)(2,1)S(1)}, bf16[512,256]{1,0:T(8,128)(2,1)S(1)}, u32[]{:S(2)}, u32[]{:S(2)}) collective-permute-start(bf16[512,256]{1,0:T(8,128)(2,1)S(1)} %shard_map.138.refs_4_.mirrored_cotangent), channel_id=1, source_target_pairs={{0,1},{1,0},{2,3},{3,2},{4,5},{5,4},{6,7},{7,6},{8,9},{9,8},{10,11... | collective-permute-start | bytes 786440 | tf_op jit(solution)/shard_map/ppermute | solution.py:396
  43.5 8.4 %collective-permute-start.23 = (bf16[512,256]{1,0:T(8,128)(2,1)S(1)}, bf16[512,256]{1,0:T(8,128)(2,1)S(1)}, u32[]{:S(2)}, u32[]{:S(2)}) collective-permute-start(bf16[512,256]{1,0:T(8,128)(2,1)S(1)} %collective-permute-done.21.refs_10_), channel_id=1, source_target_pairs={{0,1},{1,0},{2,3},{3,2},{4,5},{5,4},{6,7},{7,6},{8,9},{9,8},{10,11... | collective-permute-start | bytes 786440 | tf_op jit(solution)/shard_map/ppermute | solution.py:396
  50.2 8.3 %collective-permute-start.15 = (bf16[512,256]{1,0:T(8,128)(2,1)S(1)}, bf16[512,256]{1,0:T(8,128)(2,1)S(1)}, u32[]{:S(2)}, u32[]{:S(2)}) collective-permute-start(bf16[512,256]{1,0:T(8,128)(2,1)S(1)} %shard_map.142.refs_4_), channel_id=1, source_target_pairs={{0,2},{1,3},{2,0},{3,1},{4,6},{5,7},{6,4},{7,5},{8,10},{9,11},{10,... | collective-permute-start | bytes 786440 | tf_op jit(solution)/shard_map/ppermute | solution.py:396
  71.0 12.7 %collective-permute-start.28 = (bf16[512,256]{1,0:T(8,128)(2,1)S(1)}, bf16[512,256]{1,0:T(8,128)(2,1)S(1)}, u32[]{:S(2)}, u32[]{:S(2)}) collective-permute-start(bf16[512,256]{1,0:T(8,128)(2,1)S(1)} %get-tuple-element.94), channel_id=1, source_target_pairs={{0,8},{4,12},{8,0},{12,4},{16,24},{20,28},{24,16},{28,20},{1,9},{5... | collective-permute-start | bytes 786440 | tf_op jit(solution)/shard_map/ppermute | solution.py:396
  80.4 10.0 %collective-permute-start.29 = (bf16[576,256]{1,0:T(8,128)(2,1)S(1)}, bf16[576,256]{1,0:T(8,128)(2,1)S(1)}, u32[]{:S(2)}, u32[]{:S(2)}) collective-permute-start(bf16[576,256]{1,0:T(8,128)(2,1)S(1)} %get-tuple-element.101), channel_id=1, source_target_pairs={{0,4},{4,0},{8,12},{12,8},{16,20},{20,16},{24,28},{28,24},{1,5},{5... | collective-permute-start | bytes 884744 | tf_op jit(solution)/shard_map/ppermute | solution.py:396
  84.4 9.7 %collective-permute-start.30 = (bf16[512,256]{1,0:T(8,128)(2,1)S(1)}, bf16[512,256]{1,0:T(8,128)(2,1)S(1)}, u32[]{:S(2)}, u32[]{:S(2)}) collective-permute-start(bf16[512,256]{1,0:T(8,128)(2,1)S(1)} %get-tuple-element.108), channel_id=1, source_target_pairs={{0,4},{4,0},{8,12},{12,8},{16,20},{20,16},{24,28},{28,24},{1,5},{5... | collective-permute-start | bytes 786440 | tf_op jit(solution)/shard_map/ppermute | solution.py:396
  94.7 8.4 %collective-permute-start.31 = (bf16[288,256]{1,0:T(8,128)(2,1)S(1)}, bf16[288,256]{1,0:T(8,128)(2,1)S(1)}, u32[]{:S(2)}, u32[]{:S(2)}) collective-permute-start(bf16[288,256]{1,0:T(8,128)(2,1)S(1)} %get-tuple-element.110), channel_id=1, source_target_pairs={{0,8},{4,12},{8,0},{12,4},{16,24},{20,28},{24,16},{28,20},{1,9},{5... | collective-permute-start | bytes 442376 | tf_op jit(solution)/shard_map/ppermute | solution.py:396
  95.0 7.5 %collective-permute-start.32 = (bf16[256,256]{1,0:T(8,128)(2,1)S(1)}, bf16[256,256]{1,0:T(8,128)(2,1)S(1)}, u32[]{:S(2)}, u32[]{:S(2)}) collective-permute-start(bf16[256,256]{1,0:T(8,128)(2,1)S(1)} %get-tuple-element.114), channel_id=1, source_target_pairs={{0,16},{4,20},{8,24},{12,28},{16,0},{20,4},{24,8},{28,12},{1,17},{... | collective-permute-start | bytes 393224 | tf_op jit(solution)/shard_map/ppermute | solution.py:396
  103.7 9.6 %collective-permute-start.34 = (bf16[256,256]{1,0:T(8,128)(2,1)S(1)}, bf16[256,256]{1,0:T(8,128)(2,1)S(1)}, u32[]{:S(2)}, u32[]{:S(2)}) collective-permute-start(bf16[256,256]{1,0:T(8,128)(2,1)S(1)} %shard_map.152.refs_0_), channel_id=1, source_target_pairs={{0,16},{4,20},{8,24},{12,28},{16,0},{20,4},{24,8},{28,12},{1,17},{... | collective-permute-start | bytes 393224 | tf_op jit(solution)/shard_map/ppermute | solution.py:396
  104.5 8.3 %collective-permute-start.33 = (bf16[144,256]{1,0:T(8,128)(2,1)S(1)}, bf16[144,256]{1,0:T(8,128)(2,1)S(1)}, u32[]{:S(2)}, u32[]{:S(2)}) collective-permute-start(bf16[144,256]{1,0:T(8,128)(2,1)S(1)} %get-tuple-element.115), channel_id=1, source_target_pairs={{0,16},{4,20},{8,24},{12,28},{16,0},{20,4},{24,8},{28,12},{1,17},{... | collective-permute-start | bytes 221192 | tf_op jit(solution)/shard_map/ppermute | solution.py:396
  120.9 22.4 %collective-permute-start.39 = (bf16[1024,256]{1,0:T(8,128)(2,1)S(1)}, bf16[1024,256]{1,0:T(8,128)(2,1)S(1)}, u32[]{:S(2)}, u32[]{:S(2)}) collective-permute-start(bf16[1024,256]{1,0:T(8,128)(2,1)S(1)} %shard_map.158.refs_0_), channel_id=1, source_target_pairs={{0,8},{4,12},{8,0},{12,4},{16,24},{20,28},{24,16},{28,20},{1,9},{5... | collective-permute-start | bytes 1572872 | tf_op jit(solution)/shard_map/ppermute | solution.py:396
  121.6 13.0 %collective-permute-start.36 = (bf16[288,256]{1,0:T(8,128)(2,1)S(1)}, bf16[288,256]{1,0:T(8,128)(2,1)S(1)}, u32[]{:S(2)}, u32[]{:S(2)}) collective-permute-start(bf16[288,256]{1,0:T(8,128)(2,1)S(1)} %shard_map.155.refs_0_), channel_id=1, source_target_pairs={{0,8},{4,12},{8,0},{12,4},{16,24},{20,28},{24,16},{28,20},{1,9},{5... | collective-permute-start | bytes 442376 | tf_op jit(solution)/shard_map/ppermute | solution.py:396
  (27 other events, 154.2 us)

commit v17 on v15

--- a/solution.py
+++ b/solution.py
@@ -553,21 +553,22 @@
     out_down, out_up = down[:1] + down[2:], up[:-2] + up[-1:] + up[-2:-1]
     gate_down, gate_up = down[1:] + down[:1], up[-1:] + up[:-1]
     routes = [down + up + [("take",)], gate_down + gate_up + [None], out_down + out_up + [None]]
-    in_sent, out_other = together(in_sent, out_other)
     results = []
     for route, sent, kept, other in zip(
         routes, (in_sent, None, None), (in_kept, gate_kept, out_kept), (None, gate_other, out_other)
     ):
         if other is None:
             other = exchange(sent, "seq", route[0][1])
-        elif len(results) == 1:
-            other = gate_other
+        elif results:
+            other = gate_other if len(results) == 1 else out_other
         for number, (done, upcoming) in enumerate(zip(route, route[1:])):
             prepared = advance(place, [(done, upcoming, kept, other)], conv_w.shape[:2])[0]
             if upcoming is not None and upcoming[0] != "take":
                 sent, kept = prepared if len(prepared) == 2 else prepared * 2
                 if not results and number == 0:
                     sent, gate_other = together(sent, gate_other)
+                if not results and number == 1:
+                    sent, out_other = together(sent, out_other)
                 other = exchange(sent, "seq", upcoming[1])
         results.append(prepared)
     (grad_in, grad_conv), (sum_gate,), (sum_out,) = results

time: 135 us -> 132 us (0.978)
  waiting for transfers between devices: 49.8 us -> 42.3 us
  starting transfers between devices: 47.3 us -> 51.6 us
    ppermute x39, waiting for transfers between devices: 49.1 us -> 41.6 us  [exchange(): return lax.ppermute(block, axis, [(i, i ^ distance) for i in range(count)])]
    ppermute x39, starting transfers between devices: 36.8 us -> 41.1 us  [exchange(): return lax.ppermute(block, axis, [(i, i ^ distance) for i in range(count)])]
  transfers between devices with their start and end apart: 45 -> 45, of which waited for: 23 -> 22; matrix products, arithmetic and copies ran while one was open for 0% -> 0% of each run, Pallas kernels for 21% -> 19%
where the time goes in v17:
time: 132 us
  starting transfers between devices  51.6 us (39%)
  waiting for transfers between devices  42.3 us (32%)
  Pallas kernels  35.2 us (27%)
  local copies, waits for them, and re-layouts  1.34 us (1%)
    ppermute x39, waiting for transfers between devices, exchange(): return lax.ppermute(block, axis, [(i, i ^ distance) for i in range(count)])  41.6 us
    ppermute x39, starting transfers between devices, exchange(): return lax.ppermute(block, axis, [(i, i ^ distance) for i in range(count)])  41.1 us
    pallas_call x28, Pallas kernels, run(): pl.pallas_call(body, out_shape=[jax.ShapeDtypeStruct(shape, dtype) for sh...  35.2 us
    ppermute x2, starting transfers between devices, mirror(): lax.ppermute(block, 'seq', [(i, count - 1 - i) for i in range(count)])  5.98 us
    ppermute x4, starting transfers between devices, swap_edges(): received.append(lax.ppermute(block, 'seq', route))  4.46 us
  transfers between devices with their start and end apart: 45, of which 22 were waited for; matrix products, arithmetic and copies ran while one was open for 0% of the time, Pallas kernels for 19%

profile of v17, /device:TPU:0, one launch (start us, length us, event | category | flops | bytes accessed | tf_op | source)
XLA Modules:
  0.0 132.0 jit_solution(6985673634278783609)
XLA Ops:
  0.6 3.0 %collective-permute-start.1 = (bf16[512,256]{1,0:T(8,128)(2,1)}, bf16[512,256]{1,0:T(8,128)(2,1)S(1)}, u32[]{:S(2)}, u32[]{:S(2)}) collective-permute-start(bf16[512,256]{1,0:T(8,128)(2,1)} %cotangent.1), channel_id=1, source_target_pairs={{0,2},{1,3},{2,0},{3,1},{4,6},{5,7},{6,4},{7,5},{8,10},{9,11},{10,... | collective-permute-start | bytes 786440 | tf_op jit(solution)/shard_map/ppermute | solution.py:384
  3.6 4.6 %collective-permute-start = (bf16[512,256]{1,0:T(8,128)(2,1)}, bf16[512,256]{1,0:T(8,128)(2,1)S(1)}, u32[]{:S(2)}, u32[]{:S(2)}) collective-permute-start(bf16[512,256]{1,0:T(8,128)(2,1)} %cotangent.1), channel_id=1, source_target_pairs={{0,28},{4,24},{8,20},{12,16},{16,12},{20,8},{24,4},{28,0},{1,29},{... | collective-permute-start | bytes 786440 | tf_op jit(solution)/shard_map/ppermute | solution.py:393
  8.8 2.8 %shard_map.137 = (bf16[512,256]{1,0:T(8,128)(2,1)}, bf16[160,256]{1,0:T(8,128)(2,1)}, bf16[160,256]{1,0:T(8,128)(2,1)}, bf16[512,256]{1,0:T(8,128)(2,1)}) custom-call(s32[3]{0:T(128)} %pad_add_fusion.place, s32[1,512]{1,0:T(1,128)} %bitcast.7, bf16[512,256]{1,0:T(8,128)(2,1)} %hidden_hbm.1, bf16[4,256]{1,0:T(4,128)(2,1)} %embedding_hbm.1, ...), custom_call_target="tpu_custom_call" | custom-call | flops 100000000 | bytes 790528 | tf_op jit(solution)/shard_map/pallas_call | solution.py:30
  15.9 3.5 %collective-permute-done.7.refs_2_ = bf16[512,256]{1,0:T(8,128)(2,1)S(1)} collective-permute-done((bf16[512,256]{1,0:T(8,128)(2,1)}, bf16[512,256]{1,0:T(8,128)(2,1)S(1)}, u32[]{:S(2)}, u32[]{:S(2)}) %collective-permute-start.7) | collective-permute-done | bytes 262176 | tf_op jit(solution)/shard_map/ppermute | solution.py:384
  22.4 4.0 %collective-permute-done.4 = bf16[320,256]{1,0:T(8,128)(2,1)S(1)} collective-permute-done((bf16[320,256]{1,0:T(8,128)(2,1)S(1)}, bf16[320,256]{1,0:T(8,128)(2,1)S(1)}, u32[]{:S(2)}, u32[]{:S(2)}) %collective-permute-start.4) | collective-permute-done | bytes 163872 | tf_op jit(solution)/shard_map/ppermute | solution.py:384
  28.7 2.0 %shard_map.141 = (bf16[2192,256]{1,0:T(8,128)(2,1)S(1)}, bf16[512,256]{1,0:T(8,128)(2,1)S(1)}, bf16[512,256]{1,0:T(8,128)(2,1)S(1)}) custom-call(s32[3]{0:T(128)S(1)} %copy-done.4, bf16[640,256]{1,0:T(8,128)(2,1)S(1)} %constant_dynamic-update-slice_fusion.edges, bf16[640,256]{1,0:T(8,128)(2,1)S(1)} %collective-permute-done.5.edges_core, ...), custom_call_target="tpu_custom_call" | custom-call | flops 400000000 | bytes 2240512 | tf_op jit(solution)/shard_map/pallas_call | solution.py:30
  33.7 4.0 %collective-permute-done.21.refs_10_ = bf16[512,256]{1,0:T(8,128)(2,1)S(1)} collective-permute-done((bf16[512,256]{1,0:T(8,128)(2,1)S(1)}, bf16[512,256]{1,0:T(8,128)(2,1)S(1)}, u32[]{:S(2)}, u32[]{:S(2)}) %collective-permute-start.21) | collective-permute-done | bytes 262176 | tf_op jit(solution)/shard_map/ppermute | solution.py:384
  37.7 2.3 %collective-permute-start.22 = (bf16[512,256]{1,0:T(8,128)(2,1)S(1)}, bf16[512,256]{1,0:T(8,128)(2,1)S(1)}, u32[]{:S(2)}, u32[]{:S(2)}) collective-permute-start(bf16[512,256]{1,0:T(8,128)(2,1)S(1)} %collective-permute-done.21.refs_10_), channel_id=1, source_target_pairs={{0,4},{4,0},{8,12},{12,8},{16,20},{20,16},{24,28},{28,24},{1,5},{5... | collective-permute-start | bytes 786440 | tf_op jit(solution)/shard_map/ppermute | solution.py:384
  40.0 2.9 %collective-permute-done.12.refs_2_ = bf16[512,256]{1,0:T(8,128)(2,1)S(1)} collective-permute-done((bf16[512,256]{1,0:T(8,128)(2,1)S(1)}, bf16[512,256]{1,0:T(8,128)(2,1)S(1)}, u32[]{:S(2)}, u32[]{:S(2)}) %collective-permute-start.12) | collective-permute-done | bytes 262176 | tf_op jit(solution)/shard_map/ppermute | solution.py:384
  43.7 5.0 %collective-permute-done.22.refs_11_ = bf16[512,256]{1,0:T(8,128)(2,1)S(1)} collective-permute-done((bf16[512,256]{1,0:T(8,128)(2,1)S(1)}, bf16[512,256]{1,0:T(8,128)(2,1)S(1)}, u32[]{:S(2)}, u32[]{:S(2)}) %collective-permute-start.22) | collective-permute-done | bytes 262176 | tf_op jit(solution)/shard_map/ppermute | solution.py:384
  52.4 2.9 %shard_map.143.refs_8_ = bf16[1024,1024]{1,0:T(8,128)(2,1)S(1)} custom-call(s32[3]{0:T(128)S(1)} %copy-done.4, bf16[512,256]{1,0:T(8,128)(2,1)S(1)} %copy-done.2, bf16[512,256]{1,0:T(8,128)(2,1)S(1)} %collective-permute-done.16.refs_1_, bf16[512,256]{1,0:T(8,128)(2,1)S(1)} %collective-permute-done.1.refs_2_, ...), custom_call_target="tpu_custom_call" | custom-call | flops 2100000000 | bytes 4194304 | tf_op jit(solution)/shard_map/pallas_call | solution.py:30
  55.3 3.1 %collective-permute-done.15.refs_6_ = bf16[512,256]{1,0:T(8,128)(2,1)S(1)} collective-permute-done((bf16[512,256]{1,0:T(8,128)(2,1)S(1)}, bf16[512,256]{1,0:T(8,128)(2,1)S(1)}, u32[]{:S(2)}, u32[]{:S(2)}) %collective-permute-start.15) | collective-permute-done | bytes 262176 | tf_op jit(solution)/shard_map/ppermute | solution.py:384
  60.0 5.7 %shard_map.144 = (bf16[1024,1024]{1,0:T(8,128)(2,1)S(1)}, bf16[512,256]{1,0:T(8,128)(2,1)S(1)}, bf16[512,256]{1,0:T(8,128)(2,1)S(1)}, bf16[160,256]{1,0:T(8,128)(2,1)S(1)}, bf16[160,256]{1,0:T(8,128)(2,1)S(1)}) custom-call(s32[3]{0:T(128)S(1)} %copy-done.4, bf16[512,256]{1,0:T(8,128)(2,1)S(1)} %get-tuple-element.76.refs_0_, ...), custom_call_target="tpu_custom_call" | custom-call | flops 2500000000 | bytes 7081984 | tf_op jit(solution)/shard_map/pallas_call | solution.py:30
  65.7 2.5 %collective-permute-start.26 = (bf16[160,256]{1,0:T(8,128)(2,1)S(1)}, bf16[160,256]{1,0:T(8,128)(2,1)S(1)}, u32[]{:S(2)}, u32[]{:S(2)}) collective-permute-start(bf16[160,256]{1,0:T(8,128)(2,1)S(1)} %get-tuple-element.92), channel_id=1, source_target_pairs={{0,4},{4,0},{8,12},{12,8},{16,20},{20,16},{24,28},{28,24},{1,5},{5... | collective-permute-start | bytes 245768 | tf_op jit(solution)/shard_map/ppermute | solution.py:403
  70.9 2.5 %shard_map.147 = (bf16[576,256]{1,0:T(8,128)(2,1)S(1)}, f32[576,256]{1,0:T(8,128)S(1)}) custom-call(s32[3]{0:T(128)S(1)} %copy-done.4, bf16[512,256]{1,0:T(8,128)(2,1)S(1)} %get-tuple-element.88.upstream, bf16[160,256]{1,0:T(8,128)(2,1)S(1)} %collective-permute-done.26.first, bf16[160,256]{1,0:T(8,128)(2,1)S(1)} %collective-permute-done.27.second, ...), custom_call_target="tpu_custom_call" | custom-call | flops 500000000 | bytes 2609152 | tf_op jit(solution)/shard_map/pallas_call | solution.py:30
  73.4 5.5 %collective-permute-start.28 = (bf16[576,256]{1,0:T(8,128)(2,1)S(1)}, bf16[576,256]{1,0:T(8,128)(2,1)S(1)}, u32[]{:S(2)}, u32[]{:S(2)}) collective-permute-start(bf16[576,256]{1,0:T(8,128)(2,1)S(1)} %get-tuple-element.98), channel_id=1, source_target_pairs={{0,4},{4,0},{8,12},{12,8},{16,20},{20,16},{24,28},{28,24},{1,5},{5... | collective-permute-start | bytes 884744 | tf_op jit(solution)/shard_map/ppermute | solution.py:384
  78.9 3.1 %collective-permute-start.29 = (bf16[512,256]{1,0:T(8,128)(2,1)S(1)}, bf16[512,256]{1,0:T(8,128)(2,1)S(1)}, u32[]{:S(2)}, u32[]{:S(2)}) collective-permute-start(bf16[512,256]{1,0:T(8,128)(2,1)S(1)} %get-tuple-element.101), channel_id=1, source_target_pairs={{0,8},{4,12},{8,0},{12,4},{16,24},{20,28},{24,16},{28,20},{1,9},{5... | collective-permute-start | bytes 786440 | tf_op jit(solution)/shard_map/ppermute | solution.py:384
  82.1 3.4 %collective-permute-done.28.refs_1_ = bf16[576,256]{1,0:T(8,128)(2,1)S(1)} collective-permute-done((bf16[576,256]{1,0:T(8,128)(2,1)S(1)}, bf16[576,256]{1,0:T(8,128)(2,1)S(1)}, u32[]{:S(2)}, u32[]{:S(2)}) %collective-permute-start.28) | collective-permute-done | bytes 294944 | tf_op jit(solution)/shard_map/ppermute | solution.py:384
  87.0 1.7 %collective-permute-start.30 = (bf16[288,256]{1,0:T(8,128)(2,1)S(1)}, bf16[288,256]{1,0:T(8,128)(2,1)S(1)}, u32[]{:S(2)}, u32[]{:S(2)}) collective-permute-start(bf16[288,256]{1,0:T(8,128)(2,1)S(1)} %get-tuple-element.102), channel_id=1, source_target_pairs={{0,8},{4,12},{8,0},{12,4},{16,24},{20,28},{24,16},{28,20},{1,9},{5... | collective-permute-start | bytes 442376 | tf_op jit(solution)/shard_map/ppermute | solution.py:384
  93.7 2.2 %collective-permute-start.32 = (bf16[144,256]{1,0:T(8,128)(2,1)S(1)}, bf16[144,256]{1,0:T(8,128)(2,1)S(1)}, u32[]{:S(2)}, u32[]{:S(2)}) collective-permute-start(bf16[144,256]{1,0:T(8,128)(2,1)S(1)} %get-tuple-element.106), channel_id=1, source_target_pairs={{0,16},{4,20},{8,24},{12,28},{16,0},{20,4},{24,8},{28,12},{1,17},{... | collective-permute-start | bytes 221192 | tf_op jit(solution)/shard_map/ppermute | solution.py:384
  95.9 2.9 %collective-permute-done.36.refs_1_ = bf16[256,256]{1,0:T(8,128)(2,1)S(1)} collective-permute-done((bf16[256,256]{1,0:T(8,128)(2,1)S(1)}, bf16[256,256]{1,0:T(8,128)(2,1)S(1)}, u32[]{:S(2)}, u32[]{:S(2)}) %collective-permute-start.36) | collective-permute-done | bytes 131104 | tf_op jit(solution)/shard_map/ppermute | solution.py:384
  101.9 2.6 %collective-permute-start.33 = (bf16[144,256]{1,0:T(8,128)(2,1)S(1)}, bf16[144,256]{1,0:T(8,128)(2,1)S(1)}, u32[]{:S(2)}, u32[]{:S(2)}) collective-permute-start(bf16[144,256]{1,0:T(8,128)(2,1)S(1)} %shard_map.150.refs_0_), channel_id=1, source_target_pairs={{0,16},{4,20},{8,24},{12,28},{16,0},{20,4},{24,8},{28,12},{1,17},{... | collective-permute-start | bytes 221192 | tf_op jit(solution)/shard_map/ppermute | solution.py:384
  109.2 2.0 %collective-permute-start.34 = (bf16[288,256]{1,0:T(8,128)(2,1)S(1)}, bf16[288,256]{1,0:T(8,128)(2,1)S(1)}, u32[]{:S(2)}, u32[]{:S(2)}) collective-permute-start(bf16[288,256]{1,0:T(8,128)(2,1)S(1)} %shard_map.151.refs_0_), channel_id=1, source_target_pairs={{0,8},{4,12},{8,0},{12,4},{16,24},{20,28},{24,16},{28,20},{1,9},{5... | collective-permute-start | bytes 442376 | tf_op jit(solution)/shard_map/ppermute | solution.py:384
  123.8 2.6 %collective-permute-done.40.refs_1_ = bf16[512,256]{1,0:T(8,128)(2,1)S(1)} collective-permute-done((bf16[512,256]{1,0:T(8,128)(2,1)S(1)}, bf16[512,256]{1,0:T(8,128)(2,1)S(1)}, u32[]{:S(2)}, u32[]{:S(2)}) %collective-permute-start.40) | collective-permute-done | bytes 262176 | tf_op jit(solution)/shard_map/ppermute | solution.py:384
  (121 shorter events, 54.2 us)
Async XLA Ops:
  0.6 11.5 %collective-permute-start.1 = (bf16[512,256]{1,0:T(8,128)(2,1)}, bf16[512,256]{1,0:T(8,128)(2,1)S(1)}, u32[]{:S(2)}, u32[]{:S(2)}) collective-permute-start(bf16[512,256]{1,0:T(8,128)(2,1)} %cotangent.1), channel_id=1, source_target_pairs={{0,2},{1,3},{2,0},{3,1},{4,6},{5,7},{6,4},{7,5},{8,10},{9,11},{10,... | collective-permute-start | bytes 786440 | tf_op jit(solution)/shard_map/ppermute | solution.py:384
  3.6 11.9 %collective-permute-start = (bf16[512,256]{1,0:T(8,128)(2,1)}, bf16[512,256]{1,0:T(8,128)(2,1)S(1)}, u32[]{:S(2)}, u32[]{:S(2)}) collective-permute-start(bf16[512,256]{1,0:T(8,128)(2,1)} %cotangent.1), channel_id=1, source_target_pairs={{0,28},{4,24},{8,20},{12,16},{16,12},{20,8},{24,4},{28,0},{1,29},{... | collective-permute-start | bytes 786440 | tf_op jit(solution)/shard_map/ppermute | solution.py:393
  11.6 7.8 %collective-permute-start.7 = (bf16[512,256]{1,0:T(8,128)(2,1)}, bf16[512,256]{1,0:T(8,128)(2,1)S(1)}, u32[]{:S(2)}, u32[]{:S(2)}) collective-permute-start(bf16[512,256]{1,0:T(8,128)(2,1)} %get-tuple-element.70.refs_0_.block_in), channel_id=1, source_target_pairs={{0,2},{1,3},{2,0},{3,1},{4,6},{5,7},{6,4},{7,5},{8,10},{9,11},{10,... | collective-permute-start | bytes 786440 | tf_op jit(solution)/shard_map/ppermute | solution.py:384
  12.2 36.6 %collective-permute-start.20 = (bf16[1024,256]{1,0:T(8,128)(2,1)}, bf16[1024,256]{1,0:T(8,128)(2,1)S(1)}, u32[]{:S(2)}, u32[]{:S(2)}) collective-permute-start(bf16[1024,256]{1,0:T(8,128)(2,1)} %w_out.1), channel_id=1, source_target_pairs={{0,1},{1,0},{2,3},{3,2},{4,5},{5,4},{6,7},{7,6},{8,9},{9,8},{10,11... | collective-permute-start | bytes 1572872 | tf_op jit(solution)/shard_map/ppermute | solution.py:384
  12.2 7.2 %collective-permute-start.2 = (bf16[160,256]{1,0:T(8,128)(2,1)}, bf16[160,256]{1,0:T(8,128)(2,1)S(1)}, u32[]{:S(2)}, u32[]{:S(2)}) collective-permute-start(bf16[160,256]{1,0:T(8,128)(2,1)} %get-tuple-element.64), channel_id=1, source_target_pairs={{0,4},{4,0},{8,12},{12,8},{16,20},{20,16},{24,28},{28,24},{1,5},{5... | collective-permute-start | bytes 245768 | tf_op jit(solution)/shard_map/ppermute | solution.py:403
  19.3 7.7 %collective-permute-start.8 = (bf16[512,256]{1,0:T(8,128)(2,1)S(1)}, bf16[512,256]{1,0:T(8,128)(2,1)S(1)}, u32[]{:S(2)}, u32[]{:S(2)}) collective-permute-start(bf16[512,256]{1,0:T(8,128)(2,1)S(1)} %collective-permute-done.7.refs_2_), channel_id=1, source_target_pairs={{0,1},{1,0},{2,3},{3,2},{4,5},{5,4},{6,7},{7,6},{8,9},{9,8},{10,11... | collective-permute-start | bytes 786440 | tf_op jit(solution)/shard_map/ppermute | solution.py:384
  19.4 7.1 %collective-permute-start.4 = (bf16[320,256]{1,0:T(8,128)(2,1)S(1)}, bf16[320,256]{1,0:T(8,128)(2,1)S(1)}, u32[]{:S(2)}, u32[]{:S(2)}) collective-permute-start(bf16[320,256]{1,0:T(8,128)(2,1)S(1)} %pad_maximum_fusion), channel_id=1, source_target_pairs={{0,2},{1,3},{2,0},{3,1},{4,6},{5,7},{6,4},{7,5},{8,10},{9,11},{10,... | collective-permute-start | bytes 491528 | tf_op jit(solution)/shard_map/ppermute | solution.py:384
  20.8 12.8 %collective-permute-start.11 = (bf16[512,256]{1,0:T(8,128)(2,1)S(1)}, bf16[512,256]{1,0:T(8,128)(2,1)S(1)}, u32[]{:S(2)}, u32[]{:S(2)}) collective-permute-start(bf16[512,256]{1,0:T(8,128)(2,1)S(1)} %shard_map.138.refs_4_.mirrored_cotangent), channel_id=1, source_target_pairs={{0,2},{1,3},{2,0},{3,1},{4,6},{5,7},{6,4},{7,5},{8,10},{9,11},{10,... | collective-permute-start | bytes 786440 | tf_op jit(solution)/shard_map/ppermute | solution.py:384
  26.4 11.2 %collective-permute-start.21 = (bf16[512,256]{1,0:T(8,128)(2,1)S(1)}, bf16[512,256]{1,0:T(8,128)(2,1)S(1)}, u32[]{:S(2)}, u32[]{:S(2)}) collective-permute-start(bf16[512,256]{1,0:T(8,128)(2,1)S(1)} %copy-done.10), channel_id=1, source_target_pairs={{0,2},{1,3},{2,0},{3,1},{4,6},{5,7},{6,4},{7,5},{8,10},{9,11},{10,... | collective-permute-start | bytes 786440 | tf_op jit(solution)/shard_map/ppermute | solution.py:384
  30.7 12.2 %collective-permute-start.12 = (bf16[512,256]{1,0:T(8,128)(2,1)S(1)}, bf16[512,256]{1,0:T(8,128)(2,1)S(1)}, u32[]{:S(2)}, u32[]{:S(2)}) collective-permute-start(bf16[512,256]{1,0:T(8,128)(2,1)S(1)} %get-tuple-element.76.refs_0_), channel_id=1, source_target_pairs={{0,2},{1,3},{2,0},{3,1},{4,6},{5,7},{6,4},{7,5},{8,10},{9,11},{10,... | collective-permute-start | bytes 786440 | tf_op jit(solution)/shard_map/ppermute | solution.py:384
  32.2 11.0 %collective-permute-start.10 = (bf16[512,256]{1,0:T(8,128)(2,1)S(1)}, bf16[512,256]{1,0:T(8,128)(2,1)S(1)}, u32[]{:S(2)}, u32[]{:S(2)}) collective-permute-start(bf16[512,256]{1,0:T(8,128)(2,1)S(1)} %get-tuple-element.76.refs_0_), channel_id=1, source_target_pairs={{0,28},{4,24},{8,20},{12,16},{16,12},{20,8},{24,4},{28,0},{1,29},{... | collective-permute-start | bytes 786440 | tf_op jit(solution)/shard_map/ppermute | solution.py:393
  33.7 9.7 %collective-permute-start.16 = (bf16[512,256]{1,0:T(8,128)(2,1)S(1)}, bf16[512,256]{1,0:T(8,128)(2,1)S(1)}, u32[]{:S(2)}, u32[]{:S(2)}) collective-permute-start(bf16[512,256]{1,0:T(8,128)(2,1)S(1)} %copy-done.2), channel_id=1, source_target_pairs={{0,1},{1,0},{2,3},{3,2},{4,5},{5,4},{6,7},{7,6},{8,9},{9,8},{10,11... | collective-permute-start | bytes 786440 | tf_op jit(solution)/shard_map/ppermute | solution.py:384
  37.7 11.1 %collective-permute-start.22 = (bf16[512,256]{1,0:T(8,128)(2,1)S(1)}, bf16[512,256]{1,0:T(8,128)(2,1)S(1)}, u32[]{:S(2)}, u32[]{:S(2)}) collective-permute-start(bf16[512,256]{1,0:T(8,128)(2,1)S(1)} %collective-permute-done.21.refs_10_), channel_id=1, source_target_pairs={{0,4},{4,0},{8,12},{12,8},{16,20},{20,16},{24,28},{28,24},{1,5},{5... | collective-permute-start | bytes 786440 | tf_op jit(solution)/shard_map/ppermute | solution.py:384
  42.9 7.2 %collective-permute-start.17 = (bf16[512,256]{1,0:T(8,128)(2,1)S(1)}, bf16[512,256]{1,0:T(8,128)(2,1)S(1)}, u32[]{:S(2)}, u32[]{:S(2)}) collective-permute-start(bf16[512,256]{1,0:T(8,128)(2,1)S(1)} %collective-permute-done.1.refs_2_), channel_id=1, source_target_pairs={{0,1},{1,0},{2,3},{3,2},{4,5},{5,4},{6,7},{7,6},{8,9},{9,8},{10,11... | collective-permute-start | bytes 786440 | tf_op jit(solution)/shard_map/ppermute | solution.py:384
  43.2 8.6 %collective-permute-start.18 = (bf16[512,256]{1,0:T(8,128)(2,1)S(1)}, bf16[512,256]{1,0:T(8,128)(2,1)S(1)}, u32[]{:S(2)}, u32[]{:S(2)}) collective-permute-start(bf16[512,256]{1,0:T(8,128)(2,1)S(1)} %shard_map.138.refs_4_.mirrored_cotangent), channel_id=1, source_target_pairs={{0,1},{1,0},{2,3},{3,2},{4,5},{5,4},{6,7},{7,6},{8,9},{9,8},{10,11... | collective-permute-start | bytes 786440 | tf_op jit(solution)/shard_map/ppermute | solution.py:384
  43.4 8.4 %collective-permute-start.23 = (bf16[512,256]{1,0:T(8,128)(2,1)S(1)}, bf16[512,256]{1,0:T(8,128)(2,1)S(1)}, u32[]{:S(2)}, u32[]{:S(2)}) collective-permute-start(bf16[512,256]{1,0:T(8,128)(2,1)S(1)} %collective-permute-done.21.refs_10_), channel_id=1, source_target_pairs={{0,1},{1,0},{2,3},{3,2},{4,5},{5,4},{6,7},{7,6},{8,9},{9,8},{10,11... | collective-permute-start | bytes 786440 | tf_op jit(solution)/shard_map/ppermute | solution.py:384
  50.1 8.3 %collective-permute-start.15 = (bf16[512,256]{1,0:T(8,128)(2,1)S(1)}, bf16[512,256]{1,0:T(8,128)(2,1)S(1)}, u32[]{:S(2)}, u32[]{:S(2)}) collective-permute-start(bf16[512,256]{1,0:T(8,128)(2,1)S(1)} %shard_map.142.refs_4_), channel_id=1, source_target_pairs={{0,2},{1,3},{2,0},{3,1},{4,6},{5,7},{6,4},{7,5},{8,10},{9,11},{10,... | collective-permute-start | bytes 786440 | tf_op jit(solution)/shard_map/ppermute | solution.py:384
  73.4 12.0 %collective-permute-start.28 = (bf16[576,256]{1,0:T(8,128)(2,1)S(1)}, bf16[576,256]{1,0:T(8,128)(2,1)S(1)}, u32[]{:S(2)}, u32[]{:S(2)}) collective-permute-start(bf16[576,256]{1,0:T(8,128)(2,1)S(1)} %get-tuple-element.98), channel_id=1, source_target_pairs={{0,4},{4,0},{8,12},{12,8},{16,20},{20,16},{24,28},{28,24},{1,5},{5... | collective-permute-start | bytes 884744 | tf_op jit(solution)/shard_map/ppermute | solution.py:384
  78.9 8.0 %collective-permute-start.29 = (bf16[512,256]{1,0:T(8,128)(2,1)S(1)}, bf16[512,256]{1,0:T(8,128)(2,1)S(1)}, u32[]{:S(2)}, u32[]{:S(2)}) collective-permute-start(bf16[512,256]{1,0:T(8,128)(2,1)S(1)} %get-tuple-element.101), channel_id=1, source_target_pairs={{0,8},{4,12},{8,0},{12,4},{16,24},{20,28},{24,16},{28,20},{1,9},{5... | collective-permute-start | bytes 786440 | tf_op jit(solution)/shard_map/ppermute | solution.py:384
  91.0 7.8 %collective-permute-start.36 = (bf16[256,256]{1,0:T(8,128)(2,1)S(1)}, bf16[256,256]{1,0:T(8,128)(2,1)S(1)}, u32[]{:S(2)}, u32[]{:S(2)}) collective-permute-start(bf16[256,256]{1,0:T(8,128)(2,1)S(1)} %get-tuple-element.111), channel_id=1, source_target_pairs={{0,16},{4,20},{8,24},{12,28},{16,0},{20,4},{24,8},{28,12},{1,17},{... | collective-permute-start | bytes 393224 | tf_op jit(solution)/shard_map/ppermute | solution.py:384
  93.7 7.6 %collective-permute-start.32 = (bf16[144,256]{1,0:T(8,128)(2,1)S(1)}, bf16[144,256]{1,0:T(8,128)(2,1)S(1)}, u32[]{:S(2)}, u32[]{:S(2)}) collective-permute-start(bf16[144,256]{1,0:T(8,128)(2,1)S(1)} %get-tuple-element.106), channel_id=1, source_target_pairs={{0,16},{4,20},{8,24},{12,28},{16,0},{20,4},{24,8},{28,12},{1,17},{... | collective-permute-start | bytes 221192 | tf_op jit(solution)/shard_map/ppermute | solution.py:384
  116.4 14.2 %collective-permute-start.35 = (bf16[576,256]{1,0:T(8,128)(2,1)S(1)}, bf16[576,256]{1,0:T(8,128)(2,1)S(1)}, u32[]{:S(2)}, u32[]{:S(2)}) collective-permute-start(bf16[576,256]{1,0:T(8,128)(2,1)S(1)} %shard_map.152.refs_0_), channel_id=1, source_target_pairs={{0,4},{4,0},{8,12},{12,8},{16,20},{20,16},{24,28},{28,24},{1,5},{5... | collective-permute-start | bytes 884744 | tf_op jit(solution)/shard_map/ppermute | solution.py:384
  119.4 7.1 %collective-permute-start.40 = (bf16[512,256]{1,0:T(8,128)(2,1)S(1)}, bf16[512,256]{1,0:T(8,128)(2,1)S(1)}, u32[]{:S(2)}, u32[]{:S(2)}) collective-permute-start(bf16[512,256]{1,0:T(8,128)(2,1)S(1)} %shard_map.158.refs_0_), channel_id=1, source_target_pairs={{0,8},{4,12},{8,0},{12,4},{16,24},{20,28},{24,16},{28,20},{1,9},{5... | collective-permute-start | bytes 786440 | tf_op jit(solution)/shard_map/ppermute | solution.py:384
  121.3 8.0 %collective-permute-start.44 = (bf16[512,256]{1,0:T(8,128)(2,1)S(1)}, bf16[512,256]{1,0:T(8,128)(2,1)S(1)}, u32[]{:S(2)}, u32[]{:S(2)}) collective-permute-start(bf16[512,256]{1,0:T(8,128)(2,1)S(1)} %shard_map.163.refs_0_), channel_id=1, source_target_pairs={{0,8},{4,12},{8,0},{12,4},{16,24},{20,28},{24,16},{28,20},{1,9},{5... | collective-permute-start | bytes 786440 | tf_op jit(solution)/shard_map/ppermute | solution.py:384
  (32 other events, 181.9 us)
